TPU v7x, 128 devices: a whole 4x4x4 slice. The times are simulated.
128 devices in a mesh: dp: 4 (over y), row: 2 (over core), col: 16 (over z, x).
Axes of the slice: x: 4, y: 4, z: 4, core: 2. Of those that a mesh axis runs over, the one named last changes fastest.
Arguments:
- hidden_in: bfloat16 [32768, 1024], P(('dp', 'col', 'row')), may hold values from -6 to 6
- cotangent: bfloat16 [32768, 1024], P(('dp', 'col', 'row')), may hold values from -6 to 6
- lengths: int32 [64], P(('dp', 'col')), may hold values from 288 to 512, as said below
- routes: int32 [32768, 8], P(('dp', 'col', 'row')), may hold values from 0 to 31, all different within a row
- priority: int32 [128, 2048], P(('dp', 'col', 'row')), may hold values from 0 to 2047, each once within a row
- attn_gain: float32 [1024], replicated, may hold values from 0.5 to 1.5
- query_weight: bfloat16 [1024, 1024], P(('row', 'col')), may hold values from -0.1875 to 0.1875
- key_weight: bfloat16 [1024, 512], P(('row', 'col')), may hold values from -0.1875 to 0.1875
- value_weight: bfloat16 [1024, 512], P(('row', 'col')), may hold values from -0.1875 to 0.1875
- output_weight: bfloat16 [1024, 1024], P(('row', 'col')), may hold values from -1.5 to 1.5
- moe_gain: float32 [1024], replicated, may hold values from 0.5 to 1.5
- router: bfloat16 [1024, 32], replicated, may hold values from -0.09375 to 0.09375
- gate_weight: bfloat16 [32, 1024, 512], P(('row', 'col')), may hold values from -0.1875 to 0.1875
- up_weight: bfloat16 [32, 1024, 512], P(('row', 'col')), may hold values from -0.1875 to 0.1875
- down_weight: bfloat16 [32, 512, 1024], P(('row', 'col')), may hold values from -1 to 1
Outputs:
- hidden_out: bfloat16 [32768, 1024], P(('dp', 'col', 'row'))
- hidden_grad: float32 [32768, 1024], P(('dp', 'col', 'row'))
- attn_gain_grad: float32 [1024], replicated
- query_grad: float32 [1024, 1024], P(('row', 'col'))
- key_grad: float32 [1024, 512], P(('row', 'col'))
- value_grad: float32 [1024, 512], P(('row', 'col'))
- output_grad: float32 [1024, 1024], P(('row', 'col'))
- moe_gain_grad: float32 [1024], replicated
- router_grad: float32 [1024, 32], replicated
- gate_grad: float32 [32, 1024, 512], P(('row', 'col'))
- up_grad: float32 [32, 1024, 512], P(('row', 'col'))
- down_grad: float32 [32, 512, 1024], P(('row', 'col'))
Inputs may be any that keep to these rules, and one draw needn't show every extreme that they name: `lengths`: every sequence holds more than 256 used tokens; some sequence is full and some has the least length. `routes`: each row names 8 different experts. `priority`: each row holds every rank once.
All inputs are finite; a program needn't handle non-finite values.
Results may differ from a plain program's by a relative error of at most 0.025.
Values may be sent and summed in bfloat16 or wider, within the bound.
A program may use at most 192 MiB of HBM per device.

v0:
```python
import jax
import jax.numpy as jnp
from jax import lax
from jax.sharding import PartitionSpec as P

D = 1024
HEADS = 16
HEAD = 64
KV_HEADS = 8
EXPERTS = 32
TOP = 8
CAP = 64


epsilon = 1e-05
rotary_base = 10000.0


def cut_along(array, dim, length):
    dims = array.shape
    tiles = array.reshape(*dims[:dim], length, dims[dim] // length, *dims[dim + 1 :])
    return jnp.moveaxis(tiles, dim, 0)


def joined_along(tiles, dim):
    tiles = jnp.moveaxis(tiles, 0, dim)
    dims = tiles.shape
    return tiles.reshape(*dims[:dim], dims[dim] * dims[dim + 1], *dims[dim + 2 :])


def exchange_both(array, axis, axes, splits, concats):
    sizes = [lax.axis_size(a) for a in axes]
    tiles = cut_along(array, splits[0], sizes[0])
    tiles = jnp.moveaxis(cut_along(tiles, splits[1] + 1, sizes[1]), 0, 1)
    inside = tiles.shape[2:]
    tiles = tiles.reshape(-1, *inside)
    tiles = lax.all_to_all(tiles, axis, split_axis=0, concat_axis=0, tiled=True)
    tiles = joined_along(tiles.reshape(*sizes, *inside), concats[0] + 1)
    return joined_along(tiles, concats[1])


def sent_together(arrays, axis, dim, along):
    widths = [a.shape[along] for a in arrays]
    both = jnp.concatenate(arrays, axis=along)
    whole = lax.all_gather(both, axis, axis=dim, tiled=True)
    return tuple(jnp.split(whole, [sum(widths[:k]) for k in range(1, len(widths))], axis=along))


def summed_on_arrival(array, axis, dim):
    tiles = cut_along(array, dim, lax.axis_size(axis))
    arrived = lax.all_to_all(tiles, axis, split_axis=0, concat_axis=0, tiled=True)
    return arrived.astype(jnp.float32).sum(axis=0)


def in_one_piece(arrays, axis, dim, along):
    widths = [a.shape[along] for a in arrays]
    both = jnp.concatenate(arrays, axis=along)
    whole = summed_on_arrival(both, axis, dim)
    return tuple(jnp.split(whole, [sum(widths[:k]) for k in range(1, len(widths))], axis=along))


def padded_to(lines, length):
    spare = -lines.shape[0] % length
    if not spare:
        return lines
    return jnp.concatenate([lines, jnp.zeros((spare, *lines.shape[1:]), lines.dtype)])


def sum_in_two_steps(array, axis):
    lines = array.reshape(-1, *array.shape[1:][-1:])
    padded = padded_to(lines, lax.axis_size(axis))
    own = lax.psum_scatter(padded, axis, scatter_dimension=0, tiled=True)
    whole = lax.all_gather(own, axis, axis=0, tiled=True)
    return whole[: len(lines)].reshape(array.shape)


def rms_scale(values):
    return lax.rsqrt(jnp.mean(values * values, axis=-1, keepdims=True) + epsilon)


def norm_back(grad_rows, normed_rows, scale_rows, gain_vec):
    scaled = grad_rows * gain_vec
    inner_sum = jnp.mean(scaled * normed_rows, axis=-1, keepdims=True)
    return (
        scale_rows * (scaled - normed_rows * inner_sum),
        jnp.sum(grad_rows * normed_rows, axis=0),
    )


def rotary(values, positions, sign):
    half_dim = values.shape[-1] // 2
    frequency = rotary_base ** (-jnp.arange(half_dim, dtype=jnp.float32) / half_dim)
    angles = positions.astype(jnp.float32)[:, None] * frequency[None, :]
    cosine = jnp.cos(angles)[:, None, :]
    sine_table = jnp.sin(angles)[:, None, :] * sign
    first_half = values[..., :half_dim]
    second_half = values[..., half_dim:]
    return jnp.concatenate(
        [
            first_half * cosine - second_half * sine_table,
            second_half * cosine + first_half * sine_table,
        ],
        axis=-1,
    )


def send_rows(outgoing, row_total, col_total):
    per_device = outgoing.shape[0] // (row_total * col_total)
    cap_rows = outgoing.shape[1]
    width = outgoing.shape[2]
    shaped = outgoing.reshape(row_total, col_total, per_device, 1, 1, cap_rows, width)
    moved = exchange_both(shaped, ("row", "col"), ("row", "col"), (0, 1), (3, 4))
    return moved.reshape(per_device, row_total * col_total * cap_rows, width)


def return_rows(produced, row_total, col_total):
    per_device = produced.shape[0]
    width = produced.shape[2]
    cap_rows = produced.shape[1] // (row_total * col_total)
    shaped = produced.reshape(1, 1, per_device, row_total, col_total, cap_rows, width)
    moved = exchange_both(shaped, ("row", "col"), ("row", "col"), (3, 4), (0, 1))
    return moved.reshape(row_total * col_total * per_device, cap_rows, width)


def on_device(
    hidden_in,
    cotangent,
    lengths,
    routes,
    priority,
    attn_gain,
    query_weight,
    key_weight,
    value_weight,
    output_weight,
    moe_gain,
    router,
    gate_weight,
    up_weight,
    down_weight,
):
    row_total = lax.axis_size("row")
    col_total = lax.axis_size("col")
    tok_count = hidden_in.shape[0]
    seq_len = row_total * tok_count
    groups = HEADS // KV_HEADS
    kv_width = KV_HEADS * HEAD
    score_scale = HEAD ** (-0.5)
    positions = lax.axis_index("row") * tok_count + jnp.arange(tok_count, dtype=jnp.int32)
    seq_length = lengths[0]
    live_rows = positions < seq_length
    live_float = live_rows.astype(jnp.float32)[:, None]
    key_live = jnp.arange(seq_len) < seq_length
    inputs = hidden_in.astype(jnp.float32)
    scale_one = rms_scale(inputs)
    normed_one = inputs * scale_one
    normed = (normed_one * attn_gain).astype(jnp.bfloat16)
    w_query, w_key, w_value, w_out = sent_together(
        (query_weight, key_weight, value_weight, output_weight), ("row", "col"), 0, 1
    )
    query_pre = jnp.dot(normed, w_query, preferred_element_type=jnp.float32).reshape(
        tok_count, HEADS, HEAD
    )
    key_pre = jnp.dot(normed, w_key, preferred_element_type=jnp.float32).reshape(
        tok_count, KV_HEADS, HEAD
    )
    queries = (
        rotary(query_pre, positions, 1.0)
        .astype(jnp.bfloat16)
        .reshape(tok_count, KV_HEADS, groups, HEAD)
    )
    key_rows = rotary(key_pre, positions, 1.0).astype(jnp.bfloat16)
    values = (
        jnp.dot(normed, w_value, preferred_element_type=jnp.float32)
        .astype(jnp.bfloat16)
        .reshape(tok_count, KV_HEADS, HEAD)
    )
    all_keys, all_values = sent_together((key_rows, values), "row", 0, 1)

    def masked_scores():
        raw_scores = (
            jnp.einsum("tkgd,jkd->kgtj", queries, all_keys, preferred_element_type=jnp.float32)
            * score_scale
        )
        return jnp.where(key_live[None, None, None, :], raw_scores, -1000000000.0)

    scores = masked_scores()
    top_score = jnp.max(scores, axis=-1, keepdims=True)
    weights = jnp.exp(scores - top_score)
    totals = jnp.sum(weights, axis=-1, keepdims=True)
    log_total = top_score + jnp.log(totals)
    attn_probs = (weights / totals).astype(jnp.bfloat16)
    mixed_rows = jnp.einsum(
        "kgtj,jkd->tkgd", attn_probs, all_values, preferred_element_type=jnp.float32
    )
    mixed_rows = mixed_rows.reshape(tok_count, D).astype(jnp.bfloat16)
    middle = inputs + jnp.dot(mixed_rows, w_out, preferred_element_type=jnp.float32)
    scale_two = rms_scale(middle)
    normed_two = middle * scale_two
    routed = (normed_two * moe_gain).astype(jnp.bfloat16)
    logits = jnp.dot(routed, router, preferred_element_type=jnp.float32)
    chosen_mask = routes[:, :, None] == jnp.arange(EXPERTS, dtype=jnp.int32)[None, None, :]
    picked = jnp.sum(jnp.where(chosen_mask, logits[:, None, :], 0.0), axis=2)
    picked_exp = jnp.exp(picked - jnp.max(picked, axis=1, keepdims=True))
    gate_values = picked_exp / jnp.sum(picked_exp, axis=1, keepdims=True)
    pair_count = tok_count * TOP
    pair_expert = routes.reshape(pair_count)
    pair_live = jnp.broadcast_to(live_rows[:, None], (tok_count, TOP)).reshape(pair_count)
    rank_ids = priority.reshape(pair_count)
    sequence = (
        jnp.zeros(pair_count, jnp.int32).at[rank_ids].set(jnp.arange(pair_count, dtype=jnp.int32))
    )
    onehot = (
        (pair_expert[:, None] == jnp.arange(EXPERTS, dtype=jnp.int32)[None, :]) & pair_live[:, None]
    ).astype(jnp.int32)
    ordered = onehot[sequence]
    earlier = jnp.cumsum(ordered, axis=0) - ordered
    slot_ordered = jnp.sum(earlier * ordered, axis=1)
    slot_ids = slot_ordered[rank_ids]
    kept_pairs = pair_live & (slot_ids < CAP)
    slot_total = EXPERTS * CAP
    dest_slot = jnp.where(kept_pairs, pair_expert * CAP + slot_ids, slot_total)
    source = (
        jnp.full((slot_total + 1,), pair_count, jnp.int32)
        .at[dest_slot]
        .set(jnp.arange(pair_count, dtype=jnp.int32))[:slot_total]
    )
    source_token = jnp.where(source < pair_count, source // TOP, tok_count)
    padded = jnp.concatenate([routed, jnp.zeros((1, D), jnp.bfloat16)], axis=0)
    outgoing = padded[source_token].reshape(EXPERTS, CAP, D)
    arrived = send_rows(outgoing, row_total, col_total)
    gate_pre = jnp.einsum("erd,edf->erf", arrived, gate_weight, preferred_element_type=jnp.float32)
    up_pre = jnp.einsum("erd,edf->erf", arrived, up_weight, preferred_element_type=jnp.float32)
    gate_sig = jax.nn.sigmoid(gate_pre)
    gate_act = gate_pre * gate_sig
    active = (gate_act * up_pre).astype(jnp.bfloat16)
    produced = jnp.einsum(
        "erf,efd->erd", active, down_weight, preferred_element_type=jnp.float32
    ).astype(jnp.bfloat16)
    returned = return_rows(produced, row_total, col_total)
    returned = jnp.concatenate(
        [returned.reshape(slot_total, D), jnp.zeros((1, D), jnp.bfloat16)], axis=0
    )
    pair_out = returned[dest_slot].reshape(tok_count, TOP, D)
    mixture = jnp.sum(gate_values[:, :, None] * pair_out, axis=1)
    hidden_out = ((middle + mixture) * live_float).astype(jnp.bfloat16)
    grad_out = cotangent.astype(jnp.float32) * live_float
    gate_dot = jnp.sum(pair_out * grad_out[:, None, :], axis=2)
    picked_grad = gate_values * (gate_dot - jnp.sum(gate_values * gate_dot, axis=1, keepdims=True))
    logit_grad = jnp.sum(jnp.where(chosen_mask, picked_grad[:, :, None], 0.0), axis=1)
    router_local = jnp.dot(
        routed.astype(jnp.float32).T, logit_grad, precision=lax.Precision.HIGHEST
    )
    routed_grad = jnp.dot(logit_grad, router.astype(jnp.float32).T, precision=lax.Precision.HIGHEST)
    pair_grad = (
        (gate_values[:, :, None] * grad_out[:, None, :]).astype(jnp.bfloat16).reshape(pair_count, D)
    )
    pair_grad = jnp.concatenate([pair_grad, jnp.zeros((1, D), jnp.bfloat16)], axis=0)
    outgoing_grad = pair_grad[source].reshape(EXPERTS, CAP, D)
    arrived_grad = send_rows(outgoing_grad, row_total, col_total)
    active_grad = jnp.einsum(
        "erd,efd->erf", arrived_grad, down_weight, preferred_element_type=jnp.float32
    ).astype(jnp.bfloat16)
    down_local = jnp.einsum(
        "erf,erd->efd", active, arrived_grad, preferred_element_type=jnp.float32
    )
    gate_pre_grad = (active_grad * up_pre * gate_sig * (1.0 + gate_pre * (1.0 - gate_sig))).astype(
        jnp.bfloat16
    )
    up_pre_grad = (active_grad * gate_act).astype(jnp.bfloat16)
    gate_local = jnp.einsum(
        "erd,erf->edf", arrived, gate_pre_grad, preferred_element_type=jnp.float32
    )
    up_local = jnp.einsum("erd,erf->edf", arrived, up_pre_grad, preferred_element_type=jnp.float32)
    arrived_back = jnp.einsum(
        "erf,edf->erd", gate_pre_grad, gate_weight, preferred_element_type=jnp.float32
    )
    arrived_back = (
        arrived_back
        + jnp.einsum("erf,edf->erd", up_pre_grad, up_weight, preferred_element_type=jnp.float32)
    ).astype(jnp.bfloat16)
    returned_grad = return_rows(arrived_back, row_total, col_total)
    returned_grad = jnp.concatenate(
        [returned_grad.reshape(slot_total, D), jnp.zeros((1, D), jnp.bfloat16)], axis=0
    )
    routed_grad = routed_grad + jnp.sum(
        returned_grad[dest_slot].reshape(tok_count, TOP, D).astype(jnp.float32), axis=1
    )
    middle_norm_grad, moe_gain_local = norm_back(routed_grad, normed_two, scale_two, moe_gain)
    middle_grad = grad_out + middle_norm_grad
    branch_grad = middle_grad.astype(jnp.bfloat16)
    mixed_grad = jnp.einsum("te,de->td", branch_grad, w_out, preferred_element_type=jnp.float32)
    mixed_grad = mixed_grad.astype(jnp.bfloat16).reshape(tok_count, KV_HEADS, groups, HEAD)
    probs_again = jnp.exp(masked_scores() - log_total)
    prob_grad = jnp.einsum(
        "tkgd,jkd->kgtj", mixed_grad, all_values, preferred_element_type=jnp.float32
    )
    value_part = jnp.einsum(
        "kgtj,tkgd->jkd",
        probs_again.astype(jnp.bfloat16),
        mixed_grad,
        preferred_element_type=jnp.float32,
    )
    inner_sum = jnp.sum(probs_again * prob_grad, axis=-1, keepdims=True)
    score_grad = (probs_again * (prob_grad - inner_sum)).astype(jnp.bfloat16)
    query_rot_grad = (
        jnp.einsum("kgtj,jkd->tkgd", score_grad, all_keys, preferred_element_type=jnp.float32)
        * score_scale
    )
    key_part = (
        jnp.einsum("kgtj,tkgd->jkd", score_grad, queries, preferred_element_type=jnp.float32)
        * score_scale
    )
    key_sum, value_sum = in_one_piece(
        (key_part.astype(jnp.bfloat16), value_part.astype(jnp.bfloat16)), "row", 0, 1
    )
    query_pre_grad = (
        rotary(query_rot_grad.reshape(tok_count, HEADS, HEAD), positions, -1.0)
        .reshape(tok_count, D)
        .astype(jnp.bfloat16)
    )
    key_pre_grad = (
        rotary(key_sum, positions, -1.0).reshape(tok_count, kv_width).astype(jnp.bfloat16)
    )
    value_pre_grad = value_sum.reshape(tok_count, kv_width).astype(jnp.bfloat16)
    normed_grad = jnp.einsum(
        "tc,dc->td", query_pre_grad, w_query, preferred_element_type=jnp.float32
    )
    normed_grad = normed_grad + jnp.einsum(
        "tc,dc->td", key_pre_grad, w_key, preferred_element_type=jnp.float32
    )
    normed_grad = normed_grad + jnp.einsum(
        "tc,dc->td", value_pre_grad, w_value, preferred_element_type=jnp.float32
    )
    input_norm_grad, attn_gain_local = norm_back(normed_grad, normed_one, scale_one, attn_gain)
    hidden_grad = middle_grad + input_norm_grad
    qkv_grad = jnp.concatenate([query_pre_grad, key_pre_grad, value_pre_grad], axis=1)
    grad_part = lax.psum_scatter(
        jnp.concatenate(
            [
                jnp.einsum("tr,tc->rc", normed, qkv_grad, preferred_element_type=jnp.float32),
                jnp.einsum(
                    "tr,tc->rc", mixed_rows, branch_grad, preferred_element_type=jnp.float32
                ),
            ],
            axis=1,
        ).astype(jnp.bfloat16),
        ("row", "col"),
        scatter_dimension=0,
        tiled=True,
    )
    grad_shard, gate_sum, up_sum, down_sum = (
        sum_in_two_steps(grad_part, "dp").astype(jnp.float32),
        sum_in_two_steps(gate_local.astype(jnp.bfloat16), "dp").astype(jnp.float32),
        sum_in_two_steps(up_local.astype(jnp.bfloat16), "dp").astype(jnp.float32),
        sum_in_two_steps(down_local.astype(jnp.bfloat16), "dp").astype(jnp.float32),
    )
    attn_gain_sum, moe_gain_sum, router_sum = lax.psum(
        (attn_gain_local, moe_gain_local, router_local), ("dp", "row", "col")
    )
    query_grad = grad_shard[:, :D]
    key_grad = grad_shard[:, D : D + kv_width]
    value_grad = grad_shard[:, D + kv_width : D + 2 * kv_width]
    output_grad = grad_shard[:, D + 2 * kv_width :]
    return (
        hidden_out,
        hidden_grad,
        attn_gain_sum,
        query_grad,
        key_grad,
        value_grad,
        output_grad,
        moe_gain_sum,
        router_sum,
        gate_sum,
        up_sum,
        down_sum,
    )


def solution(mesh):
    return jax.shard_map(
        on_device,
        mesh=mesh,
        in_specs=(
            P(("dp", "col", "row"), None),
            P(("dp", "col", "row"), None),
            P(("dp", "col")),
            P(("dp", "col", "row"), None),
            P(("dp", "col", "row"), None),
            P(),
            P(("row", "col"), None),
            P(("row", "col"), None),
            P(("row", "col"), None),
            P(("row", "col"), None),
            P(),
            P(),
            P(("row", "col"), None, None),
            P(("row", "col"), None, None),
            P(("row", "col"), None, None),
        ),
        out_specs=(
            P(("dp", "col", "row"), None),
            P(("dp", "col", "row"), None),
            P(),
            P(("row", "col"), None),
            P(("row", "col"), None),
            P(("row", "col"), None),
            P(("row", "col"), None),
            P(),
            P(),
            P(("row", "col"), None, None),
            P(("row", "col"), None, None),
            P(("row", "col"), None, None),
        ),
        check_vma=False,
    )
```

profile of v0, /device:TPU:1, one launch (start us, length us, event | category | flops | bytes accessed | tf_op | source)
XLA Modules:
  0.0 704.6 jit_solution(13250766299490302532)
XLA Ops:
  7.2 1.7 pad_maximum_fusion.8
  12.6 8.0 %scatter_custom_fusion = s32[2048]{0:T(1024)S(1)} fusion(s32[2048]{0:T(1024)S(1)} %bitcast.261, s32[2048]{0:T(1024)S(1)} %iota.39, s32[]{:T(128)} %constant.58.clone.1), kind=kCustom, calls=%fused_computation.177 | custom fusion | bytes 8196 | tf_op jit(solution)/shard_map/scatter | solution.py:211
  21.3 5.5 gather_fusion
  27.1 9.1 %reduce-window.6 = s32[32,16,128]{2,1,0:T(8,128)S(1)} reduce-window(s32[32,16,128]{2,1,0:T(8,128)S(1)} %copy.117, s32[]{:T(128)} %constant.58.clone.1), window={size=1x1x128 pad=0_0x0_0x127_0}, to_apply=%region_8.9 | reduce-window | flops 8323072 | bytes 524292 | tf_op jit(solution)/shard_map/reduce-window
  36.9 1.3 copy.147
  38.2 1.6 fusion.56
  39.9 11.8 %gather_fusion.1 = s32[2048]{0:T(1024)S(1)} fusion(s32[2048]{0:T(1024)S(1)} %fusion.56, s32[2048]{0:T(1024)S(1)} %broadcast_clamp_fusion.1), kind=kCustom, calls=%fused_computation.1 | custom fusion | bytes 24576 | tf_op jit(solution)/shard_map/gather | solution.py:219
  51.7 8.6 %scatter_custom_fusion.1 = s32[2049]{0:T(1024)S(1)} fusion(s32[2048]{0:T(1024)S(1)} %bitcast.263, s32[2048]{0:T(1024)S(1)} %iota.40, s32[]{:T(128)} %constant.57.clone.1), kind=kCustom, calls=%fused_computation.172 | custom fusion | bytes 8200 | tf_op jit(solution)/shard_map/scatter | solution.py:226
  61.4 2.5 all-gather.6.cloned.1.call-done
  63.8 1.7 convolution_convert_fusion.7
  65.7 1.8 fusion.76
  70.2 2.6 fusion.25
  72.9 8.6 %all-gather.8.cloned.1.call-done = bf16[512,16,64]{0,2,1:T(8,128)(2,1)} async-done(((bf16[256,16,64]{0,2,1:T(8,128)(2,1)}), bf16[512,16,64]{0,2,1:T(8,128)(2,1)}) %all-gather.8.cloned.1.call-update) | async-done | bytes 1048592 | tf_op jit(solution)/shard_map/all_gather | solution.py:45
  81.5 2.9 bitcast_reduce_fusion
  85.7 2.1 copy-done.2
  87.8 1.6 fusion.37
  89.4 2.6 multiply_reduce_fusion.2
  93.7 1.7 fusion.5
  95.4 2.4 concatenate.57
  97.9 13.8 %gather_fusion.4 = bf16[2048,1024]{1,0:T(8,128)(2,1)} fusion(bf16[2049,1024]{1,0:T(8,128)(2,1)} %concatenate.57, s32[2048]{0:T(1024)S(1)} %copy-done.36), kind=kCustom, calls=%fused_computation.4 | custom fusion | bytes 8396800 | tf_op jit(solution)/shard_map/gather | solution.py:259
  111.7 7.4 %all-to-all-start.2 = ((bf16[32,1,1,1,1,1,64,1024]{7,6,5,4,3,2,1,0:T(8,128)(2,1)}), bf16[32,1,1,1,1,1,64,1024]{7,6,5,4,3,2,1,0:T(8,128)(2,1)}, u32[]{:S(2)}, u32[]{:S(2)}) async-start(bf16[32,1,1,1,1,1,64,1024]{7,6,5,4,3,2,1,0:T(8,128)(2,1)} %bitcast.230), calls=%async_computation.2 | async-start | bytes 8388608 | tf_op jit(solution)/shard_map/all_to_all | solution.py:37
  120.2 10.4 %gather_fusion.2 = bf16[2048,1024]{1,0:T(8,128)(2,1)} fusion(bf16[257,1024]{1,0:T(8,128)(2,1)S(1)} %concatenate.55, s32[2048]{0:T(1024)} %get-tuple-element.40), kind=kCustom, calls=%fused_computation.2 | custom fusion | bytes 8396800 | tf_op jit(solution)/shard_map/gather | solution.py:230
  130.6 43.8 %all-to-all-done.2 = bf16[32,1,1,1,1,1,64,1024]{7,6,5,4,3,2,1,0:T(8,128)(2,1)} async-done(((bf16[32,1,1,1,1,1,64,1024]{7,6,5,4,3,2,1,0:T(8,128)(2,1)}), bf16[32,1,1,1,1,1,64,1024]{7,6,5,4,3,2,1,0:T(8,128)(2,1)}, u32[]{:S(2)}, u32[]{:S(2)}) %all-to-all-start.2) | async-done | bytes 4194336 | tf_op jit(solution)/shard_map/all_to_all | solution.py:37
  174.3 5.1 all-to-all-start
  179.7 6.2 convolution_convert_fusion.2
  185.9 48.8 %all-to-all-done = bf16[32,1,1,1,1,1,64,1024]{7,6,5,4,3,2,1,0:T(8,128)(2,1)} async-done(((bf16[32,1,1,1,1,1,64,1024]{7,6,5,4,3,2,1,0:T(8,128)(2,1)}), bf16[32,1,1,1,1,1,64,1024]{7,6,5,4,3,2,1,0:T(8,128)(2,1)}, u32[]{:S(2)}, u32[]{:S(2)}) %all-to-all-start) | async-done | bytes 4194336 | tf_op jit(solution)/shard_map/all_to_all | solution.py:37
  234.7 5.0 fusion.69
  239.7 7.7 %fusion.12 = (bf16[2048,512]{1,0:T(8,128)(2,1)}, bf16[2048,512]{1,0:T(8,128)(2,1)S(1)}, bf16[2048,512]{1,0:T(8,128)(2,1)}) fusion(bf16[2048,512]{1,0:T(8,128)(2,1)S(1)} %copy-done.52, f32[2048,512]{1,0:T(8,128)S(1)} %fusion.69, bf16[2048,1024]{1,0:T(8,128)(2,1)} %bitcast.29, bf16[1,1024,512]{2,1,0:T(8,128)(2,1)S(1)} %copy-done), kind=kOutput, calls=%fused_computation.35 | convolution fusion | flops 2164260864 | bytes 17825792 | tf_op jit(solution)/shard_map/erd,edf->erf/dot_general | solution.py:233
  248.7 5.5 convolution_convert_fusion.4
  254.3 6.2 convolution_convert_fusion.6
  260.6 6.3 convolution_convert_fusion.1
  266.9 5.1 all-to-all-start.1
  272.1 6.3 convolution_convert_fusion.5
  278.4 7.5 %fusion.67 = f32[2048,1024]{1,0:T(8,128)} fusion(bf16[2048,512]{1,0:T(8,128)(2,1)} %get-tuple-element.22, bf16[1,1024,512]{2,1,0:T(8,128)(2,1)} %param.27), kind=kOutput, calls=%fused_computation.104 | convolution fusion | flops 2147483648 | bytes 11534336 | tf_op jit(solution)/shard_map/erf,edf->erd/dot_general | solution.py:275
  285.9 8.7 %add_convert_fusion = bf16[2048,1024]{1,0:T(8,128)(2,1)} fusion(f32[2048,1024]{1,0:T(8,128)} %fusion.67, bf16[2048,512]{1,0:T(8,128)(2,1)} %get-tuple-element.24, bf16[1,1024,512]{2,1,0:T(8,128)(2,1)S(1)} %copy-done), kind=kOutput, calls=%fused_computation.25 | convolution fusion | flops 2151677952 | bytes 15728640 | tf_op jit(solution)/shard_map/erf,edf->erd/dot_general | solution.py:280
  294.5 32.7 %all-to-all-done.1 = bf16[32,1,1,1,1,1,64,1024]{7,6,5,4,3,2,1,0:T(8,128)(2,1)} async-done(((bf16[32,1,1,1,1,1,64,1024]{7,6,5,4,3,2,1,0:T(8,128)(2,1)}), bf16[32,1,1,1,1,1,64,1024]{7,6,5,4,3,2,1,0:T(8,128)(2,1)}, u32[]{:S(2)}, u32[]{:S(2)}) %all-to-all-start.1) | async-done | bytes 4194336 | tf_op jit(solution)/shard_map/all_to_all | solution.py:37
  327.3 5.3 all-to-all-start.3
  334.1 4.6 concatenate.56
  338.7 14.0 %gather_fusion.3 = bf16[2048,1024]{1,0:T(8,128)(2,1)} fusion(bf16[2049,1024]{1,0:T(8,128)(2,1)} %concatenate.56, s32[2048]{0:T(1024)S(1)} %broadcast_clamp_fusion), kind=kCustom, calls=%fused_computation.3 | custom fusion | bytes 8396800 | tf_op jit(solution)/shard_map/gather | solution.py:244
  352.7 6.1 fusion.1
  359.0 28.8 %all-to-all-done.3 = bf16[32,1,1,1,1,1,64,1024]{7,6,5,4,3,2,1,0:T(8,128)(2,1)} async-done(((bf16[32,1,1,1,1,1,64,1024]{7,6,5,4,3,2,1,0:T(8,128)(2,1)}), bf16[32,1,1,1,1,1,64,1024]{7,6,5,4,3,2,1,0:T(8,128)(2,1)}, u32[]{:S(2)}, u32[]{:S(2)}) %all-to-all-start.3) | async-done | bytes 4194336 | tf_op jit(solution)/shard_map/all_to_all | solution.py:37
  387.8 4.6 concatenate.58
  392.4 14.2 %gather_fusion.5 = bf16[2048,1024]{1,0:T(8,128)(2,1)} fusion(bf16[2049,1024]{1,0:T(8,128)(2,1)} %concatenate.58, s32[2048]{0:T(1024)S(1)} %broadcast_clamp_fusion), kind=kCustom, calls=%fused_computation.5 | custom fusion | bytes 8396800 | tf_op jit(solution)/shard_map/gather | solution.py:287
  406.6 5.6 convert_reduce_fusion
  414.5 2.7 fusion.38
  417.5 4.9 fusion.46
  422.4 5.4 fusion.2
  427.9 1.8 fusion.4
  429.7 1.4 fusion.45
  431.3 4.6 all_to_all.25
  438.1 1.5 convolution_convert_fusion
  439.6 3.2 pad_maximum_fusion
  442.9 2.8 bitcast_convert_fusion
  445.7 2.8 bitcast_convert_fusion.2
  448.5 2.9 bitcast_convert_fusion.1
  451.4 2.5 fusion.23
  453.9 1.9 convolution_add_fusion.2
  455.8 2.9 fusion.54
  458.7 67.9 %reduce-scatter.6.cloned.1.call-done = bf16[32,3072]{1,0:T(8,128)(2,1)} async-done(((bf16[1024,3072]{1,0:T(8,128)(2,1)}), bf16[32,3072]{1,0:T(8,128)(2,1)}) %reduce-scatter.6.cloned.1.call-update) | async-done | bytes 196624 | tf_op jit(solution)/shard_map/reduce_scatter | solution.py:338
  527.7 66.3 %all-reduce.4 = (f32[1024]{0:T(1024)}, f32[1024]{0:T(1024)}) all-reduce(f32[1024]{0:T(1024)S(1)} %get-tuple-element.16, f32[1024]{0:T(1024)S(1)} %get-tuple-element.14), channel_id=1, replica_groups=mesh['dp'=4,'row'=2,'col'=16] {'dp','row','col'}, use_global_device_ids=true, to_apply=%region_22.23 | all-reduce | flops 2048 | bytes 16384 | tf_op jit(solution)/shard_map/psum | solution.py:358
  594.0 2.5 fusion.53
  596.4 10.2 %all_gather.20 = bf16[32,3072]{1,0:T(8,128)(2,1)S(1)} all-gather(bf16[8,3072]{1,0:T(8,128)(2,1)} %reduce-scatter.8.cloned.1.call-done), channel_id=1, replica_groups=mesh['dp'=4,'row'=2,'col'=16] {'dp'}, dimensions={0}, use_global_device_ids=true | all-gather | bytes 245760 | tf_op jit(solution)/shard_map/all_gather | solution.py:73
  608.0 88.3 %all-reduce.7.cloned.1.call-done = f32[1024,32]{0,1:T(8,128)} async-done(((f32[1024,32]{0,1:T(8,128)}), f32[1024,32]{0,1:T(8,128)}) %all-reduce.7.cloned.1.call-update) | async-done | bytes 131088 | tf_op jit(solution)/shard_map/psum | solution.py:358
  696.3 1.6 copy.153
  (207 shorter events, 23.4 us)
Async XLA Ops:
  7.2 232.5 %copy-start = (bf16[1,1024,512]{2,1,0:T(8,128)(2,1)S(1)}, bf16[1,1024,512]{2,1,0:T(8,128)(2,1)}, u32[]{:S(2)}) copy-start(bf16[1,1024,512]{2,1,0:T(8,128)(2,1)} %param.28) | copy-start | bytes 3145732
  7.2 56.6 %all-gather.6.cloned.1.call-start = ((), (), s32[]{:S(2)}) async-start(), calls=%async_computation.10 | async-start | bytes 6488064 | tf_op jit(solution)/shard_map/all_gather | solution.py:45
  8.9 72.6 %all-gather.8.cloned.1.call-start = ((), (), s32[]{:S(2)}) async-start(), calls=%async_computation.11 | async-start | bytes 1572864 | tf_op jit(solution)/shard_map/all_gather | solution.py:45
  9.7 59.4 %copy-start.47 = (f32[256]{0:T(256)}, f32[256]{0:T(256)S(1)}, u32[]{:S(2)}) copy-start(f32[256]{0:T(256)S(1)} %get-tuple-element.20) | copy-start | bytes 3076
  39.8 20.5 %copy-start.6 = (bf16[256,1024]{1,0:T(8,128)(2,1)S(1)}, bf16[256,1024]{1,0:T(8,128)(2,1)}, u32[]{:S(2)}) copy-start(bf16[256,1024]{1,0:T(8,128)(2,1)} %param.15) | copy-start | bytes 1572868
  39.8 24.0 %copy-start.45 = (f32[1024]{0:T(1024)S(1)}, f32[1024]{0:T(1024)}, u32[]{:S(2)}) copy-start(f32[1024]{0:T(1024)} %param.20) | copy-start | bytes 12292
  51.7 16.7 %copy-start.37 = (s32[2048,1]{0,1:T(1,128)}, s32[2048,1]{0,1:T(1,128)S(1)}, u32[]{:S(2)}) copy-start(s32[2048,1]{0,1:T(1,128)S(1)} %compare_select_fusion) | copy-start | bytes 24580
  60.5 9.6 %copy-start.49 = (f32[256]{0:T(256)}, f32[256]{0:T(256)S(1)}, u32[]{:S(2)}) copy-start(f32[256]{0:T(256)S(1)} %add_rsqrt_fusion.1) | copy-start | bytes 3076
  61.4 11.4 %copy-start.20 = (f32[256,32]{0,1:T(8,128)}, f32[256,32]{0,1:T(8,128)S(1)}, u32[]{:S(2)}) copy-start(f32[256,32]{0,1:T(8,128)S(1)} %get-tuple-element.43) | copy-start | bytes 98308
  61.4 7.7 %copy-start.16 = (bf16[256,1024]{1,0:T(8,128)(2,1)S(1)}, bf16[256,1024]{1,0:T(8,128)(2,1)}, u32[]{:S(2)}) copy-start(bf16[256,1024]{1,0:T(8,128)(2,1)} %param.16) | copy-start | bytes 1572868
  72.9 11.5 %copy-start.12 = (bf16[256,16,32]{0,2,1:T(8,128)(2,1)}, bf16[256,16,32]{0,2,1:T(8,128)(2,1)S(1)}, u32[]{:S(2)}) copy-start(bf16[256,16,32]{0,2,1:T(8,128)(2,1)S(1)} %get-tuple-element.30) | copy-start | bytes 786436
  84.4 3.3 copy-start.2
  84.5 3.4 copy-start.28
  84.5 3.3 copy-start.10
  89.4 3.9 copy-start.14
  89.4 2.7 copy-start.34
  89.4 3.6 copy-start.25
  89.4 3.9 copy-start.30
  92.1 5.8 copy-start.43
  93.4 4.5 copy-start.22
  93.4 4.5 copy-start.39
  93.5 4.4 copy-start.41
  95.4 2.5 copy-start.36
  111.7 62.6 %all-to-all-start.2 = ((bf16[32,1,1,1,1,1,64,1024]{7,6,5,4,3,2,1,0:T(8,128)(2,1)}), bf16[32,1,1,1,1,1,64,1024]{7,6,5,4,3,2,1,0:T(8,128)(2,1)}, u32[]{:S(2)}, u32[]{:S(2)}) async-start(bf16[32,1,1,1,1,1,64,1024]{7,6,5,4,3,2,1,0:T(8,128)(2,1)} %bitcast.230), calls=%async_computation.2 | async-start | bytes 8388608 | tf_op jit(solution)/shard_map/all_to_all | solution.py:37
  174.3 60.4 %all-to-all-start = ((bf16[32,1,1,1,1,1,64,1024]{7,6,5,4,3,2,1,0:T(8,128)(2,1)}), bf16[32,1,1,1,1,1,64,1024]{7,6,5,4,3,2,1,0:T(8,128)(2,1)}, u32[]{:S(2)}, u32[]{:S(2)}) async-start(bf16[32,1,1,1,1,1,64,1024]{7,6,5,4,3,2,1,0:T(8,128)(2,1)} %bitcast.229), calls=%async_computation | async-start | bytes 8388608 | tf_op jit(solution)/shard_map/all_to_all | solution.py:37
  179.5 106.4 %reduce-scatter.14.cloned.1.call-start = ((), (), s32[]{:S(2)}) async-start(), calls=%async_computation.19 | async-start | bytes 1310720 | tf_op jit(solution)/shard_map/reduce_scatter | solution.py:72
  234.7 5.0 copy-start.52
  254.3 78.3 %reduce-scatter.10.cloned.1.call-start = ((), (), s32[]{:S(2)}) async-start(), calls=%async_computation.15 | async-start | bytes 1310720 | tf_op jit(solution)/shard_map/reduce_scatter | solution.py:72
  266.9 60.4 %all-to-all-start.1 = ((bf16[32,1,1,1,1,1,64,1024]{7,6,5,4,3,2,1,0:T(8,128)(2,1)}), bf16[32,1,1,1,1,1,64,1024]{7,6,5,4,3,2,1,0:T(8,128)(2,1)}, u32[]{:S(2)}, u32[]{:S(2)}) async-start(bf16[32,1,1,1,1,1,64,1024]{7,6,5,4,3,2,1,0:T(8,128)(2,1)} %bitcast.236), calls=%async_computation.1 | async-start | bytes 8388608 | tf_op jit(solution)/shard_map/all_to_all | solution.py:37
  272.0 62.0 %reduce-scatter.12.cloned.1.call-start = ((), (), s32[]{:S(2)}) async-start(), calls=%async_computation.17 | async-start | bytes 1310720 | tf_op jit(solution)/shard_map/reduce_scatter | solution.py:72
  278.3 164.6 %all-gather.14.cloned.1.call-start = ((), (), s32[]{:S(2)}) async-start(), calls=%async_computation.20 | async-start | bytes 1310720 | tf_op jit(solution)/shard_map/all_gather | solution.py:73
  327.2 6.1 copy-start.38
  327.2 6.1 copy-start.29
  327.3 6.1 copy-start.33
  327.3 60.5 %all-to-all-start.3 = ((bf16[32,1,1,1,1,1,64,1024]{7,6,5,4,3,2,1,0:T(8,128)(2,1)}), bf16[32,1,1,1,1,1,64,1024]{7,6,5,4,3,2,1,0:T(8,128)(2,1)}, u32[]{:S(2)}, u32[]{:S(2)}) async-start(bf16[32,1,1,1,1,1,64,1024]{7,6,5,4,3,2,1,0:T(8,128)(2,1)} %bitcast.235), calls=%async_computation.3 | async-start | bytes 8388608 | tf_op jit(solution)/shard_map/all_to_all | solution.py:37
  332.5 113.2 %all-gather.10.cloned.1.call-start = ((), (), s32[]{:S(2)}) async-start(), calls=%async_computation.16 | async-start | bytes 1310720 | tf_op jit(solution)/shard_map/all_gather | solution.py:73
  333.3 115.3 %all-gather.12.cloned.1.call-start = ((), (), s32[]{:S(2)}) async-start(), calls=%async_computation.18 | async-start | bytes 1310720 | tf_op jit(solution)/shard_map/all_gather | solution.py:73
  334.0 192.5 %reduce-scatter.6.cloned.1.call-start = ((), (), s32[]{:S(2)}) async-start(), calls=%async_computation.12 | async-start | bytes 6488064 | tf_op jit(solution)/shard_map/reduce_scatter | solution.py:338
  338.7 14.0 %copy-start.3 = (f32[256,1024]{1,0:T(8,128)S(1)}, f32[256,1024]{1,0:T(8,128)}, u32[]{:S(2)}) copy-start(f32[256,1024]{1,0:T(8,128)} %convert_multiply_fusion.6) | copy-start | bytes 3145732
  352.7 6.2 copy-start.23
  352.7 6.2 copy-start.40
  352.7 6.2 copy-start.42
  352.7 6.2 copy-start.31
  406.5 5.6 copy-start.26
  406.6 5.6 copy-start.35
  406.6 5.6 copy-start.44
  406.6 6.6 copy-start.9
  406.6 6.6 copy-start.17
  406.6 6.6 copy-start.48
  413.2 4.2 copy-start.27
  414.5 22.9 %copy-start.4 = (f32[256,1024]{1,0:T(8,128)}, f32[256,1024]{1,0:T(8,128)S(1)}, u32[]{:S(2)}) copy-start(f32[256,1024]{1,0:T(8,128)S(1)} %get-tuple-element.31) | copy-start | bytes 3145732
  417.5 5.0 copy-start.11
  417.5 10.4 %slice-start = ((s8[8388608]{0:T(1024)(128)(4,1)}), s8[4194304]{0:T(1024)(128)(4,1)S(1)}, s32[]{:S(2)}) async-start(s8[8388608]{0:T(1024)(128)(4,1)} %bitcast.227), calls=%async_computation.21 | async-start | bytes 8388608
  422.4 5.5 slice-start.1
  427.9 1.8 copy-start.13
  431.1 5.1 copy-start.21
  431.1 5.1 copy-start.24
  437.1 2.5 copy-start.18
  442.8 153.6 %reduce-scatter.8.cloned.1.call-start = ((), (), s32[]{:S(2)}) async-start(), calls=%async_computation.13 | async-start | bytes 245760 | tf_op jit(solution)/shard_map/reduce_scatter | solution.py:72
  448.5 5.3 copy-start.19
  453.9 72.8 %copy-start.8 = (bf16[256,1024]{1,0:T(8,128)(2,1)S(1)}, bf16[256,1024]{1,0:T(8,128)(2,1)}, u32[]{:S(2)}) copy-start(bf16[256,1024]{1,0:T(8,128)(2,1)} %copy-done.7) | copy-start | bytes 1572868
  453.9 140.1 %copy-start.5 = (f32[256,1024]{1,0:T(8,128)S(1)}, f32[256,1024]{1,0:T(8,128)}, u32[]{:S(2)}) copy-start(f32[256,1024]{1,0:T(8,128)} %copy-done.4) | copy-start | bytes 3145732
  453.9 243.9 %copy-start.1 = (bf16[1,1024,512]{2,1,0:T(8,128)(2,1)S(1)}, bf16[1,1024,512]{2,1,0:T(8,128)(2,1)}, u32[]{:S(2)}) copy-start(bf16[1,1024,512]{2,1,0:T(8,128)(2,1)} %param.28) | copy-start | bytes 3145732
  526.6 169.7 %all-reduce.7.cloned.1.call-start = ((), (), s32[]{:S(2)}) async-start(), calls=%async_computation.14 | async-start | bytes 262144 | tf_op jit(solution)/shard_map/psum | solution.py:358
  (6 other events, 6.9 us)
Sparse Core Ops, SparseCore 0:
  10.9 52.9 all-gather.5
  68.6 12.9 all-gather.7
  254.4 20.8 reduce-scatter.13
  277.7 22.8 reduce-scatter.9
  303.4 23.4 reduce-scatter.11
  328.6 24.1 all-gather.13
  354.5 24.2 all-gather.9
  380.6 24.2 all-gather.11
  443.0 83.5 reduce-scatter.5
  528.8 19.6 reduce-scatter.7
  554.5 141.6 all-reduce.6
where the time goes:
time: 710 us; the launch traced here: 705 us
  waiting for transfers between devices  322 us (45%)
  local copies, waits for them, and re-layouts  111 us (16%)
  matrix products  99.3 us (14%)
  blocking collectives  81 us (11%)
  other arithmetic  51.9 us (7%)
  starting transfers between devices  23.5 us (3%)
  between operations  15.9 us (2%)
    all_to_all x4, waiting for transfers between devices, exchange_both(): tiles = lax.all_to_all(tiles, axis, split_axis=0, concat_axis=0, tiled=True)  154 us
    psum x1, waiting for transfers between devices, on_device(): lax.psum((attn_gain_local, moe_gain_local, router_local), ('dp', 'row', '...  88.3 us
    reduce_scatter x1, waiting for transfers between devices, on_device(): lax.psum_scatter(jnp.concatenate([jnp.einsum('tr,tc->rc', normed, qkv_gra...  67.9 us
    psum x1, blocking collectives, on_device(): lax.psum((attn_gain_local, moe_gain_local, router_local), ('dp', 'row', '...  66.3 us
    all_to_all x4, starting transfers between devices, exchange_both(): tiles = lax.all_to_all(tiles, axis, split_axis=0, concat_axis=0, tiled=True)  22.9 us
  transfers between devices with their start and end apart: 15, of which 8 were waited for; matrix products, arithmetic and copies ran while one was open for 29% of the time, Pallas kernels for 0%

commit v1 on v0

--- a/solution.py
+++ b/solution.py
@@ -1,6 +1,10 @@
+import functools
+
 import jax
 import jax.numpy as jnp
 from jax import lax
+from jax.experimental import pallas as pl
+from jax.experimental.pallas import tpu as pltpu
 from jax.sharding import PartitionSpec as P
 
 D = 1024
@@ -120,6 +124,289 @@
     shaped = produced.reshape(1, 1, per_device, row_total, col_total, cap_rows, width)
     moved = exchange_both(shaped, ("row", "col"), ("row", "col"), (3, 4), (0, 1))
     return moved.reshape(row_total * col_total * per_device, cap_rows, width)
+
+
+MESH = pl.DeviceIdType.MESH
+GROUP = 32
+CHUNKS = 8
+SPAN = GROUP // CHUNKS
+
+
+def place():
+    col = lax.axis_index("col")
+    return lax.axis_index("dp"), lax.axis_index("row"), lax.rem(col, 4), col // 4
+
+
+def shifted(k, sign):
+    y, r, x, z = place()
+    chunk, i = k // SPAN, lax.rem(k, SPAN)
+    dr, dx, dz = chunk // 4, i, lax.rem(i + lax.rem(chunk, 4), 4)
+    row = lax.rem(r + dr, 2)
+    col = lax.rem(z + sign * dz + 4, 4) * 4 + lax.rem(x + sign * dx + 4, 4)
+    return (y, row, col), row * 16 + col
+
+
+def eye(n):
+    return lax.broadcasted_iota(jnp.int32, (n, n), 0) == lax.broadcasted_iota(
+        jnp.int32, (n, n), 1
+    )
+
+
+def as_row(column):
+    return jnp.sum(jnp.where(eye(column.shape[0]), column, 0.0), axis=0, keepdims=True)
+
+
+def as_column(row_vec):
+    return jnp.sum(jnp.where(eye(row_vec.shape[1]), row_vec, 0.0), axis=1, keepdims=True)
+
+
+def dot(a, b, dims):
+    return lax.dot_general(a, b, (dims, ((), ())), preferred_element_type=jnp.float32)
+
+
+def plane_barrier():
+    barrier = pltpu.get_barrier_semaphore()
+
+    @pl.loop(1, GROUP)
+    def _(k):
+        device, _ = shifted(k, 1)
+        pl.semaphore_signal(barrier, inc=1, device_id=device, device_id_type=MESH)
+
+    pl.semaphore_wait(barrier, GROUP - 1)
+
+
+def expert_kernel(
+    routed_ref,
+    pos_ref,
+    gates_ref,
+    grads_ref,
+    wg_ref,
+    wu_ref,
+    wd_ref,
+    rg_ref,
+    gdot_ref,
+    prod_ref,
+    dg_ref,
+    du_ref,
+    dd_ref,
+    onehot,
+    outgoing,
+    arrived,
+    going_back,
+    come_back,
+    gate_out,
+    gate_in,
+    dot_out,
+    dot_in,
+    active,
+    weighted,
+    pre_grads,
+    send_sem,
+    recv_sem,
+    gsend_sem,
+    grecv_sem,
+):
+    plane_barrier()
+
+    def copies(k, out, into, small_out, small_into, sign, base):
+        device, _ = shifted(k, sign)
+        return (
+            pltpu.make_async_remote_copy(
+                src_ref=out.at[k],
+                dst_ref=into.at[k],
+                send_sem=send_sem.at[base + k],
+                recv_sem=recv_sem.at[base + k],
+                device_id=device,
+                device_id_type=MESH,
+            ),
+            pltpu.make_async_remote_copy(
+                src_ref=small_out.at[k],
+                dst_ref=small_into.at[k],
+                send_sem=gsend_sem.at[base + k],
+                recv_sem=grecv_sem.at[base + k],
+                device_id=device,
+                device_id_type=MESH,
+            ),
+        )
+
+    def there(k):
+        return copies(k, outgoing, arrived, gate_out, gate_in, 1, 0)
+
+    def back(k):
+        return copies(k, going_back, come_back, dot_out, dot_in, -1, GROUP)
+
+    slot_iota = lax.broadcasted_iota(jnp.int32, (CAP, routed_ref.shape[0]), 0)
+
+    @pl.loop(0, CHUNKS)
+    def _(c):
+        parts = []
+        for i in range(SPAN):
+            k = c * SPAN + i
+            _, expert = shifted(k, 1)
+            chosen = slot_iota == pos_ref[pl.ds(expert, 1), :]
+            gate_col = jnp.sum(
+                jnp.where(chosen, gates_ref[pl.ds(expert, 1), :], 0.0), axis=1, keepdims=True
+            )
+            gate_out[k, 0:1, 0:CAP] = as_row(gate_col)
+            parts.append(chosen.astype(jnp.float32).astype(jnp.bfloat16))
+        chosen = jnp.concatenate(parts, axis=0)
+        onehot[pl.ds(c * SPAN * CAP, SPAN * CAP), :] = chosen
+        rows = dot(chosen, routed_ref[...], ((1,), (0,))).astype(jnp.bfloat16)
+        for i in range(SPAN):
+            k = c * SPAN + i
+            outgoing[k] = rows[i * CAP : (i + 1) * CAP]
+
+            @pl.when(k != 0)
+            def _():
+                for copy in there(k):
+                    copy.start()
+
+    arrived[0] = outgoing[0]
+    gate_in[0] = gate_out[0]
+
+    @pl.loop(0, CHUNKS)
+    def _(c):
+        for i in range(SPAN):
+            k = c * SPAN + i
+
+            @pl.when(k != 0)
+            def _():
+                for copy in there(k):
+                    copy.wait_recv()
+
+        span = pl.ds(c * SPAN * CAP, SPAN * CAP)
+        rows, gate_cols, grads = [], [], []
+        for i in range(SPAN):
+            k = c * SPAN + i
+            _, source = shifted(k, -1)
+            rows.append(arrived[k])
+            gate_cols.append(as_column(gate_in[k, 0:1, 0:CAP]))
+            grads.append(grads_ref[source])
+        rows = jnp.concatenate(rows, axis=0)
+        gate_cols = jnp.concatenate(gate_cols, axis=0)
+        grads = jnp.concatenate(grads, axis=0).astype(jnp.float32)
+        gate_pre = dot(rows, wg_ref[...], ((1,), (0,)))
+        up_pre = dot(rows, wu_ref[...], ((1,), (0,)))
+        gate_sig = jax.nn.sigmoid(gate_pre)
+        gate_act = gate_pre * gate_sig
+        act = (gate_act * up_pre).astype(jnp.bfloat16)
+        active[span, :] = act
+        produced = dot(act, wd_ref[...], ((1,), (0,))).astype(jnp.bfloat16)
+        dots = jnp.sum(produced.astype(jnp.float32) * grads, axis=1, keepdims=True)
+        produced_grad = (gate_cols * grads).astype(jnp.bfloat16)
+        weighted[span, :] = produced_grad
+        act_grad = dot(produced_grad, wd_ref[...], ((1,), (1,))).astype(jnp.bfloat16)
+        act_grad = act_grad.astype(jnp.float32)
+        gate_grad = (
+            act_grad * up_pre * gate_sig * (1.0 + gate_pre * (1.0 - gate_sig))
+        ).astype(jnp.bfloat16)
+        up_grad = (act_grad * gate_act).astype(jnp.bfloat16)
+        pre_grads[span, 0:512] = gate_grad
+        pre_grads[span, 512:1024] = up_grad
+        row_grads = dot(gate_grad, wg_ref[...], ((1,), (1,)))
+        row_grads = row_grads + dot(up_grad, wu_ref[...], ((1,), (1,)))
+        row_grads = row_grads.astype(jnp.bfloat16)
+        for i in range(SPAN):
+            k = c * SPAN + i
+            _, source = shifted(k, -1)
+            part = slice(i * CAP, (i + 1) * CAP)
+            prod_ref[source] = produced[part]
+            going_back[k] = row_grads[part]
+            dot_out[k, 0:1, 0:CAP] = as_row(dots[part])
+
+            @pl.when(k != 0)
+            def _():
+                for copy in back(k):
+                    copy.start()
+
+    come_back[0] = going_back[0]
+    dot_in[0] = dot_out[0]
+
+    @pl.loop(0, 4)
+    def _(n):
+        span = pl.ds(pl.multiple_of(n * 256, 256), 256)
+        part = dot(arrived[:, :, span].reshape(GROUP * CAP, 256), pre_grads[...], ((0,), (0,)))
+        dg_ref[span, :] = part[:, 0:512].astype(jnp.bfloat16)
+        du_ref[span, :] = part[:, 512:1024].astype(jnp.bfloat16)
+
+    @pl.loop(0, 2)
+    def _(n):
+        span = pl.ds(pl.multiple_of(n * 256, 256), 256)
+        dd_ref[span, :] = dot(active[:, span], weighted[...], ((0,), (0,))).astype(jnp.bfloat16)
+
+    rg_ref[...] = jnp.zeros_like(rg_ref)
+
+    @pl.loop(0, CHUNKS)
+    def _(c):
+        for i in range(SPAN):
+            k = c * SPAN + i
+
+            @pl.when(k != 0)
+            def _():
+                for copy in back(k):
+                    copy.wait_recv()
+
+        span = pl.ds(c * SPAN * CAP, SPAN * CAP)
+        chosen = onehot[span, :]
+        rows = come_back[pl.ds(c * SPAN, SPAN)].reshape(SPAN * CAP, D)
+        rg_ref[...] += dot(chosen, rows, ((0,), (0,)))
+        for i in range(SPAN):
+            k = c * SPAN + i
+            _, expert = shifted(k, 1)
+            dots = as_column(dot_in[k, 0:1, 0:CAP])
+            mask = chosen[i * CAP : (i + 1) * CAP].astype(jnp.float32)
+            gdot_ref[pl.ds(expert, 1), :] = jnp.sum(mask * dots, axis=0, keepdims=True)
+
+    @pl.loop(1, GROUP)
+    def _(k):
+        for copy in there(k):
+            copy.wait_send()
+        for copy in back(k):
+            copy.wait_send()
+
+
+def experts(routed, pos, gates, grads, wg, wu, wd):
+    tokens = routed.shape[0]
+    rows = GROUP * CAP
+    f32, bf16 = jnp.float32, jnp.bfloat16
+    vmem = pl.BlockSpec(memory_space=pltpu.VMEM)
+    block = pltpu.VMEM((GROUP, CAP, D), bf16)
+    small = pltpu.VMEM((GROUP, 8, 128), f32)
+    return pl.pallas_call(
+        expert_kernel,
+        out_shape=(
+            jax.ShapeDtypeStruct((tokens, D), f32),
+            jax.ShapeDtypeStruct((EXPERTS, tokens), f32),
+            jax.ShapeDtypeStruct((GROUP, CAP, D), bf16),
+            jax.ShapeDtypeStruct(wg.shape, bf16),
+            jax.ShapeDtypeStruct(wu.shape, bf16),
+            jax.ShapeDtypeStruct(wd.shape, bf16),
+        ),
+        in_specs=[vmem] * 7,
+        out_specs=[vmem] * 6,
+        scratch_shapes=[
+            pltpu.VMEM((rows, tokens), bf16),
+            block,
+            block,
+            block,
+            block,
+            small,
+            small,
+            small,
+            small,
+            pltpu.VMEM((rows, 512), bf16),
+            pltpu.VMEM((rows, D), bf16),
+            pltpu.VMEM((rows, 1024), bf16),
+            pltpu.SemaphoreType.DMA((2 * GROUP,)),
+            pltpu.SemaphoreType.DMA((2 * GROUP,)),
+            pltpu.SemaphoreType.DMA((2 * GROUP,)),
+            pltpu.SemaphoreType.DMA((2 * GROUP,)),
+        ],
+        compiler_params=pltpu.CompilerParams(
+            collective_id=1, has_side_effects=True, vmem_limit_bytes=58 << 20
+        ),
+        name="experts",
+    )(routed, pos, gates, grads, wg, wu, wd)
 
 
 def on_device(
@@ -151,6 +438,24 @@
     live_rows = positions < seq_length
     live_float = live_rows.astype(jnp.float32)[:, None]
     key_live = jnp.arange(seq_len) < seq_length
+    expert_ids = jnp.arange(EXPERTS, dtype=jnp.int32)
+    chosen = routes[:, :, None] == expert_ids[None, None, :]
+    routed_to = jnp.any(chosen, axis=1)
+    ranks = jnp.sum(jnp.where(chosen, priority.reshape(tok_count, TOP, 1), 0), axis=1)
+    ranks = jnp.where(routed_to & live_rows[:, None], ranks, 1 << 20)
+    ranks_et = ranks.T
+    slots_et = jnp.sum((ranks_et[:, :, None] > ranks_et[:, None, :]).astype(jnp.int32), axis=2)
+    pos_et = jnp.where((ranks_et < (1 << 20)) & (slots_et < CAP), slots_et, -1)
+    onehot = (pos_et[:, None, :] == jnp.arange(CAP, dtype=jnp.int32)[None, :, None]).astype(
+        jnp.bfloat16
+    )
+    onehot = onehot.reshape(EXPERTS * CAP, tok_count)
+    outgoing_grad = jnp.dot(onehot, cotangent, preferred_element_type=jnp.float32)
+    outgoing_grad = outgoing_grad.astype(jnp.bfloat16).reshape(EXPERTS, CAP, D)
+    arrived_grad = lax.all_to_all(
+        outgoing_grad, ("row", "col"), split_axis=0, concat_axis=0, tiled=True
+    )
+    grad_out = cotangent.astype(jnp.float32) * live_float
     inputs = hidden_in.astype(jnp.float32)
     scale_one = rms_scale(inputs)
     normed_one = inputs * scale_one
@@ -199,93 +504,23 @@
     normed_two = middle * scale_two
     routed = (normed_two * moe_gain).astype(jnp.bfloat16)
     logits = jnp.dot(routed, router, preferred_element_type=jnp.float32)
-    chosen_mask = routes[:, :, None] == jnp.arange(EXPERTS, dtype=jnp.int32)[None, None, :]
-    picked = jnp.sum(jnp.where(chosen_mask, logits[:, None, :], 0.0), axis=2)
+    picked = jnp.where(routed_to, logits, -jnp.inf)
     picked_exp = jnp.exp(picked - jnp.max(picked, axis=1, keepdims=True))
-    gate_values = picked_exp / jnp.sum(picked_exp, axis=1, keepdims=True)
-    pair_count = tok_count * TOP
-    pair_expert = routes.reshape(pair_count)
-    pair_live = jnp.broadcast_to(live_rows[:, None], (tok_count, TOP)).reshape(pair_count)
-    rank_ids = priority.reshape(pair_count)
-    sequence = (
-        jnp.zeros(pair_count, jnp.int32).at[rank_ids].set(jnp.arange(pair_count, dtype=jnp.int32))
-    )
-    onehot = (
-        (pair_expert[:, None] == jnp.arange(EXPERTS, dtype=jnp.int32)[None, :]) & pair_live[:, None]
-    ).astype(jnp.int32)
-    ordered = onehot[sequence]
-    earlier = jnp.cumsum(ordered, axis=0) - ordered
-    slot_ordered = jnp.sum(earlier * ordered, axis=1)
-    slot_ids = slot_ordered[rank_ids]
-    kept_pairs = pair_live & (slot_ids < CAP)
-    slot_total = EXPERTS * CAP
-    dest_slot = jnp.where(kept_pairs, pair_expert * CAP + slot_ids, slot_total)
-    source = (
-        jnp.full((slot_total + 1,), pair_count, jnp.int32)
-        .at[dest_slot]
-        .set(jnp.arange(pair_count, dtype=jnp.int32))[:slot_total]
-    )
-    source_token = jnp.where(source < pair_count, source // TOP, tok_count)
-    padded = jnp.concatenate([routed, jnp.zeros((1, D), jnp.bfloat16)], axis=0)
-    outgoing = padded[source_token].reshape(EXPERTS, CAP, D)
-    arrived = send_rows(outgoing, row_total, col_total)
-    gate_pre = jnp.einsum("erd,edf->erf", arrived, gate_weight, preferred_element_type=jnp.float32)
-    up_pre = jnp.einsum("erd,edf->erf", arrived, up_weight, preferred_element_type=jnp.float32)
-    gate_sig = jax.nn.sigmoid(gate_pre)
-    gate_act = gate_pre * gate_sig
-    active = (gate_act * up_pre).astype(jnp.bfloat16)
-    produced = jnp.einsum(
-        "erf,efd->erd", active, down_weight, preferred_element_type=jnp.float32
-    ).astype(jnp.bfloat16)
-    returned = return_rows(produced, row_total, col_total)
-    returned = jnp.concatenate(
-        [returned.reshape(slot_total, D), jnp.zeros((1, D), jnp.bfloat16)], axis=0
-    )
-    pair_out = returned[dest_slot].reshape(tok_count, TOP, D)
-    mixture = jnp.sum(gate_values[:, :, None] * pair_out, axis=1)
-    hidden_out = ((middle + mixture) * live_float).astype(jnp.bfloat16)
-    grad_out = cotangent.astype(jnp.float32) * live_float
-    gate_dot = jnp.sum(pair_out * grad_out[:, None, :], axis=2)
-    picked_grad = gate_values * (gate_dot - jnp.sum(gate_values * gate_dot, axis=1, keepdims=True))
-    logit_grad = jnp.sum(jnp.where(chosen_mask, picked_grad[:, :, None], 0.0), axis=1)
+    gates_te = picked_exp / jnp.sum(picked_exp, axis=1, keepdims=True)
+    returned_rows, gate_dot_et, produced, gate_local, up_local, down_local = experts(
+        routed, pos_et, gates_te.T, arrived_grad, gate_weight[0], up_weight[0], down_weight[0]
+    )
+    returned = lax.all_to_all(produced, ("row", "col"), split_axis=0, concat_axis=0, tiled=True)
+    gate_dot = gate_dot_et.T
+    picked_grad = gates_te * (
+        gate_dot - jnp.sum(gates_te * gate_dot, axis=1, keepdims=True)
+    )
+    logit_grad = picked_grad
     router_local = jnp.dot(
         routed.astype(jnp.float32).T, logit_grad, precision=lax.Precision.HIGHEST
     )
     routed_grad = jnp.dot(logit_grad, router.astype(jnp.float32).T, precision=lax.Precision.HIGHEST)
-    pair_grad = (
-        (gate_values[:, :, None] * grad_out[:, None, :]).astype(jnp.bfloat16).reshape(pair_count, D)
-    )
-    pair_grad = jnp.concatenate([pair_grad, jnp.zeros((1, D), jnp.bfloat16)], axis=0)
-    outgoing_grad = pair_grad[source].reshape(EXPERTS, CAP, D)
-    arrived_grad = send_rows(outgoing_grad, row_total, col_total)
-    active_grad = jnp.einsum(
-        "erd,efd->erf", arrived_grad, down_weight, preferred_element_type=jnp.float32
-    ).astype(jnp.bfloat16)
-    down_local = jnp.einsum(
-        "erf,erd->efd", active, arrived_grad, preferred_element_type=jnp.float32
-    )
-    gate_pre_grad = (active_grad * up_pre * gate_sig * (1.0 + gate_pre * (1.0 - gate_sig))).astype(
-        jnp.bfloat16
-    )
-    up_pre_grad = (active_grad * gate_act).astype(jnp.bfloat16)
-    gate_local = jnp.einsum(
-        "erd,erf->edf", arrived, gate_pre_grad, preferred_element_type=jnp.float32
-    )
-    up_local = jnp.einsum("erd,erf->edf", arrived, up_pre_grad, preferred_element_type=jnp.float32)
-    arrived_back = jnp.einsum(
-        "erf,edf->erd", gate_pre_grad, gate_weight, preferred_element_type=jnp.float32
-    )
-    arrived_back = (
-        arrived_back
-        + jnp.einsum("erf,edf->erd", up_pre_grad, up_weight, preferred_element_type=jnp.float32)
-    ).astype(jnp.bfloat16)
-    returned_grad = return_rows(arrived_back, row_total, col_total)
-    returned_grad = jnp.concatenate(
-        [returned_grad.reshape(slot_total, D), jnp.zeros((1, D), jnp.bfloat16)], axis=0
-    )
-    routed_grad = routed_grad + jnp.sum(
-        returned_grad[dest_slot].reshape(tok_count, TOP, D).astype(jnp.float32), axis=1
-    )
+    routed_grad = routed_grad + returned_rows
     middle_norm_grad, moe_gain_local = norm_back(routed_grad, normed_two, scale_two, moe_gain)
     middle_grad = grad_out + middle_norm_grad
     branch_grad = middle_grad.astype(jnp.bfloat16)
@@ -358,6 +593,16 @@
     attn_gain_sum, moe_gain_sum, router_sum = lax.psum(
         (attn_gain_local, moe_gain_local, router_local), ("dp", "row", "col")
     )
+    gate_rows = jnp.sum(
+        jnp.where(onehot.reshape(EXPERTS, CAP, tok_count) > 0, gates_te.T[:, None, :], 0.0),
+        axis=2,
+    )
+    weighted = (returned.astype(jnp.float32) * gate_rows[:, :, None]).reshape(EXPERTS * CAP, D)
+    high = weighted.astype(jnp.bfloat16)
+    rest = (weighted - high.astype(jnp.float32)).astype(jnp.bfloat16)
+    mixture = jnp.einsum("st,sd->td", onehot, high, preferred_element_type=jnp.float32)
+    mixture = mixture + jnp.einsum("st,sd->td", onehot, rest, preferred_element_type=jnp.float32)
+    hidden_out = ((middle + mixture) * live_float).astype(jnp.bfloat16)
     query_grad = grad_shard[:, :D]
     key_grad = grad_shard[:, D : D + kv_width]
     value_grad = grad_shard[:, D + kv_width : D + 2 * kv_width]
@@ -372,9 +617,9 @@
         output_grad,
         moe_gain_sum,
         router_sum,
-        gate_sum,
-        up_sum,
-        down_sum,
+        gate_sum[None],
+        up_sum[None],
+        down_sum[None],
     )
 
 

time: 710 us -> 693 us (0.976)
  Pallas kernels: 0 us -> 123 us
  local copies, waits for them, and re-layouts: 111 us -> 7.91 us
  matrix products: 99.3 us -> 54.1 us
  waiting for transfers between devices: 322 us -> 356 us
  other arithmetic: 51.9 us -> 37.3 us
    pallas_call x0 -> x1, Pallas kernels: none -> 123 us  [experts(): pl.pallas_call(expert_kernel, out_shape=(jax.ShapeDtypeStruct((tokens, D)...]
    all_to_all x4 -> x3, waiting for transfers between devices: 154 us -> 42.4 us  [the longest x1 41.1 us: on_device(): lax.all_to_all(outgoing_grad, ('row', 'col'), split_axis=0, concat_axis=0...]
    gather x6 -> x0, local copies, waits for them, and re-layouts: 69.6 us -> none  [the longest x1 14.2 us: on_device(): returned_grad[dest_slot].reshape(tok_count, TOP, D).astype(jnp.float32)]
    psum x1, waiting for transfers between devices: 88.3 us -> 137 us  [on_device(): lax.psum((attn_gain_local, moe_gain_local, router_local), ('dp', 'row', '...]
    dot_general x9 -> x3, matrix products: 59.3 us -> 11.6 us  [the longest x1 4.54 us: on_device(): jnp.einsum('st,sd->td', onehot, high, preferred_element_type=jnp.float32)]
    reduce_scatter x4, waiting for transfers between devices: 0.02 us -> 44.5 us  [sum_in_two_steps(): own = lax.psum_scatter(padded, axis, scatter_dimension=0, tiled=True)]
    all_gather x2, waiting for transfers between devices: 11.1 us -> 45.4 us  [sent_together(): whole = lax.all_gather(both, axis, axis=dim, tiled=True)]
    reduce_scatter x1, waiting for transfers between devices: 67.9 us -> 85.8 us  [on_device(): lax.psum_scatter(jnp.concatenate([jnp.einsum('tr,tc->rc', normed, qkv_gra...]
  transfers between devices with their start and end apart: 15 -> 14, of which waited for: 8 -> 8; matrix products, arithmetic and copies ran while one was open for 29% -> 13% of each run, Pallas kernels for 0% -> 0%
where the time goes in v1:
time: 693 us; the launch traced here: 691 us
  waiting for transfers between devices  356 us (51%)
  Pallas kernels  123 us (18%)
  blocking collectives  76.5 us (11%)
  matrix products  54.1 us (8%)
  other arithmetic  37.3 us (5%)
  starting transfers between devices  20.3 us (3%)
  between operations  15.3 us (2%)
  local copies, waits for them, and re-layouts  7.91 us (1%)
    psum x1, waiting for transfers between devices, on_device(): lax.psum((attn_gain_local, moe_gain_local, router_local), ('dp', 'row', '...  137 us
    pallas_call x1, Pallas kernels, experts(): pl.pallas_call(expert_kernel, out_shape=(jax.ShapeDtypeStruct((tokens, D)...  123 us
    reduce_scatter x1, waiting for transfers between devices, on_device(): lax.psum_scatter(jnp.concatenate([jnp.einsum('tr,tc->rc', normed, qkv_gra...  85.8 us
    psum x1, blocking collectives, on_device(): lax.psum((attn_gain_local, moe_gain_local, router_local), ('dp', 'row', '...  66.8 us
    all_gather x2, waiting for transfers between devices, sent_together(): whole = lax.all_gather(both, axis, axis=dim, tiled=True)  45.4 us
    reduce_scatter x4, waiting for transfers between devices, sum_in_two_steps(): own = lax.psum_scatter(padded, axis, scatter_dimension=0, tiled=True)  44.5 us
    all_to_all x1, waiting for transfers between devices, on_device(): lax.all_to_all(outgoing_grad, ('row', 'col'), split_axis=0, concat_axis=0...  41.1 us
  transfers between devices with their start and end apart: 14, of which 8 were waited for; matrix products, arithmetic and copies ran while one was open for 13% of the time, Pallas kernels for 0%

profile of v1, /device:TPU:1, one launch (start us, length us, event | category | flops | bytes accessed | tf_op | source)
XLA Modules:
  0.0 691.1 jit_solution(13827990732683797552)
XLA Ops:
  7.3 1.7 pad_maximum_fusion.8
  10.2 1.4 reduce.3
  11.7 0.6 fusion.106
  12.3 0.7 fusion.86
  13.0 0.7 select_reduce_fusion.1
  13.8 1.2 fusion.70
  15.0 2.6 convert_reduce_fusion
  17.6 0.8 broadcast_multiply_fusion
  18.4 45.4 %all-gather.6.cloned.1.call-done = bf16[1024,3072]{1,0:T(8,128)(2,1)} async-done(((bf16[32,3072]{1,0:T(8,128)(2,1)}), bf16[1024,3072]{1,0:T(8,128)(2,1)}) %all-gather.6.cloned.1.call-update) | async-done | bytes 6291472 | tf_op jit(solution)/shard_map/all_gather | solution.py:49
  63.8 1.9 convolution_convert_fusion.3
  65.8 2.0 fusion.81
  67.9 0.8 pad_maximum_fusion.2
  69.3 3.2 convolution_convert_fusion.1
  72.6 4.9 all-to-all-start
  77.8 2.7 fusion.24
  80.7 0.7 copy-done.8
  81.3 2.9 bitcast_reduce_fusion
  84.2 1.2 fusion.6
  85.4 0.8 copy-done.7
  86.2 1.6 fusion.52
  87.8 2.6 multiply_reduce_fusion.2
  91.0 0.6 fusion.101.gates_ref
  91.6 41.1 %all-to-all-done.grads_ref = bf16[32,64,1024]{2,1,0:T(8,128)(2,1)} async-done(((bf16[32,64,1024]{2,1,0:T(8,128)(2,1)}), bf16[32,64,1024]{2,1,0:T(8,128)(2,1)}, u32[]{:S(2)}, u32[]{:S(2)}) %all-to-all-start) | async-done | bytes 4194336 | tf_op jit(solution)/shard_map/all_to_all | solution.py:455
  132.7 123.4 %experts.1 = (f32[256,1024]{1,0:T(8,128)}, f32[32,256]{1,0:T(8,128)}, bf16[32,64,1024]{2,1,0:T(8,128)(2,1)}, bf16[1024,512]{1,0:T(8,128)(2,1)}, bf16[1024,512]{1,0:T(8,128)(2,1)}, /*index=5*/bf16[512,1024]{1,0:T(8,128)(2,1)}) custom-call(bf16[256,1024]{1,0:T(8,128)(2,1)} %copy-done.5, s32[32,256]{1,0:T(8,128)} %copy-done.14, f32[32,256]{1,0:T(8,128)} %fusion.101.gates_ref, ...), custom_call_target="tpu_custom_call" | custom-call | tf_op jit(solution)/shard_map/experts/pallas_call | solution.py:375
  256.4 0.8 fusion.87
  257.2 2.8 multiply_reduce_fusion
  260.1 1.1 multiply_add_fusion
  261.2 3.1 fusion.53
  264.3 1.2 copy.73
  265.5 0.7 log_add_fusion
  266.3 5.6 fusion
  271.9 4.9 fusion.2
  276.9 1.4 fusion.60
  278.3 1.4 fusion.61
  279.8 1.1 copy.92
  281.0 5.1 all-to-all-start.2
  286.7 1.3 all-to-all-done.2
  288.0 1.5 convert_reduce_fusion.1
  289.7 3.2 convolution_multiply_fusion
  293.2 0.7 convolution_convert_fusion.2
  294.0 1.5 convolution_convert_fusion
  295.4 3.2 pad_maximum_fusion
  298.8 0.7 all-gather.10.cloned.1.call-update
  299.5 14.2 %reduce-scatter.12.cloned.1.call-done = bf16[256,512]{1,0:T(8,128)(2,1)} async-done(((bf16[1024,512]{1,0:T(8,128)(2,1)}), bf16[256,512]{1,0:T(8,128)(2,1)}) %reduce-scatter.12.cloned.1.call-update) | async-done | bytes 262160 | tf_op jit(solution)/shard_map/reduce_scatter | solution.py:76
  313.8 25.5 %reduce-scatter.14.cloned.1.call-done = bf16[128,1024]{1,0:T(8,128)(2,1)} async-done(((bf16[512,1024]{1,0:T(8,128)(2,1)}), bf16[128,1024]{1,0:T(8,128)(2,1)}) %reduce-scatter.14.cloned.1.call-update) | async-done | bytes 262160 | tf_op jit(solution)/shard_map/reduce_scatter | solution.py:76
  339.2 9.2 %all-to-all-start.1 = ((bf16[32,64,1024]{2,1,0:T(8,128)(2,1)}), bf16[32,64,1024]{2,1,0:T(8,128)(2,1)}, u32[]{:S(2)}, u32[]{:S(2)}) async-start(bf16[32,64,1024]{2,1,0:T(8,128)(2,1)} %get-tuple-element.18), calls=%async_computation.1 | async-start | bytes 8388608 | tf_op jit(solution)/shard_map/all_to_all | solution.py:513
  348.5 85.8 %reduce-scatter.6.cloned.1.call-done = bf16[32,3072]{1,0:T(8,128)(2,1)} async-done(((bf16[1024,3072]{1,0:T(8,128)(2,1)}), bf16[32,3072]{1,0:T(8,128)(2,1)}) %reduce-scatter.6.cloned.1.call-update) | async-done | bytes 196624 | tf_op jit(solution)/shard_map/reduce_scatter | solution.py:573
  434.6 1.7 fusion.91
  436.3 2.5 fusion.22
  438.9 1.8 convolution_add_fusion.2
  440.7 2.8 fusion.69
  443.5 66.8 %all-reduce = (f32[1024]{0:T(1024)}, f32[1024]{0:T(1024)}) all-reduce(f32[1024]{0:T(1024)S(1)} %get-tuple-element.26, f32[1024]{0:T(1024)S(1)} %copy-done.26), channel_id=1, replica_groups=mesh['dp'=4,'row'=2,'col'=16] {'dp','row','col'}, use_global_device_ids=true, to_apply=%region_16.17 | all-reduce | flops 2048 | bytes 16384 | tf_op jit(solution)/shard_map/psum | solution.py:593
  510.7 2.5 fusion.68
  513.2 2.8 bitcast_convert_fusion.2
  516.0 2.8 bitcast_convert_fusion.1
  518.9 2.8 bitcast_convert_fusion
  521.7 3.9 fusion.30
  525.6 4.5 fusion.49
  530.1 4.8 reduce-scatter.8.cloned.1.call-done
  535.0 9.7 %all_gather.20 = bf16[32,3072]{1,0:T(8,128)(2,1)S(1)} all-gather(bf16[8,3072]{1,0:T(8,128)(2,1)} %reduce-scatter.8.cloned.1.call-done), channel_id=1, replica_groups=mesh['dp'=4,'row'=2,'col'=16] {'dp'}, dimensions={0}, use_global_device_ids=true | all-gather | bytes 245760 | tf_op jit(solution)/shard_map/all_gather | solution.py:77
  544.7 0.7 fusion.108
  545.4 0.7 fusion.109
  546.1 136.9 %all-reduce.3.cloned.1.call-done = f32[1024,32]{0,1:T(8,128)} async-done(((f32[1024,32]{0,1:T(8,128)}), f32[1024,32]{0,1:T(8,128)}) %all-reduce.3.cloned.1.call-update) | async-done | bytes 131088 | tf_op jit(solution)/shard_map/psum | solution.py:593
  683.0 1.6 copy.97
  (126 shorter events, 5.0 us)
Async XLA Ops:
  7.2 83.5 %copy-start = (bf16[1024,32]{0,1:T(8,128)(2,1)S(1)}, bf16[1024,32]{0,1:T(8,128)(2,1)}, u32[]{:S(2)}) copy-start(bf16[1024,32]{0,1:T(8,128)(2,1)} %param.26) | copy-start | bytes 196612
  7.2 62.1 %copy-start.12 = (bf16[256,1024]{1,0:T(8,128)(2,1)S(1)}, bf16[256,1024]{1,0:T(8,128)(2,1)}, u32[]{:S(2)}) copy-start(bf16[256,1024]{1,0:T(8,128)(2,1)} %param.16) | copy-start | bytes 1572868
  7.2 56.6 %all-gather.6.cloned.1.call-start = ((), (), s32[]{:S(2)}) async-start(), calls=%async_computation.8 | async-start | bytes 6488064 | tf_op jit(solution)/shard_map/all_gather | solution.py:49
  8.9 71.7 %all-gather.8.cloned.1.call-start = ((), (), s32[]{:S(2)}) async-start(), calls=%async_computation.9 | async-start | bytes 1572864 | tf_op jit(solution)/shard_map/all_gather | solution.py:49
  17.6 60.1 %copy-start.31 = (f32[256]{0:T(256)}, f32[256]{0:T(256)S(1)}, u32[]{:S(2)}) copy-start(f32[256]{0:T(256)S(1)} %add_rsqrt_fusion.1) | copy-start | bytes 3076
  68.8 3.8 copy-start.14
  69.3 8.4 %copy-start.4 = (bf16[256,1024]{1,0:T(8,128)(2,1)S(1)}, bf16[256,1024]{1,0:T(8,128)(2,1)}, u32[]{:S(2)}) copy-start(bf16[256,1024]{1,0:T(8,128)(2,1)} %param.15) | copy-start | bytes 1572868
  69.3 8.4 %copy-start.28 = (f32[1024]{0:T(1024)S(1)}, f32[1024]{0:T(1024)}, u32[]{:S(2)}) copy-start(f32[1024]{0:T(1024)} %param.20) | copy-start | bytes 12292
  72.6 60.2 %all-to-all-start = ((bf16[32,64,1024]{2,1,0:T(8,128)(2,1)}), bf16[32,64,1024]{2,1,0:T(8,128)(2,1)}, u32[]{:S(2)}, u32[]{:S(2)}) async-start(bf16[32,64,1024]{2,1,0:T(8,128)(2,1)} %bitcast.157), calls=%async_computation | async-start | bytes 8388608 | tf_op jit(solution)/shard_map/all_to_all | solution.py:455
  77.5 221.2 %reduce-scatter.10.cloned.1.call-start = ((), (), s32[]{:S(2)}) async-start(), calls=%async_computation.13 | async-start | bytes 1310720 | tf_op jit(solution)/shard_map/reduce_scatter | solution.py:76
  80.6 0.7 copy-start.8
  84.2 3.6 copy-start.2
  84.2 2.0 copy-start.7
  86.2 1.6 copy-start.20
  86.2 4.2 copy-start.21
  87.8 2.6 copy-start.10
  90.5 169.6 %copy-start.27 = (f32[256]{0:T(256)}, f32[256]{0:T(256)S(1)}, u32[]{:S(2)}) copy-start(f32[256]{0:T(256)S(1)} %add_rsqrt_fusion) | copy-start | bytes 3076
  90.7 42.1 %copy-start.5 = (bf16[256,1024]{1,0:T(8,128)(2,1)}, bf16[256,1024]{1,0:T(8,128)(2,1)S(1)}, u32[]{:S(2)}) copy-start(bf16[256,1024]{1,0:T(8,128)(2,1)S(1)} %multiply_convert_fusion.routed_ref) | copy-start | bytes 1572868
  91.0 169.1 %copy-start.22 = (f32[256]{0:T(256)}, f32[256]{0:T(256)S(1)}, u32[]{:S(2)}) copy-start(f32[256]{0:T(256)S(1)} %get-tuple-element.51) | copy-start | bytes 3076
  91.0 169.1 %copy-start.24 = (f32[256]{0:T(256)}, f32[256]{0:T(256)S(1)}, u32[]{:S(2)}) copy-start(f32[256]{0:T(256)S(1)} %fusion.90) | copy-start | bytes 3076
  256.2 57.5 %reduce-scatter.12.cloned.1.call-start = ((), (), s32[]{:S(2)}) async-start(), calls=%async_computation.15 | async-start | bytes 1310720 | tf_op jit(solution)/shard_map/reduce_scatter | solution.py:76
  257.2 2.8 copy-start.30
  266.3 12.0 %slice-start = ((s8[8388608]{0:T(1024)(128)(4,1)}), s8[4194304]{0:T(1024)(128)(4,1)S(1)}, s32[]{:S(2)}) async-start(s8[8388608]{0:T(1024)(128)(4,1)} %bitcast.155), calls=%async_computation.19 | async-start | bytes 8388608
  271.9 5.0 copy-start.9
  271.9 6.4 slice-start.1
  276.9 2.9 copy-start.3
  279.7 9.8 %copy-start.19 = (f32[256,32]{0,1:T(8,128)S(1)}, f32[256,32]{0,1:T(8,128)}, u32[]{:S(2)}) copy-start(f32[256,32]{0,1:T(8,128)} %get-tuple-element.44) | copy-start | bytes 98308
  281.0 7.0 %all-to-all-start.2 = ((bf16[2,256,16,64]{1,3,2,0:T(8,128)(2,1)}), bf16[2,256,16,64]{1,3,2,0:T(8,128)(2,1)}, u32[]{:S(2)}, u32[]{:S(2)}) async-start(bf16[2,256,16,64]{1,3,2,0:T(8,128)(2,1)} %bitcast.161), calls=%async_computation.2 | async-start | bytes 2097152 | tf_op jit(solution)/shard_map/all_to_all | solution.py:55
  286.1 53.1 %reduce-scatter.14.cloned.1.call-start = ((), (), s32[]{:S(2)}) async-start(), calls=%async_computation.17 | async-start | bytes 1310720 | tf_op jit(solution)/shard_map/reduce_scatter | solution.py:76
  286.7 147.6 %reduce-scatter.6.cloned.1.call-start = ((), (), s32[]{:S(2)}) async-start(), calls=%async_computation.10 | async-start | bytes 6488064 | tf_op jit(solution)/shard_map/reduce_scatter | solution.py:573
  289.6 4.3 copy-start.13
  289.7 3.5 copy-start.11
  289.7 4.3 copy-start.29
  289.7 4.3 copy-start.32
  293.2 0.8 copy-start.16
  298.6 135.9 %copy-start.6 = (bf16[256,1024]{1,0:T(8,128)(2,1)S(1)}, bf16[256,1024]{1,0:T(8,128)(2,1)}, u32[]{:S(2)}) copy-start(bf16[256,1024]{1,0:T(8,128)(2,1)} %copy-done.5) | copy-start | bytes 1572868
  298.6 135.9 %copy-start.17 = (f32[32,256]{1,0:T(8,128)S(1)}, f32[32,256]{1,0:T(8,128)}, u32[]{:S(2)}) copy-start(f32[32,256]{1,0:T(8,128)} %get-tuple-element.19) | copy-start | bytes 98308
  298.6 136.0 %copy-start.23 = (f32[256]{0:T(256)S(1)}, f32[256]{0:T(256)}, u32[]{:S(2)}) copy-start(f32[256]{0:T(256)} %copy-done.22) | copy-start | bytes 3076
  298.6 136.0 %copy-start.25 = (f32[256]{0:T(256)S(1)}, f32[256]{0:T(256)}, u32[]{:S(2)}) copy-start(f32[256]{0:T(256)} %copy-done.24) | copy-start | bytes 3076
  298.7 214.5 %all-gather.10.cloned.1.call-start = ((), (), s32[]{:S(2)}) async-start(), calls=%async_computation.14 | async-start | bytes 1310720 | tf_op jit(solution)/shard_map/all_gather | solution.py:77
  299.4 216.6 %all-gather.12.cloned.1.call-start = ((), (), s32[]{:S(2)}) async-start(), calls=%async_computation.16 | async-start | bytes 1310720 | tf_op jit(solution)/shard_map/all_gather | solution.py:77
  313.7 205.2 %all-gather.14.cloned.1.call-start = ((), (), s32[]{:S(2)}) async-start(), calls=%async_computation.18 | async-start | bytes 1310720 | tf_op jit(solution)/shard_map/all_gather | solution.py:77
  339.2 182.4 %all-to-all-start.1 = ((bf16[32,64,1024]{2,1,0:T(8,128)(2,1)}), bf16[32,64,1024]{2,1,0:T(8,128)(2,1)}, u32[]{:S(2)}, u32[]{:S(2)}) async-start(bf16[32,64,1024]{2,1,0:T(8,128)(2,1)} %get-tuple-element.18), calls=%async_computation.1 | async-start | bytes 8388608 | tf_op jit(solution)/shard_map/all_to_all | solution.py:513
  348.4 95.1 %copy-start.26 = (f32[1024]{0:T(1024)S(1)}, f32[1024]{0:T(1024)}, u32[]{:S(2)}) copy-start(f32[1024]{0:T(1024)} %get-tuple-element.24) | copy-start | bytes 12292
  348.4 161.9 %copy-start.15 = (s32[32,256]{1,0:T(8,128)S(1)}, s32[32,256]{1,0:T(8,128)}, u32[]{:S(2)}) copy-start(s32[32,256]{1,0:T(8,128)} %copy-done.14) | copy-start | bytes 98308
  348.4 161.8 %copy-start.18 = (f32[32,256]{1,0:T(8,128)S(1)}, f32[32,256]{1,0:T(8,128)}, u32[]{:S(2)}) copy-start(f32[32,256]{1,0:T(8,128)} %fusion.101.gates_ref) | copy-start | bytes 98308
  348.4 186.5 %reduce-scatter.8.cloned.1.call-start = ((), (), s32[]{:S(2)}) async-start(), calls=%async_computation.11 | async-start | bytes 245760 | tf_op jit(solution)/shard_map/reduce_scatter | solution.py:76
  434.3 248.8 %all-reduce.3.cloned.1.call-start = ((), (), s32[]{:S(2)}) async-start(), calls=%async_computation.12 | async-start | bytes 262144 | tf_op jit(solution)/shard_map/psum | solution.py:593
  521.7 3.9 copy-start.33
  521.7 162.9 %copy-start.1 = (bf16[1024,32]{0,1:T(8,128)(2,1)S(1)}, bf16[1024,32]{0,1:T(8,128)(2,1)}, u32[]{:S(2)}) copy-start(bf16[1024,32]{0,1:T(8,128)(2,1)} %param.26) | copy-start | bytes 196612
Sparse Core Ops, SparseCore 0:
  10.9 52.8 all-gather.5
  68.9 10.5 all-gather.7
  256.3 31.6 reduce-scatter.9
  290.4 23.2 reduce-scatter.11
  315.9 23.2 reduce-scatter.13
  343.3 90.9 reduce-scatter.5
  435.9 24.0 all-gather.9
  461.7 24.9 all-gather.11
  488.3 24.9 all-gather.13
  515.5 19.4 reduce-scatter.7
  541.0 141.9 all-reduce.2

commit v2 on v1

--- a/solution.py
+++ b/solution.py
@@ -20,29 +20,6 @@
 rotary_base = 10000.0
 
 
-def cut_along(array, dim, length):
-    dims = array.shape
-    tiles = array.reshape(*dims[:dim], length, dims[dim] // length, *dims[dim + 1 :])
-    return jnp.moveaxis(tiles, dim, 0)
-
-
-def joined_along(tiles, dim):
-    tiles = jnp.moveaxis(tiles, 0, dim)
-    dims = tiles.shape
-    return tiles.reshape(*dims[:dim], dims[dim] * dims[dim + 1], *dims[dim + 2 :])
-
-
-def exchange_both(array, axis, axes, splits, concats):
-    sizes = [lax.axis_size(a) for a in axes]
-    tiles = cut_along(array, splits[0], sizes[0])
-    tiles = jnp.moveaxis(cut_along(tiles, splits[1] + 1, sizes[1]), 0, 1)
-    inside = tiles.shape[2:]
-    tiles = tiles.reshape(-1, *inside)
-    tiles = lax.all_to_all(tiles, axis, split_axis=0, concat_axis=0, tiled=True)
-    tiles = joined_along(tiles.reshape(*sizes, *inside), concats[0] + 1)
-    return joined_along(tiles, concats[1])
-
-
 def sent_together(arrays, axis, dim, along):
     widths = [a.shape[along] for a in arrays]
     both = jnp.concatenate(arrays, axis=along)
@@ -50,45 +27,8 @@
     return tuple(jnp.split(whole, [sum(widths[:k]) for k in range(1, len(widths))], axis=along))
 
 
-def summed_on_arrival(array, axis, dim):
-    tiles = cut_along(array, dim, lax.axis_size(axis))
-    arrived = lax.all_to_all(tiles, axis, split_axis=0, concat_axis=0, tiled=True)
-    return arrived.astype(jnp.float32).sum(axis=0)
-
-
-def in_one_piece(arrays, axis, dim, along):
-    widths = [a.shape[along] for a in arrays]
-    both = jnp.concatenate(arrays, axis=along)
-    whole = summed_on_arrival(both, axis, dim)
-    return tuple(jnp.split(whole, [sum(widths[:k]) for k in range(1, len(widths))], axis=along))
-
-
-def padded_to(lines, length):
-    spare = -lines.shape[0] % length
-    if not spare:
-        return lines
-    return jnp.concatenate([lines, jnp.zeros((spare, *lines.shape[1:]), lines.dtype)])
-
-
-def sum_in_two_steps(array, axis):
-    lines = array.reshape(-1, *array.shape[1:][-1:])
-    padded = padded_to(lines, lax.axis_size(axis))
-    own = lax.psum_scatter(padded, axis, scatter_dimension=0, tiled=True)
-    whole = lax.all_gather(own, axis, axis=0, tiled=True)
-    return whole[: len(lines)].reshape(array.shape)
-
-
 def rms_scale(values):
     return lax.rsqrt(jnp.mean(values * values, axis=-1, keepdims=True) + epsilon)
-
-
-def norm_back(grad_rows, normed_rows, scale_rows, gain_vec):
-    scaled = grad_rows * gain_vec
-    inner_sum = jnp.mean(scaled * normed_rows, axis=-1, keepdims=True)
-    return (
-        scale_rows * (scaled - normed_rows * inner_sum),
-        jnp.sum(grad_rows * normed_rows, axis=0),
-    )
 
 
 def rotary(values, positions, sign):
@@ -106,24 +46,6 @@
         ],
         axis=-1,
     )
-
-
-def send_rows(outgoing, row_total, col_total):
-    per_device = outgoing.shape[0] // (row_total * col_total)
-    cap_rows = outgoing.shape[1]
-    width = outgoing.shape[2]
-    shaped = outgoing.reshape(row_total, col_total, per_device, 1, 1, cap_rows, width)
-    moved = exchange_both(shaped, ("row", "col"), ("row", "col"), (0, 1), (3, 4))
-    return moved.reshape(per_device, row_total * col_total * cap_rows, width)
-
-
-def return_rows(produced, row_total, col_total):
-    per_device = produced.shape[0]
-    width = produced.shape[2]
-    cap_rows = produced.shape[1] // (row_total * col_total)
-    shaped = produced.reshape(1, 1, per_device, row_total, col_total, cap_rows, width)
-    moved = exchange_both(shaped, ("row", "col"), ("row", "col"), (3, 4), (0, 1))
-    return moved.reshape(row_total * col_total * per_device, cap_rows, width)
 
 
 MESH = pl.DeviceIdType.MESH
@@ -310,7 +232,7 @@
             k = c * SPAN + i
             _, source = shifted(k, -1)
             part = slice(i * CAP, (i + 1) * CAP)
-            prod_ref[source] = produced[part]
+            prod_ref[k] = produced[part]
             going_back[k] = row_grads[part]
             dot_out[k, 0:1, 0:CAP] = as_row(dots[part])
 
@@ -409,6 +331,557 @@
     )(routed, pos, gates, grads, wg, wu, wd)
 
 
+PLANES = 4
+CHIPS = 16
+HALF = D // 2
+NEG = -1000000000.0
+
+
+def chip_shift(q, sign):
+    y, r, x, z = place()
+    dx, dz = lax.rem(q, 4), lax.rem(lax.rem(q, 4) + q // 4, 4)
+    col = lax.rem(z + sign * dz + 4, 4) * 4 + lax.rem(x + sign * dx + 4, 4)
+    return (y, r, col), col
+
+
+def plane_shift(n):
+    y, r, x, z = place()
+    other = lax.rem(y + n, PLANES)
+    return (other, r, z * 4 + x), other
+
+
+def split_two(values):
+    high = values.astype(jnp.bfloat16)
+    return high, (values - high.astype(jnp.float32)).astype(jnp.bfloat16)
+
+
+def turned_back(rows, cosine, sine):
+    first, second = rows[0:32], rows[32:64]
+    return jnp.concatenate(
+        [first * cosine + second * sine, second * cosine - first * sine], axis=0
+    )
+
+
+def remote(src, dst, send_sem, recv_sem, device):
+    return pltpu.make_async_remote_copy(
+        src_ref=src,
+        dst_ref=dst,
+        send_sem=send_sem,
+        recv_sem=recv_sem,
+        device_id=device,
+        device_id_type=MESH,
+    )
+
+
+def finish_kernel(
+    length_ref,
+    prod_ref,
+    pos_ref,
+    gates_ref,
+    rg_ref,
+    gdot_ref,
+    dg_ref,
+    du_ref,
+    dd_ref,
+    routed_ref,
+    router_ref,
+    middle_ref,
+    cot_ref,
+    hidden_ref,
+    again_ref,
+    mgain_ref,
+    normed_ref,
+    mixed_ref,
+    w_ref,
+    q_ref,
+    k_ref,
+    v_ref,
+    lse_ref,
+    cos_ref,
+    sin_ref,
+    hout_ref,
+    hgrad_ref,
+    again_out,
+    mgain_out,
+    router_out,
+    own_out,
+    gsum_ref,
+    usum_ref,
+    dsum_ref,
+    back,
+    y_in,
+    branch_own,
+    branch_sib,
+    normed_sib,
+    mixed_sib,
+    mg_t,
+    grad_t,
+    grad_sib,
+    kv_own,
+    kv_out,
+    kv_in,
+    weight_part,
+    weight_in,
+    y_out,
+    y_parts,
+    small_out,
+    small_in,
+    small_y,
+    small_y_in,
+    gain_out,
+    gain_in,
+    gain_y,
+    gain_y_in,
+    router_all,
+    c_send,
+    c_recv,
+    y1_send,
+    y1_recv,
+    y2_send,
+    y2_recv,
+    sib_send,
+    sib_recv,
+    rs_send,
+    rs_recv,
+    ys_send,
+    ys_recv,
+    sm_send,
+    sm_recv,
+):
+    y, r, x, z = place()
+    me = r * 16 + z * 4 + x
+    sibling = (y, 1 - r, z * 4 + x)
+    tokens = routed_ref.shape[0]
+    f32, bf16 = jnp.float32, jnp.bfloat16
+
+    barrier = pltpu.get_barrier_semaphore()
+
+    @pl.loop(1, GROUP)
+    def _(k):
+        device, _ = shifted(k, 1)
+        pl.semaphore_signal(barrier, inc=1, device_id=device, device_id_type=MESH)
+
+    for n in range(1, PLANES):
+        device, _ = plane_shift(n)
+        pl.semaphore_signal(barrier, inc=1, device_id=device, device_id_type=MESH)
+    pl.semaphore_wait(barrier, GROUP - 1 + PLANES - 1)
+
+    def result(k):
+        device, _ = shifted(k, -1)
+        return remote(prod_ref.at[k], back.at[k], c_send.at[k], c_recv.at[k], device)
+
+    parts = ((dg_ref, gsum_ref, 256), (du_ref, usum_ref, 256), (dd_ref, dsum_ref, 128))
+
+    def quarter(j, n):
+        device, other = plane_shift(n)
+        source, _, rows = parts[j]
+        at = 3 * j + n - 1
+        return remote(
+            source.at[pl.ds(other * rows, rows)],
+            y_in[j].at[n - 1],
+            y1_send.at[at],
+            y1_recv.at[at],
+            device,
+        )
+
+    def summed_quarter(j, n):
+        device, _ = plane_shift(n)
+        _, total, rows = parts[j]
+        at = 3 * j + n - 1
+        mine = total.at[pl.ds(y * rows, rows)]
+        return remote(mine, mine, y2_send.at[at], y2_recv.at[at], device)
+
+    half = pl.ds(pl.multiple_of((1 - r) * HALF, HALF), HALF)
+    sib_normed = remote(normed_ref.at[:, half], normed_sib, sib_send.at[0], sib_recv.at[0], sibling)
+    sib_mixed = remote(mixed_ref.at[:, half], mixed_sib, sib_send.at[1], sib_recv.at[1], sibling)
+    sib_branch = remote(branch_own, branch_sib, sib_send.at[2], sib_recv.at[2], sibling)
+    sib_kv = remote(kv_out, kv_in, sib_send.at[3], sib_recv.at[3], sibling)
+    sib_query = remote(
+        grad_t.at[pl.ds(0, D)], grad_sib.at[pl.ds(0, D)], sib_send.at[4], sib_recv.at[4], sibling
+    )
+    sib_keyval = remote(
+        grad_t.at[pl.ds(D, D)], grad_sib.at[pl.ds(D, D)], sib_send.at[5], sib_recv.at[5], sibling
+    )
+
+    sib_mixed.start()
+    sib_normed.start()
+    for n in range(1, PLANES):
+        for j in range(3):
+            quarter(j, n).start()
+
+    @pl.loop(1, GROUP)
+    def _(k):
+        result(k).start()
+
+    back[0] = prod_ref[0]
+
+    gates = gates_ref[...]
+    gdot = gdot_ref[...]
+    logit_grad = gates * (gdot - jnp.sum(gates * gdot, axis=0, keepdims=True))
+    high, rest = split_two(logit_grad)
+    router_part = dot(high, routed_ref[...], ((1,), (0,)))
+    router_part = router_part + dot(rest, routed_ref[...], ((1,), (0,)))
+    routed_grad = dot(high, router_ref[...], ((0,), (0,)))
+    routed_grad = routed_grad + dot(rest, router_ref[...], ((0,), (0,)))
+    routed_grad = routed_grad + rg_ref[...]
+    live = (
+        r * tokens + lax.broadcasted_iota(jnp.int32, (tokens, 1), 0) < length_ref[0]
+    ).astype(f32)
+    middle = middle_ref[...]
+    scale = lax.rsqrt(jnp.mean(middle * middle, axis=1, keepdims=True) + epsilon)
+    rows = middle * scale
+    moe_part = jnp.sum(routed_grad * rows, axis=0, keepdims=True)
+    scaled = routed_grad * mgain_ref[...]
+    inner = jnp.mean(scaled * rows, axis=1, keepdims=True)
+    middle_grad = cot_ref[...].astype(f32) * live + scale * (scaled - rows * inner)
+    hgrad_ref[...] = middle_grad
+    branch_own[...] = middle_grad.astype(bf16)
+    sib_branch.start()
+    for j in range(8):
+        part = slice(128 * j, 128 * j + 128)
+        small_out[:, j, :] = router_part[:, part]
+        small_out[:, 8 + j, :] = jnp.broadcast_to(moe_part[:, part], (GROUP, 128))
+
+    def small(k):
+        device, other = shifted(k, 1)
+        return remote(small_out.at[other], small_in.at[me], sm_send.at[k], sm_recv.at[k], device)
+
+    @pl.loop(1, GROUP)
+    def _(k):
+        small(k).start()
+
+    small_in[me] = small_out[me]
+
+    mg_t[...] = dot(w_ref[:, 2 * D : 3 * D], branch_own[...], ((1,), (1,))).astype(bf16)
+
+    sib_mixed.wait_recv()
+    sib_branch.wait_recv()
+    mine = pl.ds(pl.multiple_of(r * HALF, HALF), HALF)
+
+    def rows_part(q, at, first, width):
+        device, other = chip_shift(q, 1)
+        _, own = chip_shift(0, 1)
+        return remote(
+            weight_part.at[pl.ds(other * 32, 32), pl.ds(first, width)],
+            weight_in.at[own, :, pl.ds(first, width)],
+            rs_send.at[at * CHIPS + q],
+            rs_recv.at[at * CHIPS + q],
+            device,
+        )
+
+    pieces = ((2 * D, D), (0, D), (D, D))
+
+    def send_part(at, left_own, left_sib, right_own, right_sib, contract):
+        first, width = pieces[at]
+        total = dot(left_own, right_own, ((0,), (contract,)))
+        total = total + dot(left_sib, right_sib, ((0,), (contract,)))
+        weight_part[:, first : first + width] = total.astype(bf16)
+
+        @pl.loop(1, CHIPS)
+        def _(q):
+            rows_part(q, at, first, width).start()
+
+        _, own = chip_shift(0, 1)
+        weight_in[own, :, first : first + width] = weight_part[
+            pl.ds(own * 32, 32), first : first + width
+        ]
+
+    def sum_part(at):
+        first, width = pieces[at]
+
+        @pl.loop(1, CHIPS)
+        def _(q):
+            rows_part(q, at, first, width).wait_recv()
+
+        total = weight_in[0, :, first : first + width].astype(f32)
+        for s in range(1, CHIPS):
+            total = total + weight_in[s, :, first : first + width].astype(f32)
+        y_out[:, first : first + width] = total.astype(bf16)
+        y_parts[y, :, first : first + width] = total.astype(bf16)
+        for n in range(1, PLANES):
+            across(at, n).start()
+
+    def across(at, n):
+        first, width = pieces[at]
+        device, _ = plane_shift(n)
+        return remote(
+            y_out.at[:, pl.ds(first, width)],
+            y_parts.at[y, :, pl.ds(first, width)],
+            ys_send.at[at * 3 + n - 1],
+            ys_recv.at[at * 3 + n - 1],
+            device,
+        )
+
+    send_part(0, mixed_ref[:, mine], mixed_sib[...], branch_own[...], branch_sib[...], 0)
+
+    key_live = lax.broadcasted_iota(jnp.int32, (2 * tokens, 1), 0) < length_ref[0]
+    score_scale = HEAD ** (-0.5)
+    cosine, sine = cos_ref[...], sin_ref[...]
+
+    def key_head(g):
+        head = pl.ds(pl.multiple_of(g * HEAD, HEAD), HEAD)
+        keys, values = k_ref[head, :], v_ref[head, :]
+        key_sum, value_sum = None, None
+        for j in range(2):
+            at = pl.ds(pl.multiple_of((2 * g + j) * HEAD, HEAD), HEAD)
+            query, mixed_grad = q_ref[at, :], mg_t[at, :]
+            scores = dot(keys, query, ((0,), (0,))) * score_scale
+            scores = jnp.where(key_live, scores, NEG)
+            probs = jnp.exp(scores - lse_ref[pl.ds(2 * g + j, 1), :])
+            prob_grad = dot(values, mixed_grad, ((0,), (0,)))
+            value_part = dot(mixed_grad, probs.astype(bf16), ((1,), (1,)))
+            inner = jnp.sum(probs * prob_grad, axis=0, keepdims=True)
+            score_grad = (probs * (prob_grad - inner)).astype(bf16)
+            key_part = dot(query, score_grad, ((1,), (1,)))
+            query_grad = dot(keys, score_grad, ((1,), (0,))) * score_scale
+            grad_t[at, :] = turned_back(query_grad, cosine, sine).astype(bf16)
+            key_sum = key_part if key_sum is None else key_sum + key_part
+            value_sum = value_part if value_sum is None else value_sum + value_part
+        key_sum = key_sum * score_scale
+        low = pl.ds(pl.multiple_of(g * HEAD, HEAD), HEAD)
+        high = pl.ds(pl.multiple_of(HALF + g * HEAD, HEAD), HEAD)
+        first = r == 0
+        kv_own[low, :] = jnp.where(first, key_sum[:, :tokens], key_sum[:, tokens:])
+        kv_own[high, :] = jnp.where(first, value_sum[:, :tokens], value_sum[:, tokens:])
+        kv_out[low, :] = jnp.where(first, key_sum[:, tokens:], key_sum[:, :tokens]).astype(bf16)
+        kv_out[high, :] = jnp.where(first, value_sum[:, tokens:], value_sum[:, :tokens]).astype(bf16)
+
+    pl.loop(0, 4)(key_head)
+
+    for j in range(3):
+        source, total, rows_of = parts[j]
+        mine_y = pl.ds(y * rows_of, rows_of)
+        acc = source[mine_y, :].astype(f32)
+        for n in range(1, PLANES):
+            quarter(j, n).wait_recv()
+        for n in range(1, PLANES):
+            acc = acc + y_in[j][n - 1].astype(f32)
+        total[mine_y, :] = acc.astype(bf16)
+        for n in range(1, PLANES):
+            summed_quarter(j, n).start()
+
+    @pl.loop(1, GROUP)
+    def _(k):
+        small(k).wait_recv()
+
+    def small_across(n):
+        device, _ = plane_shift(n)
+        return remote(
+            small_y, small_y_in.at[y], sm_send.at[GROUP + n], sm_recv.at[GROUP + n], device
+        )
+
+    small_y[...] = jnp.sum(small_in[...], axis=0)
+    small_y_in[y] = small_y[...]
+    for n in range(1, PLANES):
+        small_across(n).start()
+
+    pl.loop(4, 8)(key_head)
+
+    sib_kv.start()
+    sib_query.start()
+
+    for n in range(1, PLANES):
+        small_across(n).wait_recv()
+    totals = small_y_in[0] + small_y_in[1] + small_y_in[2] + small_y_in[3]
+    mgain_out[...] = totals[8:16]
+    router_all[me] = totals[0:8]
+
+    def router_row(k):
+        device, _ = shifted(k, 1)
+        at = 2 * GROUP + k
+        return remote(
+            router_all.at[me], router_all.at[me], sm_send.at[at], sm_recv.at[at], device
+        )
+
+    @pl.loop(1, GROUP)
+    def _(k):
+        router_row(k).start()
+
+    sib_normed.wait_recv()
+    sib_query.wait_recv()
+    send_part(1, normed_ref[:, mine], normed_sib[...], grad_t[0:D, :], grad_sib[0:D, :], 1)
+    sib_kv.wait_recv()
+
+    @pl.loop(0, 8)
+    def _(g):
+        low = pl.ds(pl.multiple_of(g * HEAD, HEAD), HEAD)
+        total = kv_own[low, :] + kv_in[low, :].astype(f32)
+        to = pl.ds(pl.multiple_of(D + g * HEAD, HEAD), HEAD)
+        grad_t[to, :] = turned_back(total, cosine, sine).astype(bf16)
+
+    grad_t[D + HALF : 2 * D, :] = (
+        kv_own[HALF:D, :] + kv_in[HALF:D, :].astype(f32)
+    ).astype(bf16)
+    sib_keyval.start()
+    normed_grad = dot(grad_t[0:D, :], w_ref[:, 0:D], ((0,), (1,)))
+    sib_keyval.wait_recv()
+    send_part(2, normed_ref[:, mine], normed_sib[...], grad_t[D:, :], grad_sib[D:, :], 1)
+    normed_grad = normed_grad + dot(grad_t[D:, :], w_ref[:, D : 2 * D], ((0,), (1,)))
+
+    inputs = hidden_ref[...].astype(f32)
+    scale = lax.rsqrt(jnp.mean(inputs * inputs, axis=1, keepdims=True) + epsilon)
+    rows = inputs * scale
+    attn_part = jnp.sum(normed_grad * rows, axis=0, keepdims=True)
+    for j in range(8):
+        gain_out[j : j + 1, :] = attn_part[:, 128 * j : 128 * j + 128]
+
+    def gain(k):
+        device, _ = shifted(k, 1)
+        at = 3 * GROUP + k
+        return remote(gain_out, gain_in.at[me], sm_send.at[at], sm_recv.at[at], device)
+
+    @pl.loop(1, GROUP)
+    def _(k):
+        gain(k).start()
+
+    gain_in[me] = gain_out[...]
+    scaled = normed_grad * again_ref[...]
+    inner = jnp.mean(scaled * rows, axis=1, keepdims=True)
+    hgrad_ref[...] += scale * (scaled - rows * inner)
+
+    slot_iota = lax.broadcasted_iota(jnp.int32, (CAP, tokens), 0)
+
+    def mix(c, total):
+        chosen = []
+        for i in range(SPAN):
+            k = c * SPAN + i
+
+            @pl.when(k != 0)
+            def _():
+                result(k).wait_recv()
+
+            _, expert = shifted(k, 1)
+            picked = slot_iota == pos_ref[pl.ds(expert, 1), :]
+            chosen.append(jnp.where(picked, gates_ref[pl.ds(expert, 1), :], 0.0))
+        high, rest = split_two(jnp.concatenate(chosen, axis=0))
+        rows = back[pl.ds(c * SPAN, SPAN)].reshape(SPAN * CAP, D)
+        total = total + dot(high, rows, ((0,), (0,)))
+        return total + dot(rest, rows, ((0,), (0,)))
+
+    mixture = lax.fori_loop(0, CHUNKS, mix, jnp.zeros((tokens, D), f32))
+    hout_ref[...] = ((middle_ref[...] + mixture) * live).astype(bf16)
+
+    for at in range(3):
+        sum_part(at)
+
+    @pl.loop(1, GROUP)
+    def _(k):
+        gain(k).wait_recv()
+
+    gain_y[...] = jnp.sum(gain_in[...], axis=0)
+    gain_y_in[y] = gain_y[...]
+
+    def gain_across(n):
+        device, _ = plane_shift(n)
+        at = 4 * GROUP + n
+        return remote(gain_y, gain_y_in.at[y], sm_send.at[at], sm_recv.at[at], device)
+
+    for n in range(1, PLANES):
+        gain_across(n).start()
+    for at in range(3):
+        for n in range(1, PLANES):
+            across(at, n).wait_recv()
+    own_out[...] = (y_parts[0].astype(f32) + y_parts[1].astype(f32)) + (
+        y_parts[2].astype(f32) + y_parts[3].astype(f32)
+    )
+    for n in range(1, PLANES):
+        gain_across(n).wait_recv()
+    again_out[...] = (gain_y_in[0] + gain_y_in[1]) + (gain_y_in[2] + gain_y_in[3])
+
+    @pl.loop(1, GROUP)
+    def _(k):
+        router_row(k).wait_recv()
+
+    router_out[...] = router_all[...]
+
+    @pl.loop(1, GROUP)
+    def _(k):
+        result(k).wait_send()
+        small(k).wait_send()
+        router_row(k).wait_send()
+        gain(k).wait_send()
+
+    for at in range(3):
+        first, width = pieces[at]
+
+        @pl.loop(1, CHIPS)
+        def _(q):
+            rows_part(q, at, first, width).wait_send()
+
+    for n in range(1, PLANES):
+        for j in range(3):
+            quarter(j, n).wait_send()
+            summed_quarter(j, n).wait()
+            across(j, n).wait_send()
+        small_across(n).wait_send()
+        gain_across(n).wait_send()
+    for copy in (sib_normed, sib_mixed, sib_branch, sib_kv, sib_query, sib_keyval):
+        copy.wait_send()
+
+
+def finish(length, *arrays):
+    (prod, pos, gates, rg, gdot, dg, du, dd, routed) = arrays[:9]
+    tokens = routed.shape[0]
+    f32, bf16 = jnp.float32, jnp.bfloat16
+    vmem = pl.BlockSpec(memory_space=pltpu.VMEM)
+    shape = jax.ShapeDtypeStruct
+    sems = pltpu.SemaphoreType.DMA
+    scratch = [
+        pltpu.VMEM((GROUP, CAP, D), bf16),
+        [
+            pltpu.VMEM((3, 256, 512), bf16),
+            pltpu.VMEM((3, 256, 512), bf16),
+            pltpu.VMEM((3, 128, 1024), bf16),
+        ],
+        pltpu.VMEM((tokens, D), bf16),
+        pltpu.VMEM((tokens, D), bf16),
+        pltpu.VMEM((tokens, HALF), bf16),
+        pltpu.VMEM((tokens, HALF), bf16),
+        pltpu.VMEM((D, tokens), bf16),
+        pltpu.VMEM((2 * D, tokens), bf16),
+        pltpu.VMEM((2 * D, tokens), bf16),
+        pltpu.VMEM((D, tokens), f32),
+        pltpu.VMEM((D, tokens), bf16),
+        pltpu.VMEM((D, tokens), bf16),
+        pltpu.VMEM((HALF, 3 * D), bf16),
+        pltpu.VMEM((CHIPS, 32, 3 * D), bf16),
+        pltpu.VMEM((32, 3 * D), bf16),
+        pltpu.VMEM((PLANES, 32, 3 * D), bf16),
+        pltpu.VMEM((GROUP, 16, 128), f32),
+        pltpu.VMEM((GROUP, 16, 128), f32),
+        pltpu.VMEM((16, 128), f32),
+        pltpu.VMEM((PLANES, 16, 128), f32),
+        pltpu.VMEM((8, 128), f32),
+        pltpu.VMEM((GROUP, 8, 128), f32),
+        pltpu.VMEM((8, 128), f32),
+        pltpu.VMEM((PLANES, 8, 128), f32),
+        pltpu.VMEM((GROUP, 8, 128), f32),
+    ]
+    for count in (GROUP, 9, 9, 6, 3 * CHIPS, 9, 5 * GROUP):
+        scratch += [sems((count,)), sems((count,))]
+    return pl.pallas_call(
+        finish_kernel,
+        out_shape=(
+            shape((tokens, D), bf16),
+            shape((tokens, D), f32),
+            shape((8, 128), f32),
+            shape((8, 128), f32),
+            shape((GROUP, 8, 128), f32),
+            shape((32, 3 * D), f32),
+            shape(dg.shape, bf16),
+            shape(du.shape, bf16),
+            shape(dd.shape, bf16),
+        ),
+        in_specs=[pl.BlockSpec(memory_space=pltpu.SMEM)] + [vmem] * len(arrays),
+        out_specs=[vmem] * 9,
+        scratch_shapes=scratch,
+        compiler_params=pltpu.CompilerParams(
+            collective_id=2, has_side_effects=True, vmem_limit_bytes=60 << 20
+        ),
+        name="finish",
+    )(length, *arrays)
+
+
 def on_device(
     hidden_in,
     cotangent,
@@ -427,7 +900,6 @@
     down_weight,
 ):
     row_total = lax.axis_size("row")
-    col_total = lax.axis_size("col")
     tok_count = hidden_in.shape[0]
     seq_len = row_total * tok_count
     groups = HEADS // KV_HEADS
@@ -455,7 +927,6 @@
     arrived_grad = lax.all_to_all(
         outgoing_grad, ("row", "col"), split_axis=0, concat_axis=0, tiled=True
     )
-    grad_out = cotangent.astype(jnp.float32) * live_float
     inputs = hidden_in.astype(jnp.float32)
     scale_one = rms_scale(inputs)
     normed_one = inputs * scale_one
@@ -507,119 +978,63 @@
     picked = jnp.where(routed_to, logits, -jnp.inf)
     picked_exp = jnp.exp(picked - jnp.max(picked, axis=1, keepdims=True))
     gates_te = picked_exp / jnp.sum(picked_exp, axis=1, keepdims=True)
+    gates_et = gates_te.T
     returned_rows, gate_dot_et, produced, gate_local, up_local, down_local = experts(
-        routed, pos_et, gates_te.T, arrived_grad, gate_weight[0], up_weight[0], down_weight[0]
-    )
-    returned = lax.all_to_all(produced, ("row", "col"), split_axis=0, concat_axis=0, tiled=True)
-    gate_dot = gate_dot_et.T
-    picked_grad = gates_te * (
-        gate_dot - jnp.sum(gates_te * gate_dot, axis=1, keepdims=True)
-    )
-    logit_grad = picked_grad
-    router_local = jnp.dot(
-        routed.astype(jnp.float32).T, logit_grad, precision=lax.Precision.HIGHEST
-    )
-    routed_grad = jnp.dot(logit_grad, router.astype(jnp.float32).T, precision=lax.Precision.HIGHEST)
-    routed_grad = routed_grad + returned_rows
-    middle_norm_grad, moe_gain_local = norm_back(routed_grad, normed_two, scale_two, moe_gain)
-    middle_grad = grad_out + middle_norm_grad
-    branch_grad = middle_grad.astype(jnp.bfloat16)
-    mixed_grad = jnp.einsum("te,de->td", branch_grad, w_out, preferred_element_type=jnp.float32)
-    mixed_grad = mixed_grad.astype(jnp.bfloat16).reshape(tok_count, KV_HEADS, groups, HEAD)
-    probs_again = jnp.exp(masked_scores() - log_total)
-    prob_grad = jnp.einsum(
-        "tkgd,jkd->kgtj", mixed_grad, all_values, preferred_element_type=jnp.float32
-    )
-    value_part = jnp.einsum(
-        "kgtj,tkgd->jkd",
-        probs_again.astype(jnp.bfloat16),
-        mixed_grad,
-        preferred_element_type=jnp.float32,
-    )
-    inner_sum = jnp.sum(probs_again * prob_grad, axis=-1, keepdims=True)
-    score_grad = (probs_again * (prob_grad - inner_sum)).astype(jnp.bfloat16)
-    query_rot_grad = (
-        jnp.einsum("kgtj,jkd->tkgd", score_grad, all_keys, preferred_element_type=jnp.float32)
-        * score_scale
-    )
-    key_part = (
-        jnp.einsum("kgtj,tkgd->jkd", score_grad, queries, preferred_element_type=jnp.float32)
-        * score_scale
-    )
-    key_sum, value_sum = in_one_piece(
-        (key_part.astype(jnp.bfloat16), value_part.astype(jnp.bfloat16)), "row", 0, 1
-    )
-    query_pre_grad = (
-        rotary(query_rot_grad.reshape(tok_count, HEADS, HEAD), positions, -1.0)
-        .reshape(tok_count, D)
-        .astype(jnp.bfloat16)
-    )
-    key_pre_grad = (
-        rotary(key_sum, positions, -1.0).reshape(tok_count, kv_width).astype(jnp.bfloat16)
-    )
-    value_pre_grad = value_sum.reshape(tok_count, kv_width).astype(jnp.bfloat16)
-    normed_grad = jnp.einsum(
-        "tc,dc->td", query_pre_grad, w_query, preferred_element_type=jnp.float32
-    )
-    normed_grad = normed_grad + jnp.einsum(
-        "tc,dc->td", key_pre_grad, w_key, preferred_element_type=jnp.float32
-    )
-    normed_grad = normed_grad + jnp.einsum(
-        "tc,dc->td", value_pre_grad, w_value, preferred_element_type=jnp.float32
-    )
-    input_norm_grad, attn_gain_local = norm_back(normed_grad, normed_one, scale_one, attn_gain)
-    hidden_grad = middle_grad + input_norm_grad
-    qkv_grad = jnp.concatenate([query_pre_grad, key_pre_grad, value_pre_grad], axis=1)
-    grad_part = lax.psum_scatter(
-        jnp.concatenate(
-            [
-                jnp.einsum("tr,tc->rc", normed, qkv_grad, preferred_element_type=jnp.float32),
-                jnp.einsum(
-                    "tr,tc->rc", mixed_rows, branch_grad, preferred_element_type=jnp.float32
-                ),
-            ],
-            axis=1,
-        ).astype(jnp.bfloat16),
-        ("row", "col"),
-        scatter_dimension=0,
-        tiled=True,
-    )
-    grad_shard, gate_sum, up_sum, down_sum = (
-        sum_in_two_steps(grad_part, "dp").astype(jnp.float32),
-        sum_in_two_steps(gate_local.astype(jnp.bfloat16), "dp").astype(jnp.float32),
-        sum_in_two_steps(up_local.astype(jnp.bfloat16), "dp").astype(jnp.float32),
-        sum_in_two_steps(down_local.astype(jnp.bfloat16), "dp").astype(jnp.float32),
-    )
-    attn_gain_sum, moe_gain_sum, router_sum = lax.psum(
-        (attn_gain_local, moe_gain_local, router_local), ("dp", "row", "col")
-    )
-    gate_rows = jnp.sum(
-        jnp.where(onehot.reshape(EXPERTS, CAP, tok_count) > 0, gates_te.T[:, None, :], 0.0),
-        axis=2,
-    )
-    weighted = (returned.astype(jnp.float32) * gate_rows[:, :, None]).reshape(EXPERTS * CAP, D)
-    high = weighted.astype(jnp.bfloat16)
-    rest = (weighted - high.astype(jnp.float32)).astype(jnp.bfloat16)
-    mixture = jnp.einsum("st,sd->td", onehot, high, preferred_element_type=jnp.float32)
-    mixture = mixture + jnp.einsum("st,sd->td", onehot, rest, preferred_element_type=jnp.float32)
-    hidden_out = ((middle + mixture) * live_float).astype(jnp.bfloat16)
-    query_grad = grad_shard[:, :D]
-    key_grad = grad_shard[:, D : D + kv_width]
-    value_grad = grad_shard[:, D + kv_width : D + 2 * kv_width]
-    output_grad = grad_shard[:, D + 2 * kv_width :]
+        routed, pos_et, gates_et, arrived_grad, gate_weight[0], up_weight[0], down_weight[0]
+    )
+    half_dim = HEAD // 2
+    frequency = rotary_base ** (-jnp.arange(half_dim, dtype=jnp.float32) / half_dim)
+    angles = frequency[:, None] * positions.astype(jnp.float32)[None, :]
+    (
+        hidden_out,
+        hidden_grad,
+        attn_gain_sum,
+        moe_gain_sum,
+        router_sum,
+        own_rows,
+        gate_sum,
+        up_sum,
+        down_sum,
+    ) = finish(
+        lengths,
+        produced,
+        pos_et,
+        gates_et,
+        returned_rows,
+        gate_dot_et,
+        gate_local,
+        up_local,
+        down_local,
+        routed,
+        router.T,
+        middle,
+        cotangent,
+        hidden_in,
+        attn_gain[None],
+        moe_gain[None],
+        normed,
+        mixed_rows,
+        jnp.concatenate([w_query, w_key, w_value, w_out], axis=1),
+        queries.reshape(tok_count, D).T,
+        all_keys.reshape(seq_len, kv_width).T,
+        all_values.reshape(seq_len, kv_width).T,
+        log_total.reshape(HEADS, tok_count),
+        jnp.cos(angles),
+        jnp.sin(angles),
+    )
     return (
         hidden_out,
         hidden_grad,
-        attn_gain_sum,
-        query_grad,
-        key_grad,
-        value_grad,
-        output_grad,
-        moe_gain_sum,
-        router_sum,
-        gate_sum[None],
-        up_sum[None],
-        down_sum[None],
+        attn_gain_sum.reshape(D),
+        own_rows[:, :D],
+        own_rows[:, D : D + kv_width],
+        own_rows[:, D + kv_width : 2 * D],
+        own_rows[:, 2 * D :],
+        moe_gain_sum.reshape(D),
+        router_sum.reshape(EXPERTS, D).T,
+        gate_sum.astype(jnp.float32)[None],
+        up_sum.astype(jnp.float32)[None],
+        down_sum.astype(jnp.float32)[None],
     )
 
 

time: 693 us -> 408 us (0.59)
  waiting for transfers between devices: 356 us -> 76.1 us
  Pallas kernels: 123 us -> 254 us
  blocking collectives: 76.5 us -> 0 us
  matrix products: 54.1 us -> 19.8 us
  starting transfers between devices: 20.3 us -> 5.01 us
  other arithmetic: 37.3 us -> 22.7 us
    psum x1 -> x0, waiting for transfers between devices: 137 us -> none  [on_device(): lax.psum((attn_gain_local, moe_gain_local, router_local), ('dp', 'row', '...]
    reduce_scatter x5 -> x0, waiting for transfers between devices: 130 us -> none  [the longest x1 85.8 us: on_device(): lax.psum_scatter(jnp.concatenate([jnp.einsum('tr,tc->rc', normed, qkv_gra...]
    pallas_call x0 -> x1, Pallas kernels: none -> 129 us  [finish(): pl.pallas_call(finish_kernel, out_shape=(shape((tokens, D), bf16), shape(...]
    psum x1 -> x0, blocking collectives: 66.8 us -> none  [on_device(): lax.psum((attn_gain_local, moe_gain_local, router_local), ('dp', 'row', '...]
    dot_general x14 -> x0, matrix products: 37 us -> none  [the longest x1 5.59 us: on_device(): jnp.einsum('tkgd,jkd->kgtj', mixed_grad, all_values, preferred_element_ty...]
    all_to_all x2 -> x0, starting transfers between devices: 14.3 us -> none  [the longest x1 9.16 us: on_device(): lax.all_to_all(produced, ('row', 'col'), split_axis=0, concat_axis=0, til...]
    all_gather x1 -> x0, blocking collectives: 9.75 us -> none  [sum_in_two_steps(): whole = lax.all_gather(own, axis, axis=0, tiled=True)]
    all_to_all x1, waiting for transfers between devices: 41.1 us -> 31.4 us  [on_device(): lax.all_to_all(outgoing_grad, ('row', 'col'), split_axis=0, concat_axis=0...]
  transfers between devices with their start and end apart: 14 -> 3, of which waited for: 8 -> 2; matrix products, arithmetic and copies ran while one was open for 13% -> 8% of each run, Pallas kernels for 0% -> 0%
where the time goes in v2:
time: 408 us; the launch traced here: 407 us
  Pallas kernels  254 us (62%)
  waiting for transfers between devices  76.1 us (19%)
  other arithmetic  22.7 us (6%)
  matrix products  19.8 us (5%)
  between operations  15 us (4%)
  local copies, waits for them, and re-layouts  14.7 us (4%)
  starting transfers between devices  5.01 us (1%)
    pallas_call x1, Pallas kernels, finish(): pl.pallas_call(finish_kernel, out_shape=(shape((tokens, D), bf16), shape(...  129 us
    pallas_call x1, Pallas kernels, experts(): pl.pallas_call(expert_kernel, out_shape=(jax.ShapeDtypeStruct((tokens, D)...  125 us
    all_gather x2, waiting for transfers between devices, sent_together(): whole = lax.all_gather(both, axis, axis=dim, tiled=True)  44.7 us
    all_to_all x1, waiting for transfers between devices, on_device(): lax.all_to_all(outgoing_grad, ('row', 'col'), split_axis=0, concat_axis=0...  31.4 us
    unnamed x34, local copies, waits for them, and re-layouts  8.32 us
  transfers between devices with their start and end apart: 3, of which 2 were waited for; matrix products, arithmetic and copies ran while one was open for 8% of the time, Pallas kernels for 0%

profile of v2, /device:TPU:1, one launch (start us, length us, event | category | flops | bytes accessed | tf_op | source)
XLA Modules:
  0.0 407.3 jit_solution(7183304074224582258)
XLA Ops:
  7.2 0.0 copy-start.6
  7.2 0.0 all-gather.3.cloned.1.call-start
  7.2 1.6 pad_maximum_fusion.2
  8.9 0.0 all-gather.3.cloned.1.call-update
  8.9 0.0 all-gather.5.cloned.1.call-start
  9.6 0.1 eq.39
  9.7 0.5 broadcast.143
  10.2 1.4 reduce.3
  11.6 0.1 broadcast_in_dim.92
  11.7 0.1 copy.45
  11.7 0.7 fusion.22
  12.5 0.7 select_reduce_fusion
  13.2 2.6 convert_reduce_fusion
  15.8 0.0 copy-start.8
  15.9 0.5 bitcast_compare_fusion
  16.4 1.2 fusion.10
  17.6 0.2 multiply_cosine_fusion.1
  17.8 1.2 fusion.12.normed_ref
  19.0 0.0 copy-start.5
  19.0 44.7 %all-gather.3.cloned.1.call-done.w_ref = bf16[1024,3072]{1,0:T(8,128)(2,1)} async-done(((bf16[32,3072]{1,0:T(8,128)(2,1)}), bf16[1024,3072]{1,0:T(8,128)(2,1)}) %all-gather.3.cloned.1.call-update) | async-done | bytes 6291472 | tf_op jit(solution)/shard_map/all_gather | solution.py:26
  63.8 1.7 convolution_convert_fusion.1
  65.4 0.1 copy.42
  65.6 1.8 fusion.14
  67.3 0.1 subtract_convert_fusion.1
  67.4 0.8 pad_maximum_fusion
  68.2 0.0 all-gather.5.cloned.1.call-update
  68.3 0.0 copy-done.6
  68.3 3.3 convolution_convert_fusion
  71.5 0.0 copy-done.8
  71.6 4.9 %all-to-all-start = ((bf16[32,64,1024]{2,1,0:T(8,128)(2,1)}), bf16[32,64,1024]{2,1,0:T(8,128)(2,1)}, u32[]{:S(2)}, u32[]{:S(2)}) async-start(bf16[32,64,1024]{2,1,0:T(8,128)(2,1)} %bitcast.86), calls=%async_computation | async-start | bytes 8388608 | tf_op jit(solution)/shard_map/all_to_all | solution.py:927
  76.5 0.8 multiply_sine_fusion
  77.3 0.0 copy-done.5
  77.3 2.6 fusion.5
  79.9 0.2 subtract_convert_fusion
  80.1 0.8 pad_maximum_fusion.1
  80.9 3.0 bitcast_reduce_fusion
  83.9 3.2 copy-done
  87.1 2.0 fusion.1
  89.2 0.6 add.59.lse_ref
  89.8 4.8 %fusion.9 = bf16[8,64,2,256]{3,1,2,0:T(8,128)(2,1)S(1)} fusion(f32[8,512,256,2]{2,1,3,0:T(8,128)} %copy-done, f32[8,2,256]{2,1,0:T(2,128)S(1)} %fusion.1, f32[8,2,256]{2,1,0:T(2,128)S(1)} %get-tuple-element.56, pred[512]{0:T(512)(128)(4,1)S(1)} %iota_compare_fusion.1, bf16[512,16,64]{0,2,1:T(8,128)(2,1)S(1)} %copy-done.4), kind=kOutput, calls=%fused_computation.17 | convolution fusion | flops 279183360 | bytes 9470464 | tf_op jit(solution)/shard_map/kgtj,jkd->tkgd/dot_general | solution.py:969
  94.6 0.0 copy-start.10
  94.6 1.0 copy.46.mixed_ref
  95.6 0.0 copy-done.2
  95.6 2.4 multiply_reduce_fusion
  98.1 0.0 copy-start.1
  98.1 0.2 multiply_convert_fusion.routed_ref
  98.3 0.0 copy-start.3
  98.3 0.3 fusion.34
  98.6 0.6 divide_bitcast_fusion.gates_ref
  99.2 1.1 fusion.31
  100.3 31.4 %all-to-all-done.grads_ref = bf16[32,64,1024]{2,1,0:T(8,128)(2,1)} async-done(((bf16[32,64,1024]{2,1,0:T(8,128)(2,1)}), bf16[32,64,1024]{2,1,0:T(8,128)(2,1)}, u32[]{:S(2)}, u32[]{:S(2)}) %all-to-all-start) | async-done | bytes 4194336 | tf_op jit(solution)/shard_map/all_to_all | solution.py:927
  131.7 0.0 copy-done.3
  131.7 124.7 %experts.1 = (f32[256,1024]{1,0:T(8,128)}, f32[32,256]{1,0:T(8,128)}, bf16[32,64,1024]{2,1,0:T(8,128)(2,1)}, bf16[1024,512]{1,0:T(8,128)(2,1)}, bf16[1024,512]{1,0:T(8,128)(2,1)}, /*index=5*/bf16[512,1024]{1,0:T(8,128)(2,1)}) custom-call(bf16[256,1024]{1,0:T(8,128)(2,1)} %copy-done.3, s32[32,256]{1,0:T(8,128)} %copy-done.8, ...), custom_call_target="tpu_custom_call" | custom-call | tf_op jit(solution)/shard_map/experts/pallas_call | solution.py:297
  256.4 0.0 copy-done.1
  256.4 129.2 %finish.1 = (bf16[256,1024]{1,0:T(8,128)(2,1)}, f32[256,1024]{1,0:T(8,128)}, f32[8,128]{1,0:T(8,128)}, f32[8,128]{1,0:T(8,128)}, f32[32,8,128]{2,1,0:T(8,128)}, ...) custom-call(s32[1]{0:T(128)} %copy.61.length_ref, ...), custom_call_target="tpu_custom_call" | custom-call | tf_op jit(solution)/shard_map/finish/pallas_call | solution.py:862
  385.6 1.6 fusion.33
  387.3 1.7 fusion.32
  389.0 1.6 copy.54
  390.6 2.8 bitcast_convert_fusion
  393.3 4.1 %bitcast_convert_fusion.1 = (f32[1,1024,512]{2,1,0:T(8,128)}, f32[1,1024,512]{2,1,0:T(8,128)}) fusion(bf16[1024,512]{1,0:T(8,128)(2,1)} %get-tuple-element.40, bf16[1024,512]{1,0:T(8,128)(2,1)} %get-tuple-element.39), kind=kLoop, calls=%fused_computation.27 | loop fusion | flops 1048576 | bytes 6291456 | tf_op jit(solution)/shard_map/broadcast_in_dim | solution.py:1036
  397.5 0.8 copy.62
  398.3 1.0 copy.63
  399.3 0.6 copy.64
  399.9 0.6 copy.65
  (27 shorter events, 0.1 us)
Async XLA Ops:
  7.2 61.1 %copy-start.6 = (bf16[256,1024]{1,0:T(8,128)(2,1)S(1)}, bf16[256,1024]{1,0:T(8,128)(2,1)}, u32[]{:S(2)}) copy-start(bf16[256,1024]{1,0:T(8,128)(2,1)} %cot_ref.1) | copy-start | bytes 1572868
  7.2 56.6 %all-gather.3.cloned.1.call-start = ((), (), s32[]{:S(2)}) async-start(), calls=%async_computation.1 | async-start | bytes 6488064 | tf_op jit(solution)/shard_map/all_gather | solution.py:26
  8.9 72.0 %all-gather.5.cloned.1.call-start = ((), (), s32[]{:S(2)}) async-start(), calls=%async_computation.2 | async-start | bytes 1572864 | tf_op jit(solution)/shard_map/all_gather | solution.py:26
  15.8 55.7 %copy-start.8 = (s32[32,256]{1,0:T(8,128)}, s32[32,256]{1,0:T(8,128)S(1)}, u32[]{:S(2)}) copy-start(s32[32,256]{1,0:T(8,128)S(1)} %and_select_fusion.pos_ref) | copy-start | bytes 98308
  19.0 58.3 %copy-start.5 = (bf16[256,1024]{1,0:T(8,128)(2,1)}, bf16[256,1024]{1,0:T(8,128)(2,1)S(1)}, u32[]{:S(2)}) copy-start(bf16[256,1024]{1,0:T(8,128)(2,1)S(1)} %fusion.12.normed_ref) | copy-start | bytes 1572868
  71.6 60.2 %all-to-all-start = ((bf16[32,64,1024]{2,1,0:T(8,128)(2,1)}), bf16[32,64,1024]{2,1,0:T(8,128)(2,1)}, u32[]{:S(2)}, u32[]{:S(2)}) async-start(bf16[32,64,1024]{2,1,0:T(8,128)(2,1)} %bitcast.86), calls=%async_computation | async-start | bytes 8388608 | tf_op jit(solution)/shard_map/all_to_all | solution.py:927
  83.9 3.2 copy-start
  83.9 5.9 %copy-start.4 = (bf16[512,16,64]{0,2,1:T(8,128)(2,1)S(1)}, bf16[512,16,64]{0,2,1:T(8,128)(2,1)}, u32[]{:S(2)}) copy-start(bf16[512,16,64]{0,2,1:T(8,128)(2,1)} %all-gather.5.cloned.1.call-done) | copy-start | bytes 3145732
  89.8 5.9 %copy-start.2 = (bf16[256,1024]{1,0:T(8,128)(2,1)S(1)}, bf16[256,1024]{1,0:T(8,128)(2,1)}, u32[]{:S(2)}) copy-start(bf16[256,1024]{1,0:T(8,128)(2,1)} %hidden_ref.1) | copy-start | bytes 1572868
  89.8 8.3 %copy-start.11 = (f32[1024]{0:T(1024)S(1)}, f32[1024]{0:T(1024)}, u32[]{:S(2)}) copy-start(f32[1024]{0:T(1024)} %param.25) | copy-start | bytes 12292
  94.6 3.6 copy-start.10
  98.1 158.3 %copy-start.1 = (f32[256,1024]{1,0:T(8,128)}, f32[256,1024]{1,0:T(8,128)S(1)}, u32[]{:S(2)}) copy-start(f32[256,1024]{1,0:T(8,128)S(1)} %get-tuple-element.59.middle_ref) | copy-start | bytes 3145732
  98.3 33.5 %copy-start.3 = (bf16[256,1024]{1,0:T(8,128)(2,1)}, bf16[256,1024]{1,0:T(8,128)(2,1)S(1)}, u32[]{:S(2)}) copy-start(bf16[256,1024]{1,0:T(8,128)(2,1)S(1)} %multiply_convert_fusion.routed_ref) | copy-start | bytes 1572868
  385.6 11.9 %copy-start.9 = (bf16[256,1024]{1,0:T(8,128)(2,1)S(1)}, bf16[256,1024]{1,0:T(8,128)(2,1)}, u32[]{:S(2)}) copy-start(bf16[256,1024]{1,0:T(8,128)(2,1)} %get-tuple-element.76) | copy-start | bytes 1572868
  385.6 12.7 %copy-start.7 = (f32[256,1024]{1,0:T(8,128)S(1)}, f32[256,1024]{1,0:T(8,128)}, u32[]{:S(2)}) copy-start(f32[256,1024]{1,0:T(8,128)} %get-tuple-element.77) | copy-start | bytes 3145732
  390.5 8.7 %copy-start.13 = (f32[8,128]{1,0:T(8,128)S(1)}, f32[8,128]{1,0:T(8,128)}, u32[]{:S(2)}) copy-start(f32[8,128]{1,0:T(8,128)} %get-tuple-element.35) | copy-start | bytes 12292
  390.6 9.3 %copy-start.12 = (f32[8,128]{1,0:T(8,128)S(1)}, f32[8,128]{1,0:T(8,128)}, u32[]{:S(2)}) copy-start(f32[8,128]{1,0:T(8,128)} %get-tuple-element.37) | copy-start | bytes 12292
Sparse Core Ops, SparseCore 0:
  10.8 52.8 all-gather.2
  68.4 10.5 all-gather.4

commit v3 on v2

v3 whole, which is shorter than its diff:
```python
import jax
import jax.numpy as jnp
from jax import lax
from jax.experimental import pallas as pl
from jax.experimental.pallas import tpu as pltpu
from jax.sharding import PartitionSpec as P

D = 1024
HEADS = 16
HEAD = 64
KV_HEADS = 8
EXPERTS = 32
TOP = 8
CAP = 64


epsilon = 1e-05
rotary_base = 10000.0


MESH = pl.DeviceIdType.MESH
GROUP = 32
PLANES = 4
CHIPS = 16
HALF = D // 2
TOKENS = 256
NEG = -1000000000.0


def place():
    col = lax.axis_index("col")
    return lax.axis_index("dp"), lax.axis_index("row"), lax.rem(col, 4), col // 4


def moved(dx, dz, core):
    y, r, x, z = place()
    col = lax.rem(z + dz + 4, 4) * 4 + lax.rem(x + dx + 4, 4)
    return (y, core, col), core * CHIPS + col


def plane_shift(n):
    y, r, x, z = place()
    other = lax.rem(y + n, PLANES)
    return (other, r, z * 4 + x), other


def step_of(k, sign):
    y, r, x, z = place()
    return moved(sign * lax.rem(k, 4), sign * lax.rem(k // 4, 4), lax.rem(r + k // CHIPS, 2))


def remote(src, dst, send_sem, recv_sem, device):
    return pltpu.make_async_remote_copy(
        src_ref=src,
        dst_ref=dst,
        send_sem=send_sem,
        recv_sem=recv_sem,
        device_id=device,
        device_id_type=MESH,
    )


def meet(plane, planes):
    barrier = pltpu.get_barrier_semaphore()
    y, r, x, z = place()

    def greet(device):
        pl.semaphore_signal(barrier, inc=1, device_id=device, device_id_type=MESH)

    if plane:

        @pl.loop(1, GROUP)
        def _(k):
            greet(step_of(k, 1)[0])

        count = GROUP - 1
    else:
        for core in range(2):

            @pl.loop(1, 4)
            def _(d):
                greet(moved(d, 0, core)[0])
                greet(moved(0, d, core)[0])

        greet(moved(0, 0, 1 - r)[0])
        count = 13
    if planes:
        for n in range(1, PLANES):
            greet(plane_shift(n)[0])
        count += PLANES - 1
    pl.semaphore_wait(barrier, count)


def eye(n):
    return lax.broadcasted_iota(jnp.int32, (n, n), 0) == lax.broadcasted_iota(
        jnp.int32, (n, n), 1
    )


def as_row(column):
    return jnp.sum(jnp.where(eye(column.shape[0]), column, 0.0), axis=0, keepdims=True)


def as_column(row_vec):
    return jnp.sum(jnp.where(eye(row_vec.shape[1]), row_vec, 0.0), axis=1, keepdims=True)


def dot(a, b, dims):
    return lax.dot_general(a, b, (dims, ((), ())), preferred_element_type=jnp.float32)


def split_two(values):
    high = values.astype(jnp.bfloat16)
    return high, (values - high.astype(jnp.float32)).astype(jnp.bfloat16)


def picks(positions):
    slots = lax.broadcasted_iota(jnp.int32, (CAP, positions.shape[1]), 0)
    return slots == positions


def as_hot(mask):
    return mask.astype(jnp.float32).astype(jnp.bfloat16)


LEFT = pl.ds(0, HALF)
RIGHT = pl.ds(HALF, HALF)


def spread(d, source, tok_z, tok_x, send_sem, recv_sem):
    y, r, x, z = place()
    return (
        remote(
            source.at[:, LEFT], tok_z.at[d], send_sem.at[d], recv_sem.at[d], moved(0, d, r)[0]
        ),
        remote(
            source.at[:, RIGHT],
            tok_x.at[d],
            send_sem.at[4 + d],
            recv_sem.at[4 + d],
            moved(d, 0, r)[0],
        ),
    )


def slot_copies(out, into, core, there, dz, dx, send_sem, recv_sem, sign):
    y, r, x, z = place()
    at = there * CHIPS + dz * 4 + dx
    to = core * CHIPS + dz * 4 + dx
    return (
        lambda: remote(
            out.at[there, dz, dx, :, LEFT],
            into.at[core, dz, dx, :, LEFT],
            send_sem.at[at],
            recv_sem.at[to],
            moved(sign * dx, 0, there)[0],
        ),
        lambda: remote(
            out.at[there, dz, dx, :, RIGHT],
            into.at[core, dz, dx, :, RIGHT],
            send_sem.at[GROUP + at],
            recv_sem.at[GROUP + to],
            moved(0, sign * dz, there)[0],
        ),
    )


def is_local(core, offset):
    y, r, x, z = place()
    return (core == r) & (offset == 0)


def send_slots(out, into, there, dz, dx, send_sem, recv_sem, sign):
    y, r, x, z = place()
    left, right = slot_copies(out, into, r, there, dz, dx, send_sem, recv_sem, sign)

    @pl.when(jnp.logical_not(is_local(there, dx)))
    def _():
        left().start()

    @pl.when(is_local(there, dx))
    def _():
        into[r, dz, dx, :, 0:HALF] = out[there, dz, dx, :, 0:HALF]

    @pl.when(jnp.logical_not(is_local(there, dz)))
    def _():
        right().start()

    @pl.when(is_local(there, dz))
    def _():
        into[r, dz, dx, :, HALF:D] = out[there, dz, dx, :, HALF:D]


def slots_arrived(out, into, core, dz, dx, send_sem, recv_sem, left=True, right=True):
    copies = slot_copies(out, into, core, core, dz, dx, send_sem, recv_sem, 1)
    for copy, offset, wanted in zip(copies, (dx, dz), (left, right)):
        if wanted:

            @pl.when(jnp.logical_not(is_local(core, offset)))
            def _():
                copy().wait_recv()


def slots_sent(out, into, send_sem, recv_sem):
    @pl.loop(0, GROUP)
    def _(k):
        there, dz, dx = k // CHIPS, lax.rem(k // 4, 4), lax.rem(k, 4)
        copies = slot_copies(out, into, there, there, dz, dx, send_sem, recv_sem, 1)
        for copy, offset in zip(copies, (dx, dz)):

            @pl.when(jnp.logical_not(is_local(there, offset)))
            def _():
                copy().wait_send()


def line_rows(line, d, axis):
    y, r, x, z = place()
    own = x if axis == 0 else z
    return [
        line[d, pl.ds(core * 4 + lax.rem(own + i, 4), 1), :] for core in range(2) for i in range(4)
    ]


def line_hot(line, d, axis):
    return as_hot(jnp.concatenate([picks(p) for p in line_rows(line, d, axis)], axis=0))


def add_up(mid, line, d, axis):
    if axis == 0:
        rows = mid[:, d, :, :, 0:HALF]
    else:
        rows = mid[:, :, d, :, HALF:D]
    return dot(line_hot(line, d, axis), rows.reshape(8 * CAP, HALF), ((0,), (0,))).astype(
        jnp.bfloat16
    )


def part_copies(d, out, into, send_sem, recv_sem):
    y, r, x, z = place()
    return (
        lambda: remote(
            out.at[d, :, LEFT],
            into.at[d, :, LEFT],
            send_sem.at[d],
            recv_sem.at[d],
            moved(0, -d, r)[0],
        ),
        lambda: remote(
            out.at[d, :, RIGHT],
            into.at[d, :, RIGHT],
            send_sem.at[4 + d],
            recv_sem.at[4 + d],
            moved(-d, 0, r)[0],
        ),
    )


def fold_parts(out, into, mid, slots, slot_send, slot_recv, posz_ref, posx_ref, send_sem, recv_sem):
    @pl.loop(0, 4)
    def _(d):
        for core in range(2):
            for i in range(4):
                slots_arrived(slots, mid, core, d, i, slot_send, slot_recv, right=False)
        left = add_up(mid, posz_ref, d, 0)

        @pl.when(d == 0)
        def _():
            into[0, :, 0:HALF] = left

        @pl.when(d != 0)
        def _():
            out[d, :, 0:HALF] = left
            part_copies(d, out, into, send_sem, recv_sem)[0]().start()

        for core in range(2):
            for i in range(4):
                slots_arrived(slots, mid, core, i, d, slot_send, slot_recv, left=False)
        right = add_up(mid, posx_ref, d, 1)

        @pl.when(d == 0)
        def _():
            into[0, :, HALF:D] = right

        @pl.when(d != 0)
        def _():
            out[d, :, HALF:D] = right
            part_copies(d, out, into, send_sem, recv_sem)[1]().start()


def parts_arrived(out, into, send_sem, recv_sem):
    @pl.loop(1, 4)
    def _(d):
        for copy in part_copies(d, out, into, send_sem, recv_sem):
            copy().wait_recv()


def parts_sent(out, into, send_sem, recv_sem):
    @pl.loop(1, 4)
    def _(d):
        for copy in part_copies(d, out, into, send_sem, recv_sem):
            copy().wait_send()


def front_kernel(
    length_ref,
    hidden_ref,
    cot_ref,
    routes_ref,
    prio_ref,
    again_ref,
    mgain_ref,
    wq_ref,
    wk_ref,
    wv_ref,
    wo_ref,
    router_ref,
    cos_ref,
    sin_ref,
    w_ref,
    normed_ref,
    q_ref,
    k_ref,
    v_ref,
    lse_ref,
    mixed_ref,
    middle_ref,
    routed_ref,
    gates_ref,
    pos_ref,
    posz_ref,
    posx_ref,
    grads_ref,
    mixed_t,
    posz_out,
    posx_out,
    tok_z,
    tok_x,
    outgoing,
    w_send,
    w_recv,
    core_send,
    core_recv,
    kv_send,
    kv_recv,
    first_send,
    first_recv,
    slot_send,
    slot_recv,
    pos_send,
    pos_recv,
):
    y, r, x, z = place()
    f32, bf16 = jnp.float32, jnp.bfloat16
    sibling = moved(0, 0, 1 - r)[0]
    meet(False, False)

    w_ref[r, z, x, :, 0:D] = wq_ref[...]
    w_ref[r, z, x, :, D : D + HALF] = wk_ref[...]
    w_ref[r, z, x, :, D + HALF : 2 * D] = wv_ref[...]
    w_ref[r, z, x, :, 2 * D : 3 * D] = wo_ref[...]
    front, rear = pl.ds(0, D + HALF), pl.ds(D + HALF, D + HALF)

    def line_step(d):
        mine_q, mine_o = w_ref.at[r, z, x, :, front], w_ref.at[r, z, x, :, rear]
        return (
            remote(mine_q, mine_q, w_send.at[d], w_recv.at[d], moved(0, d, r)[0]),
            remote(mine_o, mine_o, w_send.at[4 + d], w_recv.at[4 + d], moved(d, 0, r)[0]),
        )

    def cross_step(e, d):
        at = 8 + 4 * e + d
        from_z = w_ref.at[r, lax.rem(z - e + 4, 4), x, :, front]
        from_x = w_ref.at[r, z, lax.rem(x - e + 4, 4), :, rear]
        return (
            remote(from_z, from_z, w_send.at[at], w_recv.at[at], moved(d, 0, r)[0]),
            remote(from_x, from_x, w_send.at[16 + at], w_recv.at[16 + at], moved(0, d, r)[0]),
        )

    def core_step(d):
        from_x = w_ref.at[r, :, lax.rem(x - d + 4, 4), :, front]
        from_z = w_ref.at[r, lax.rem(z - d + 4, 4), :, :, rear]
        return (
            remote(from_x, from_x, core_send.at[d], core_recv.at[d], sibling),
            remote(from_z, from_z, core_send.at[4 + d], core_recv.at[4 + d], sibling),
        )

    @pl.loop(1, 4)
    def _(d):
        for copy in line_step(d):
            copy.start()

    @pl.loop(1, 4)
    def _(d):
        for copy in cross_step(0, d):
            copy.start()

    tokens = hidden_ref.shape[0]
    experts_iota = lax.broadcasted_iota(jnp.int32, (EXPERTS, tokens), 0)
    live = r * tokens + lax.broadcasted_iota(jnp.int32, (1, tokens), 1) < length_ref[0]
    routed_to = jnp.zeros((EXPERTS, tokens), f32)
    ranks = jnp.zeros((EXPERTS, tokens), f32)
    for j in range(TOP):
        match = experts_iota == routes_ref[j : j + 1, :]
        routed_to = jnp.where(match, 1.0, routed_to)
        ranks = jnp.where(match, prio_ref[j : j + 1, :].astype(f32), ranks)
    far = float(1 << 20)
    ranks = jnp.where((routed_to > 0.0) & live, ranks, far)
    ranks_t = ranks.T
    rows = []
    for e in range(EXPERTS):
        earlier = ranks_t[:, e : e + 1] < ranks[e : e + 1, :]
        rows.append(jnp.sum(earlier.astype(f32), axis=0, keepdims=True))
    slots = jnp.concatenate(rows, axis=0)
    pos = jnp.where((ranks < far) & (slots < CAP), slots, -1.0).astype(jnp.int32)
    pos_ref[...] = pos
    for core in range(2):
        for i in range(4):
            at = core * CHIPS + 4 * i
            posz_out[i, 4 * core : 4 * core + 4, :] = pos[at : at + 4, :]
            for j in range(4):
                posx_out[j, 4 * core + i : 4 * core + i + 1, :] = pos[at + j : at + j + 1, :]
    posz_ref[0] = posz_out[z]
    posx_ref[0] = posx_out[x]
    tok_z[0] = cot_ref[:, 0:HALF]
    tok_x[0] = cot_ref[:, HALF:D]

    def pos_step(d):
        to_z, to_x = lax.rem(z + d, 4), lax.rem(x + d, 4)
        return (
            remote(
                posz_out.at[to_z],
                posz_ref.at[d],
                pos_send.at[d],
                pos_recv.at[d],
                moved(0, d, r)[0],
            ),
            remote(
                posx_out.at[to_x],
                posx_ref.at[d],
                pos_send.at[4 + d],
                pos_recv.at[4 + d],
                moved(d, 0, r)[0],
            ),
        )

    @pl.loop(1, 4)
    def _(d):
        for copy in pos_step(d):
            copy.start()

    @pl.loop(1, 4)
    def _(e):
        for copy in line_step(e):
            copy.wait_recv()

        @pl.loop(1, 4)
        def _(d):
            for copy in cross_step(e, d):
                copy.start()

    for copy in core_step(0):
        copy.start()

    inputs = hidden_ref[...].astype(f32)
    scale = lax.rsqrt(jnp.mean(inputs * inputs, axis=1, keepdims=True) + epsilon)
    normed_ref[...] = (inputs * scale * again_ref[...]).astype(bf16)

    @pl.loop(1, 4)
    def _(d):
        @pl.loop(0, 4)
        def _(e):
            for copy in cross_step(e, d):
                copy.wait_recv()

        for copy in core_step(d):
            copy.start()

    @pl.loop(1, 4)
    def _(d):
        for copy in spread(d, cot_ref, tok_z, tok_x, first_send, first_recv):
            copy.start()

    @pl.loop(0, 4)
    def _(d):
        for copy in core_step(d):
            copy.wait_recv()

    cosine, sine = cos_ref[...], sin_ref[...]
    here = pl.ds(pl.multiple_of(r * tokens, tokens), tokens)

    def projected(first):
        weight = w_ref[:, :, :, :, first : first + HALF].reshape(D, HALF)
        return dot(normed_ref[...], weight, ((1,), (0,))).T

    def turned(rows):
        parts = []
        for h in range(rows.shape[0] // HEAD):
            first, second = rows[HEAD * h : HEAD * h + 32], rows[HEAD * h + 32 : HEAD * h + HEAD]
            parts += [first * cosine - second * sine, second * cosine + first * sine]
        return jnp.concatenate(parts, axis=0).astype(bf16)

    key_copy = remote(
        k_ref.at[:, here], k_ref.at[:, here], kv_send.at[0], kv_recv.at[0], sibling
    )
    value_copy = remote(
        v_ref.at[:, here], v_ref.at[:, here], kv_send.at[1], kv_recv.at[1], sibling
    )
    k_ref[:, here] = turned(projected(D))
    key_copy.start()
    v_ref[:, here] = projected(D + HALF).astype(bf16)
    value_copy.start()
    q_ref[0:HALF, :] = turned(projected(0))
    q_ref[HALF:D, :] = turned(projected(HALF))

    @pl.loop(1, 4)
    def _(d):
        for copy in spread(d, cot_ref, tok_z, tok_x, first_send, first_recv):
            copy.wait_recv()
        for copy in pos_step(d):
            copy.wait_recv()

    @pl.loop(0, 4)
    def _(d):
        left = dot(line_hot(posz_ref, d, 0), tok_z[d], ((1,), (0,))).astype(bf16)
        right = dot(line_hot(posx_ref, d, 1), tok_x[d], ((1,), (0,))).astype(bf16)
        for core in range(2):
            for i in range(4):
                part = slice((core * 4 + i) * CAP, (core * 4 + i + 1) * CAP)
                outgoing[core, d, i, :, 0:HALF] = left[part]
                outgoing[core, i, d, :, HALF:D] = right[part]

    @pl.loop(0, CHIPS)
    def _(k):
        dx = lax.rem(k, 4)
        dz = lax.rem(dx + k // 4, 4)
        for core in range(2):
            send_slots(outgoing, grads_ref, core, dz, dx, slot_send, slot_recv, 1)

    key_copy.wait_recv()
    value_copy.wait_recv()

    key_live = lax.broadcasted_iota(jnp.int32, (2 * tokens, 1), 0) < length_ref[0]
    score_scale = HEAD ** (-0.5)

    @pl.loop(0, KV_HEADS)
    def _(g):
        head = pl.ds(pl.multiple_of(g * HEAD, HEAD), HEAD)
        keys, values = k_ref[head, :], v_ref[head, :]
        for j in range(2):
            at = pl.ds(pl.multiple_of((2 * g + j) * HEAD, HEAD), HEAD)
            scores = dot(keys, q_ref[at, :], ((0,), (0,))) * score_scale
            scores = jnp.where(key_live, scores, NEG)
            top = jnp.max(scores, axis=0, keepdims=True)
            weights = jnp.exp(scores - top)
            total = jnp.sum(weights, axis=0, keepdims=True)
            lse_ref[pl.ds(2 * g + j, 1), :] = top + jnp.log(total)
            probs = (weights * (1.0 / total)).astype(bf16)
            mixed_t[at, :] = dot(values, probs, ((1,), (0,))).astype(bf16)

    mixed_ref[...] = mixed_t[...].T
    w_out = w_ref[:, :, :, :, 2 * D : 3 * D].reshape(D, D)
    middle = hidden_ref[...].astype(f32) + dot(mixed_ref[...], w_out, ((1,), (0,)))
    middle_ref[...] = middle
    scale = lax.rsqrt(jnp.mean(middle * middle, axis=1, keepdims=True) + epsilon)
    routed_ref[...] = (middle * scale * mgain_ref[...]).astype(bf16)
    logits = dot(router_ref[...], routed_ref[...], ((1,), (1,)))
    logits = jnp.where(routed_to > 0.0, logits, -jnp.inf)
    picked = jnp.exp(logits - jnp.max(logits, axis=0, keepdims=True))
    gates_ref[...] = picked / jnp.sum(picked, axis=0, keepdims=True)

    @pl.loop(0, GROUP)
    def _(k):
        slots_arrived(
            outgoing,
            grads_ref,
            k // CHIPS,
            lax.rem(k // 4, 4),
            lax.rem(k, 4),
            slot_send,
            slot_recv,
        )

    slots_sent(outgoing, grads_ref, slot_send, slot_recv)

    @pl.loop(1, 4)
    def _(d):
        for copies in (
            line_step(d),
            core_step(d),
            pos_step(d),
            spread(d, cot_ref, tok_z, tok_x, first_send, first_recv),
        ):
            for copy in copies:
                copy.wait_send()

        @pl.loop(0, 4)
        def _(e):
            for copy in cross_step(e, d):
                copy.wait_send()

    for copy in core_step(0):
        copy.wait_send()
    key_copy.wait_send()
    value_copy.wait_send()


def front(length, *arrays):
    f32, bf16, i32 = jnp.float32, jnp.bfloat16, jnp.int32
    vmem = pl.BlockSpec(memory_space=pltpu.VMEM)
    shape = jax.ShapeDtypeStruct
    out_shape = (
        shape((2, 4, 4, 32, 3 * D), bf16),
        shape((TOKENS, D), bf16),
        shape((D, TOKENS), bf16),
        shape((HALF, 2 * TOKENS), bf16),
        shape((HALF, 2 * TOKENS), bf16),
        shape((HEADS, TOKENS), f32),
        shape((TOKENS, D), bf16),
        shape((TOKENS, D), f32),
        shape((TOKENS, D), bf16),
        shape((EXPERTS, TOKENS), f32),
        shape((EXPERTS, TOKENS), i32),
        shape((4, 8, TOKENS), i32),
        shape((4, 8, TOKENS), i32),
        shape((2, 4, 4, CAP, D), bf16),
    )
    scratch = [
        pltpu.VMEM((D, TOKENS), bf16),
        pltpu.VMEM((4, 8, TOKENS), i32),
        pltpu.VMEM((4, 8, TOKENS), i32),
        pltpu.VMEM((4, TOKENS, HALF), bf16),
        pltpu.VMEM((4, TOKENS, HALF), bf16),
        pltpu.VMEM((2, 4, 4, CAP, D), bf16),
    ]
    for count in (40, 8, 2, 8, 2 * GROUP, 8):
        scratch += [pltpu.SemaphoreType.DMA((count,))] * 2
    return pl.pallas_call(
        front_kernel,
        out_shape=out_shape,
        in_specs=[pl.BlockSpec(memory_space=pltpu.SMEM)] + [vmem] * len(arrays),
        out_specs=[vmem] * len(out_shape),
        scratch_shapes=scratch,
        compiler_params=pltpu.CompilerParams(
            collective_id=3, has_side_effects=True, vmem_limit_bytes=60 << 20
        ),
        name="front",
    )(length, *arrays)


def expert_kernel(
    routed_ref,
    pos_ref,
    posz_ref,
    posx_ref,
    gates_ref,
    grads_ref,
    wg_ref,
    wu_ref,
    wd_ref,
    rg_ref,
    gdot_ref,
    prod_ref,
    dg_ref,
    du_ref,
    dd_ref,
    tok_z,
    tok_x,
    outgoing,
    arrived,
    going_back,
    mid,
    parts_out,
    parts_in,
    gate_out,
    gate_in,
    dot_out,
    dot_in,
    active,
    weighted,
    pre_grads,
    first_send,
    first_recv,
    slot_send,
    slot_recv,
    back_send,
    back_recv,
    part_send,
    part_recv,
    small_send,
    small_recv,
):
    y, r, x, z = place()
    f32, bf16 = jnp.float32, jnp.bfloat16
    meet(True, False)

    @pl.loop(1, 4)
    def _(d):
        for copy in spread(d, routed_ref, tok_z, tok_x, first_send, first_recv):
            copy.start()

    tok_z[0] = routed_ref[:, 0:HALF]
    tok_x[0] = routed_ref[:, HALF:D]

    def small(k, out, into, sign, base, arriving=False):
        there, dz, dx = k // CHIPS, lax.rem(k // 4, 4), lax.rem(k, 4)
        slot = k if arriving else r * CHIPS + lax.rem(k, CHIPS)
        return remote(
            out.at[k],
            into.at[slot],
            small_send.at[base + k],
            small_recv.at[base + slot],
            moved(sign * dx, sign * dz, there)[0],
        )

    def own_slot(k):
        return k == r * CHIPS

    @pl.loop(0, GROUP)
    def _(k):
        there, dz, dx = k // CHIPS, lax.rem(k // 4, 4), lax.rem(k, 4)
        _, expert = moved(dx, dz, there)
        chosen = picks(pos_ref[pl.ds(expert, 1), :])
        gate_col = jnp.sum(
            jnp.where(chosen, gates_ref[pl.ds(expert, 1), :], 0.0), axis=1, keepdims=True
        )
        gate_out[k, 0:1, 0:CAP] = as_row(gate_col)

        @pl.when(own_slot(k))
        def _():
            gate_in[k] = gate_out[k]

        @pl.when(jnp.logical_not(own_slot(k)))
        def _():
            small(k, gate_out, gate_in, 1, 0).start()

    @pl.loop(1, 4)
    def _(d):
        for copy in spread(d, routed_ref, tok_z, tok_x, first_send, first_recv):
            copy.wait_recv()

    @pl.loop(0, 4)
    def _(g):
        for dx in range(4):
            dz = lax.rem(dx + g, 4)
            left_rows, right_rows = [], []
            for core in range(2):
                at_x = core * 4 + lax.rem(x + dx, 4)
                at_z = core * 4 + lax.rem(z + dz, 4)
                left_rows.append(picks(posz_ref[dz, pl.ds(at_x, 1), :]))
                right_rows.append(picks(posx_ref[dx, pl.ds(at_z, 1), :]))
            left = dot(as_hot(jnp.concatenate(left_rows, axis=0)), tok_z[dz], ((1,), (0,)))
            right = dot(as_hot(jnp.concatenate(right_rows, axis=0)), tok_x[dx], ((1,), (0,)))
            for core in range(2):
                part = slice(core * CAP, core * CAP + CAP)
                outgoing[core, dz, dx, :, 0:HALF] = left[part].astype(bf16)
                outgoing[core, dz, dx, :, HALF:D] = right[part].astype(bf16)
                send_slots(outgoing, arrived, core, dz, dx, slot_send, slot_recv, 1)

    @pl.loop(0, 8)
    def _(c):
        g, core = c // 2, lax.rem(c, 2)
        rows, gate_cols, grads = [], [], []
        for dx in range(4):
            dz = lax.rem(dx + g, 4)
            k = core * CHIPS + dz * 4 + dx
            slots_arrived(outgoing, arrived, core, dz, dx, slot_send, slot_recv)

            @pl.when(jnp.logical_not(own_slot(k)))
            def _():
                small(k, gate_out, gate_in, 1, 0, True).wait_recv()

            rows.append(arrived[core, dz, dx])
            gate_cols.append(as_column(gate_in[k, 0:1, 0:CAP]))
            grads.append(grads_ref[core, dz, dx])
        rows = jnp.concatenate(rows, axis=0)
        gate_cols = jnp.concatenate(gate_cols, axis=0)
        grads = jnp.concatenate(grads, axis=0).astype(f32)
        gate_pre = dot(rows, wg_ref[...], ((1,), (0,)))
        up_pre = dot(rows, wu_ref[...], ((1,), (0,)))
        gate_sig = jax.nn.sigmoid(gate_pre)
        gate_act = gate_pre * gate_sig
        act = (gate_act * up_pre).astype(bf16)
        produced = dot(act, wd_ref[...], ((1,), (0,))).astype(bf16).astype(f32)
        dots = jnp.sum(produced * grads, axis=1, keepdims=True)
        produced_grad = (gate_cols * grads).astype(bf16)
        act_grad = dot(produced_grad, wd_ref[...], ((1,), (1,))).astype(bf16).astype(f32)
        gate_grad = (
            act_grad * up_pre * gate_sig * (1.0 + gate_pre * (1.0 - gate_sig))
        ).astype(bf16)
        up_grad = (act_grad * gate_act).astype(bf16)
        row_grads = dot(gate_grad, wg_ref[...], ((1,), (1,)))
        row_grads = (row_grads + dot(up_grad, wu_ref[...], ((1,), (1,)))).astype(bf16)
        produced = (produced * gate_cols).astype(bf16)
        for dx in range(4):
            dz = lax.rem(dx + g, 4)
            k = core * CHIPS + dz * 4 + dx
            part = slice(dx * CAP, dx * CAP + CAP)
            going_back[core, dz, dx] = row_grads[part]
            send_slots(going_back, mid, core, dz, dx, back_send, back_recv, -1)
            dot_out[k, 0:1, 0:CAP] = as_row(dots[part])

            @pl.when(own_slot(k))
            def _():
                dot_in[k] = dot_out[k]

            @pl.when(jnp.logical_not(own_slot(k)))
            def _():
                small(k, dot_out, dot_in, -1, GROUP).start()

            prod_ref[core, dz, dx] = produced[part]
            active[core, dz, dx] = act[part]
            weighted[core, dz, dx] = produced_grad[part]
            pre_grads[core, dz, dx, :, 0:HALF] = gate_grad[part]
            pre_grads[core, dz, dx, :, HALF:D] = up_grad[part]

    all_rows = GROUP * CAP

    @pl.loop(0, 2)
    def _(n):
        span = pl.ds(pl.multiple_of(n * 256, 256), 256)
        left = active[:, :, :, :, span].reshape(all_rows, 256)
        right = weighted[...].reshape(all_rows, D)
        dd_ref[span, :] = dot(left, right, ((0,), (0,))).astype(bf16)

    fold_parts(
        parts_out,
        parts_in,
        mid,
        going_back,
        back_send,
        back_recv,
        posz_ref,
        posx_ref,
        part_send,
        part_recv,
    )

    @pl.loop(0, 4)
    def _(n):
        span = pl.ds(pl.multiple_of(n * 256, 256), 256)
        left = arrived[:, :, :, :, span].reshape(all_rows, 256)
        part = dot(left, pre_grads[...].reshape(all_rows, D), ((0,), (0,)))
        dg_ref[span, :] = part[:, 0:HALF].astype(bf16)
        du_ref[span, :] = part[:, HALF:D].astype(bf16)

    @pl.loop(0, GROUP)
    def _(k):
        @pl.when(jnp.logical_not(own_slot(k)))
        def _():
            small(k, dot_out, dot_in, -1, GROUP, True).wait_recv()

        there, dz, dx = k // CHIPS, lax.rem(k // 4, 4), lax.rem(k, 4)
        _, expert = moved(dx, dz, there)
        at = pl.ds(expert, 1)
        dots = as_column(dot_in[k, 0:1, 0:CAP])
        gdot_ref[at, :] = jnp.sum(
            jnp.where(picks(pos_ref[at, :]), dots, 0.0), axis=0, keepdims=True
        )

    parts_arrived(parts_out, parts_in, part_send, part_recv)
    rg_ref[...] = (parts_in[0].astype(f32) + parts_in[1].astype(f32)) + (
        parts_in[2].astype(f32) + parts_in[3].astype(f32)
    )
    slots_sent(outgoing, arrived, slot_send, slot_recv)
    slots_sent(going_back, mid, back_send, back_recv)
    parts_sent(parts_out, parts_in, part_send, part_recv)

    @pl.loop(1, 4)
    def _(d):
        for copy in spread(d, routed_ref, tok_z, tok_x, first_send, first_recv):
            copy.wait_send()

    @pl.loop(0, GROUP)
    def _(k):
        @pl.when(jnp.logical_not(own_slot(k)))
        def _():
            small(k, gate_out, gate_in, 1, 0).wait_send()
            small(k, dot_out, dot_in, -1, GROUP).wait_send()


def experts(*arrays):
    f32, bf16 = jnp.float32, jnp.bfloat16
    wg, wu, wd = arrays[-3:]
    vmem = pl.BlockSpec(memory_space=pltpu.VMEM)
    shape = jax.ShapeDtypeStruct
    block = pltpu.VMEM((2, 4, 4, CAP, D), bf16)
    narrow = pltpu.VMEM((2, 4, 4, CAP, HALF), bf16)
    line = pltpu.VMEM((4, TOKENS, HALF), bf16)
    wide = pltpu.VMEM((4, TOKENS, D), bf16)
    little = pltpu.VMEM((GROUP, 8, 128), f32)
    scratch = [line, line, block, block, block, block, wide, wide]
    scratch += [little] * 4 + [narrow, block, block]
    for count in (8, 2 * GROUP, 2 * GROUP, 8, 2 * GROUP):
        scratch += [pltpu.SemaphoreType.DMA((count,))] * 2
    out_shape = (
        shape((TOKENS, D), f32),
        shape((EXPERTS, TOKENS), f32),
        shape((2, 4, 4, CAP, D), bf16),
        shape(wg.shape, bf16),
        shape(wu.shape, bf16),
        shape(wd.shape, bf16),
    )
    return pl.pallas_call(
        expert_kernel,
        out_shape=out_shape,
        in_specs=[vmem] * len(arrays),
        out_specs=[vmem] * len(out_shape),
        scratch_shapes=scratch,
        compiler_params=pltpu.CompilerParams(
            collective_id=1, has_side_effects=True, vmem_limit_bytes=60 << 20
        ),
        name="experts",
    )(*arrays)


def chip_shift(q, sign):
    y, r, x, z = place()
    dx, dz = lax.rem(q, 4), lax.rem(lax.rem(q, 4) + q // 4, 4)
    col = lax.rem(z + sign * dz + 4, 4) * 4 + lax.rem(x + sign * dx + 4, 4)
    return (y, r, col), col


def turned_back(rows, cosine, sine):
    first, second = rows[0:32], rows[32:64]
    return jnp.concatenate(
        [first * cosine + second * sine, second * cosine - first * sine], axis=0
    )


def finish_kernel(
    length_ref,
    prod_ref,
    posz_ref,
    posx_ref,
    gates_ref,
    rg_ref,
    gdot_ref,
    dg_ref,
    du_ref,
    dd_ref,
    routed_ref,
    router_ref,
    middle_ref,
    cot_ref,
    hidden_ref,
    again_ref,
    mgain_ref,
    normed_ref,
    mixed_ref,
    w_ref,
    q_ref,
    k_ref,
    v_ref,
    lse_ref,
    cos_ref,
    sin_ref,
    hout_ref,
    hgrad_ref,
    again_out,
    mgain_out,
    router_out,
    own_out,
    gsum_ref,
    usum_ref,
    dsum_ref,
    mid,
    parts_out,
    parts_in,
    y_in,
    branch_own,
    branch_sib,
    normed_sib,
    mixed_sib,
    mg_t,
    grad_t,
    grad_sib,
    kv_own,
    kv_out,
    kv_in,
    weight_part,
    weight_in,
    y_out,
    y_parts,
    small_out,
    small_in,
    small_y,
    small_y_in,
    gain_out,
    gain_in,
    gain_y,
    gain_y_in,
    router_all,
    c_send,
    c_recv,
    part_send,
    part_recv,
    y1_send,
    y1_recv,
    y2_send,
    y2_recv,
    sib_send,
    sib_recv,
    rs_send,
    rs_recv,
    ys_send,
    ys_recv,
    sm_send,
    sm_recv,
):
    y, r, x, z = place()
    me = r * 16 + z * 4 + x
    sibling = (y, 1 - r, z * 4 + x)
    tokens = routed_ref.shape[0]
    f32, bf16 = jnp.float32, jnp.bfloat16

    meet(True, True)

    parts = ((dg_ref, gsum_ref, 256), (du_ref, usum_ref, 256), (dd_ref, dsum_ref, 128))

    def quarter(j, n):
        device, other = plane_shift(n)
        source, _, rows = parts[j]
        at = 3 * j + n - 1
        return remote(
            source.at[pl.ds(other * rows, rows)],
            y_in[j].at[n - 1],
            y1_send.at[at],
            y1_recv.at[at],
            device,
        )

    def summed_quarter(j, n):
        device, _ = plane_shift(n)
        _, total, rows = parts[j]
        at = 3 * j + n - 1
        mine = total.at[pl.ds(y * rows, rows)]
        return remote(mine, mine, y2_send.at[at], y2_recv.at[at], device)

    def weight(first, width):
        return w_ref[:, :, :, :, first : first + width].reshape(D, width)

    half = pl.ds(pl.multiple_of((1 - r) * HALF, HALF), HALF)
    sib_normed = remote(normed_ref.at[:, half], normed_sib, sib_send.at[0], sib_recv.at[0], sibling)
    sib_mixed = remote(mixed_ref.at[:, half], mixed_sib, sib_send.at[1], sib_recv.at[1], sibling)
    sib_branch = remote(branch_own, branch_sib, sib_send.at[2], sib_recv.at[2], sibling)
    sib_kv = remote(kv_out, kv_in, sib_send.at[3], sib_recv.at[3], sibling)
    sib_query = remote(
        grad_t.at[pl.ds(0, D)], grad_sib.at[pl.ds(0, D)], sib_send.at[4], sib_recv.at[4], sibling
    )
    sib_keyval = remote(
        grad_t.at[pl.ds(D, D)], grad_sib.at[pl.ds(D, D)], sib_send.at[5], sib_recv.at[5], sibling
    )

    sib_mixed.start()
    sib_normed.start()
    for n in range(1, PLANES):
        for j in range(3):
            quarter(j, n).start()

    @pl.loop(0, CHIPS)
    def _(k):
        dx = lax.rem(k, 4)
        dz = lax.rem(dx + k // 4, 4)
        for core in range(2):
            send_slots(prod_ref, mid, core, dz, dx, c_send, c_recv, -1)

    gates = gates_ref[...]
    gdot = gdot_ref[...]
    logit_grad = gates * (gdot - jnp.sum(gates * gdot, axis=0, keepdims=True))
    high, rest = split_two(logit_grad)
    router_part = dot(high, routed_ref[...], ((1,), (0,)))
    router_part = router_part + dot(rest, routed_ref[...], ((1,), (0,)))
    routed_grad = dot(high, router_ref[...], ((0,), (0,)))
    routed_grad = routed_grad + dot(rest, router_ref[...], ((0,), (0,)))
    routed_grad = routed_grad + rg_ref[...]
    live = (
        r * tokens + lax.broadcasted_iota(jnp.int32, (tokens, 1), 0) < length_ref[0]
    ).astype(f32)
    middle = middle_ref[...]
    scale = lax.rsqrt(jnp.mean(middle * middle, axis=1, keepdims=True) + epsilon)
    rows = middle * scale
    moe_part = jnp.sum(routed_grad * rows, axis=0, keepdims=True)
    scaled = routed_grad * mgain_ref[...]
    inner = jnp.mean(scaled * rows, axis=1, keepdims=True)
    middle_grad = cot_ref[...].astype(f32) * live + scale * (scaled - rows * inner)
    hgrad_ref[...] = middle_grad
    branch_own[...] = middle_grad.astype(bf16)
    sib_branch.start()
    for j in range(8):
        part = slice(128 * j, 128 * j + 128)
        small_out[:, j, :] = router_part[:, part]
        small_out[:, 8 + j, :] = jnp.broadcast_to(moe_part[:, part], (GROUP, 128))

    def small(k):
        device, other = step_of(k, 1)
        return remote(small_out.at[other], small_in.at[me], sm_send.at[k], sm_recv.at[k], device)

    @pl.loop(1, GROUP)
    def _(k):
        small(k).start()

    small_in[me] = small_out[me]

    mg_t[...] = dot(weight(2 * D, D), branch_own[...], ((1,), (1,))).astype(bf16)

    sib_mixed.wait_recv()
    sib_branch.wait_recv()
    mine = pl.ds(pl.multiple_of(r * HALF, HALF), HALF)

    def rows_part(q, at, first, width):
        device, other = chip_shift(q, 1)
        _, own = chip_shift(0, 1)
        return remote(
            weight_part.at[pl.ds(other * 32, 32), pl.ds(first, width)],
            weight_in.at[own, :, pl.ds(first, width)],
            rs_send.at[at * CHIPS + q],
            rs_recv.at[at * CHIPS + q],
            device,
        )

    pieces = ((2 * D, D), (0, D), (D, D))

    def send_part(at, left_own, left_sib, right_own, right_sib, contract):
        first, width = pieces[at]
        total = dot(left_own, right_own, ((0,), (contract,)))
        total = total + dot(left_sib, right_sib, ((0,), (contract,)))
        weight_part[:, first : first + width] = total.astype(bf16)

        @pl.loop(1, CHIPS)
        def _(q):
            rows_part(q, at, first, width).start()

        _, own = chip_shift(0, 1)
        weight_in[own, :, first : first + width] = weight_part[
            pl.ds(own * 32, 32), first : first + width
        ]

    def sum_part(at):
        first, width = pieces[at]

        @pl.loop(1, CHIPS)
        def _(q):
            rows_part(q, at, first, width).wait_recv()

        total = weight_in[0, :, first : first + width].astype(f32)
        for s in range(1, CHIPS):
            total = total + weight_in[s, :, first : first + width].astype(f32)
        y_out[:, first : first + width] = total.astype(bf16)
        y_parts[y, :, first : first + width] = total.astype(bf16)
        for n in range(1, PLANES):
            across(at, n).start()

    def across(at, n):
        first, width = pieces[at]
        device, _ = plane_shift(n)
        return remote(
            y_out.at[:, pl.ds(first, width)],
            y_parts.at[y, :, pl.ds(first, width)],
            ys_send.at[at * 3 + n - 1],
            ys_recv.at[at * 3 + n - 1],
            device,
        )

    send_part(0, mixed_ref[:, mine], mixed_sib[...], branch_own[...], branch_sib[...], 0)

    key_live = lax.broadcasted_iota(jnp.int32, (2 * tokens, 1), 0) < length_ref[0]
    score_scale = HEAD ** (-0.5)
    cosine, sine = cos_ref[...], sin_ref[...]

    def key_head(g):
        head = pl.ds(pl.multiple_of(g * HEAD, HEAD), HEAD)
        keys, values = k_ref[head, :], v_ref[head, :]
        key_sum, value_sum = None, None
        for j in range(2):
            at = pl.ds(pl.multiple_of((2 * g + j) * HEAD, HEAD), HEAD)
            query, mixed_grad = q_ref[at, :], mg_t[at, :]
            scores = dot(keys, query, ((0,), (0,))) * score_scale
            scores = jnp.where(key_live, scores, NEG)
            probs = jnp.exp(scores - lse_ref[pl.ds(2 * g + j, 1), :])
            prob_grad = dot(values, mixed_grad, ((0,), (0,)))
            value_part = dot(mixed_grad, probs.astype(bf16), ((1,), (1,)))
            inner = jnp.sum(probs * prob_grad, axis=0, keepdims=True)
            score_grad = (probs * (prob_grad - inner)).astype(bf16)
            key_part = dot(query, score_grad, ((1,), (1,)))
            query_grad = dot(keys, score_grad, ((1,), (0,))) * score_scale
            grad_t[at, :] = turned_back(query_grad, cosine, sine).astype(bf16)
            key_sum = key_part if key_sum is None else key_sum + key_part
            value_sum = value_part if value_sum is None else value_sum + value_part
        key_sum = key_sum * score_scale
        low = pl.ds(pl.multiple_of(g * HEAD, HEAD), HEAD)
        high = pl.ds(pl.multiple_of(HALF + g * HEAD, HEAD), HEAD)
        first = r == 0
        kv_own[low, :] = jnp.where(first, key_sum[:, :tokens], key_sum[:, tokens:])
        kv_own[high, :] = jnp.where(first, value_sum[:, :tokens], value_sum[:, tokens:])
        kv_out[low, :] = jnp.where(first, key_sum[:, tokens:], key_sum[:, :tokens]).astype(bf16)
        kv_out[high, :] = jnp.where(first, value_sum[:, tokens:], value_sum[:, :tokens]).astype(bf16)

    pl.loop(0, 4)(key_head)

    for j in range(3):
        source, total, rows_of = parts[j]
        mine_y = pl.ds(y * rows_of, rows_of)
        acc = source[mine_y, :].astype(f32)
        for n in range(1, PLANES):
            quarter(j, n).wait_recv()
        for n in range(1, PLANES):
            acc = acc + y_in[j][n - 1].astype(f32)
        total[mine_y, :] = acc.astype(bf16)
        for n in range(1, PLANES):
            summed_quarter(j, n).start()

    @pl.loop(1, GROUP)
    def _(k):
        small(k).wait_recv()

    def small_across(n):
        device, _ = plane_shift(n)
        return remote(
            small_y, small_y_in.at[y], sm_send.at[GROUP + n], sm_recv.at[GROUP + n], device
        )

    small_y[...] = jnp.sum(small_in[...], axis=0)
    small_y_in[y] = small_y[...]
    for n in range(1, PLANES):
        small_across(n).start()

    fold_parts(
        parts_out,
        parts_in,
        mid,
        prod_ref,
        c_send,
        c_recv,
        posz_ref,
        posx_ref,
        part_send,
        part_recv,
    )
    pl.loop(4, 8)(key_head)

    sib_kv.start()
    sib_query.start()

    for n in range(1, PLANES):
        small_across(n).wait_recv()
    totals = small_y_in[0] + small_y_in[1] + small_y_in[2] + small_y_in[3]
    mgain_out[...] = totals[8:16]
    router_all[me] = totals[0:8]

    def router_row(k):
        device, _ = step_of(k, 1)
        at = 2 * GROUP + k
        return remote(
            router_all.at[me], router_all.at[me], sm_send.at[at], sm_recv.at[at], device
        )

    @pl.loop(1, GROUP)
    def _(k):
        router_row(k).start()

    sib_normed.wait_recv()
    sib_query.wait_recv()
    send_part(1, normed_ref[:, mine], normed_sib[...], grad_t[0:D, :], grad_sib[0:D, :], 1)
    sib_kv.wait_recv()

    @pl.loop(0, 8)
    def _(g):
        low = pl.ds(pl.multiple_of(g * HEAD, HEAD), HEAD)
        total = kv_own[low, :] + kv_in[low, :].astype(f32)
        to = pl.ds(pl.multiple_of(D + g * HEAD, HEAD), HEAD)
        grad_t[to, :] = turned_back(total, cosine, sine).astype(bf16)

    grad_t[D + HALF : 2 * D, :] = (
        kv_own[HALF:D, :] + kv_in[HALF:D, :].astype(f32)
    ).astype(bf16)
    sib_keyval.start()
    normed_grad = dot(grad_t[0:D, :], weight(0, D), ((0,), (1,)))
    sib_keyval.wait_recv()
    send_part(2, normed_ref[:, mine], normed_sib[...], grad_t[D:, :], grad_sib[D:, :], 1)
    normed_grad = normed_grad + dot(grad_t[D:, :], weight(D, D), ((0,), (1,)))

    inputs = hidden_ref[...].astype(f32)
    scale = lax.rsqrt(jnp.mean(inputs * inputs, axis=1, keepdims=True) + epsilon)
    rows = inputs * scale
    attn_part = jnp.sum(normed_grad * rows, axis=0, keepdims=True)
    for j in range(8):
        gain_out[j : j + 1, :] = attn_part[:, 128 * j : 128 * j + 128]

    def gain(k):
        device, _ = step_of(k, 1)
        at = 3 * GROUP + k
        return remote(gain_out, gain_in.at[me], sm_send.at[at], sm_recv.at[at], device)

    @pl.loop(1, GROUP)
    def _(k):
        gain(k).start()

    gain_in[me] = gain_out[...]
    scaled = normed_grad * again_ref[...]
    inner = jnp.mean(scaled * rows, axis=1, keepdims=True)
    hgrad_ref[...] += scale * (scaled - rows * inner)

    parts_arrived(parts_out, parts_in, part_send, part_recv)
    mixture = (parts_in[0].astype(f32) + parts_in[1].astype(f32)) + (
        parts_in[2].astype(f32) + parts_in[3].astype(f32)
    )
    hout_ref[...] = ((middle_ref[...] + mixture) * live).astype(bf16)

    for at in range(3):
        sum_part(at)

    @pl.loop(1, GROUP)
    def _(k):
        gain(k).wait_recv()

    gain_y[...] = jnp.sum(gain_in[...], axis=0)
    gain_y_in[y] = gain_y[...]

    def gain_across(n):
        device, _ = plane_shift(n)
        at = 4 * GROUP + n
        return remote(gain_y, gain_y_in.at[y], sm_send.at[at], sm_recv.at[at], device)

    for n in range(1, PLANES):
        gain_across(n).start()
    for at in range(3):
        for n in range(1, PLANES):
            across(at, n).wait_recv()
    own_out[...] = (y_parts[0].astype(f32) + y_parts[1].astype(f32)) + (
        y_parts[2].astype(f32) + y_parts[3].astype(f32)
    )
    for n in range(1, PLANES):
        gain_across(n).wait_recv()
    again_out[...] = (gain_y_in[0] + gain_y_in[1]) + (gain_y_in[2] + gain_y_in[3])

    @pl.loop(1, GROUP)
    def _(k):
        router_row(k).wait_recv()

    router_out[...] = router_all[...]

    slots_sent(prod_ref, mid, c_send, c_recv)
    parts_sent(parts_out, parts_in, part_send, part_recv)

    @pl.loop(1, GROUP)
    def _(k):
        small(k).wait_send()
        router_row(k).wait_send()
        gain(k).wait_send()

    for at in range(3):
        first, width = pieces[at]

        @pl.loop(1, CHIPS)
        def _(q):
            rows_part(q, at, first, width).wait_send()

    for n in range(1, PLANES):
        for j in range(3):
            quarter(j, n).wait_send()
            summed_quarter(j, n).wait()
            across(j, n).wait_send()
        small_across(n).wait_send()
        gain_across(n).wait_send()
    for copy in (sib_normed, sib_mixed, sib_branch, sib_kv, sib_query, sib_keyval):
        copy.wait_send()


def finish(length, *arrays):
    dg, du, dd = arrays[6:9]
    tokens = TOKENS
    f32, bf16 = jnp.float32, jnp.bfloat16
    vmem = pl.BlockSpec(memory_space=pltpu.VMEM)
    shape = jax.ShapeDtypeStruct
    sems = pltpu.SemaphoreType.DMA
    scratch = [
        pltpu.VMEM((2, 4, 4, CAP, D), bf16),
        pltpu.VMEM((4, tokens, D), bf16),
        pltpu.VMEM((4, tokens, D), bf16),
        [
            pltpu.VMEM((3, 256, 512), bf16),
            pltpu.VMEM((3, 256, 512), bf16),
            pltpu.VMEM((3, 128, 1024), bf16),
        ],
        pltpu.VMEM((tokens, D), bf16),
        pltpu.VMEM((tokens, D), bf16),
        pltpu.VMEM((tokens, HALF), bf16),
        pltpu.VMEM((tokens, HALF), bf16),
        pltpu.VMEM((D, tokens), bf16),
        pltpu.VMEM((2 * D, tokens), bf16),
        pltpu.VMEM((2 * D, tokens), bf16),
        pltpu.VMEM((D, tokens), f32),
        pltpu.VMEM((D, tokens), bf16),
        pltpu.VMEM((D, tokens), bf16),
        pltpu.VMEM((HALF, 3 * D), bf16),
        pltpu.VMEM((CHIPS, 32, 3 * D), bf16),
        pltpu.VMEM((32, 3 * D), bf16),
        pltpu.VMEM((PLANES, 32, 3 * D), bf16),
        pltpu.VMEM((GROUP, 16, 128), f32),
        pltpu.VMEM((GROUP, 16, 128), f32),
        pltpu.VMEM((16, 128), f32),
        pltpu.VMEM((PLANES, 16, 128), f32),
        pltpu.VMEM((8, 128), f32),
        pltpu.VMEM((GROUP, 8, 128), f32),
        pltpu.VMEM((8, 128), f32),
        pltpu.VMEM((PLANES, 8, 128), f32),
        pltpu.VMEM((GROUP, 8, 128), f32),
    ]
    for count in (2 * GROUP, 8, 9, 9, 6, 3 * CHIPS, 9, 5 * GROUP):
        scratch += [sems((count,)), sems((count,))]
    return pl.pallas_call(
        finish_kernel,
        out_shape=(
            shape((tokens, D), bf16),
            shape((tokens, D), f32),
            shape((8, 128), f32),
            shape((8, 128), f32),
            shape((GROUP, 8, 128), f32),
            shape((32, 3 * D), f32),
            shape(dg.shape, bf16),
            shape(du.shape, bf16),
            shape(dd.shape, bf16),
        ),
        in_specs=[pl.BlockSpec(memory_space=pltpu.SMEM)] + [vmem] * len(arrays),
        out_specs=[vmem] * 9,
        scratch_shapes=scratch,
        compiler_params=pltpu.CompilerParams(
            collective_id=2, has_side_effects=True, vmem_limit_bytes=60 << 20
        ),
        name="finish",
    )(length, *arrays)


def on_device(
    hidden_in,
    cotangent,
    lengths,
    routes,
    priority,
    attn_gain,
    query_weight,
    key_weight,
    value_weight,
    output_weight,
    moe_gain,
    router,
    gate_weight,
    up_weight,
    down_weight,
):
    tok_count = hidden_in.shape[0]
    kv_width = KV_HEADS * HEAD
    positions = lax.axis_index("row") * tok_count + jnp.arange(tok_count, dtype=jnp.int32)
    half_dim = HEAD // 2
    frequency = rotary_base ** (-jnp.arange(half_dim, dtype=jnp.float32) / half_dim)
    angles = frequency[:, None] * positions.astype(jnp.float32)[None, :]
    cosine, sine = jnp.cos(angles), jnp.sin(angles)
    router_t = router.T
    (
        weights,
        normed,
        queries,
        keys,
        values,
        log_total,
        mixed_rows,
        middle,
        routed,
        gates,
        pos,
        posz,
        posx,
        arrived_grad,
    ) = front(
        lengths,
        hidden_in,
        cotangent,
        routes.T,
        priority.reshape(tok_count, TOP).T,
        attn_gain[None],
        moe_gain[None],
        query_weight,
        key_weight,
        value_weight,
        output_weight,
        router_t,
        cosine,
        sine,
    )
    returned_rows, gate_dot, produced, gate_local, up_local, down_local = experts(
        routed,
        pos,
        posz,
        posx,
        gates,
        arrived_grad,
        gate_weight[0],
        up_weight[0],
        down_weight[0],
    )
    (
        hidden_out,
        hidden_grad,
        attn_gain_sum,
        moe_gain_sum,
        router_sum,
        own_rows,
        gate_sum,
        up_sum,
        down_sum,
    ) = finish(
        lengths,
        produced,
        posz,
        posx,
        gates,
        returned_rows,
        gate_dot,
        gate_local,
        up_local,
        down_local,
        routed,
        router_t,
        middle,
        cotangent,
        hidden_in,
        attn_gain[None],
        moe_gain[None],
        normed,
        mixed_rows,
        weights,
        queries,
        keys,
        values,
        log_total,
        cosine,
        sine,
    )
    return (
        hidden_out,
        hidden_grad,
        attn_gain_sum.reshape(D),
        own_rows[:, :D],
        own_rows[:, D : D + kv_width],
        own_rows[:, D + kv_width : 2 * D],
        own_rows[:, 2 * D :],
        moe_gain_sum.reshape(D),
        router_sum.reshape(EXPERTS, D).T,
        gate_sum.astype(jnp.float32)[None],
        up_sum.astype(jnp.float32)[None],
        down_sum.astype(jnp.float32)[None],
    )


def solution(mesh):
    return jax.shard_map(
        on_device,
        mesh=mesh,
        in_specs=(
            P(("dp", "col", "row"), None),
            P(("dp", "col", "row"), None),
            P(("dp", "col")),
            P(("dp", "col", "row"), None),
            P(("dp", "col", "row"), None),
            P(),
            P(("row", "col"), None),
            P(("row", "col"), None),
            P(("row", "col"), None),
            P(("row", "col"), None),
            P(),
            P(),
            P(("row", "col"), None, None),
            P(("row", "col"), None, None),
            P(("row", "col"), None, None),
        ),
        out_specs=(
            P(("dp", "col", "row"), None),
            P(("dp", "col", "row"), None),
            P(),
            P(("row", "col"), None),
            P(("row", "col"), None),
            P(("row", "col"), None),
            P(("row", "col"), None),
            P(),
            P(),
            P(("row", "col"), None, None),
            P(("row", "col"), None, None),
            P(("row", "col"), None, None),
        ),
        check_vma=False,
    )
```

time: 408 us -> 316 us (0.77)
  waiting for transfers between devices: 76.1 us -> 0 us
  Pallas kernels: 254 us -> 297 us
  matrix products: 19.8 us -> 0 us
  other arithmetic: 22.7 us -> 7.6 us
  between operations: 15 us -> 1.37 us
  local copies, waits for them, and re-layouts: 14.7 us -> 9.19 us
  starting transfers between devices: 5.01 us -> 0 us
    pallas_call x1 -> x2, Pallas kernels: 125 us -> 173 us  [the longest x1 92 us: experts(): pl.pallas_call(expert_kernel, out_shape=out_shape, in_specs=[vmem] * len(...]
    all_gather x2 -> x0, waiting for transfers between devices: 44.7 us -> none  [sent_together(): whole = lax.all_gather(both, axis, axis=dim, tiled=True)]
    all_to_all x1 -> x0, waiting for transfers between devices: 31.4 us -> none  [on_device(): lax.all_to_all(outgoing_grad, ('row', 'col'), split_axis=0, concat_axis=0...]
    dot_general x8 -> x0, matrix products: 19.8 us -> none  [the longest x1 4.83 us: on_device(): jnp.einsum('kgtj,jkd->tkgd', attn_probs, all_values, preferred_element_ty...]
    reduce_sum x5 -> x0, other arithmetic: 6.56 us -> none  [the longest x1 2.59 us: on_device(): jnp.sum((ranks_et[:, :, None] > ranks_et[:, None, :]).astype(jnp.int32),...]
    all_to_all x1 -> x0, starting transfers between devices: 4.93 us -> none  [on_device(): lax.all_to_all(outgoing_grad, ('row', 'col'), split_axis=0, concat_axis=0...]
    pallas_call x1, Pallas kernels: 129 us -> 125 us  [finish(): pl.pallas_call(finish_kernel, out_shape=(shape((tokens, D), bf16), shape(...]
    unnamed x34 -> x18, local copies, waits for them, and re-layouts: 8.32 us -> 5.22 us
  transfers between devices with their start and end apart: 3 -> 0, of which waited for: 2 -> 0; matrix products, arithmetic and copies ran while one was open for 8% -> 0% of each run, Pallas kernels for 0% -> 0%
where the time goes in v3:
time: 316 us
  Pallas kernels  297 us (94%)
  local copies, waits for them, and re-layouts  9.19 us (3%)
  other arithmetic  7.6 us (2%)
    pallas_call x1, Pallas kernels, finish(): pl.pallas_call(finish_kernel, out_shape=(shape((tokens, D), bf16), shape(...  125 us
    pallas_call x1, Pallas kernels, experts(): pl.pallas_call(expert_kernel, out_shape=out_shape, in_specs=[vmem] * len(...  92 us
    pallas_call x1, Pallas kernels, front(): pl.pallas_call(front_kernel, out_shape=out_shape, in_specs=[pl.BlockSpec(...  80.9 us

profile of v3, /device:TPU:1, one launch (start us, length us, event | category | flops | bytes accessed | tf_op | source)
XLA Modules:
  0.0 315.6 jit_solution(2661303423979040396)
XLA Ops:
  1.3 0.5 broadcast.16
  1.8 1.4 reduce.3
  3.2 0.8 multiply_sine_fusion
  4.0 0.1 reshape.47
  4.1 0.7 copy.27
  4.8 80.9 %front.1 = (bf16[2,4,4,32,3072]{4,3,2,1,0:T(8,128)(2,1)}, bf16[256,1024]{1,0:T(8,128)(2,1)}, bf16[1024,256]{1,0:T(8,128)(2,1)}, bf16[512,512]{1,0:T(8,128)(2,1)}...) custom-call(s32[1]{0:T(128)S(6)} %copy.35.length_ref, ...), custom_call_target="tpu_custom_call" | custom-call | tf_op jit(solution)/shard_map/front/pallas_call | solution.py:637
  85.7 92.0 %experts.1 = (f32[256,1024]{1,0:T(8,128)}, f32[32,256]{1,0:T(8,128)}, bf16[2,4,4,64,1024]{4,3,2,1,0:T(8,128)(2,1)}, bf16[1024,512]{1,0:T(8,128)(2,1)}, bf16[1024...) custom-call(bf16[256,1024]{1,0:T(8,128)(2,1)} %get-tuple-element.41.routed_ref, s32[32,256]{1,0:T(8,128)} %get-tuple-element.42.pos_ref, ...), custom_call_target="tpu_custom_call" | custom-call | tf_op jit(solution)/shard_map/experts/pallas_call | solution.py:903
  177.7 124.5 %finish.1 = (bf16[256,1024]{1,0:T(8,128)(2,1)}, f32[256,1024]{1,0:T(8,128)}, f32[8,128]{1,0:T(8,128)}, f32[8,128]{1,0:T(8,128)}, f32[32,8,128]{2,1,0:T(8,128)}, ...) custom-call(s32[1]{0:T(128)S(6)} %copy.35.length_ref, ...), custom_call_target="tpu_custom_call" | custom-call | tf_op jit(solution)/shard_map/finish/pallas_call | solution.py:1411
  302.3 0.0 copy-start.1
  302.3 0.0 copy-start.2
  302.3 1.7 copy.30
  304.0 1.5 fusion.1
  305.5 1.7 fusion
  307.2 2.8 bitcast_convert_fusion
  310.0 0.0 copy-done.1
  310.0 0.0 copy-done.2
  310.0 0.0 copy-start.3
  310.0 0.0 copy-start
  310.0 2.6 bitcast_convert_fusion.1
  312.6 0.0 copy-start.5
  312.6 0.0 copy-start.4
  312.6 0.0 copy-done.3
  312.6 0.8 copy.36
  313.4 0.0 copy-done
  313.4 1.0 copy.37
  314.4 0.0 copy-done.5
  314.4 0.6 copy.38
  315.0 0.0 copy-done.4
  315.0 0.6 copy.39
  (2 shorter events, 0.0 us)
Async XLA Ops:
  302.3 7.8 %copy-start.1 = (bf16[1024,512]{1,0:T(8,128)(2,1)S(1)}, bf16[1024,512]{1,0:T(8,128)(2,1)}, u32[]{:S(2)}) copy-start(bf16[1024,512]{1,0:T(8,128)(2,1)} %get-tuple-element.67) | copy-start | bytes 3145732
  302.3 7.7 %copy-start.2 = (bf16[1024,512]{1,0:T(8,128)(2,1)S(1)}, bf16[1024,512]{1,0:T(8,128)(2,1)}, u32[]{:S(2)}) copy-start(bf16[1024,512]{1,0:T(8,128)(2,1)} %get-tuple-element.68) | copy-start | bytes 3145732
  310.0 2.6 copy-start.3
  310.0 3.4 %copy-start = (f32[256,1024]{1,0:T(8,128)S(1)}, f32[256,1024]{1,0:T(8,128)}, u32[]{:S(2)}) copy-start(f32[256,1024]{1,0:T(8,128)} %get-tuple-element.91) | copy-start | bytes 3145732
  312.6 1.8 copy-start.5
  312.6 2.4 copy-start.4

commit v4 on v3

--- a/solution.py
+++ b/solution.py
@@ -170,8 +170,18 @@
     return (core == r) & (offset == 0)
 
 
-def send_slots(out, into, there, dz, dx, send_sem, recv_sem, sign):
+def send_slots(out, into, there, dz, dx, send_sem, recv_sem, sign, local_sem=None):
     y, r, x, z = place()
+
+    def keep(cols):
+        source, target = out.at[there, dz, dx, :, cols], into.at[r, dz, dx, :, cols]
+        if local_sem is None:
+            target[...] = source[...]
+        else:
+            copy = pltpu.make_async_copy(source, target, local_sem)
+            copy.start()
+            copy.wait()
+
     left, right = slot_copies(out, into, r, there, dz, dx, send_sem, recv_sem, sign)
 
     @pl.when(jnp.logical_not(is_local(there, dx)))
@@ -180,7 +190,7 @@
 
     @pl.when(is_local(there, dx))
     def _():
-        into[r, dz, dx, :, 0:HALF] = out[there, dz, dx, :, 0:HALF]
+        keep(LEFT)
 
     @pl.when(jnp.logical_not(is_local(there, dz)))
     def _():
@@ -188,7 +198,7 @@
 
     @pl.when(is_local(there, dz))
     def _():
-        into[r, dz, dx, :, HALF:D] = out[there, dz, dx, :, HALF:D]
+        keep(RIGHT)
 
 
 def slots_arrived(out, into, core, dz, dx, send_sem, recv_sem, left=True, right=True):
@@ -354,9 +364,11 @@
     sibling = moved(0, 0, 1 - r)[0]
     meet(False, False)
 
-    w_ref[r, z, x, :, 0:D] = wq_ref[...]
-    w_ref[r, z, x, :, D : D + HALF] = wk_ref[...]
-    w_ref[r, z, x, :, D + HALF : 2 * D] = wv_ref[...]
+    for p in range(2):
+        part = slice(256 * p, 256 * p + 256)
+        w_ref[r, z, x, :, D * p : D * p + HALF] = wq_ref[:, HALF * p : HALF * p + HALF]
+        w_ref[r, z, x, :, D * p + HALF : D * p + 768] = wk_ref[:, part]
+        w_ref[r, z, x, :, D * p + 768 : D * p + D] = wv_ref[:, part]
     w_ref[r, z, x, :, 2 * D : 3 * D] = wo_ref[...]
     front, rear = pl.ds(0, D + HALF), pl.ds(D + HALF, D + HALF)
 
@@ -458,59 +470,17 @@
             for copy in cross_step(e, d):
                 copy.start()
 
-    for copy in core_step(0):
-        copy.start()
-
-    inputs = hidden_ref[...].astype(f32)
-    scale = lax.rsqrt(jnp.mean(inputs * inputs, axis=1, keepdims=True) + epsilon)
-    normed_ref[...] = (inputs * scale * again_ref[...]).astype(bf16)
-
-    @pl.loop(1, 4)
-    def _(d):
-        @pl.loop(0, 4)
-        def _(e):
-            for copy in cross_step(e, d):
-                copy.wait_recv()
-
-        for copy in core_step(d):
-            copy.start()
-
     @pl.loop(1, 4)
     def _(d):
         for copy in spread(d, cot_ref, tok_z, tok_x, first_send, first_recv):
             copy.start()
 
-    @pl.loop(0, 4)
-    def _(d):
-        for copy in core_step(d):
-            copy.wait_recv()
-
-    cosine, sine = cos_ref[...], sin_ref[...]
-    here = pl.ds(pl.multiple_of(r * tokens, tokens), tokens)
-
-    def projected(first):
-        weight = w_ref[:, :, :, :, first : first + HALF].reshape(D, HALF)
-        return dot(normed_ref[...], weight, ((1,), (0,))).T
-
-    def turned(rows):
-        parts = []
-        for h in range(rows.shape[0] // HEAD):
-            first, second = rows[HEAD * h : HEAD * h + 32], rows[HEAD * h + 32 : HEAD * h + HEAD]
-            parts += [first * cosine - second * sine, second * cosine + first * sine]
-        return jnp.concatenate(parts, axis=0).astype(bf16)
-
-    key_copy = remote(
-        k_ref.at[:, here], k_ref.at[:, here], kv_send.at[0], kv_recv.at[0], sibling
-    )
-    value_copy = remote(
-        v_ref.at[:, here], v_ref.at[:, here], kv_send.at[1], kv_recv.at[1], sibling
-    )
-    k_ref[:, here] = turned(projected(D))
-    key_copy.start()
-    v_ref[:, here] = projected(D + HALF).astype(bf16)
-    value_copy.start()
-    q_ref[0:HALF, :] = turned(projected(0))
-    q_ref[HALF:D, :] = turned(projected(HALF))
+    for copy in core_step(0):
+        copy.start()
+
+    inputs = hidden_ref[...].astype(f32)
+    scale = lax.rsqrt(jnp.mean(inputs * inputs, axis=1, keepdims=True) + epsilon)
+    normed_ref[...] = (inputs * scale * again_ref[...]).astype(bf16)
 
     @pl.loop(1, 4)
     def _(d):
@@ -529,12 +499,56 @@
                 outgoing[core, d, i, :, 0:HALF] = left[part]
                 outgoing[core, i, d, :, HALF:D] = right[part]
 
+    @pl.loop(1, 4)
+    def _(d):
+        @pl.loop(0, 4)
+        def _(e):
+            for copy in cross_step(e, d):
+                copy.wait_recv()
+
+        for copy in core_step(d):
+            copy.start()
+
     @pl.loop(0, CHIPS)
     def _(k):
         dx = lax.rem(k, 4)
         dz = lax.rem(dx + k // 4, 4)
         for core in range(2):
             send_slots(outgoing, grads_ref, core, dz, dx, slot_send, slot_recv, 1)
+
+    @pl.loop(0, 4)
+    def _(d):
+        for copy in core_step(d):
+            copy.wait_recv()
+
+    cosine, sine = cos_ref[...], sin_ref[...]
+    here = pl.ds(pl.multiple_of(r * tokens, tokens), tokens)
+
+    def projected(first):
+        weight = w_ref[:, :, :, :, first : first + HALF].reshape(D, HALF)
+        return dot(normed_ref[...], weight, ((1,), (0,))).T
+
+    def turned(rows):
+        parts = []
+        for h in range(rows.shape[0] // HEAD):
+            first, second = rows[HEAD * h : HEAD * h + 32], rows[HEAD * h + 32 : HEAD * h + HEAD]
+            parts += [first * cosine - second * sine, second * cosine + first * sine]
+        return jnp.concatenate(parts, axis=0).astype(bf16)
+
+    key_copy = remote(
+        k_ref.at[:, here], k_ref.at[:, here], kv_send.at[0], kv_recv.at[0], sibling
+    )
+    value_copy = remote(
+        v_ref.at[:, here], v_ref.at[:, here], kv_send.at[1], kv_recv.at[1], sibling
+    )
+    for p in range(2):
+        both = projected(D * p + HALF)
+        k_ref[256 * p : 256 * p + 256, here] = turned(both[0:256])
+        v_ref[256 * p : 256 * p + 256, here] = both[256:512].astype(bf16)
+    key_copy.start()
+    value_copy.start()
+    for p in range(2):
+        q_ref[HALF * p : HALF * p + HALF, :] = turned(projected(D * p))
 
     key_copy.wait_recv()
     value_copy.wait_recv()
@@ -660,9 +674,7 @@
     rg_ref,
     gdot_ref,
     prod_ref,
-    dg_ref,
-    du_ref,
-    dd_ref,
+    grad_ref,
     tok_z,
     tok_x,
     outgoing,
@@ -820,7 +832,12 @@
         span = pl.ds(pl.multiple_of(n * 256, 256), 256)
         left = active[:, :, :, :, span].reshape(all_rows, 256)
         right = weighted[...].reshape(all_rows, D)
-        dd_ref[span, :] = dot(left, right, ((0,), (0,))).astype(bf16)
+        part = dot(left, right, ((0,), (0,))).astype(bf16)
+        for i in range(2):
+            for h in range(2):
+                rows = part[128 * i + 64 * h : 128 * i + 64 * h + 64]
+                grad_ref[2 * n + i, h, 256:320, :] = rows[:, 0:HALF]
+                grad_ref[2 * n + i, h, 320:384, :] = rows[:, HALF:D]
 
     fold_parts(
         parts_out,
@@ -840,8 +857,10 @@
         span = pl.ds(pl.multiple_of(n * 256, 256), 256)
         left = arrived[:, :, :, :, span].reshape(all_rows, 256)
         part = dot(left, pre_grads[...].reshape(all_rows, D), ((0,), (0,)))
-        dg_ref[span, :] = part[:, 0:HALF].astype(bf16)
-        du_ref[span, :] = part[:, HALF:D].astype(bf16)
+        for h in range(2):
+            rows = part[128 * h : 128 * h + 128].astype(bf16)
+            grad_ref[n, h, 0:128, :] = rows[:, 0:HALF]
+            grad_ref[n, h, 128:256, :] = rows[:, HALF:D]
 
     @pl.loop(0, GROUP)
     def _(k):
@@ -880,7 +899,6 @@
 
 def experts(*arrays):
     f32, bf16 = jnp.float32, jnp.bfloat16
-    wg, wu, wd = arrays[-3:]
     vmem = pl.BlockSpec(memory_space=pltpu.VMEM)
     shape = jax.ShapeDtypeStruct
     block = pltpu.VMEM((2, 4, 4, CAP, D), bf16)
@@ -896,9 +914,7 @@
         shape((TOKENS, D), f32),
         shape((EXPERTS, TOKENS), f32),
         shape((2, 4, 4, CAP, D), bf16),
-        shape(wg.shape, bf16),
-        shape(wu.shape, bf16),
-        shape(wd.shape, bf16),
+        shape((4, 2, 384, HALF), bf16),
     )
     return pl.pallas_call(
         expert_kernel,
@@ -913,13 +929,6 @@
     )(*arrays)
 
 
-def chip_shift(q, sign):
-    y, r, x, z = place()
-    dx, dz = lax.rem(q, 4), lax.rem(lax.rem(q, 4) + q // 4, 4)
-    col = lax.rem(z + sign * dz + 4, 4) * 4 + lax.rem(x + sign * dx + 4, 4)
-    return (y, r, col), col
-
-
 def turned_back(rows, cosine, sine):
     first, second = rows[0:32], rows[32:64]
     return jnp.concatenate(
@@ -935,9 +944,7 @@
     gates_ref,
     rg_ref,
     gdot_ref,
-    dg_ref,
-    du_ref,
-    dd_ref,
+    expert_ref,
     routed_ref,
     router_ref,
     middle_ref,
@@ -947,7 +954,7 @@
     mgain_ref,
     normed_ref,
     mixed_ref,
-    w_ref,
+    w_hbm,
     q_ref,
     k_ref,
     v_ref,
@@ -960,12 +967,13 @@
     mgain_out,
     router_out,
     own_out,
-    gsum_ref,
-    usum_ref,
-    dsum_ref,
+    esum_ref,
+    w_ref,
     mid,
     parts_out,
     parts_in,
+    relay_in,
+    relay_out,
     y_in,
     branch_own,
     branch_sib,
@@ -978,7 +986,9 @@
     kv_out,
     kv_in,
     weight_part,
-    weight_in,
+    rs_in,
+    rs_out,
+    rs_in2,
     y_out,
     y_parts,
     small_out,
@@ -990,79 +1000,100 @@
     gain_y,
     gain_y_in,
     router_all,
+    w_sem,
     c_send,
     c_recv,
     part_send,
     part_recv,
-    y1_send,
-    y1_recv,
-    y2_send,
-    y2_recv,
+    ex_send,
+    ex_recv,
     sib_send,
     sib_recv,
     rs_send,
     rs_recv,
+    rs_send2,
+    rs_recv2,
     ys_send,
     ys_recv,
     sm_send,
     sm_recv,
 ):
     y, r, x, z = place()
-    me = r * 16 + z * 4 + x
-    sibling = (y, 1 - r, z * 4 + x)
+    me = r * CHIPS + z * 4 + x
+    sibling = moved(0, 0, 1 - r)[0]
     tokens = routed_ref.shape[0]
     f32, bf16 = jnp.float32, jnp.bfloat16
-
+    weights_in = pltpu.make_async_copy(w_hbm, w_ref, w_sem)
+    weights_in.start()
     meet(True, True)
 
-    parts = ((dg_ref, gsum_ref, 256), (du_ref, usum_ref, 256), (dd_ref, dsum_ref, 128))
-
-    def quarter(j, n):
-        device, other = plane_shift(n)
-        source, _, rows = parts[j]
-        at = 3 * j + n - 1
+    above, below = plane_shift(1), plane_shift(3)
+    opposite = plane_shift(2)[1]
+
+    def relayed(n):
+        device = (above, below)[n][0]
         return remote(
-            source.at[pl.ds(other * rows, rows)],
-            y_in[j].at[n - 1],
-            y1_send.at[at],
-            y1_recv.at[at],
+            expert_ref.at[opposite, n], relay_in.at[n], ex_send.at[n], ex_recv.at[n], device
+        )
+
+    def direct(n):
+        device, other = (above, below)[n]
+        return remote(
+            expert_ref.at[other, 1 - n],
+            y_in.at[n, 1 - n],
+            ex_send.at[2 + n],
+            ex_recv.at[2 + n],
             device,
         )
 
-    def summed_quarter(j, n):
-        device, _ = plane_shift(n)
-        _, total, rows = parts[j]
-        at = 3 * j + n - 1
-        mine = total.at[pl.ds(y * rows, rows)]
-        return remote(mine, mine, y2_send.at[at], y2_recv.at[at], device)
+    def merged(n):
+        device = (above, below)[n][0]
+        return remote(
+            relay_out.at[n], y_in.at[n, n], ex_send.at[4 + n], ex_recv.at[4 + n], device
+        )
+
+    def handed(n):
+        device = (above, below)[n][0]
+        return remote(
+            esum_ref.at[y], esum_ref.at[y], ex_send.at[6 + n], ex_recv.at[6 + n], device
+        )
+
+    def passed_on(n):
+        device, came_from = (above, below)[n][0], (below, above)[n][1]
+        part = esum_ref.at[came_from, n]
+        return remote(part, part, ex_send.at[8 + n], ex_recv.at[8 + n], device)
 
     def weight(first, width):
         return w_ref[:, :, :, :, first : first + width].reshape(D, width)
 
+    def to_sibling(at, src, dst):
+        return remote(src, dst, sib_send.at[at], sib_recv.at[at], sibling)
+
     half = pl.ds(pl.multiple_of((1 - r) * HALF, HALF), HALF)
-    sib_normed = remote(normed_ref.at[:, half], normed_sib, sib_send.at[0], sib_recv.at[0], sibling)
-    sib_mixed = remote(mixed_ref.at[:, half], mixed_sib, sib_send.at[1], sib_recv.at[1], sibling)
-    sib_branch = remote(branch_own, branch_sib, sib_send.at[2], sib_recv.at[2], sibling)
-    sib_kv = remote(kv_out, kv_in, sib_send.at[3], sib_recv.at[3], sibling)
-    sib_query = remote(
-        grad_t.at[pl.ds(0, D)], grad_sib.at[pl.ds(0, D)], sib_send.at[4], sib_recv.at[4], sibling
-    )
-    sib_keyval = remote(
-        grad_t.at[pl.ds(D, D)], grad_sib.at[pl.ds(D, D)], sib_send.at[5], sib_recv.at[5], sibling
-    )
-
+    sib_normed = to_sibling(0, normed_ref.at[:, half], normed_sib)
+    sib_mixed = to_sibling(1, mixed_ref.at[:, half], mixed_sib)
+    sib_branch = to_sibling(2, branch_own, branch_sib)
+
+    def sib_keyval(p):
+        return to_sibling(3 + p, kv_out.at[p], kv_in.at[p])
+
+    def sib_grads(p, part):
+        rows = pl.ds(p * D + part * HALF, HALF)
+        return to_sibling(5 + 2 * p + part, grad_t.at[rows], grad_sib.at[rows])
+
+    for n in range(2):
+        relayed(n).start()
+    for n in range(2):
+        direct(n).start()
     sib_mixed.start()
     sib_normed.start()
-    for n in range(1, PLANES):
-        for j in range(3):
-            quarter(j, n).start()
 
     @pl.loop(0, CHIPS)
     def _(k):
         dx = lax.rem(k, 4)
         dz = lax.rem(dx + k // 4, 4)
         for core in range(2):
-            send_slots(prod_ref, mid, core, dz, dx, c_send, c_recv, -1)
+            send_slots(prod_ref, mid, core, dz, dx, c_send, c_recv, -1, c_send.at[2 * GROUP])
 
     gates = gates_ref[...]
     gdot = gdot_ref[...]
@@ -1101,73 +1132,133 @@
 
     small_in[me] = small_out[me]
 
+    weights_in.wait()
     mg_t[...] = dot(weight(2 * D, D), branch_own[...], ((1,), (1,))).astype(bf16)
+
+    for n in range(2):
+        relayed(n).wait_recv()
+        target = (above, below)[n][1]
+        total = relay_in[n].astype(f32) + expert_ref[target, n].astype(f32)
+        relay_out[n] = total.astype(bf16)
+        merged(n).start()
+
+    mine = pl.ds(pl.multiple_of(r * HALF, HALF), HALF)
+
+    def columns(p):
+        return pl.ds(p * D, HALF), pl.ds(p * D + HALF, HALF)
+
+    def first_step(p, d):
+        left, right = columns(p)
+        at = 8 * p + d
+        return (
+            remote(
+                weight_part.at[lax.rem(z + d, 4), :, :, left],
+                rs_in.at[d, :, :, left],
+                rs_send.at[at],
+                rs_recv.at[at],
+                moved(0, d, r)[0],
+            ),
+            remote(
+                weight_part.at[:, lax.rem(x + d, 4), :, right],
+                rs_in.at[d, :, :, right],
+                rs_send.at[4 + at],
+                rs_recv.at[4 + at],
+                moved(d, 0, r)[0],
+            ),
+        )
+
+    def second_step(p, d):
+        left, right = columns(p)
+        at = 8 * p + d
+        return (
+            remote(
+                rs_out.at[lax.rem(x + d, 4), :, left],
+                rs_in2.at[d, :, left],
+                rs_send2.at[at],
+                rs_recv2.at[at],
+                moved(d, 0, r)[0],
+            ),
+            remote(
+                rs_out.at[lax.rem(z + d, 4), :, right],
+                rs_in2.at[d, :, right],
+                rs_send2.at[4 + at],
+                rs_recv2.at[4 + at],
+                moved(0, d, r)[0],
+            ),
+        )
+
+    def across(p, n):
+        cols = pl.ds(p * D, D)
+        at = 3 * p + n - 1
+        return remote(
+            y_out.at[:, cols],
+            y_parts.at[y, :, cols],
+            ys_send.at[at],
+            ys_recv.at[at],
+            plane_shift(n)[0],
+        )
+
+    def sum_first(p, total):
+        weight_part[:, :, :, p * D : p * D + D] = total.astype(bf16).reshape(4, 4, 32, D)
+
+        @pl.loop(1, 4)
+        def _(d):
+            for copy in first_step(p, d):
+                copy.start()
+
+    def sum_second(p):
+        left, right = columns(p)
+
+        @pl.loop(1, 4)
+        def _(d):
+            for copy in first_step(p, d):
+                copy.wait_recv()
+
+        total = weight_part[z, :, :, left].astype(f32)
+        other = weight_part[:, x, :, right].astype(f32)
+        for d in range(1, 4):
+            total = total + rs_in[d, :, :, left].astype(f32)
+            other = other + rs_in[d, :, :, right].astype(f32)
+        rs_out[:, :, left] = total.astype(bf16)
+        rs_out[:, :, right] = other.astype(bf16)
+
+        @pl.loop(1, 4)
+        def _(d):
+            for copy in second_step(p, d):
+                copy.start()
+
+    def sum_third(p):
+        left, right = columns(p)
+
+        @pl.loop(1, 4)
+        def _(d):
+            for copy in second_step(p, d):
+                copy.wait_recv()
+
+        total = rs_out[x, :, left].astype(f32)
+        other = rs_out[z, :, right].astype(f32)
+        for d in range(1, 4):
+            total = total + rs_in2[d, :, left].astype(f32)
+            other = other + rs_in2[d, :, right].astype(f32)
+        y_out[:, left] = total.astype(bf16)
+        y_out[:, right] = other.astype(bf16)
+        y_parts[y, :, left] = total.astype(bf16)
+        y_parts[y, :, right] = other.astype(bf16)
+        for n in range(1, PLANES):
+            across(p, n).start()
 
     sib_mixed.wait_recv()
     sib_branch.wait_recv()
-    mine = pl.ds(pl.multiple_of(r * HALF, HALF), HALF)
-
-    def rows_part(q, at, first, width):
-        device, other = chip_shift(q, 1)
-        _, own = chip_shift(0, 1)
-        return remote(
-            weight_part.at[pl.ds(other * 32, 32), pl.ds(first, width)],
-            weight_in.at[own, :, pl.ds(first, width)],
-            rs_send.at[at * CHIPS + q],
-            rs_recv.at[at * CHIPS + q],
-            device,
-        )
-
-    pieces = ((2 * D, D), (0, D), (D, D))
-
-    def send_part(at, left_own, left_sib, right_own, right_sib, contract):
-        first, width = pieces[at]
-        total = dot(left_own, right_own, ((0,), (contract,)))
-        total = total + dot(left_sib, right_sib, ((0,), (contract,)))
-        weight_part[:, first : first + width] = total.astype(bf16)
-
-        @pl.loop(1, CHIPS)
-        def _(q):
-            rows_part(q, at, first, width).start()
-
-        _, own = chip_shift(0, 1)
-        weight_in[own, :, first : first + width] = weight_part[
-            pl.ds(own * 32, 32), first : first + width
-        ]
-
-    def sum_part(at):
-        first, width = pieces[at]
-
-        @pl.loop(1, CHIPS)
-        def _(q):
-            rows_part(q, at, first, width).wait_recv()
-
-        total = weight_in[0, :, first : first + width].astype(f32)
-        for s in range(1, CHIPS):
-            total = total + weight_in[s, :, first : first + width].astype(f32)
-        y_out[:, first : first + width] = total.astype(bf16)
-        y_parts[y, :, first : first + width] = total.astype(bf16)
-        for n in range(1, PLANES):
-            across(at, n).start()
-
-    def across(at, n):
-        first, width = pieces[at]
-        device, _ = plane_shift(n)
-        return remote(
-            y_out.at[:, pl.ds(first, width)],
-            y_parts.at[y, :, pl.ds(first, width)],
-            ys_send.at[at * 3 + n - 1],
-            ys_recv.at[at * 3 + n - 1],
-            device,
-        )
-
-    send_part(0, mixed_ref[:, mine], mixed_sib[...], branch_own[...], branch_sib[...], 0)
+    total = dot(mixed_ref[:, mine], branch_own[...], ((0,), (0,)))
+    sum_first(2, total + dot(mixed_sib[...], branch_sib[...], ((0,), (0,))))
 
     key_live = lax.broadcasted_iota(jnp.int32, (2 * tokens, 1), 0) < length_ref[0]
     score_scale = HEAD ** (-0.5)
     cosine, sine = cos_ref[...], sin_ref[...]
-
-    def key_head(g):
+    first_core = r == 0
+
+    def key_head(p, i):
+        g = 4 * p + i
         head = pl.ds(pl.multiple_of(g * HEAD, HEAD), HEAD)
         keys, values = k_ref[head, :], v_ref[head, :]
         key_sum, value_sum = None, None
@@ -1183,31 +1274,57 @@
             score_grad = (probs * (prob_grad - inner)).astype(bf16)
             key_part = dot(query, score_grad, ((1,), (1,)))
             query_grad = dot(keys, score_grad, ((1,), (0,))) * score_scale
-            grad_t[at, :] = turned_back(query_grad, cosine, sine).astype(bf16)
+            to = pl.ds(pl.multiple_of(p * D + (2 * i + j) * HEAD, HEAD), HEAD)
+            grad_t[to, :] = turned_back(query_grad, cosine, sine).astype(bf16)
             key_sum = key_part if key_sum is None else key_sum + key_part
             value_sum = value_part if value_sum is None else value_sum + value_part
         key_sum = key_sum * score_scale
-        low = pl.ds(pl.multiple_of(g * HEAD, HEAD), HEAD)
-        high = pl.ds(pl.multiple_of(HALF + g * HEAD, HEAD), HEAD)
-        first = r == 0
-        kv_own[low, :] = jnp.where(first, key_sum[:, :tokens], key_sum[:, tokens:])
-        kv_own[high, :] = jnp.where(first, value_sum[:, :tokens], value_sum[:, tokens:])
-        kv_out[low, :] = jnp.where(first, key_sum[:, tokens:], key_sum[:, :tokens]).astype(bf16)
-        kv_out[high, :] = jnp.where(first, value_sum[:, tokens:], value_sum[:, :tokens]).astype(bf16)
-
-    pl.loop(0, 4)(key_head)
-
-    for j in range(3):
-        source, total, rows_of = parts[j]
-        mine_y = pl.ds(y * rows_of, rows_of)
-        acc = source[mine_y, :].astype(f32)
-        for n in range(1, PLANES):
-            quarter(j, n).wait_recv()
-        for n in range(1, PLANES):
-            acc = acc + y_in[j][n - 1].astype(f32)
-        total[mine_y, :] = acc.astype(bf16)
-        for n in range(1, PLANES):
-            summed_quarter(j, n).start()
+        for n, part in enumerate((key_sum, value_sum)):
+            to = pl.ds(pl.multiple_of(256 * n + i * HEAD, HEAD), HEAD)
+            kv_own[p, to, :] = jnp.where(first_core, part[:, :tokens], part[:, tokens:])
+            away = jnp.where(first_core, part[:, tokens:], part[:, :tokens])
+            kv_out[p, to, :] = away.astype(bf16)
+
+    def heads(p, first, last):
+        @pl.loop(first, last)
+        def _(i):
+            key_head(p, i)
+
+    def whole_keyval(p):
+        sib_keyval(p).wait_recv()
+        for i in range(4):
+            rows = slice(HEAD * i, HEAD * i + HEAD)
+            total = kv_own[p, rows, :] + kv_in[p, rows, :].astype(f32)
+            to = p * D + HALF + HEAD * i
+            grad_t[to : to + HEAD, :] = turned_back(total, cosine, sine).astype(bf16)
+        total = kv_own[p, 256:512, :] + kv_in[p, 256:512, :].astype(f32)
+        grad_t[p * D + HALF + 256 : p * D + D, :] = total.astype(bf16)
+        sib_grads(p, 1).start()
+
+    def projections(p):
+        rows = slice(p * D, p * D + D)
+        for part in range(2):
+            sib_grads(p, part).wait_recv()
+        total = dot(normed_ref[:, mine], grad_t[rows, :], ((0,), (1,)))
+        sum_first(p, total + dot(normed_sib[...], grad_sib[rows, :], ((0,), (1,))))
+
+    def inputs_part(p):
+        return dot(grad_t[p * D : p * D + D, :], weight(p * D, D), ((0,), (1,)))
+
+    heads(0, 0, 4)
+    sib_keyval(0).start()
+    sib_grads(0, 0).start()
+
+    for n in range(2):
+        direct(n).wait_recv()
+        merged(n).wait_recv()
+    for n in range(2):
+        total = expert_ref[y, n].astype(f32) + (y_in[0, n].astype(f32) + y_in[1, n].astype(f32))
+        esum_ref[y, n] = total.astype(bf16)
+    for n in range(2):
+        handed(n).start()
+
+    whole_keyval(0)
 
     @pl.loop(1, GROUP)
     def _(k):
@@ -1223,6 +1340,62 @@
     small_y_in[y] = small_y[...]
     for n in range(1, PLANES):
         small_across(n).start()
+
+    sum_second(2)
+    sib_normed.wait_recv()
+    projections(0)
+    heads(1, 0, 4)
+    sib_keyval(1).start()
+    sib_grads(1, 0).start()
+
+    for n in range(1, PLANES):
+        small_across(n).wait_recv()
+    totals = small_y_in[0] + small_y_in[1] + small_y_in[2] + small_y_in[3]
+    mgain_out[...] = totals[8:16]
+    router_all[me] = totals[0:8]
+
+    def router_row(k):
+        device, _ = step_of(k, 1)
+        at = 2 * GROUP + k
+        return remote(
+            router_all.at[me], router_all.at[me], sm_send.at[at], sm_recv.at[at], device
+        )
+
+    @pl.loop(1, GROUP)
+    def _(k):
+        router_row(k).start()
+
+    whole_keyval(1)
+    normed_grad = inputs_part(0)
+    projections(1)
+    sum_second(0)
+    sum_third(2)
+    normed_grad = normed_grad + inputs_part(1)
+
+    inputs = hidden_ref[...].astype(f32)
+    scale = lax.rsqrt(jnp.mean(inputs * inputs, axis=1, keepdims=True) + epsilon)
+    rows = inputs * scale
+    attn_part = jnp.sum(normed_grad * rows, axis=0, keepdims=True)
+    for j in range(8):
+        gain_out[j : j + 1, :] = attn_part[:, 128 * j : 128 * j + 128]
+
+    def gain(k):
+        device, _ = step_of(k, 1)
+        at = 3 * GROUP + k
+        return remote(gain_out, gain_in.at[me], sm_send.at[at], sm_recv.at[at], device)
+
+    @pl.loop(1, GROUP)
+    def _(k):
+        gain(k).start()
+
+    gain_in[me] = gain_out[...]
+    scaled = normed_grad * again_ref[...]
+    inner = jnp.mean(scaled * rows, axis=1, keepdims=True)
+    hgrad_ref[...] += scale * (scaled - rows * inner)
+
+    for n in range(2):
+        handed(n).wait_recv()
+        passed_on(n).start()
 
     fold_parts(
         parts_out,
@@ -1236,78 +1409,8 @@
         part_send,
         part_recv,
     )
-    pl.loop(4, 8)(key_head)
-
-    sib_kv.start()
-    sib_query.start()
-
-    for n in range(1, PLANES):
-        small_across(n).wait_recv()
-    totals = small_y_in[0] + small_y_in[1] + small_y_in[2] + small_y_in[3]
-    mgain_out[...] = totals[8:16]
-    router_all[me] = totals[0:8]
-
-    def router_row(k):
-        device, _ = step_of(k, 1)
-        at = 2 * GROUP + k
-        return remote(
-            router_all.at[me], router_all.at[me], sm_send.at[at], sm_recv.at[at], device
-        )
-
-    @pl.loop(1, GROUP)
-    def _(k):
-        router_row(k).start()
-
-    sib_normed.wait_recv()
-    sib_query.wait_recv()
-    send_part(1, normed_ref[:, mine], normed_sib[...], grad_t[0:D, :], grad_sib[0:D, :], 1)
-    sib_kv.wait_recv()
-
-    @pl.loop(0, 8)
-    def _(g):
-        low = pl.ds(pl.multiple_of(g * HEAD, HEAD), HEAD)
-        total = kv_own[low, :] + kv_in[low, :].astype(f32)
-        to = pl.ds(pl.multiple_of(D + g * HEAD, HEAD), HEAD)
-        grad_t[to, :] = turned_back(total, cosine, sine).astype(bf16)
-
-    grad_t[D + HALF : 2 * D, :] = (
-        kv_own[HALF:D, :] + kv_in[HALF:D, :].astype(f32)
-    ).astype(bf16)
-    sib_keyval.start()
-    normed_grad = dot(grad_t[0:D, :], weight(0, D), ((0,), (1,)))
-    sib_keyval.wait_recv()
-    send_part(2, normed_ref[:, mine], normed_sib[...], grad_t[D:, :], grad_sib[D:, :], 1)
-    normed_grad = normed_grad + dot(grad_t[D:, :], weight(D, D), ((0,), (1,)))
-
-    inputs = hidden_ref[...].astype(f32)
-    scale = lax.rsqrt(jnp.mean(inputs * inputs, axis=1, keepdims=True) + epsilon)
-    rows = inputs * scale
-    attn_part = jnp.sum(normed_grad * rows, axis=0, keepdims=True)
-    for j in range(8):
-        gain_out[j : j + 1, :] = attn_part[:, 128 * j : 128 * j + 128]
-
-    def gain(k):
-        device, _ = step_of(k, 1)
-        at = 3 * GROUP + k
-        return remote(gain_out, gain_in.at[me], sm_send.at[at], sm_recv.at[at], device)
-
-    @pl.loop(1, GROUP)
-    def _(k):
-        gain(k).start()
-
-    gain_in[me] = gain_out[...]
-    scaled = normed_grad * again_ref[...]
-    inner = jnp.mean(scaled * rows, axis=1, keepdims=True)
-    hgrad_ref[...] += scale * (scaled - rows * inner)
-
-    parts_arrived(parts_out, parts_in, part_send, part_recv)
-    mixture = (parts_in[0].astype(f32) + parts_in[1].astype(f32)) + (
-        parts_in[2].astype(f32) + parts_in[3].astype(f32)
-    )
-    hout_ref[...] = ((middle_ref[...] + mixture) * live).astype(bf16)
-
-    for at in range(3):
-        sum_part(at)
+    sum_second(1)
+    sum_third(0)
 
     @pl.loop(1, GROUP)
     def _(k):
@@ -1323,12 +1426,15 @@
 
     for n in range(1, PLANES):
         gain_across(n).start()
-    for at in range(3):
-        for n in range(1, PLANES):
-            across(at, n).wait_recv()
-    own_out[...] = (y_parts[0].astype(f32) + y_parts[1].astype(f32)) + (
-        y_parts[2].astype(f32) + y_parts[3].astype(f32)
-    )
+
+    sum_third(1)
+
+    parts_arrived(parts_out, parts_in, part_send, part_recv)
+    mixture = (parts_in[0].astype(f32) + parts_in[1].astype(f32)) + (
+        parts_in[2].astype(f32) + parts_in[3].astype(f32)
+    )
+    hout_ref[...] = ((middle_ref[...] + mixture) * live).astype(bf16)
+
     for n in range(1, PLANES):
         gain_across(n).wait_recv()
     again_out[...] = (gain_y_in[0] + gain_y_in[1]) + (gain_y_in[2] + gain_y_in[3])
@@ -1348,40 +1454,50 @@
         router_row(k).wait_send()
         gain(k).wait_send()
 
-    for at in range(3):
-        first, width = pieces[at]
-
-        @pl.loop(1, CHIPS)
-        def _(q):
-            rows_part(q, at, first, width).wait_send()
-
+    @pl.loop(1, 4)
+    def _(d):
+        for p in range(3):
+            for copy in first_step(p, d) + second_step(p, d):
+                copy.wait_send()
+
+    for n in range(2):
+        for copy in (relayed(n), direct(n), merged(n), handed(n), passed_on(n)):
+            copy.wait_send()
+    for copy in (sib_normed, sib_mixed, sib_branch):
+        copy.wait_send()
+    for p in range(2):
+        sib_keyval(p).wait_send()
+        for part in range(2):
+            sib_grads(p, part).wait_send()
     for n in range(1, PLANES):
-        for j in range(3):
-            quarter(j, n).wait_send()
-            summed_quarter(j, n).wait()
-            across(j, n).wait_send()
         small_across(n).wait_send()
         gain_across(n).wait_send()
-    for copy in (sib_normed, sib_mixed, sib_branch, sib_kv, sib_query, sib_keyval):
-        copy.wait_send()
+        for p in range(3):
+            across(p, n).wait()
+    for n in range(2):
+        passed_on(n).wait_recv()
+    own_out[...] = (y_parts[0].astype(f32) + y_parts[1].astype(f32)) + (
+        y_parts[2].astype(f32) + y_parts[3].astype(f32)
+    )
 
 
 def finish(length, *arrays):
-    dg, du, dd = arrays[6:9]
     tokens = TOKENS
     f32, bf16 = jnp.float32, jnp.bfloat16
     vmem = pl.BlockSpec(memory_space=pltpu.VMEM)
     shape = jax.ShapeDtypeStruct
     sems = pltpu.SemaphoreType.DMA
+    in_specs = [pl.BlockSpec(memory_space=pltpu.SMEM)] + [vmem] * len(arrays)
+    in_specs[1] = pl.BlockSpec(memory_space=pl.ANY)
+    in_specs[17] = pl.BlockSpec(memory_space=pl.ANY)
     scratch = [
+        pltpu.VMEM((2, 4, 4, 32, 3 * D), bf16),
         pltpu.VMEM((2, 4, 4, CAP, D), bf16),
         pltpu.VMEM((4, tokens, D), bf16),
         pltpu.VMEM((4, tokens, D), bf16),
-        [
-            pltpu.VMEM((3, 256, 512), bf16),
-            pltpu.VMEM((3, 256, 512), bf16),
-            pltpu.VMEM((3, 128, 1024), bf16),
-        ],
+        pltpu.VMEM((2, 384, HALF), bf16),
+        pltpu.VMEM((2, 384, HALF), bf16),
+        pltpu.VMEM((2, 2, 384, HALF), bf16),
         pltpu.VMEM((tokens, D), bf16),
         pltpu.VMEM((tokens, D), bf16),
         pltpu.VMEM((tokens, HALF), bf16),
@@ -1389,11 +1505,13 @@
         pltpu.VMEM((D, tokens), bf16),
         pltpu.VMEM((2 * D, tokens), bf16),
         pltpu.VMEM((2 * D, tokens), bf16),
-        pltpu.VMEM((D, tokens), f32),
-        pltpu.VMEM((D, tokens), bf16),
-        pltpu.VMEM((D, tokens), bf16),
-        pltpu.VMEM((HALF, 3 * D), bf16),
-        pltpu.VMEM((CHIPS, 32, 3 * D), bf16),
+        pltpu.VMEM((2, HALF, tokens), f32),
+        pltpu.VMEM((2, HALF, tokens), bf16),
+        pltpu.VMEM((2, HALF, tokens), bf16),
+        pltpu.VMEM((4, 4, 32, 3 * D), bf16),
+        pltpu.VMEM((4, 4, 32, 3 * D), bf16),
+        pltpu.VMEM((4, 32, 3 * D), bf16),
+        pltpu.VMEM((4, 32, 3 * D), bf16),
         pltpu.VMEM((32, 3 * D), bf16),
         pltpu.VMEM((PLANES, 32, 3 * D), bf16),
         pltpu.VMEM((GROUP, 16, 128), f32),
@@ -1405,8 +1523,9 @@
         pltpu.VMEM((8, 128), f32),
         pltpu.VMEM((PLANES, 8, 128), f32),
         pltpu.VMEM((GROUP, 8, 128), f32),
+        sems,
     ]
-    for count in (2 * GROUP, 8, 9, 9, 6, 3 * CHIPS, 9, 5 * GROUP):
+    for count in (2 * GROUP + 1, 8, 10, 9, 24, 24, 9, 5 * GROUP):
         scratch += [sems((count,)), sems((count,))]
     return pl.pallas_call(
         finish_kernel,
@@ -1417,18 +1536,101 @@
             shape((8, 128), f32),
             shape((GROUP, 8, 128), f32),
             shape((32, 3 * D), f32),
-            shape(dg.shape, bf16),
-            shape(du.shape, bf16),
-            shape(dd.shape, bf16),
+            shape((4, 2, 384, HALF), bf16),
         ),
-        in_specs=[pl.BlockSpec(memory_space=pltpu.SMEM)] + [vmem] * len(arrays),
-        out_specs=[vmem] * 9,
+        in_specs=in_specs,
+        out_specs=[vmem] * 7,
         scratch_shapes=scratch,
         compiler_params=pltpu.CompilerParams(
             collective_id=2, has_side_effects=True, vmem_limit_bytes=60 << 20
         ),
         name="finish",
     )(length, *arrays)
+
+
+def spread_kernel(
+    hout_ref,
+    hgrad_ref,
+    own_ref,
+    esum_ref,
+    router_ref,
+    hout_out,
+    hgrad_out,
+    q_out,
+    k_out,
+    v_out,
+    o_out,
+    gate_out,
+    up_out,
+    down_out,
+    router_out,
+):
+    f32 = jnp.float32
+    hout_out[...] = hout_ref[...]
+    hgrad_out[...] = hgrad_ref[...]
+    for p in range(2):
+        q_out[:, p * HALF : p * HALF + HALF] = own_ref[:, p * D : p * D + HALF]
+        k_out[:, p * 256 : p * 256 + 256] = own_ref[:, p * D + HALF : p * D + 768]
+        v_out[:, p * 256 : p * 256 + 256] = own_ref[:, p * D + 768 : p * D + D]
+    o_out[...] = own_ref[:, 2 * D : 3 * D]
+    for h in range(2):
+        gate_out[0, 128 * h : 128 * h + 128, :] = esum_ref[0, h, 0:128, :].astype(f32)
+        up_out[0, 128 * h : 128 * h + 128, :] = esum_ref[0, h, 128:256, :].astype(f32)
+        down_out[0, 64 * h : 64 * h + 64, 0:HALF] = esum_ref[0, h, 256:320, :].astype(f32)
+        down_out[0, 64 * h : 64 * h + 64, HALF:D] = esum_ref[0, h, 320:384, :].astype(f32)
+    for j in range(8):
+        router_out[128 * j : 128 * j + 128, :] = router_ref[:, j, :].T
+
+
+def spread_out(*arrays):
+    f32, bf16 = jnp.float32, jnp.bfloat16
+    shape = jax.ShapeDtypeStruct
+
+    def whole(*dims):
+        return pl.BlockSpec(dims, lambda i: (0,) * len(dims))
+
+    def rows(count, width):
+        return pl.BlockSpec((count, width), lambda i: (i, 0))
+
+    def expert_rows(count, width):
+        return pl.BlockSpec((1, count, width), lambda i: (0, i, 0))
+
+    return pl.pallas_call(
+        spread_kernel,
+        grid=(4,),
+        out_shape=(
+            shape((TOKENS, D), bf16),
+            shape((TOKENS, D), f32),
+            shape((32, D), f32),
+            shape((32, HALF), f32),
+            shape((32, HALF), f32),
+            shape((32, D), f32),
+            shape((1, D, HALF), f32),
+            shape((1, D, HALF), f32),
+            shape((1, HALF, D), f32),
+            shape((D, EXPERTS), f32),
+        ),
+        in_specs=[
+            rows(64, D),
+            rows(64, D),
+            whole(32, 3 * D),
+            pl.BlockSpec((1, 2, 384, HALF), lambda i: (i, 0, 0, 0)),
+            whole(GROUP, 8, 128),
+        ],
+        out_specs=[
+            rows(64, D),
+            rows(64, D),
+            whole(32, D),
+            whole(32, HALF),
+            whole(32, HALF),
+            whole(32, D),
+            expert_rows(256, HALF),
+            expert_rows(256, HALF),
+            expert_rows(128, D),
+            whole(D, EXPERTS),
+        ],
+        name="spread_out",
+    )(*arrays)
 
 
 def on_device(
@@ -1449,7 +1651,6 @@
     down_weight,
 ):
     tok_count = hidden_in.shape[0]
-    kv_width = KV_HEADS * HEAD
     positions = lax.axis_index("row") * tok_count + jnp.arange(tok_count, dtype=jnp.int32)
     half_dim = HEAD // 2
     frequency = rotary_base ** (-jnp.arange(half_dim, dtype=jnp.float32) / half_dim)
@@ -1487,7 +1688,7 @@
         cosine,
         sine,
     )
-    returned_rows, gate_dot, produced, gate_local, up_local, down_local = experts(
+    returned_rows, gate_dot, produced, expert_grads = experts(
         routed,
         pos,
         posz,
@@ -1505,9 +1706,7 @@
         moe_gain_sum,
         router_sum,
         own_rows,
-        gate_sum,
-        up_sum,
-        down_sum,
+        expert_sum,
     ) = finish(
         lengths,
         produced,
@@ -1516,9 +1715,7 @@
         gates,
         returned_rows,
         gate_dot,
-        gate_local,
-        up_local,
-        down_local,
+        expert_grads,
         routed,
         router_t,
         middle,
@@ -1536,19 +1733,31 @@
         cosine,
         sine,
     )
+    (
+        hidden_out,
+        hidden_grad,
+        query_grad,
+        key_grad,
+        value_grad,
+        output_grad,
+        gate_grad,
+        up_grad,
+        down_grad,
+        router_grad,
+    ) = spread_out(hidden_out, hidden_grad, own_rows, expert_sum, router_sum)
     return (
         hidden_out,
         hidden_grad,
         attn_gain_sum.reshape(D),
-        own_rows[:, :D],
-        own_rows[:, D : D + kv_width],
-        own_rows[:, D + kv_width : 2 * D],
-        own_rows[:, 2 * D :],
+        query_grad,
+        key_grad,
+        value_grad,
+        output_grad,
         moe_gain_sum.reshape(D),
-        router_sum.reshape(EXPERTS, D).T,
-        gate_sum.astype(jnp.float32)[None],
-        up_sum.astype(jnp.float32)[None],
-        down_sum.astype(jnp.float32)[None],
+        router_grad,
+        gate_grad,
+        up_grad,
+        down_grad,
     )
 
 

time: 316 us -> 282 us (0.89)
  Pallas kernels: 297 us -> 273 us
  other arithmetic: 7.6 us -> 2.21 us
  local copies, waits for them, and re-layouts: 9.19 us -> 4.34 us
    pallas_call x1, Pallas kernels: 125 us -> 95.9 us  [finish(): pl.pallas_call(finish_kernel, out_shape=(shape((tokens, D), bf16), shape(...]
    pallas_call x0 -> x1, Pallas kernels: none -> 6.48 us  [spread_out(): pl.pallas_call(spread_kernel, grid=(4,), out_shape=(shape((TOKENS, D), bf...]
    broadcast_in_dim x2 -> x0, other arithmetic: 5.4 us -> none  [the longest x1 2.79 us: on_device(): down_sum.astype(jnp.float32)[None]]
    slice x2 -> x0, local copies, waits for them, and re-layouts: 3.21 us -> none  [the longest x1 1.68 us: on_device(): own_rows[:, 2 * D:]]
where the time goes in v4:
time: 282 us; the launch traced here: 281 us
  Pallas kernels  273 us (97%)
  local copies, waits for them, and re-layouts  4.34 us (2%)
    pallas_call x1, Pallas kernels, finish(): pl.pallas_call(finish_kernel, out_shape=(shape((tokens, D), bf16), shape(...  95.9 us
    pallas_call x1, Pallas kernels, experts(): pl.pallas_call(expert_kernel, out_shape=out_shape, in_specs=[vmem] * len(...  92.2 us
    pallas_call x1, Pallas kernels, front(): pl.pallas_call(front_kernel, out_shape=out_shape, in_specs=[pl.BlockSpec(...  78.5 us
    pallas_call x1, Pallas kernels, spread_out(): pl.pallas_call(spread_kernel, grid=(4,), out_shape=(shape((TOKENS, D), bf...  6.48 us

profile of v4, /device:TPU:1, one launch (start us, length us, event | category | flops | bytes accessed | tf_op | source)
XLA Modules:
  0.0 281.0 jit_solution(12959916175450838149)
XLA Ops:
  1.3 0.5 broadcast.16
  1.8 1.4 reduce.3
  3.2 0.8 multiply_sine_fusion
  4.0 0.1 reshape.44
  4.1 0.7 copy.28
  4.8 78.5 %front.1 = (bf16[2,4,4,32,3072]{4,3,2,1,0:T(8,128)(2,1)}, bf16[256,1024]{1,0:T(8,128)(2,1)}, bf16[1024,256]{1,0:T(8,128)(2,1)}, bf16[512,512]{1,0:T(8,128)(2,1)}...) custom-call(s32[1]{0:T(128)S(6)} %copy.32.length_ref, ...), custom_call_target="tpu_custom_call" | custom-call | tf_op jit(solution)/shard_map/front/pallas_call | solution.py:651
  83.3 92.2 %experts.1 = (f32[256,1024]{1,0:T(8,128)}, f32[32,256]{1,0:T(8,128)}, bf16[2,4,4,64,1024]{4,3,2,1,0:T(8,128)(2,1)}, bf16[4,2,384,512]{3,2,1,0:T(8,128)(2,1)}) custom-call(bf16[256,1024]{1,0:T(8,128)(2,1)} %get-tuple-element.47.routed_ref, s32[32,256]{1,0:T(8,128)} %get-tuple-element.48.pos_ref, s32[4,8,256]{2,1,0:T(8,128)} %get-tuple-element.49.posz_ref, ...), custom_call_target="tpu_custom_call" | custom-call | tf_op jit(solution)/shard_map/experts/pallas_call | solution.py:919
  175.5 95.9 %finish.1 = (bf16[256,1024]{1,0:T(8,128)(2,1)}, f32[256,1024]{1,0:T(8,128)}, f32[8,128]{1,0:T(8,128)}, f32[8,128]{1,0:T(8,128)}, f32[32,8,128]{2,1,0:T(8,128)}, ...) custom-call(s32[1]{0:T(128)S(6)} %copy.32.length_ref, bf16[2,4,4,64,1024]{4,3,2,1,0:T(8,128)(2,1)} %get-tuple-element.53.prod_ref, ...), custom_call_target="tpu_custom_call" | custom-call | tf_op jit(solution)/shard_map/finish/pallas_call | solution.py:1530
  271.5 0.0 copy-start.1
  271.5 0.0 copy-start
  271.5 6.5 %spread_out.1 = (bf16[256,1024]{1,0:T(8,128)(2,1)}, f32[256,1024]{1,0:T(8,128)}, f32[32,1024]{1,0:T(8,128)}, f32[32,512]{1,0:T(8,128)}, f32[32,512]{1,0:T(8,128)...) custom-call(bf16[256,1024]{1,0:T(8,128)(2,1)} %get-tuple-element.65., ...), custom_call_target="tpu_custom_call" | custom-call | tf_op jit(solution)/shard_map/spread_out/pallas_call | solution.py:1598
  278.0 1.9 copy.29
  279.8 0.0 copy-done.1
  279.8 0.6 copy.33
  280.4 0.0 copy-done
  280.4 0.6 copy.34
  (2 shorter events, 0.0 us)
Async XLA Ops:
  271.5 8.4 %copy-start.1 = (f32[8,128]{1,0:T(8,128)S(1)}, f32[8,128]{1,0:T(8,128)}, u32[]{:S(2)}) copy-start(f32[8,128]{1,0:T(8,128)} %get-tuple-element.72) | copy-start | bytes 12292
  271.5 9.0 %copy-start = (f32[8,128]{1,0:T(8,128)S(1)}, f32[8,128]{1,0:T(8,128)}, u32[]{:S(2)}) copy-start(f32[8,128]{1,0:T(8,128)} %get-tuple-element.77) | copy-start | bytes 12292

commit v5 on v4

--- a/solution.py
+++ b/solution.py
@@ -310,7 +310,6 @@
         for copy in part_copies(d, out, into, send_sem, recv_sem):
             copy().wait_send()
 
-
 def front_kernel(
     length_ref,
     hidden_ref,
@@ -326,7 +325,7 @@
     router_ref,
     cos_ref,
     sin_ref,
-    w_ref,
+    w_hbm,
     normed_ref,
     q_ref,
     k_ref,
@@ -340,14 +339,18 @@
     posz_ref,
     posx_ref,
     grads_ref,
+    w_ref,
     mixed_t,
     posz_out,
     posx_out,
     tok_z,
     tok_x,
     outgoing,
+    store_sem,
     w_send,
     w_recv,
+    o_send,
+    o_recv,
     core_send,
     core_recv,
     kv_send,
@@ -362,15 +365,15 @@
     y, r, x, z = place()
     f32, bf16 = jnp.float32, jnp.bfloat16
     sibling = moved(0, 0, 1 - r)[0]
-    meet(False, False)
+    meet(False, True)
 
     for p in range(2):
         part = slice(256 * p, 256 * p + 256)
         w_ref[r, z, x, :, D * p : D * p + HALF] = wq_ref[:, HALF * p : HALF * p + HALF]
         w_ref[r, z, x, :, D * p + HALF : D * p + 768] = wk_ref[:, part]
         w_ref[r, z, x, :, D * p + 768 : D * p + D] = wv_ref[:, part]
-    w_ref[r, z, x, :, 2 * D : 3 * D] = wo_ref[...]
-    front, rear = pl.ds(0, D + HALF), pl.ds(D + HALF, D + HALF)
+    front, rear, output = pl.ds(0, D), pl.ds(D, D), pl.ds(2 * D, D)
+    quarter = pl.ds(pl.multiple_of(2 * D + 256 * y, 256), 256)
 
     def line_step(d):
         mine_q, mine_o = w_ref.at[r, z, x, :, front], w_ref.at[r, z, x, :, rear]
@@ -388,6 +391,24 @@
             remote(from_x, from_x, w_send.at[16 + at], w_recv.at[16 + at], moved(0, d, r)[0]),
         )
 
+    w_ref[r, z, x, :, quarter] = wo_ref[:, pl.ds(pl.multiple_of(256 * y, 256), 256)]
+
+    def output_line(d):
+        own = w_ref.at[r, z, x, :, quarter]
+        return remote(own, own, o_send.at[d], o_recv.at[d], moved(0, d, r)[0])
+
+    def output_cross(d):
+        own = w_ref.at[r, :, x, :, quarter]
+        return remote(own, own, o_send.at[4 + d], o_recv.at[4 + d], moved(d, 0, r)[0])
+
+    def output_plane(n):
+        own = w_ref.at[r, :, :, :, quarter]
+        return remote(own, own, o_send.at[8 + n], o_recv.at[8 + n], plane_shift(n)[0])
+
+    def output_core():
+        own = w_ref.at[r, :, :, :, output]
+        return remote(own, own, o_send.at[0], o_recv.at[0], sibling)
+
     def core_step(d):
         from_x = w_ref.at[r, :, lax.rem(x - d + 4, 4), :, front]
         from_z = w_ref.at[r, lax.rem(z - d + 4, 4), :, :, rear]
@@ -405,16 +426,19 @@
     def _(d):
         for copy in cross_step(0, d):
             copy.start()
+        output_line(d).start()
 
     tokens = hidden_ref.shape[0]
-    experts_iota = lax.broadcasted_iota(jnp.int32, (EXPERTS, tokens), 0)
+    experts_iota = lax.broadcasted_iota(jnp.int32, (EXPERTS, tokens), 0).astype(f32)
     live = r * tokens + lax.broadcasted_iota(jnp.int32, (1, tokens), 1) < length_ref[0]
     routed_to = jnp.zeros((EXPERTS, tokens), f32)
     ranks = jnp.zeros((EXPERTS, tokens), f32)
+    routes = routes_ref[...].astype(f32).T
+    priority = prio_ref[...].astype(f32).T
     for j in range(TOP):
-        match = experts_iota == routes_ref[j : j + 1, :]
+        match = experts_iota == routes[j : j + 1, :]
         routed_to = jnp.where(match, 1.0, routed_to)
-        ranks = jnp.where(match, prio_ref[j : j + 1, :].astype(f32), ranks)
+        ranks = jnp.where(match, priority[j : j + 1, :], ranks)
     far = float(1 << 20)
     ranks = jnp.where((routed_to > 0.0) & live, ranks, far)
     ranks_t = ranks.T
@@ -461,6 +485,14 @@
             copy.start()
 
     @pl.loop(1, 4)
+    def _(d):
+        output_line(d).wait_recv()
+
+    @pl.loop(1, 4)
+    def _(d):
+        output_cross(d).start()
+
+    @pl.loop(1, 4)
     def _(e):
         for copy in line_step(e):
             copy.wait_recv()
@@ -501,6 +533,13 @@
 
     @pl.loop(1, 4)
     def _(d):
+        output_cross(d).wait_recv()
+
+    for n in range(1, PLANES):
+        output_plane(n).start()
+
+    @pl.loop(1, 4)
+    def _(d):
         @pl.loop(0, 4)
         def _(e):
             for copy in cross_step(e, d):
@@ -514,7 +553,9 @@
         dx = lax.rem(k, 4)
         dz = lax.rem(dx + k // 4, 4)
         for core in range(2):
-            send_slots(outgoing, grads_ref, core, dz, dx, slot_send, slot_recv, 1)
+            send_slots(
+                outgoing, grads_ref, core, dz, dx, slot_send, slot_recv, 1, store_sem.at[1]
+            )
 
     @pl.loop(0, 4)
     def _(d):
@@ -552,6 +593,10 @@
 
     key_copy.wait_recv()
     value_copy.wait_recv()
+
+    for n in range(1, PLANES):
+        output_plane(n).wait_recv()
+    output_core().start()
 
     key_live = lax.broadcasted_iota(jnp.int32, (2 * tokens, 1), 0) < length_ref[0]
     score_scale = HEAD ** (-0.5)
@@ -572,6 +617,9 @@
             mixed_t[at, :] = dot(values, probs, ((1,), (0,))).astype(bf16)
 
     mixed_ref[...] = mixed_t[...].T
+    output_core().wait_recv()
+    weights_out = pltpu.make_async_copy(w_ref, w_hbm, store_sem.at[0])
+    weights_out.start()
     w_out = w_ref[:, :, :, :, 2 * D : 3 * D].reshape(D, D)
     middle = hidden_ref[...].astype(f32) + dot(mixed_ref[...], w_out, ((1,), (0,)))
     middle_ref[...] = middle
@@ -612,6 +660,14 @@
             for copy in cross_step(e, d):
                 copy.wait_send()
 
+    @pl.loop(1, 4)
+    def _(d):
+        output_line(d).wait_send()
+        output_cross(d).wait_send()
+        output_plane(d).wait_send()
+
+    output_core().wait_send()
+    weights_out.wait()
     for copy in core_step(0):
         copy.wait_send()
     key_copy.wait_send()
@@ -621,6 +677,7 @@
 def front(length, *arrays):
     f32, bf16, i32 = jnp.float32, jnp.bfloat16, jnp.int32
     vmem = pl.BlockSpec(memory_space=pltpu.VMEM)
+    hbm = pl.BlockSpec(memory_space=pl.ANY)
     shape = jax.ShapeDtypeStruct
     out_shape = (
         shape((2, 4, 4, 32, 3 * D), bf16),
@@ -639,6 +696,7 @@
         shape((2, 4, 4, CAP, D), bf16),
     )
     scratch = [
+        pltpu.VMEM((2, 4, 4, 32, 3 * D), bf16),
         pltpu.VMEM((D, TOKENS), bf16),
         pltpu.VMEM((4, 8, TOKENS), i32),
         pltpu.VMEM((4, 8, TOKENS), i32),
@@ -646,13 +704,14 @@
         pltpu.VMEM((4, TOKENS, HALF), bf16),
         pltpu.VMEM((2, 4, 4, CAP, D), bf16),
     ]
-    for count in (40, 8, 2, 8, 2 * GROUP, 8):
+    scratch += [pltpu.SemaphoreType.DMA((2,))]
+    for count in (40, 12, 8, 2, 8, 2 * GROUP, 8):
         scratch += [pltpu.SemaphoreType.DMA((count,))] * 2
     return pl.pallas_call(
         front_kernel,
         out_shape=out_shape,
         in_specs=[pl.BlockSpec(memory_space=pltpu.SMEM)] + [vmem] * len(arrays),
-        out_specs=[vmem] * len(out_shape),
+        out_specs=[hbm] + [vmem] * (len(out_shape) - 2) + [hbm],
         scratch_shapes=scratch,
         compiler_params=pltpu.CompilerParams(
             collective_id=3, has_side_effects=True, vmem_limit_bytes=60 << 20
@@ -660,19 +719,24 @@
         name="front",
     )(length, *arrays)
 
-
 def expert_kernel(
     routed_ref,
     pos_ref,
     posz_ref,
     posx_ref,
     gates_ref,
+    grads_hbm,
+    wg_hbm,
+    wu_hbm,
+    wd_hbm,
+    rg_ref,
+    gdot_ref,
+    prod_hbm,
+    grad_hbm,
     grads_ref,
     wg_ref,
     wu_ref,
     wd_ref,
-    rg_ref,
-    gdot_ref,
     prod_ref,
     grad_ref,
     tok_z,
@@ -690,6 +754,8 @@
     active,
     weighted,
     pre_grads,
+    load_sem,
+    store_sem,
     first_send,
     first_recv,
     slot_send,
@@ -703,6 +769,19 @@
 ):
     y, r, x, z = place()
     f32, bf16 = jnp.float32, jnp.bfloat16
+    loads = [
+        pltpu.make_async_copy(source, target, load_sem.at[n])
+        for n, (source, target) in enumerate(
+            (
+                (wg_hbm, wg_ref),
+                (wu_hbm, wu_ref),
+                (wd_hbm, wd_ref),
+                (grads_hbm, grads_ref),
+            )
+        )
+    ]
+    for load in loads:
+        load.start()
     meet(True, False)
 
     @pl.loop(1, 4)
@@ -767,6 +846,15 @@
                 outgoing[core, dz, dx, :, 0:HALF] = left[part].astype(bf16)
                 outgoing[core, dz, dx, :, HALF:D] = right[part].astype(bf16)
                 send_slots(outgoing, arrived, core, dz, dx, slot_send, slot_recv, 1)
+
+    def keep_produced(k):
+        core, dz, dx = k // CHIPS, lax.rem(k // 4, 4), lax.rem(k, 4)
+        return pltpu.make_async_copy(
+            prod_ref.at[core, dz, dx], prod_hbm.at[core, dz, dx], store_sem.at[k]
+        )
+
+    for load in loads:
+        load.wait()
 
     @pl.loop(0, 8)
     def _(c):
@@ -820,12 +908,16 @@
                 small(k, dot_out, dot_in, -1, GROUP).start()
 
             prod_ref[core, dz, dx] = produced[part]
+            keep_produced(k).start()
             active[core, dz, dx] = act[part]
             weighted[core, dz, dx] = produced_grad[part]
             pre_grads[core, dz, dx, :, 0:HALF] = gate_grad[part]
             pre_grads[core, dz, dx, :, HALF:D] = up_grad[part]
 
     all_rows = GROUP * CAP
+
+    def keep_grads(n):
+        return pltpu.make_async_copy(grad_ref.at[n], grad_hbm.at[n], store_sem.at[GROUP + n])
 
     @pl.loop(0, 2)
     def _(n):
@@ -861,6 +953,7 @@
             rows = part[128 * h : 128 * h + 128].astype(bf16)
             grad_ref[n, h, 0:128, :] = rows[:, 0:HALF]
             grad_ref[n, h, 128:256, :] = rows[:, HALF:D]
+        keep_grads(n).start()
 
     @pl.loop(0, GROUP)
     def _(k):
@@ -880,6 +973,14 @@
     rg_ref[...] = (parts_in[0].astype(f32) + parts_in[1].astype(f32)) + (
         parts_in[2].astype(f32) + parts_in[3].astype(f32)
     )
+    @pl.loop(0, GROUP)
+    def _(k):
+        keep_produced(k).wait()
+
+    @pl.loop(0, 4)
+    def _(n):
+        keep_grads(n).wait()
+
     slots_sent(outgoing, arrived, slot_send, slot_recv)
     slots_sent(going_back, mid, back_send, back_recv)
     parts_sent(parts_out, parts_in, part_send, part_recv)
@@ -900,14 +1001,19 @@
 def experts(*arrays):
     f32, bf16 = jnp.float32, jnp.bfloat16
     vmem = pl.BlockSpec(memory_space=pltpu.VMEM)
+    hbm = pl.BlockSpec(memory_space=pl.ANY)
     shape = jax.ShapeDtypeStruct
     block = pltpu.VMEM((2, 4, 4, CAP, D), bf16)
     narrow = pltpu.VMEM((2, 4, 4, CAP, HALF), bf16)
     line = pltpu.VMEM((4, TOKENS, HALF), bf16)
     wide = pltpu.VMEM((4, TOKENS, D), bf16)
     little = pltpu.VMEM((GROUP, 8, 128), f32)
-    scratch = [line, line, block, block, block, block, wide, wide]
+    scratch = [block]
+    scratch += [pltpu.VMEM(w.shape, bf16) for w in arrays[-3:]]
+    scratch += [block, pltpu.VMEM((4, 2, 384, HALF), bf16)]
+    scratch += [line, line, block, block, block, block, wide, wide]
     scratch += [little] * 4 + [narrow, block, block]
+    scratch += [pltpu.SemaphoreType.DMA((4,)), pltpu.SemaphoreType.DMA((GROUP + 4,))]
     for count in (8, 2 * GROUP, 2 * GROUP, 8, 2 * GROUP):
         scratch += [pltpu.SemaphoreType.DMA((count,))] * 2
     out_shape = (
@@ -919,8 +1025,8 @@
     return pl.pallas_call(
         expert_kernel,
         out_shape=out_shape,
-        in_specs=[vmem] * len(arrays),
-        out_specs=[vmem] * len(out_shape),
+        in_specs=[vmem] * (len(arrays) - 4) + [hbm] * 4,
+        out_specs=[vmem, vmem, hbm, hbm],
         scratch_shapes=scratch,
         compiler_params=pltpu.CompilerParams(
             collective_id=1, has_side_effects=True, vmem_limit_bytes=60 << 20
@@ -944,7 +1050,7 @@
     gates_ref,
     rg_ref,
     gdot_ref,
-    expert_ref,
+    expert_hbm,
     routed_ref,
     router_ref,
     middle_ref,
@@ -967,8 +1073,11 @@
     mgain_out,
     router_out,
     own_out,
-    esum_ref,
+    esum_hbm,
     w_ref,
+    own_quarter,
+    next_quarter,
+    quarter_sum,
     mid,
     parts_out,
     parts_in,
@@ -1000,7 +1109,7 @@
     gain_y,
     gain_y_in,
     router_all,
-    w_sem,
+    load_sem,
     c_send,
     c_recv,
     part_send,
@@ -1023,23 +1132,28 @@
     sibling = moved(0, 0, 1 - r)[0]
     tokens = routed_ref.shape[0]
     f32, bf16 = jnp.float32, jnp.bfloat16
-    weights_in = pltpu.make_async_copy(w_hbm, w_ref, w_sem)
-    weights_in.start()
-    meet(True, True)
 
     above, below = plane_shift(1), plane_shift(3)
     opposite = plane_shift(2)[1]
+    loads = [pltpu.make_async_copy(w_hbm, w_ref, load_sem.at[0])]
+    loads.append(pltpu.make_async_copy(expert_hbm.at[y], own_quarter, load_sem.at[1]))
+    for n in range(2):
+        source = expert_hbm.at[(above, below)[n][1], n]
+        loads.append(pltpu.make_async_copy(source, next_quarter.at[n], load_sem.at[2 + n]))
+    for load in loads:
+        load.start()
+    meet(True, True)
 
     def relayed(n):
         device = (above, below)[n][0]
         return remote(
-            expert_ref.at[opposite, n], relay_in.at[n], ex_send.at[n], ex_recv.at[n], device
+            expert_hbm.at[opposite, n], relay_in.at[n], ex_send.at[n], ex_recv.at[n], device
         )
 
     def direct(n):
         device, other = (above, below)[n]
         return remote(
-            expert_ref.at[other, 1 - n],
+            expert_hbm.at[other, 1 - n],
             y_in.at[n, 1 - n],
             ex_send.at[2 + n],
             ex_recv.at[2 + n],
@@ -1055,12 +1169,12 @@
     def handed(n):
         device = (above, below)[n][0]
         return remote(
-            esum_ref.at[y], esum_ref.at[y], ex_send.at[6 + n], ex_recv.at[6 + n], device
+            quarter_sum, esum_hbm.at[y], ex_send.at[6 + n], ex_recv.at[6 + n], device
         )
 
     def passed_on(n):
         device, came_from = (above, below)[n][0], (below, above)[n][1]
-        part = esum_ref.at[came_from, n]
+        part = esum_hbm.at[came_from, n]
         return remote(part, part, ex_send.at[8 + n], ex_recv.at[8 + n], device)
 
     def weight(first, width):
@@ -1083,8 +1197,6 @@
 
     for n in range(2):
         relayed(n).start()
-    for n in range(2):
-        direct(n).start()
     sib_mixed.start()
     sib_normed.start()
 
@@ -1132,15 +1244,10 @@
 
     small_in[me] = small_out[me]
 
-    weights_in.wait()
+    for n in range(2):
+        direct(n).start()
+    loads[0].wait()
     mg_t[...] = dot(weight(2 * D, D), branch_own[...], ((1,), (1,))).astype(bf16)
-
-    for n in range(2):
-        relayed(n).wait_recv()
-        target = (above, below)[n][1]
-        total = relay_in[n].astype(f32) + expert_ref[target, n].astype(f32)
-        relay_out[n] = total.astype(bf16)
-        merged(n).start()
 
     mine = pl.ds(pl.multiple_of(r * HALF, HALF), HALF)
 
@@ -1316,60 +1423,21 @@
     sib_grads(0, 0).start()
 
     for n in range(2):
-        direct(n).wait_recv()
-        merged(n).wait_recv()
-    for n in range(2):
-        total = expert_ref[y, n].astype(f32) + (y_in[0, n].astype(f32) + y_in[1, n].astype(f32))
-        esum_ref[y, n] = total.astype(bf16)
-    for n in range(2):
-        handed(n).start()
-
-    whole_keyval(0)
-
-    @pl.loop(1, GROUP)
-    def _(k):
-        small(k).wait_recv()
-
-    def small_across(n):
-        device, _ = plane_shift(n)
-        return remote(
-            small_y, small_y_in.at[y], sm_send.at[GROUP + n], sm_recv.at[GROUP + n], device
-        )
-
-    small_y[...] = jnp.sum(small_in[...], axis=0)
-    small_y_in[y] = small_y[...]
-    for n in range(1, PLANES):
-        small_across(n).start()
-
-    sum_second(2)
-    sib_normed.wait_recv()
-    projections(0)
+        relayed(n).wait_recv()
+        loads[2 + n].wait()
+        total = relay_in[n].astype(f32) + next_quarter[n].astype(f32)
+        relay_out[n] = total.astype(bf16)
+        merged(n).start()
+
     heads(1, 0, 4)
     sib_keyval(1).start()
     sib_grads(1, 0).start()
-
-    for n in range(1, PLANES):
-        small_across(n).wait_recv()
-    totals = small_y_in[0] + small_y_in[1] + small_y_in[2] + small_y_in[3]
-    mgain_out[...] = totals[8:16]
-    router_all[me] = totals[0:8]
-
-    def router_row(k):
-        device, _ = step_of(k, 1)
-        at = 2 * GROUP + k
-        return remote(
-            router_all.at[me], router_all.at[me], sm_send.at[at], sm_recv.at[at], device
-        )
-
-    @pl.loop(1, GROUP)
-    def _(k):
-        router_row(k).start()
-
+    whole_keyval(0)
+    sib_normed.wait_recv()
+    projections(0)
     whole_keyval(1)
     normed_grad = inputs_part(0)
     projections(1)
-    sum_second(0)
-    sum_third(2)
     normed_grad = normed_grad + inputs_part(1)
 
     inputs = hidden_ref[...].astype(f32)
@@ -1393,9 +1461,34 @@
     inner = jnp.mean(scaled * rows, axis=1, keepdims=True)
     hgrad_ref[...] += scale * (scaled - rows * inner)
 
+    loads[1].wait()
     for n in range(2):
-        handed(n).wait_recv()
-        passed_on(n).start()
+        direct(n).wait_recv()
+        merged(n).wait_recv()
+    for n in range(2):
+        total = own_quarter[n].astype(f32) + (y_in[0, n].astype(f32) + y_in[1, n].astype(f32))
+        quarter_sum[n] = total.astype(bf16)
+    quarter_out = pltpu.make_async_copy(quarter_sum, esum_hbm.at[y], load_sem.at[4])
+    quarter_out.start()
+    for n in range(2):
+        handed(n).start()
+
+    sum_second(2)
+
+    @pl.loop(1, GROUP)
+    def _(k):
+        small(k).wait_recv()
+
+    def small_across(n):
+        device, _ = plane_shift(n)
+        return remote(
+            small_y, small_y_in.at[y], sm_send.at[GROUP + n], sm_recv.at[GROUP + n], device
+        )
+
+    small_y[...] = jnp.sum(small_in[...], axis=0)
+    small_y_in[y] = small_y[...]
+    for n in range(1, PLANES):
+        small_across(n).start()
 
     fold_parts(
         parts_out,
@@ -1409,8 +1502,25 @@
         part_send,
         part_recv,
     )
-    sum_second(1)
-    sum_third(0)
+    sum_third(2)
+    sum_second(0)
+
+    for n in range(1, PLANES):
+        small_across(n).wait_recv()
+    totals = small_y_in[0] + small_y_in[1] + small_y_in[2] + small_y_in[3]
+    mgain_out[...] = totals[8:16]
+    router_all[me] = totals[0:8]
+
+    def router_row(k):
+        device, _ = step_of(k, 1)
+        at = 2 * GROUP + k
+        return remote(
+            router_all.at[me], router_all.at[me], sm_send.at[at], sm_recv.at[at], device
+        )
+
+    @pl.loop(1, GROUP)
+    def _(k):
+        router_row(k).start()
 
     @pl.loop(1, GROUP)
     def _(k):
@@ -1426,6 +1536,13 @@
 
     for n in range(1, PLANES):
         gain_across(n).start()
+
+    sum_second(1)
+    sum_third(0)
+
+    for n in range(2):
+        handed(n).wait_recv()
+        passed_on(n).start()
 
     sum_third(1)
 
@@ -1476,6 +1593,7 @@
             across(p, n).wait()
     for n in range(2):
         passed_on(n).wait_recv()
+    quarter_out.wait()
     own_out[...] = (y_parts[0].astype(f32) + y_parts[1].astype(f32)) + (
         y_parts[2].astype(f32) + y_parts[3].astype(f32)
     )
@@ -1489,9 +1607,13 @@
     sems = pltpu.SemaphoreType.DMA
     in_specs = [pl.BlockSpec(memory_space=pltpu.SMEM)] + [vmem] * len(arrays)
     in_specs[1] = pl.BlockSpec(memory_space=pl.ANY)
+    in_specs[7] = pl.BlockSpec(memory_space=pl.ANY)
     in_specs[17] = pl.BlockSpec(memory_space=pl.ANY)
     scratch = [
         pltpu.VMEM((2, 4, 4, 32, 3 * D), bf16),
+        pltpu.VMEM((2, 384, HALF), bf16),
+        pltpu.VMEM((2, 384, HALF), bf16),
+        pltpu.VMEM((2, 384, HALF), bf16),
         pltpu.VMEM((2, 4, 4, CAP, D), bf16),
         pltpu.VMEM((4, tokens, D), bf16),
         pltpu.VMEM((4, tokens, D), bf16),
@@ -1523,7 +1645,7 @@
         pltpu.VMEM((8, 128), f32),
         pltpu.VMEM((PLANES, 8, 128), f32),
         pltpu.VMEM((GROUP, 8, 128), f32),
-        sems,
+        sems((5,)),
     ]
     for count in (2 * GROUP + 1, 8, 10, 9, 24, 24, 9, 5 * GROUP):
         scratch += [sems((count,)), sems((count,))]
@@ -1539,7 +1661,7 @@
             shape((4, 2, 384, HALF), bf16),
         ),
         in_specs=in_specs,
-        out_specs=[vmem] * 7,
+        out_specs=[vmem] * 6 + [pl.BlockSpec(memory_space=pl.ANY)],
         scratch_shapes=scratch,
         compiler_params=pltpu.CompilerParams(
             collective_id=2, has_side_effects=True, vmem_limit_bytes=60 << 20
@@ -1676,8 +1798,8 @@
         lengths,
         hidden_in,
         cotangent,
-        routes.T,
-        priority.reshape(tok_count, TOP).T,
+        routes,
+        priority.reshape(tok_count, TOP),
         attn_gain[None],
         moe_gain[None],
         query_weight,

time: 282 us -> 273 us (0.968)
  Pallas kernels: 273 us -> 263 us
    pallas_call x1, Pallas kernels: 92.2 us -> 88.3 us  [experts(): pl.pallas_call(expert_kernel, out_shape=out_shape, in_specs=[vmem] * (len...]
    pallas_call x1, Pallas kernels: 78.5 us -> 74.8 us  [front(): pl.pallas_call(front_kernel, out_shape=out_shape, in_specs=[pl.BlockSpec(...]
    pallas_call x1, Pallas kernels: 95.9 us -> 93.1 us  [finish(): pl.pallas_call(finish_kernel, out_shape=(shape((tokens, D), bf16), shape(...]
where the time goes in v5:
time: 273 us; the launch traced here: 272 us
  Pallas kernels  263 us (96%)
  local copies, waits for them, and re-layouts  5.82 us (2%)
    pallas_call x1, Pallas kernels, finish(): pl.pallas_call(finish_kernel, out_shape=(shape((tokens, D), bf16), shape(...  93.1 us
    pallas_call x1, Pallas kernels, experts(): pl.pallas_call(expert_kernel, out_shape=out_shape, in_specs=[vmem] * (len...  88.3 us
    pallas_call x1, Pallas kernels, front(): pl.pallas_call(front_kernel, out_shape=out_shape, in_specs=[pl.BlockSpec(...  74.8 us
    pallas_call x1, Pallas kernels, spread_out(): pl.pallas_call(spread_kernel, grid=(4,), out_shape=(shape((TOKENS, D), bf...  6.48 us

profile of v5, /device:TPU:1, one launch (start us, length us, event | category | flops | bytes accessed | tf_op | source)
XLA Modules:
  0.0 272.0 jit_solution(18266541754324892123)
XLA Ops:
  1.3 0.5 broadcast.16
  1.8 1.4 reduce.3
  3.2 0.8 multiply_sine_fusion
  4.0 0.8 reshape.44.prio_ref
  4.8 1.5 copy.29.routes_ref
  6.3 74.8 %front.1 = (bf16[2,4,4,32,3072]{4,3,2,1,0:T(8,128)(2,1)}, bf16[256,1024]{1,0:T(8,128)(2,1)}, bf16[1024,256]{1,0:T(8,128)(2,1)}, bf16[512,512]{1,0:T(8,128)(2,1)}...) custom-call(s32[1]{0:T(128)S(6)} %copy.33.length_ref, ...), custom_call_target="tpu_custom_call" | custom-call | tf_op jit(solution)/shard_map/front/pallas_call | solution.py:710
  81.1 88.3 %experts.1 = (f32[256,1024]{1,0:T(8,128)}, f32[32,256]{1,0:T(8,128)}, bf16[2,4,4,64,1024]{4,3,2,1,0:T(8,128)(2,1)}, bf16[4,2,384,512]{3,2,1,0:T(8,128)(2,1)}) custom-call(bf16[256,1024]{1,0:T(8,128)(2,1)} %get-tuple-element.47.routed_ref, s32[32,256]{1,0:T(8,128)} %get-tuple-element.48.pos_ref, s32[4,8,256]{2,1,0:T(8,128)} %get-tuple-element.49.posz_ref, ...), custom_call_target="tpu_custom_call" | custom-call | tf_op jit(solution)/shard_map/experts/pallas_call | solution.py:1025
  169.4 93.1 %finish.1 = (bf16[256,1024]{1,0:T(8,128)(2,1)}, f32[256,1024]{1,0:T(8,128)}, f32[8,128]{1,0:T(8,128)}, f32[8,128]{1,0:T(8,128)}, f32[32,8,128]{2,1,0:T(8,128)}, ...) custom-call(s32[1]{0:T(128)S(6)} %copy.33.length_ref, bf16[2,4,4,64,1024]{4,3,2,1,0:T(8,128)(2,1)} %get-tuple-element.53.prod_ref, ...), custom_call_target="tpu_custom_call" | custom-call | tf_op jit(solution)/shard_map/finish/pallas_call | solution.py:1652
  262.4 0.0 copy-start.1
  262.5 0.0 copy-start
  262.5 6.5 %spread_out.1 = (bf16[256,1024]{1,0:T(8,128)(2,1)}, f32[256,1024]{1,0:T(8,128)}, f32[32,1024]{1,0:T(8,128)}, f32[32,512]{1,0:T(8,128)}, f32[32,512]{1,0:T(8,128)...) custom-call(bf16[256,1024]{1,0:T(8,128)(2,1)} %get-tuple-element.65., ...), custom_call_target="tpu_custom_call" | custom-call | tf_op jit(solution)/shard_map/spread_out/pallas_call | solution.py:1720
  268.9 1.9 copy.30
  270.8 0.0 copy-done.1
  270.8 0.6 copy.34
  271.4 0.0 copy-done
  271.4 0.6 copy.35
  (2 shorter events, 0.0 us)
Async XLA Ops:
  262.4 8.4 %copy-start.1 = (f32[8,128]{1,0:T(8,128)S(1)}, f32[8,128]{1,0:T(8,128)}, u32[]{:S(2)}) copy-start(f32[8,128]{1,0:T(8,128)} %get-tuple-element.72) | copy-start | bytes 12292
  262.5 9.0 %copy-start = (f32[8,128]{1,0:T(8,128)S(1)}, f32[8,128]{1,0:T(8,128)}, u32[]{:S(2)}) copy-start(f32[8,128]{1,0:T(8,128)} %get-tuple-element.77) | copy-start | bytes 12292

commit v6 on v5

v6 whole, which is shorter than its diff:
```python
import jax
import jax.numpy as jnp
from jax import lax
from jax.experimental import pallas as pl
from jax.experimental.pallas import tpu as pltpu
from jax.sharding import PartitionSpec as P

D = 1024
HEADS = 16
HEAD = 64
KV_HEADS = 8
EXPERTS = 32
TOP = 8
CAP = 64


epsilon = 1e-05
rotary_base = 10000.0


MESH = pl.DeviceIdType.MESH
GROUP = 32
PLANES = 4
CHIPS = 16
HALF = D // 2
TOKENS = 256
NEG = -1000000000.0


def place():
    col = lax.axis_index("col")
    return lax.axis_index("dp"), lax.axis_index("row"), lax.rem(col, 4), col // 4


def moved(dx, dz, core):
    y, r, x, z = place()
    col = lax.rem(z + dz + 4, 4) * 4 + lax.rem(x + dx + 4, 4)
    return (y, core, col), core * CHIPS + col


def plane_shift(n):
    y, r, x, z = place()
    other = lax.rem(y + n, PLANES)
    return (other, r, z * 4 + x), other


def step_of(k, sign):
    y, r, x, z = place()
    return moved(sign * lax.rem(k, 4), sign * lax.rem(k // 4, 4), lax.rem(r + k // CHIPS, 2))


def remote(src, dst, send_sem, recv_sem, device):
    return pltpu.make_async_remote_copy(
        src_ref=src,
        dst_ref=dst,
        send_sem=send_sem,
        recv_sem=recv_sem,
        device_id=device,
        device_id_type=MESH,
    )


def meet(plane, planes):
    barrier = pltpu.get_barrier_semaphore()
    y, r, x, z = place()

    def greet(device):
        pl.semaphore_signal(barrier, inc=1, device_id=device, device_id_type=MESH)

    if plane:

        @pl.loop(1, GROUP)
        def _(k):
            greet(step_of(k, 1)[0])

        count = GROUP - 1
    else:
        for core in range(2):

            @pl.loop(1, 4)
            def _(d):
                greet(moved(d, 0, core)[0])
                greet(moved(0, d, core)[0])

        greet(moved(0, 0, 1 - r)[0])
        count = 13
    if planes:
        for n in range(1, PLANES):
            greet(plane_shift(n)[0])
        count += PLANES - 1
    pl.semaphore_wait(barrier, count)


def eye(n):
    return lax.broadcasted_iota(jnp.int32, (n, n), 0) == lax.broadcasted_iota(
        jnp.int32, (n, n), 1
    )


def as_row(column):
    return jnp.sum(jnp.where(eye(column.shape[0]), column, 0.0), axis=0, keepdims=True)


def as_column(row_vec):
    return jnp.sum(jnp.where(eye(row_vec.shape[1]), row_vec, 0.0), axis=1, keepdims=True)


def dot(a, b, dims):
    return lax.dot_general(a, b, (dims, ((), ())), preferred_element_type=jnp.float32)


def split_two(values):
    high = values.astype(jnp.bfloat16)
    return high, (values - high.astype(jnp.float32)).astype(jnp.bfloat16)


def picks(positions):
    slots = lax.broadcasted_iota(jnp.int32, (CAP, positions.shape[1]), 0)
    return slots == positions


def as_hot(mask):
    return mask.astype(jnp.float32).astype(jnp.bfloat16)


LEFT = pl.ds(0, HALF)
RIGHT = pl.ds(HALF, HALF)


def spread(d, source, tok_z, tok_x, send_sem, recv_sem):
    y, r, x, z = place()
    return (
        remote(
            source.at[:, LEFT], tok_z.at[d], send_sem.at[d], recv_sem.at[d], moved(0, d, r)[0]
        ),
        remote(
            source.at[:, RIGHT],
            tok_x.at[d],
            send_sem.at[4 + d],
            recv_sem.at[4 + d],
            moved(d, 0, r)[0],
        ),
    )


def slot_copies(out, into, core, there, dz, dx, send_sem, recv_sem, sign):
    y, r, x, z = place()
    at = there * CHIPS + dz * 4 + dx
    to = core * CHIPS + dz * 4 + dx
    return (
        lambda: remote(
            out.at[there, dz, dx, :, LEFT],
            into.at[core, dz, dx, :, LEFT],
            send_sem.at[at],
            recv_sem.at[to],
            moved(sign * dx, 0, there)[0],
        ),
        lambda: remote(
            out.at[there, dz, dx, :, RIGHT],
            into.at[core, dz, dx, :, RIGHT],
            send_sem.at[GROUP + at],
            recv_sem.at[GROUP + to],
            moved(0, sign * dz, there)[0],
        ),
    )


def is_local(core, offset):
    y, r, x, z = place()
    return (core == r) & (offset == 0)


def send_slots(out, into, there, dz, dx, send_sem, recv_sem, sign, local_sem=None):
    y, r, x, z = place()

    def keep(cols):
        source, target = out.at[there, dz, dx, :, cols], into.at[r, dz, dx, :, cols]
        if local_sem is None:
            target[...] = source[...]
        else:
            copy = pltpu.make_async_copy(source, target, local_sem)
            copy.start()
            copy.wait()

    left, right = slot_copies(out, into, r, there, dz, dx, send_sem, recv_sem, sign)

    @pl.when(jnp.logical_not(is_local(there, dx)))
    def _():
        left().start()

    @pl.when(is_local(there, dx))
    def _():
        keep(LEFT)

    @pl.when(jnp.logical_not(is_local(there, dz)))
    def _():
        right().start()

    @pl.when(is_local(there, dz))
    def _():
        keep(RIGHT)


def slots_arrived(out, into, core, dz, dx, send_sem, recv_sem, left=True, right=True):
    copies = slot_copies(out, into, core, core, dz, dx, send_sem, recv_sem, 1)
    for copy, offset, wanted in zip(copies, (dx, dz), (left, right)):
        if wanted:

            @pl.when(jnp.logical_not(is_local(core, offset)))
            def _():
                copy().wait_recv()


def block_sent(out, into, there, dz, dx, send_sem, recv_sem):
    copies = slot_copies(out, into, there, there, dz, dx, send_sem, recv_sem, 1)
    for copy, offset in zip(copies, (dx, dz)):

        @pl.when(jnp.logical_not(is_local(there, offset)))
        def _():
            copy().wait_send()


def slots_sent(out, into, send_sem, recv_sem):
    @pl.loop(0, GROUP)
    def _(k):
        block_sent(out, into, k // CHIPS, lax.rem(k // 4, 4), lax.rem(k, 4), send_sem, recv_sem)


def line_rows(line, d, axis):
    y, r, x, z = place()
    own = x if axis == 0 else z
    return [
        line[d, pl.ds(core * 4 + lax.rem(own + i, 4), 1), :] for core in range(2) for i in range(4)
    ]


def line_hot(line, d, axis):
    return as_hot(jnp.concatenate([picks(p) for p in line_rows(line, d, axis)], axis=0))


def add_up(mid, line, d, axis):
    if axis == 0:
        rows = mid[:, d, :, :, 0:HALF]
    else:
        rows = mid[:, :, d, :, HALF:D]
    return dot(line_hot(line, d, axis), rows.reshape(8 * CAP, HALF), ((0,), (0,))).astype(
        jnp.bfloat16
    )


def part_copies(d, out, into, send_sem, recv_sem):
    y, r, x, z = place()
    return (
        lambda: remote(
            out.at[d, :, LEFT],
            into.at[d, :, LEFT],
            send_sem.at[d],
            recv_sem.at[d],
            moved(0, -d, r)[0],
        ),
        lambda: remote(
            out.at[d, :, RIGHT],
            into.at[d, :, RIGHT],
            send_sem.at[4 + d],
            recv_sem.at[4 + d],
            moved(-d, 0, r)[0],
        ),
    )


def fold_parts(out, into, mid, slots, slot_send, slot_recv, posz_ref, posx_ref, send_sem, recv_sem):
    @pl.loop(0, 4)
    def _(d):
        if slots is not None:
            for core in range(2):
                for i in range(4):
                    slots_arrived(slots, mid, core, d, i, slot_send, slot_recv, right=False)
        left = add_up(mid, posz_ref, d, 0)

        @pl.when(d == 0)
        def _():
            into[0, :, 0:HALF] = left

        @pl.when(d != 0)
        def _():
            out[d, :, 0:HALF] = left
            part_copies(d, out, into, send_sem, recv_sem)[0]().start()

        if slots is not None:
            for core in range(2):
                for i in range(4):
                    slots_arrived(slots, mid, core, i, d, slot_send, slot_recv, left=False)
        right = add_up(mid, posx_ref, d, 1)

        @pl.when(d == 0)
        def _():
            into[0, :, HALF:D] = right

        @pl.when(d != 0)
        def _():
            out[d, :, HALF:D] = right
            part_copies(d, out, into, send_sem, recv_sem)[1]().start()


def parts_arrived(out, into, send_sem, recv_sem):
    @pl.loop(1, 4)
    def _(d):
        for copy in part_copies(d, out, into, send_sem, recv_sem):
            copy().wait_recv()


def parts_sent(out, into, send_sem, recv_sem):
    @pl.loop(1, 4)
    def _(d):
        for copy in part_copies(d, out, into, send_sem, recv_sem):
            copy().wait_send()

def front_kernel(
    length_ref,
    hidden_ref,
    cot_ref,
    routes_ref,
    prio_ref,
    again_ref,
    mgain_ref,
    wq_ref,
    wk_ref,
    wv_ref,
    wo_ref,
    router_ref,
    cos_ref,
    sin_ref,
    w_hbm,
    normed_ref,
    q_ref,
    k_ref,
    v_ref,
    lse_ref,
    mixed_ref,
    middle_ref,
    routed_ref,
    gates_ref,
    pos_ref,
    posz_ref,
    posx_ref,
    grads_ref,
    w_ref,
    mixed_t,
    posz_out,
    posx_out,
    tok_z,
    tok_x,
    outgoing,
    store_sem,
    w_send,
    w_recv,
    o_send,
    o_recv,
    core_send,
    core_recv,
    kv_send,
    kv_recv,
    first_send,
    first_recv,
    slot_send,
    slot_recv,
    pos_send,
    pos_recv,
):
    y, r, x, z = place()
    f32, bf16 = jnp.float32, jnp.bfloat16
    sibling = moved(0, 0, 1 - r)[0]
    meet(False, True)

    for p in range(2):
        part = slice(256 * p, 256 * p + 256)
        w_ref[r, z, x, :, D * p : D * p + HALF] = wq_ref[:, HALF * p : HALF * p + HALF]
        w_ref[r, z, x, :, D * p + HALF : D * p + 768] = wk_ref[:, part]
        w_ref[r, z, x, :, D * p + 768 : D * p + D] = wv_ref[:, part]
    front, rear, output = pl.ds(0, D), pl.ds(D, D), pl.ds(2 * D, D)
    quarter = pl.ds(pl.multiple_of(2 * D + 256 * y, 256), 256)

    def line_step(d):
        mine_q, mine_o = w_ref.at[r, z, x, :, front], w_ref.at[r, z, x, :, rear]
        return (
            remote(mine_q, mine_q, w_send.at[d], w_recv.at[d], moved(0, d, r)[0]),
            remote(mine_o, mine_o, w_send.at[4 + d], w_recv.at[4 + d], moved(d, 0, r)[0]),
        )

    def cross_step(e, d):
        at = 8 + 4 * e + d
        from_z = w_ref.at[r, lax.rem(z - e + 4, 4), x, :, front]
        from_x = w_ref.at[r, z, lax.rem(x - e + 4, 4), :, rear]
        return (
            remote(from_z, from_z, w_send.at[at], w_recv.at[at], moved(d, 0, r)[0]),
            remote(from_x, from_x, w_send.at[16 + at], w_recv.at[16 + at], moved(0, d, r)[0]),
        )

    w_ref[r, z, x, :, quarter] = wo_ref[:, pl.ds(pl.multiple_of(256 * y, 256), 256)]

    def output_line(d):
        own = w_ref.at[r, z, x, :, quarter]
        return remote(own, own, o_send.at[d], o_recv.at[d], moved(0, d, r)[0])

    def output_cross(d):
        own = w_ref.at[r, :, x, :, quarter]
        return remote(own, own, o_send.at[4 + d], o_recv.at[4 + d], moved(d, 0, r)[0])

    def output_plane(n):
        own = w_ref.at[r, :, :, :, quarter]
        return remote(own, own, o_send.at[8 + n], o_recv.at[8 + n], plane_shift(n)[0])

    def output_core():
        own = w_ref.at[r, :, :, :, output]
        return remote(own, own, o_send.at[0], o_recv.at[0], sibling)

    def core_step(d):
        from_x = w_ref.at[r, :, lax.rem(x - d + 4, 4), :, front]
        from_z = w_ref.at[r, lax.rem(z - d + 4, 4), :, :, rear]
        return (
            remote(from_x, from_x, core_send.at[d], core_recv.at[d], sibling),
            remote(from_z, from_z, core_send.at[4 + d], core_recv.at[4 + d], sibling),
        )

    @pl.loop(1, 4)
    def _(d):
        for copy in line_step(d):
            copy.start()

    @pl.loop(1, 4)
    def _(d):
        for copy in cross_step(0, d):
            copy.start()
        output_line(d).start()

    tokens = hidden_ref.shape[0]
    experts_iota = lax.broadcasted_iota(jnp.int32, (EXPERTS, tokens), 0).astype(f32)
    live = r * tokens + lax.broadcasted_iota(jnp.int32, (1, tokens), 1) < length_ref[0]
    routed_to = jnp.zeros((EXPERTS, tokens), f32)
    ranks = jnp.zeros((EXPERTS, tokens), f32)
    prio = prio_ref[...]
    lines = jnp.concatenate([prio[:, 128 * i : 128 * i + 128] for i in range(CHIPS)], axis=0)
    token = lax.broadcasted_iota(jnp.int32, (tokens, CHIPS), 0) // CHIPS
    owner = (token == lax.broadcasted_iota(jnp.int32, (tokens, CHIPS), 1)).astype(f32)
    token = lax.rem(lax.broadcasted_iota(jnp.int32, (tokens, 128), 0), CHIPS)
    lane = lax.broadcasted_iota(jnp.int32, (tokens, 128), 1)
    place_of = lax.rem(lax.broadcasted_iota(jnp.int32, (TOP, 128), 1), TOP)
    place_of = (place_of == lax.broadcasted_iota(jnp.int32, (TOP, 128), 0)).astype(f32)
    priority = jnp.zeros((TOP, tokens), f32)
    for unit, part in ((64.0, lines // 64), (1.0, lax.rem(lines, 64))):
        part = part.astype(f32).astype(bf16)
        rows = dot(owner.astype(bf16), part, ((1,), (0,)))
        rows = jnp.where(lane // TOP == token, rows, 0.0).astype(bf16)
        priority = priority + unit * dot(place_of.astype(bf16), rows, ((1,), (1,)))
    routes = routes_ref[...].astype(f32)
    for j in range(TOP):
        match = experts_iota == routes[j : j + 1, :]
        routed_to = jnp.where(match, 1.0, routed_to)
        ranks = jnp.where(match, priority[j : j + 1, :], ranks)
    far = float(1 << 20)
    ranks = jnp.where((routed_to > 0.0) & live, ranks, far)
    ranks_t = ranks.T
    rows = []
    for e in range(EXPERTS):
        earlier = ranks_t[:, e : e + 1] < ranks[e : e + 1, :]
        rows.append(jnp.sum(earlier.astype(f32), axis=0, keepdims=True))
    slots = jnp.concatenate(rows, axis=0)
    pos = jnp.where((ranks < far) & (slots < CAP), slots, -1.0).astype(jnp.int32)
    pos_ref[...] = pos
    for core in range(2):
        for i in range(4):
            at = core * CHIPS + 4 * i
            posz_out[i, 4 * core : 4 * core + 4, :] = pos[at : at + 4, :]
            for j in range(4):
                posx_out[j, 4 * core + i : 4 * core + i + 1, :] = pos[at + j : at + j + 1, :]
    posz_ref[0] = posz_out[z]
    posx_ref[0] = posx_out[x]
    tok_z[0] = cot_ref[:, 0:HALF]
    tok_x[0] = cot_ref[:, HALF:D]

    def pos_step(d):
        to_z, to_x = lax.rem(z + d, 4), lax.rem(x + d, 4)
        return (
            remote(
                posz_out.at[to_z],
                posz_ref.at[d],
                pos_send.at[d],
                pos_recv.at[d],
                moved(0, d, r)[0],
            ),
            remote(
                posx_out.at[to_x],
                posx_ref.at[d],
                pos_send.at[4 + d],
                pos_recv.at[4 + d],
                moved(d, 0, r)[0],
            ),
        )

    @pl.loop(1, 4)
    def _(d):
        for copy in pos_step(d):
            copy.start()

    @pl.loop(1, 4)
    def _(d):
        output_line(d).wait_recv()

    @pl.loop(1, 4)
    def _(d):
        output_cross(d).start()

    @pl.loop(1, 4)
    def _(e):
        for copy in line_step(e):
            copy.wait_recv()

        @pl.loop(1, 4)
        def _(d):
            for copy in cross_step(e, d):
                copy.start()

    @pl.loop(1, 4)
    def _(d):
        for copy in spread(d, cot_ref, tok_z, tok_x, first_send, first_recv):
            copy.start()

    for copy in core_step(0):
        copy.start()

    inputs = hidden_ref[...].astype(f32)
    scale = lax.rsqrt(jnp.mean(inputs * inputs, axis=1, keepdims=True) + epsilon)
    normed_ref[...] = (inputs * scale * again_ref[...]).astype(bf16)

    @pl.loop(1, 4)
    def _(d):
        for copy in spread(d, cot_ref, tok_z, tok_x, first_send, first_recv):
            copy.wait_recv()
        for copy in pos_step(d):
            copy.wait_recv()

    @pl.loop(0, 4)
    def _(d):
        left = dot(line_hot(posz_ref, d, 0), tok_z[d], ((1,), (0,))).astype(bf16)
        right = dot(line_hot(posx_ref, d, 1), tok_x[d], ((1,), (0,))).astype(bf16)
        for core in range(2):
            for i in range(4):
                part = slice((core * 4 + i) * CAP, (core * 4 + i + 1) * CAP)
                outgoing[core, d, i, :, 0:HALF] = left[part]
                outgoing[core, i, d, :, HALF:D] = right[part]

    @pl.loop(1, 4)
    def _(d):
        output_cross(d).wait_recv()

    for n in range(1, PLANES):
        output_plane(n).start()

    @pl.loop(1, 4)
    def _(d):
        @pl.loop(0, 4)
        def _(e):
            for copy in cross_step(e, d):
                copy.wait_recv()

        for copy in core_step(d):
            copy.start()

    @pl.loop(0, CHIPS)
    def _(k):
        dx = lax.rem(k, 4)
        dz = lax.rem(dx + k // 4, 4)
        for core in range(2):
            send_slots(
                outgoing, grads_ref, core, dz, dx, slot_send, slot_recv, 1, store_sem.at[1]
            )

    @pl.loop(0, 4)
    def _(d):
        for copy in core_step(d):
            copy.wait_recv()

    cosine, sine = cos_ref[...], sin_ref[...]
    here = pl.ds(pl.multiple_of(r * tokens, tokens), tokens)

    def projected(first):
        weight = w_ref[:, :, :, :, first : first + HALF].reshape(D, HALF)
        return dot(normed_ref[...], weight, ((1,), (0,))).T

    def turned(rows):
        parts = []
        for h in range(rows.shape[0] // HEAD):
            first, second = rows[HEAD * h : HEAD * h + 32], rows[HEAD * h + 32 : HEAD * h + HEAD]
            parts += [first * cosine - second * sine, second * cosine + first * sine]
        return jnp.concatenate(parts, axis=0).astype(bf16)

    key_copy = remote(
        k_ref.at[:, here], k_ref.at[:, here], kv_send.at[0], kv_recv.at[0], sibling
    )
    value_copy = remote(
        v_ref.at[:, here], v_ref.at[:, here], kv_send.at[1], kv_recv.at[1], sibling
    )
    for p in range(2):
        both = projected(D * p + HALF)
        k_ref[256 * p : 256 * p + 256, here] = turned(both[0:256])
        v_ref[256 * p : 256 * p + 256, here] = both[256:512].astype(bf16)
    key_copy.start()
    value_copy.start()
    for p in range(2):
        q_ref[HALF * p : HALF * p + HALF, :] = turned(projected(D * p))

    key_copy.wait_recv()
    value_copy.wait_recv()

    for n in range(1, PLANES):
        output_plane(n).wait_recv()
    output_core().start()

    key_live = lax.broadcasted_iota(jnp.int32, (2 * tokens, 1), 0) < length_ref[0]
    score_scale = HEAD ** (-0.5)

    @pl.loop(0, KV_HEADS)
    def _(g):
        head = pl.ds(pl.multiple_of(g * HEAD, HEAD), HEAD)
        keys, values = k_ref[head, :], v_ref[head, :]
        for j in range(2):
            at = pl.ds(pl.multiple_of((2 * g + j) * HEAD, HEAD), HEAD)
            scores = dot(keys, q_ref[at, :], ((0,), (0,))) * score_scale
            scores = jnp.where(key_live, scores, NEG)
            top = jnp.max(scores, axis=0, keepdims=True)
            weights = jnp.exp(scores - top)
            total = jnp.sum(weights, axis=0, keepdims=True)
            lse_ref[pl.ds(2 * g + j, 1), :] = top + jnp.log(total)
            probs = (weights * (1.0 / total)).astype(bf16)
            mixed_t[at, :] = dot(values, probs, ((1,), (0,))).astype(bf16)

    mixed_ref[...] = mixed_t[...].T
    output_core().wait_recv()
    weights_out = pltpu.make_async_copy(w_ref, w_hbm, store_sem.at[0])
    weights_out.start()
    w_out = w_ref[:, :, :, :, 2 * D : 3 * D].reshape(D, D)
    middle = hidden_ref[...].astype(f32) + dot(mixed_ref[...], w_out, ((1,), (0,)))
    middle_ref[...] = middle
    scale = lax.rsqrt(jnp.mean(middle * middle, axis=1, keepdims=True) + epsilon)
    routed_ref[...] = (middle * scale * mgain_ref[...]).astype(bf16)
    logits = dot(router_ref[...], routed_ref[...], ((1,), (1,)))
    logits = jnp.where(routed_to > 0.0, logits, -jnp.inf)
    picked = jnp.exp(logits - jnp.max(logits, axis=0, keepdims=True))
    gates_ref[...] = picked / jnp.sum(picked, axis=0, keepdims=True)

    @pl.loop(0, GROUP)
    def _(k):
        slots_arrived(
            outgoing,
            grads_ref,
            k // CHIPS,
            lax.rem(k // 4, 4),
            lax.rem(k, 4),
            slot_send,
            slot_recv,
        )

    slots_sent(outgoing, grads_ref, slot_send, slot_recv)

    @pl.loop(1, 4)
    def _(d):
        for copies in (
            line_step(d),
            core_step(d),
            pos_step(d),
            spread(d, cot_ref, tok_z, tok_x, first_send, first_recv),
        ):
            for copy in copies:
                copy.wait_send()

        @pl.loop(0, 4)
        def _(e):
            for copy in cross_step(e, d):
                copy.wait_send()

    @pl.loop(1, 4)
    def _(d):
        output_line(d).wait_send()
        output_cross(d).wait_send()
        output_plane(d).wait_send()

    output_core().wait_send()
    weights_out.wait()
    for copy in core_step(0):
        copy.wait_send()
    key_copy.wait_send()
    value_copy.wait_send()


def front(length, *arrays):
    f32, bf16, i32 = jnp.float32, jnp.bfloat16, jnp.int32
    vmem = pl.BlockSpec(memory_space=pltpu.VMEM)
    hbm = pl.BlockSpec(memory_space=pl.ANY)
    shape = jax.ShapeDtypeStruct
    out_shape = (
        shape((2, 4, 4, 32, 3 * D), bf16),
        shape((TOKENS, D), bf16),
        shape((D, TOKENS), bf16),
        shape((HALF, 2 * TOKENS), bf16),
        shape((HALF, 2 * TOKENS), bf16),
        shape((HEADS, TOKENS), f32),
        shape((TOKENS, D), bf16),
        shape((TOKENS, D), f32),
        shape((TOKENS, D), bf16),
        shape((EXPERTS, TOKENS), f32),
        shape((EXPERTS, TOKENS), i32),
        shape((4, 8, TOKENS), i32),
        shape((4, 8, TOKENS), i32),
        shape((2, 4, 4, CAP, D), bf16),
    )
    scratch = [
        pltpu.VMEM((2, 4, 4, 32, 3 * D), bf16),
        pltpu.VMEM((D, TOKENS), bf16),
        pltpu.VMEM((4, 8, TOKENS), i32),
        pltpu.VMEM((4, 8, TOKENS), i32),
        pltpu.VMEM((4, TOKENS, HALF), bf16),
        pltpu.VMEM((4, TOKENS, HALF), bf16),
        pltpu.VMEM((2, 4, 4, CAP, D), bf16),
    ]
    scratch += [pltpu.SemaphoreType.DMA((2,))]
    for count in (40, 12, 8, 2, 8, 2 * GROUP, 8):
        scratch += [pltpu.SemaphoreType.DMA((count,))] * 2
    return pl.pallas_call(
        front_kernel,
        out_shape=out_shape,
        in_specs=[pl.BlockSpec(memory_space=pltpu.SMEM)] + [vmem] * len(arrays),
        out_specs=[hbm] + [vmem] * (len(out_shape) - 2) + [hbm],
        scratch_shapes=scratch,
        compiler_params=pltpu.CompilerParams(
            collective_id=3, has_side_effects=True, vmem_limit_bytes=60 << 20
        ),
        name="front",
    )(length, *arrays)


def turned_back(rows, cosine, sine):
    first, second = rows[0:32], rows[32:64]
    return jnp.concatenate(
        [first * cosine + second * sine, second * cosine - first * sine], axis=0
    )


def rest_kernel(
    length_ref,
    routed_ref,
    pos_ref,
    posz_ref,
    posx_ref,
    gates_ref,
    grads_hbm,
    wg_hbm,
    wu_hbm,
    wd_hbm,
    router_ref,
    middle_ref,
    cot_ref,
    hidden_hbm,
    again_ref,
    mgain_ref,
    normed_hbm,
    mixed_hbm,
    w_hbm,
    q_hbm,
    k_hbm,
    v_hbm,
    lse_ref,
    cos_ref,
    sin_ref,
    hout_ref,
    hgrad_ref,
    again_out,
    mgain_out,
    router_out,
    own_out,
    esum_hbm,
    prod_hbm,
    mid_hbm,
    tok_z,
    tok_x,
    arrived,
    mid,
    parts_in,
    parts_in2,
    gate_out,
    gate_in,
    dot_out,
    dot_in,
    rg_ref,
    gdot_ref,
    expert_ref,
    relay_in,
    y_in,
    branch_sib,
    normed_sib,
    mixed_sib,
    grad_sib,
    kv_in,
    rs_in,
    rs_in2,
    y_parts,
    small_in,
    small_y_in,
    gain_in,
    gain_y_in,
    router_all,
    load_sem,
    store_sem,
    first_send,
    first_recv,
    slot_send,
    slot_recv,
    back_send,
    back_recv,
    part_send,
    part_recv,
    small_send,
    small_recv,
    c_send,
    c_recv,
    part_send2,
    part_recv2,
    ex_send,
    ex_recv,
    sib_send,
    sib_recv,
    rs_send,
    rs_recv,
    rs_send2,
    rs_recv2,
    ys_send,
    ys_recv,
    sm_send,
    sm_recv,
):
    y, r, x, z = place()
    me = r * CHIPS + z * 4 + x
    sibling = moved(0, 0, 1 - r)[0]
    tokens = TOKENS
    f32, bf16 = jnp.float32, jnp.bfloat16

    above, below = plane_shift(1), plane_shift(3)
    opposite = plane_shift(2)[1]
    def relayed(n):
        device = (above, below)[n][0]
        return remote(
            expert_ref.at[0, n], relay_in.at[n], ex_send.at[n], ex_recv.at[n], device
        )

    def direct(n):
        device = (above, below)[n][0]
        return remote(
            expert_ref.at[1 + n, 1 - n],
            y_in.at[n, 1 - n],
            ex_send.at[2 + n],
            ex_recv.at[2 + n],
            device,
        )

    def passed_on(n):
        device, came_from = (above, below)[n][0], (below, above)[n][1]
        part = esum_hbm.at[came_from, n]
        return remote(part, part, ex_send.at[8 + n], ex_recv.at[8 + n], device)

    def to_sibling(at, src, dst):
        return remote(src, dst, sib_send.at[at], sib_recv.at[at], sibling)

    half = pl.ds(pl.multiple_of((1 - r) * HALF, HALF), HALF)
    sib_normed = to_sibling(0, normed_hbm.at[:, half], normed_sib)
    sib_mixed = to_sibling(1, mixed_hbm.at[:, half], mixed_sib)

    meet(True, True)
    sib_mixed.start()
    sib_normed.start()

    def expert_phase(grads_ref, wg_ref, wu_ref, wd_ref, outgoing, parts_out, active, weighted, pre_grads):
        loads = [
            pltpu.make_async_copy(source, target, load_sem.at[n])
            for n, (source, target) in enumerate(
                (
                    (wg_hbm, wg_ref),
                    (wu_hbm, wu_ref),
                    (wd_hbm, wd_ref),
                    (grads_hbm, grads_ref),
                )
            )
        ]
        for load in loads:
            load.start()
        @pl.loop(1, 4)
        def _(d):
            for copy in spread(d, routed_ref, tok_z, tok_x, first_send, first_recv):
                copy.start()

        tok_z[0] = routed_ref[:, 0:HALF]
        tok_x[0] = routed_ref[:, HALF:D]

        def small(k, out, into, sign, base, arriving=False):
            there, dz, dx = k // CHIPS, lax.rem(k // 4, 4), lax.rem(k, 4)
            slot = k if arriving else r * CHIPS + lax.rem(k, CHIPS)
            return remote(
                out.at[k],
                into.at[slot],
                small_send.at[base + k],
                small_recv.at[base + slot],
                moved(sign * dx, sign * dz, there)[0],
            )

        def own_slot(k):
            return k == r * CHIPS

        @pl.loop(0, GROUP)
        def _(k):
            there, dz, dx = k // CHIPS, lax.rem(k // 4, 4), lax.rem(k, 4)
            _, expert = moved(dx, dz, there)
            chosen = picks(pos_ref[pl.ds(expert, 1), :])
            gate_col = jnp.sum(
                jnp.where(chosen, gates_ref[pl.ds(expert, 1), :], 0.0), axis=1, keepdims=True
            )
            gate_out[k, 0:1, 0:CAP] = as_row(gate_col)

            @pl.when(own_slot(k))
            def _():
                gate_in[k] = gate_out[k]

            @pl.when(jnp.logical_not(own_slot(k)))
            def _():
                small(k, gate_out, gate_in, 1, 0).start()

        @pl.loop(1, 4)
        def _(d):
            for copy in spread(d, routed_ref, tok_z, tok_x, first_send, first_recv):
                copy.wait_recv()

        @pl.loop(0, 4)
        def _(g):
            for dx in range(4):
                dz = lax.rem(dx + g, 4)
                left_rows, right_rows = [], []
                for core in range(2):
                    at_x = core * 4 + lax.rem(x + dx, 4)
                    at_z = core * 4 + lax.rem(z + dz, 4)
                    left_rows.append(picks(posz_ref[dz, pl.ds(at_x, 1), :]))
                    right_rows.append(picks(posx_ref[dx, pl.ds(at_z, 1), :]))
                left = dot(as_hot(jnp.concatenate(left_rows, axis=0)), tok_z[dz], ((1,), (0,)))
                right = dot(as_hot(jnp.concatenate(right_rows, axis=0)), tok_x[dx], ((1,), (0,)))
                for core in range(2):
                    part = slice(core * CAP, core * CAP + CAP)
                    outgoing[core, dz, dx, :, 0:HALF] = left[part].astype(bf16)
                    outgoing[core, dz, dx, :, HALF:D] = right[part].astype(bf16)
                    send_slots(outgoing, arrived, core, dz, dx, slot_send, slot_recv, 1)

        def keep_produced(k):
            core, dz, dx = k // CHIPS, lax.rem(k // 4, 4), lax.rem(k, 4)
            return pltpu.make_async_copy(
                grads_ref.at[core, dz, dx], prod_hbm.at[core, dz, dx], store_sem.at[k]
            )

        for load in loads:
            load.wait()

        @pl.loop(0, 8)
        def _(c):
            g, core = c // 2, lax.rem(c, 2)
            rows, gate_cols, grads = [], [], []
            for dx in range(4):
                dz = lax.rem(dx + g, 4)
                k = core * CHIPS + dz * 4 + dx
                slots_arrived(outgoing, arrived, core, dz, dx, slot_send, slot_recv)

                @pl.when(jnp.logical_not(own_slot(k)))
                def _():
                    small(k, gate_out, gate_in, 1, 0, True).wait_recv()

                rows.append(arrived[core, dz, dx])
                gate_cols.append(as_column(gate_in[k, 0:1, 0:CAP]))
                grads.append(grads_ref[core, dz, dx])
            rows = jnp.concatenate(rows, axis=0)
            gate_cols = jnp.concatenate(gate_cols, axis=0)
            grads = jnp.concatenate(grads, axis=0).astype(f32)
            gate_pre = dot(rows, wg_ref[...], ((1,), (0,)))
            up_pre = dot(rows, wu_ref[...], ((1,), (0,)))
            gate_sig = jax.nn.sigmoid(gate_pre)
            gate_act = gate_pre * gate_sig
            act = (gate_act * up_pre).astype(bf16)
            produced = dot(act, wd_ref[...], ((1,), (0,))).astype(bf16).astype(f32)
            dots = jnp.sum(produced * grads, axis=1, keepdims=True)
            produced_grad = (gate_cols * grads).astype(bf16)
            act_grad = dot(produced_grad, wd_ref[...], ((1,), (1,))).astype(bf16).astype(f32)
            gate_grad = (
                act_grad * up_pre * gate_sig * (1.0 + gate_pre * (1.0 - gate_sig))
            ).astype(bf16)
            up_grad = (act_grad * gate_act).astype(bf16)
            row_grads = dot(gate_grad, wg_ref[...], ((1,), (1,)))
            row_grads = (row_grads + dot(up_grad, wu_ref[...], ((1,), (1,)))).astype(bf16)
            produced = (produced * gate_cols).astype(bf16)
            for dx in range(4):
                dz = lax.rem(dx + g, 4)
                k = core * CHIPS + dz * 4 + dx
                part = slice(dx * CAP, dx * CAP + CAP)
                block_sent(outgoing, arrived, core, dz, dx, slot_send, slot_recv)
                outgoing[core, dz, dx] = row_grads[part]
                send_slots(outgoing, mid, core, dz, dx, back_send, back_recv, -1)
                dot_out[k, 0:1, 0:CAP] = as_row(dots[part])

                @pl.when(own_slot(k))
                def _():
                    dot_in[k] = dot_out[k]

                @pl.when(jnp.logical_not(own_slot(k)))
                def _():
                    small(k, dot_out, dot_in, -1, GROUP).start()

                grads_ref[core, dz, dx] = produced[part]
                keep_produced(k).start()
                active[core, dz, dx] = act[part]
                weighted[core, dz, dx] = produced_grad[part]
                pre_grads[core, dz, dx, :, 0:HALF] = gate_grad[part]
                pre_grads[core, dz, dx, :, HALF:D] = up_grad[part]

        def send_results(g):
            for dx in range(4):
                dz = (dx + g) % 4
                for core in range(2):
                    keep_produced(core * CHIPS + dz * 4 + dx).wait()
                    send_slots(prod_hbm, mid_hbm, core, dz, dx, c_send, c_recv, -1, load_sem.at[4])

        send_results(0)

        all_rows = GROUP * CAP

        def quarter_grads(slot, n):
            span = pl.ds(pl.multiple_of(n * 256, 256), 256)
            left = arrived[:, :, :, :, span].reshape(all_rows, 256)
            part = dot(left, pre_grads[...].reshape(all_rows, D), ((0,), (0,))).astype(bf16)
            narrow = pl.ds(pl.multiple_of(n * 128, 128), 128)
            left = active[:, :, :, :, narrow].reshape(all_rows, 128)
            down = dot(left, weighted[...].reshape(all_rows, D), ((0,), (0,))).astype(bf16)
            for h in range(2):
                rows = part[128 * h : 128 * h + 128]
                expert_ref[slot, h, 0:128, :] = rows[:, 0:HALF]
                expert_ref[slot, h, 128:256, :] = rows[:, HALF:D]
                rows = down[64 * h : 64 * h + 64]
                expert_ref[slot, h, 256:320, :] = rows[:, 0:HALF]
                expert_ref[slot, h, 320:384, :] = rows[:, HALF:D]

        quarter_grads(0, opposite)
        for n in range(2):
            relayed(n).start()

        fold_parts(
            parts_out,
            parts_in,
            mid,
            outgoing,
            back_send,
            back_recv,
            posz_ref,
            posx_ref,
            part_send,
            part_recv,
        )
        for g in range(1, 4):
            send_results(g)

        @pl.loop(1, 4)
        def _(slot):
            quarter_grads(slot, lax.rem(y + jnp.where(slot == 1, 1, jnp.where(slot == 2, 3, 0)), 4))

        for n in range(2):
            direct(n).start()

        @pl.loop(0, GROUP)
        def _(k):
            @pl.when(jnp.logical_not(own_slot(k)))
            def _():
                small(k, dot_out, dot_in, -1, GROUP, True).wait_recv()

            there, dz, dx = k // CHIPS, lax.rem(k // 4, 4), lax.rem(k, 4)
            _, expert = moved(dx, dz, there)
            at = pl.ds(expert, 1)
            dots = as_column(dot_in[k, 0:1, 0:CAP])
            gdot_ref[at, :] = jnp.sum(
                jnp.where(picks(pos_ref[at, :]), dots, 0.0), axis=0, keepdims=True
            )

        parts_arrived(parts_out, parts_in, part_send, part_recv)
        rg_ref[...] = (parts_in[0].astype(f32) + parts_in[1].astype(f32)) + (
            parts_in[2].astype(f32) + parts_in[3].astype(f32)
        )
        slots_sent(outgoing, mid, back_send, back_recv)
        parts_sent(parts_out, parts_in, part_send, part_recv)

        @pl.loop(1, 4)
        def _(d):
            for copy in spread(d, routed_ref, tok_z, tok_x, first_send, first_recv):
                copy.wait_send()

        @pl.loop(0, GROUP)
        def _(k):
            @pl.when(jnp.logical_not(own_slot(k)))
            def _():
                small(k, gate_out, gate_in, 1, 0).wait_send()
                small(k, dot_out, dot_in, -1, GROUP).wait_send()

    pl.run_scoped(
        expert_phase,
        pltpu.VMEM((2, 4, 4, CAP, D), bf16),
        pltpu.VMEM((D, HALF), bf16),
        pltpu.VMEM((D, HALF), bf16),
        pltpu.VMEM((HALF, D), bf16),
        pltpu.VMEM((2, 4, 4, CAP, D), bf16),
        pltpu.VMEM((4, tokens, D), bf16),
        pltpu.VMEM((2, 4, 4, CAP, HALF), bf16),
        pltpu.VMEM((2, 4, 4, CAP, D), bf16),
        pltpu.VMEM((2, 4, 4, CAP, D), bf16),
    )

    def finish_phase(w_ref, q_ref, k_ref, v_ref, normed_ref, mixed_ref, hidden_ref, parts_out2, quarter_sum, relay_out, branch_own, mg_t, grad_t, kv_own, kv_out, weight_part, rs_out, y_out, small_out, small_y, gain_out, gain_y):
        loads = [
            pltpu.make_async_copy(source, target, load_sem.at[n])
            for n, (source, target) in enumerate(
                (
                    (w_hbm, w_ref),
                    (q_hbm, q_ref),
                    (k_hbm, k_ref),
                    (v_hbm, v_ref),
                    (normed_hbm, normed_ref),
                    (mixed_hbm, mixed_ref),
                    (hidden_hbm, hidden_ref),
                )
            )
        ]
        for load in loads:
            load.start()

        def weight(first, width):
            return w_ref[:, :, :, :, first : first + width].reshape(D, width)

        def merged(n):
            device = (above, below)[n][0]
            return remote(
                relay_out.at[n], y_in.at[n, n], ex_send.at[4 + n], ex_recv.at[4 + n], device
            )

        def handed(n):
            device = (above, below)[n][0]
            return remote(
                quarter_sum, esum_hbm.at[y], ex_send.at[6 + n], ex_recv.at[6 + n], device
            )

        def sib_keyval(p):
            return to_sibling(3 + p, kv_out.at[p], kv_in.at[p])

        def sib_grads(p, part):
            rows = pl.ds(p * D + part * HALF, HALF)
            return to_sibling(5 + 2 * p + part, grad_t.at[rows], grad_sib.at[rows])

        sib_branch = to_sibling(2, branch_own, branch_sib)

        for n in range(2):
            relayed(n).wait_recv()
            total = relay_in[n].astype(f32) + expert_ref[1 + n, n].astype(f32)
            relay_out[n] = total.astype(bf16)
            merged(n).start()

        gates = gates_ref[...]
        gdot = gdot_ref[...]
        logit_grad = gates * (gdot - jnp.sum(gates * gdot, axis=0, keepdims=True))
        high, rest = split_two(logit_grad)
        router_part = dot(high, routed_ref[...], ((1,), (0,)))
        router_part = router_part + dot(rest, routed_ref[...], ((1,), (0,)))
        routed_grad = dot(high, router_ref[...], ((0,), (0,)))
        routed_grad = routed_grad + dot(rest, router_ref[...], ((0,), (0,)))
        routed_grad = routed_grad + rg_ref[...]
        live = (
            r * tokens + lax.broadcasted_iota(jnp.int32, (tokens, 1), 0) < length_ref[0]
        ).astype(f32)
        middle = middle_ref[...]
        scale = lax.rsqrt(jnp.mean(middle * middle, axis=1, keepdims=True) + epsilon)
        rows = middle * scale
        moe_part = jnp.sum(routed_grad * rows, axis=0, keepdims=True)
        scaled = routed_grad * mgain_ref[...]
        inner = jnp.mean(scaled * rows, axis=1, keepdims=True)
        middle_grad = cot_ref[...].astype(f32) * live + scale * (scaled - rows * inner)
        hgrad_ref[...] = middle_grad
        branch_own[...] = middle_grad.astype(bf16)
        sib_branch.start()
        for j in range(8):
            part = slice(128 * j, 128 * j + 128)
            small_out[:, j, :] = router_part[:, part]
            small_out[:, 8 + j, :] = jnp.broadcast_to(moe_part[:, part], (GROUP, 128))

        def tiny(k):
            device, other = step_of(k, 1)
            return remote(small_out.at[other], small_in.at[me], sm_send.at[k], sm_recv.at[k], device)

        @pl.loop(1, GROUP)
        def _(k):
            tiny(k).start()

        small_in[me] = small_out[me]

        for load in loads:
            load.wait()
        mg_t[...] = dot(weight(2 * D, D), branch_own[...], ((1,), (1,))).astype(bf16)

        mine = pl.ds(pl.multiple_of(r * HALF, HALF), HALF)

        def columns(p):
            return pl.ds(p * D, HALF), pl.ds(p * D + HALF, HALF)

        def first_step(p, d):
            left, right = columns(p)
            at = 8 * p + d
            return (
                remote(
                    weight_part.at[lax.rem(z + d, 4), :, :, left],
                    rs_in.at[d, :, :, left],
                    rs_send.at[at],
                    rs_recv.at[at],
                    moved(0, d, r)[0],
                ),
                remote(
                    weight_part.at[:, lax.rem(x + d, 4), :, right],
                    rs_in.at[d, :, :, right],
                    rs_send.at[4 + at],
                    rs_recv.at[4 + at],
                    moved(d, 0, r)[0],
                ),
            )

        def second_step(p, d):
            left, right = columns(p)
            at = 8 * p + d
            return (
                remote(
                    rs_out.at[lax.rem(x + d, 4), :, left],
                    rs_in2.at[d, :, left],
                    rs_send2.at[at],
                    rs_recv2.at[at],
                    moved(d, 0, r)[0],
                ),
                remote(
                    rs_out.at[lax.rem(z + d, 4), :, right],
                    rs_in2.at[d, :, right],
                    rs_send2.at[4 + at],
                    rs_recv2.at[4 + at],
                    moved(0, d, r)[0],
                ),
            )

        def across(p, n):
            cols = pl.ds(p * D, D)
            at = 3 * p + n - 1
            return remote(
                y_out.at[:, cols],
                y_parts.at[y, :, cols],
                ys_send.at[at],
                ys_recv.at[at],
                plane_shift(n)[0],
            )

        def sum_first(p, total):
            weight_part[:, :, :, p * D : p * D + D] = total.astype(bf16).reshape(4, 4, 32, D)

            @pl.loop(1, 4)
            def _(d):
                for copy in first_step(p, d):
                    copy.start()

        def sum_second(p):
            left, right = columns(p)

            @pl.loop(1, 4)
            def _(d):
                for copy in first_step(p, d):
                    copy.wait_recv()

            total = weight_part[z, :, :, left].astype(f32)
            other = weight_part[:, x, :, right].astype(f32)
            for d in range(1, 4):
                total = total + rs_in[d, :, :, left].astype(f32)
                other = other + rs_in[d, :, :, right].astype(f32)
            rs_out[:, :, left] = total.astype(bf16)
            rs_out[:, :, right] = other.astype(bf16)

            @pl.loop(1, 4)
            def _(d):
                for copy in second_step(p, d):
                    copy.start()

        def sum_third(p):
            left, right = columns(p)

            @pl.loop(1, 4)
            def _(d):
                for copy in second_step(p, d):
                    copy.wait_recv()

            total = rs_out[x, :, left].astype(f32)
            other = rs_out[z, :, right].astype(f32)
            for d in range(1, 4):
                total = total + rs_in2[d, :, left].astype(f32)
                other = other + rs_in2[d, :, right].astype(f32)
            y_out[:, left] = total.astype(bf16)
            y_out[:, right] = other.astype(bf16)
            y_parts[y, :, left] = total.astype(bf16)
            y_parts[y, :, right] = other.astype(bf16)
            for n in range(1, PLANES):
                across(p, n).start()

        sib_mixed.wait_recv()
        sib_branch.wait_recv()
        total = dot(mixed_ref[:, mine], branch_own[...], ((0,), (0,)))
        sum_first(2, total + dot(mixed_sib[...], branch_sib[...], ((0,), (0,))))

        key_live = lax.broadcasted_iota(jnp.int32, (2 * tokens, 1), 0) < length_ref[0]
        score_scale = HEAD ** (-0.5)
        cosine, sine = cos_ref[...], sin_ref[...]
        first_core = r == 0

        def key_head(p, i):
            g = 4 * p + i
            head = pl.ds(pl.multiple_of(g * HEAD, HEAD), HEAD)
            keys, values = k_ref[head, :], v_ref[head, :]
            key_sum, value_sum = None, None
            for j in range(2):
                at = pl.ds(pl.multiple_of((2 * g + j) * HEAD, HEAD), HEAD)
                query, mixed_grad = q_ref[at, :], mg_t[at, :]
                scores = dot(keys, query, ((0,), (0,))) * score_scale
                scores = jnp.where(key_live, scores, NEG)
                probs = jnp.exp(scores - lse_ref[pl.ds(2 * g + j, 1), :])
                prob_grad = dot(values, mixed_grad, ((0,), (0,)))
                value_part = dot(mixed_grad, probs.astype(bf16), ((1,), (1,)))
                inner = jnp.sum(probs * prob_grad, axis=0, keepdims=True)
                score_grad = (probs * (prob_grad - inner)).astype(bf16)
                key_part = dot(query, score_grad, ((1,), (1,)))
                query_grad = dot(keys, score_grad, ((1,), (0,))) * score_scale
                to = pl.ds(pl.multiple_of(p * D + (2 * i + j) * HEAD, HEAD), HEAD)
                grad_t[to, :] = turned_back(query_grad, cosine, sine).astype(bf16)
                key_sum = key_part if key_sum is None else key_sum + key_part
                value_sum = value_part if value_sum is None else value_sum + value_part
            key_sum = key_sum * score_scale
            for n, part in enumerate((key_sum, value_sum)):
                to = pl.ds(pl.multiple_of(256 * n + i * HEAD, HEAD), HEAD)
                kv_own[p, to, :] = jnp.where(first_core, part[:, :tokens], part[:, tokens:])
                away = jnp.where(first_core, part[:, tokens:], part[:, :tokens])
                kv_out[p, to, :] = away.astype(bf16)

        def heads(p, first, last):
            @pl.loop(first, last)
            def _(i):
                key_head(p, i)

        def whole_keyval(p):
            sib_keyval(p).wait_recv()
            for i in range(4):
                rows = slice(HEAD * i, HEAD * i + HEAD)
                total = kv_own[p, rows, :] + kv_in[p, rows, :].astype(f32)
                to = p * D + HALF + HEAD * i
                grad_t[to : to + HEAD, :] = turned_back(total, cosine, sine).astype(bf16)
            total = kv_own[p, 256:512, :] + kv_in[p, 256:512, :].astype(f32)
            grad_t[p * D + HALF + 256 : p * D + D, :] = total.astype(bf16)
            sib_grads(p, 1).start()

        def projections(p):
            rows = slice(p * D, p * D + D)
            for part in range(2):
                sib_grads(p, part).wait_recv()
            total = dot(normed_ref[:, mine], grad_t[rows, :], ((0,), (1,)))
            sum_first(p, total + dot(normed_sib[...], grad_sib[rows, :], ((0,), (1,))))

        def inputs_part(p):
            return dot(grad_t[p * D : p * D + D, :], weight(p * D, D), ((0,), (1,)))

        heads(0, 0, 4)
        sib_keyval(0).start()
        sib_grads(0, 0).start()

        heads(1, 0, 4)
        sib_keyval(1).start()
        sib_grads(1, 0).start()
        whole_keyval(0)
        sib_normed.wait_recv()
        projections(0)
        whole_keyval(1)
        normed_grad = inputs_part(0)
        projections(1)
        normed_grad = normed_grad + inputs_part(1)

        inputs = hidden_ref[...].astype(f32)
        scale = lax.rsqrt(jnp.mean(inputs * inputs, axis=1, keepdims=True) + epsilon)
        rows = inputs * scale
        attn_part = jnp.sum(normed_grad * rows, axis=0, keepdims=True)
        for j in range(8):
            gain_out[j : j + 1, :] = attn_part[:, 128 * j : 128 * j + 128]

        def gain(k):
            device, _ = step_of(k, 1)
            at = 3 * GROUP + k
            return remote(gain_out, gain_in.at[me], sm_send.at[at], sm_recv.at[at], device)

        @pl.loop(1, GROUP)
        def _(k):
            gain(k).start()

        gain_in[me] = gain_out[...]
        scaled = normed_grad * again_ref[...]
        inner = jnp.mean(scaled * rows, axis=1, keepdims=True)
        hgrad_ref[...] += scale * (scaled - rows * inner)

        for n in range(2):
            direct(n).wait_recv()
            merged(n).wait_recv()
        for n in range(2):
            total = expert_ref[3, n].astype(f32) + (y_in[0, n].astype(f32) + y_in[1, n].astype(f32))
            quarter_sum[n] = total.astype(bf16)
        quarter_out = pltpu.make_async_copy(quarter_sum, esum_hbm.at[y], load_sem.at[9])
        quarter_out.start()
        for n in range(2):
            handed(n).start()

        sum_second(2)

        @pl.loop(1, GROUP)
        def _(k):
            tiny(k).wait_recv()

        def small_across(n):
            device, _ = plane_shift(n)
            return remote(
                small_y, small_y_in.at[y], sm_send.at[GROUP + n], sm_recv.at[GROUP + n], device
            )

        small_y[...] = jnp.sum(small_in[...], axis=0)
        small_y_in[y] = small_y[...]
        for n in range(1, PLANES):
            small_across(n).start()

        @pl.loop(0, GROUP)
        def _(k):
            slots_arrived(
                prod_hbm, mid_hbm, k // CHIPS, lax.rem(k // 4, 4), lax.rem(k, 4), c_send, c_recv
            )

        results_in = pltpu.make_async_copy(mid_hbm, mid, load_sem.at[10])
        results_in.start()
        results_in.wait()
        fold_parts(
            parts_out2,
            parts_in2,
            mid,
            None,
            c_send,
            c_recv,
            posz_ref,
            posx_ref,
            part_send2,
            part_recv2,
        )
        sum_third(2)
        sum_second(0)

        for n in range(1, PLANES):
            small_across(n).wait_recv()
        totals = small_y_in[0] + small_y_in[1] + small_y_in[2] + small_y_in[3]
        mgain_out[...] = totals[8:16]
        router_all[me] = totals[0:8]

        def router_row(k):
            device, _ = step_of(k, 1)
            at = 2 * GROUP + k
            return remote(
                router_all.at[me], router_all.at[me], sm_send.at[at], sm_recv.at[at], device
            )

        @pl.loop(1, GROUP)
        def _(k):
            router_row(k).start()

        @pl.loop(1, GROUP)
        def _(k):
            gain(k).wait_recv()

        gain_y[...] = jnp.sum(gain_in[...], axis=0)
        gain_y_in[y] = gain_y[...]

        def gain_across(n):
            device, _ = plane_shift(n)
            at = 4 * GROUP + n
            return remote(gain_y, gain_y_in.at[y], sm_send.at[at], sm_recv.at[at], device)

        for n in range(1, PLANES):
            gain_across(n).start()

        sum_second(1)
        sum_third(0)

        for n in range(2):
            handed(n).wait_recv()
            passed_on(n).start()

        sum_third(1)

        parts_arrived(parts_out2, parts_in2, part_send2, part_recv2)
        mixture = (parts_in2[0].astype(f32) + parts_in2[1].astype(f32)) + (
            parts_in2[2].astype(f32) + parts_in2[3].astype(f32)
        )
        hout_ref[...] = ((middle_ref[...] + mixture) * live).astype(bf16)

        for n in range(1, PLANES):
            gain_across(n).wait_recv()
        again_out[...] = (gain_y_in[0] + gain_y_in[1]) + (gain_y_in[2] + gain_y_in[3])

        @pl.loop(1, GROUP)
        def _(k):
            router_row(k).wait_recv()

        router_out[...] = router_all[...]

        slots_sent(prod_hbm, mid_hbm, c_send, c_recv)
        parts_sent(parts_out2, parts_in2, part_send2, part_recv2)

        @pl.loop(1, GROUP)
        def _(k):
            tiny(k).wait_send()
            router_row(k).wait_send()
            gain(k).wait_send()

        @pl.loop(1, 4)
        def _(d):
            for p in range(3):
                for copy in first_step(p, d) + second_step(p, d):
                    copy.wait_send()

        for n in range(2):
            for copy in (relayed(n), direct(n), merged(n), handed(n), passed_on(n)):
                copy.wait_send()
        for copy in (sib_normed, sib_mixed, sib_branch):
            copy.wait_send()
        for p in range(2):
            sib_keyval(p).wait_send()
            for part in range(2):
                sib_grads(p, part).wait_send()
        for n in range(1, PLANES):
            small_across(n).wait_send()
            gain_across(n).wait_send()
            for p in range(3):
                across(p, n).wait()
        for n in range(2):
            passed_on(n).wait_recv()
        quarter_out.wait()
        own_out[...] = (y_parts[0].astype(f32) + y_parts[1].astype(f32)) + (
            y_parts[2].astype(f32) + y_parts[3].astype(f32)
        )

    pl.run_scoped(
        finish_phase,
        pltpu.VMEM((2, 4, 4, 32, 3 * D), bf16),
        pltpu.VMEM((D, tokens), bf16),
        pltpu.VMEM((HALF, 2 * tokens), bf16),
        pltpu.VMEM((HALF, 2 * tokens), bf16),
        pltpu.VMEM((tokens, D), bf16),
        pltpu.VMEM((tokens, D), bf16),
        pltpu.VMEM((tokens, D), bf16),
        pltpu.VMEM((4, tokens, D), bf16),
        pltpu.VMEM((2, 384, HALF), bf16),
        pltpu.VMEM((2, 384, HALF), bf16),
        pltpu.VMEM((tokens, D), bf16),
        pltpu.VMEM((D, tokens), bf16),
        pltpu.VMEM((2 * D, tokens), bf16),
        pltpu.VMEM((2, HALF, tokens), f32),
        pltpu.VMEM((2, HALF, tokens), bf16),
        pltpu.VMEM((4, 4, 32, 3 * D), bf16),
        pltpu.VMEM((4, 32, 3 * D), bf16),
        pltpu.VMEM((32, 3 * D), bf16),
        pltpu.VMEM((GROUP, 16, 128), f32),
        pltpu.VMEM((16, 128), f32),
        pltpu.VMEM((8, 128), f32),
        pltpu.VMEM((8, 128), f32),
    )


def rest(length, *arrays):
    tokens = TOKENS
    f32, bf16 = jnp.float32, jnp.bfloat16
    vmem = pl.BlockSpec(memory_space=pltpu.VMEM)
    hbm = pl.BlockSpec(memory_space=pl.ANY)
    shape = jax.ShapeDtypeStruct
    sems = pltpu.SemaphoreType.DMA
    scratch = [
        pltpu.VMEM((4, tokens, HALF), bf16),
        pltpu.VMEM((4, tokens, HALF), bf16),
        pltpu.VMEM((2, 4, 4, CAP, D), bf16),
        pltpu.VMEM((2, 4, 4, CAP, D), bf16),
        pltpu.VMEM((4, tokens, D), bf16),
        pltpu.VMEM((4, tokens, D), bf16),
        pltpu.VMEM((GROUP, 8, 128), f32),
        pltpu.VMEM((GROUP, 8, 128), f32),
        pltpu.VMEM((GROUP, 8, 128), f32),
        pltpu.VMEM((GROUP, 8, 128), f32),
        pltpu.VMEM((tokens, D), f32),
        pltpu.VMEM((EXPERTS, tokens), f32),
        pltpu.VMEM((4, 2, 384, HALF), bf16),
        pltpu.VMEM((2, 384, HALF), bf16),
        pltpu.VMEM((2, 2, 384, HALF), bf16),
        pltpu.VMEM((tokens, D), bf16),
        pltpu.VMEM((tokens, HALF), bf16),
        pltpu.VMEM((tokens, HALF), bf16),
        pltpu.VMEM((2 * D, tokens), bf16),
        pltpu.VMEM((2, HALF, tokens), bf16),
        pltpu.VMEM((4, 4, 32, 3 * D), bf16),
        pltpu.VMEM((4, 32, 3 * D), bf16),
        pltpu.VMEM((PLANES, 32, 3 * D), bf16),
        pltpu.VMEM((GROUP, 16, 128), f32),
        pltpu.VMEM((PLANES, 16, 128), f32),
        pltpu.VMEM((GROUP, 8, 128), f32),
        pltpu.VMEM((PLANES, 8, 128), f32),
        pltpu.VMEM((GROUP, 8, 128), f32),
    ]
    for count in (11, GROUP, 8, 8, 2 * GROUP, 2 * GROUP, 2 * GROUP, 2 * GROUP, 8, 8, 2 * GROUP, 2 * GROUP, 2 * GROUP, 2 * GROUP, 8, 8, 10, 10, 9, 9, 24, 24, 24, 24, 9, 9, 5 * GROUP, 5 * GROUP):
        scratch += [sems((count,))]
    in_specs = [pl.BlockSpec(memory_space=pltpu.SMEM)] + [vmem] * len(arrays)
    for n in (6, 7, 8, 9, 13, 16, 17, 18, 19, 20, 21):
        in_specs[n] = hbm
    return pl.pallas_call(
        rest_kernel,
        out_shape=(
            shape((tokens, D), bf16),
            shape((tokens, D), f32),
            shape((8, 128), f32),
            shape((8, 128), f32),
            shape((GROUP, 8, 128), f32),
            shape((32, 3 * D), f32),
            shape((4, 2, 384, HALF), bf16),
            shape((2, 4, 4, CAP, D), bf16),
            shape((2, 4, 4, CAP, D), bf16),
        ),
        in_specs=in_specs,
        out_specs=[vmem] * 6 + [hbm] * 3,
        scratch_shapes=scratch,
        compiler_params=pltpu.CompilerParams(
            collective_id=2, has_side_effects=True, vmem_limit_bytes=62 << 20
        ),
        name="rest",
    )(length, *arrays)[:7]


def spread_kernel(
    hout_ref,
    hgrad_ref,
    own_ref,
    esum_ref,
    router_ref,
    again_ref,
    mgain_ref,
    hout_out,
    hgrad_out,
    q_out,
    k_out,
    v_out,
    o_out,
    gate_out,
    up_out,
    down_out,
    router_out,
    again_out,
    mgain_out,
):
    f32 = jnp.float32
    hout_out[...] = hout_ref[...]
    hgrad_out[...] = hgrad_ref[...]
    for p in range(2):
        q_out[:, p * HALF : p * HALF + HALF] = own_ref[:, p * D : p * D + HALF]
        k_out[:, p * 256 : p * 256 + 256] = own_ref[:, p * D + HALF : p * D + 768]
        v_out[:, p * 256 : p * 256 + 256] = own_ref[:, p * D + 768 : p * D + D]
    o_out[...] = own_ref[:, 2 * D : 3 * D]
    for h in range(2):
        gate_out[0, 128 * h : 128 * h + 128, :] = esum_ref[0, h, 0:128, :].astype(f32)
        up_out[0, 128 * h : 128 * h + 128, :] = esum_ref[0, h, 128:256, :].astype(f32)
        down_out[0, 64 * h : 64 * h + 64, 0:HALF] = esum_ref[0, h, 256:320, :].astype(f32)
        down_out[0, 64 * h : 64 * h + 64, HALF:D] = esum_ref[0, h, 320:384, :].astype(f32)
    for j in range(8):
        router_out[:, 128 * j : 128 * j + 128] = router_ref[:, j, :]
    again_out[...] = again_ref[...]
    mgain_out[...] = mgain_ref[...]


def spread_out(*arrays):
    f32, bf16 = jnp.float32, jnp.bfloat16
    shape = jax.ShapeDtypeStruct

    def whole(*dims):
        return pl.BlockSpec(dims, lambda i: (0,) * len(dims))

    def rows(count, width):
        return pl.BlockSpec((count, width), lambda i: (i, 0))

    def expert_rows(count, width):
        return pl.BlockSpec((1, count, width), lambda i: (0, i, 0))

    return pl.pallas_call(
        spread_kernel,
        grid=(4,),
        out_shape=(
            shape((TOKENS, D), bf16),
            shape((TOKENS, D), f32),
            shape((32, D), f32),
            shape((32, HALF), f32),
            shape((32, HALF), f32),
            shape((32, D), f32),
            shape((1, D, HALF), f32),
            shape((1, D, HALF), f32),
            shape((1, HALF, D), f32),
            shape((EXPERTS, D), f32),
            shape((8, 128), f32),
            shape((8, 128), f32),
        ),
        in_specs=[
            rows(64, D),
            rows(64, D),
            whole(32, 3 * D),
            pl.BlockSpec((1, 2, 384, HALF), lambda i: (i, 0, 0, 0)),
            whole(GROUP, 8, 128),
            whole(8, 128),
            whole(8, 128),
        ],
        out_specs=[
            rows(64, D),
            rows(64, D),
            whole(32, D),
            whole(32, HALF),
            whole(32, HALF),
            whole(32, D),
            expert_rows(256, HALF),
            expert_rows(256, HALF),
            expert_rows(128, D),
            whole(EXPERTS, D),
            whole(8, 128),
            whole(8, 128),
        ],
        name="spread_out",
    )(*arrays)


def on_device(
    hidden_in,
    cotangent,
    lengths,
    routes,
    priority,
    attn_gain,
    query_weight,
    key_weight,
    value_weight,
    output_weight,
    moe_gain,
    router,
    gate_weight,
    up_weight,
    down_weight,
):
    tok_count = hidden_in.shape[0]
    positions = lax.axis_index("row") * tok_count + jnp.arange(tok_count, dtype=jnp.int32)
    half_dim = HEAD // 2
    frequency = rotary_base ** (-jnp.arange(half_dim, dtype=jnp.float32) / half_dim)
    angles = frequency[:, None] * positions.astype(jnp.float32)[None, :]
    cosine, sine = jnp.cos(angles), jnp.sin(angles)
    router_t = router.T
    (
        weights,
        normed,
        queries,
        keys,
        values,
        log_total,
        mixed_rows,
        middle,
        routed,
        gates,
        pos,
        posz,
        posx,
        arrived_grad,
    ) = front(
        lengths,
        hidden_in,
        cotangent,
        routes.T,
        priority,
        attn_gain[None],
        moe_gain[None],
        query_weight,
        key_weight,
        value_weight,
        output_weight,
        router_t,
        cosine,
        sine,
    )
    summed = rest(
        lengths,
        routed,
        pos,
        posz,
        posx,
        gates,
        arrived_grad,
        gate_weight[0],
        up_weight[0],
        down_weight[0],
        router_t,
        middle,
        cotangent,
        hidden_in,
        attn_gain[None],
        moe_gain[None],
        normed,
        mixed_rows,
        weights,
        queries,
        keys,
        values,
        log_total,
        cosine,
        sine,
    )
    hidden_out, hidden_grad, attn_gain_sum, moe_gain_sum, router_sum, own_rows, expert_sum = summed
    (
        hidden_out,
        hidden_grad,
        query_grad,
        key_grad,
        value_grad,
        output_grad,
        gate_grad,
        up_grad,
        down_grad,
        router_grad,
        attn_gain_sum,
        moe_gain_sum,
    ) = spread_out(
        hidden_out, hidden_grad, own_rows, expert_sum, router_sum, attn_gain_sum, moe_gain_sum
    )
    return (
        hidden_out,
        hidden_grad,
        attn_gain_sum.reshape(D),
        query_grad,
        key_grad,
        value_grad,
        output_grad,
        moe_gain_sum.reshape(D),
        router_grad.T,
        gate_grad,
        up_grad,
        down_grad,
    )


def solution(mesh):
    return jax.shard_map(
        on_device,
        mesh=mesh,
        in_specs=(
            P(("dp", "col", "row"), None),
            P(("dp", "col", "row"), None),
            P(("dp", "col")),
            P(("dp", "col", "row"), None),
            P(("dp", "col", "row"), None),
            P(),
            P(("row", "col"), None),
            P(("row", "col"), None),
            P(("row", "col"), None),
            P(("row", "col"), None),
            P(),
            P(),
            P(("row", "col"), None, None),
            P(("row", "col"), None, None),
            P(("row", "col"), None, None),
        ),
        out_specs=(
            P(("dp", "col", "row"), None),
            P(("dp", "col", "row"), None),
            P(),
            P(("row", "col"), None),
            P(("row", "col"), None),
            P(("row", "col"), None),
            P(("row", "col"), None),
            P(),
            P(),
            P(("row", "col"), None, None),
            P(("row", "col"), None, None),
            P(("row", "col"), None, None),
        ),
        check_vma=False,
    )
```

time: 273 us -> 260 us (0.952)
  Pallas kernels: 263 us -> 257 us
  local copies, waits for them, and re-layouts: 5.82 us -> 0 us
    unnamed x9 -> x0, local copies, waits for them, and re-layouts: 5.06 us -> none
    pallas_call x2 -> x1, Pallas kernels: 181 us -> 176 us  [rest(): pl.pallas_call(rest_kernel, out_shape=(shape((tokens, D), bf16), shape((t...]
where the time goes in v6:
time: 260 us
  Pallas kernels  257 us (99%)
    pallas_call x1, Pallas kernels, rest(): pl.pallas_call(rest_kernel, out_shape=(shape((tokens, D), bf16), shape((t...  176 us
    pallas_call x1, Pallas kernels, front(): pl.pallas_call(front_kernel, out_shape=out_shape, in_specs=[pl.BlockSpec(...  74.7 us
    pallas_call x1, Pallas kernels, spread_out(): pl.pallas_call(spread_kernel, grid=(4,), out_shape=(shape((TOKENS, D), bf...  6.1 us

profile of v6, /device:TPU:1, one launch (start us, length us, event | category | flops | bytes accessed | tf_op | source)
XLA Modules:
  0.0 259.5 jit_solution(8865850430188433251)
XLA Ops:
  1.3 0.8 multiply_sine_fusion
  2.1 74.7 %front.1 = (bf16[2,4,4,32,3072]{4,3,2,1,0:T(8,128)(2,1)}, bf16[256,1024]{1,0:T(8,128)(2,1)}, bf16[1024,256]{1,0:T(8,128)(2,1)}, bf16[512,512]{1,0:T(8,128)(2,1)}...) custom-call(s32[1]{0:T(128)S(6)} %copy.27.length_ref, ...), custom_call_target="tpu_custom_call" | custom-call | tf_op jit(solution)/shard_map/front/pallas_call | solution.py:728
  76.9 176.3 %rest.1 = (bf16[256,1024]{1,0:T(8,128)(2,1)}, f32[256,1024]{1,0:T(8,128)}, f32[8,128]{1,0:T(8,128)}, f32[8,128]{1,0:T(8,128)}, f32[32,8,128]{2,1,0:T(8,128)}, /*...) custom-call(s32[1]{0:T(128)S(6)} %copy.27.length_ref, ...), custom_call_target="tpu_custom_call" | custom-call | tf_op jit(solution)/shard_map/rest/pallas_call | solution.py:1631
  253.2 6.1 %spread_out.1 = (bf16[256,1024]{1,0:T(8,128)(2,1)}, f32[256,1024]{1,0:T(8,128)}, f32[32,1024]{1,0:T(8,128)}, f32[32,512]{1,0:T(8,128)}, f32[32,512]{1,0:T(8,128)...) custom-call(bf16[256,1024]{1,0:T(8,128)(2,1)} %get-tuple-element.59., ...), custom_call_target="tpu_custom_call" | custom-call | tf_op jit(solution)/shard_map/spread_out/pallas_call | solution.py:1707
  (2 shorter events, 0.0 us)

commit v7 on v6

--- a/solution.py
+++ b/solution.py
@@ -60,6 +60,10 @@
     )
 
 
+def done(ref, sem):
+    pltpu.make_async_copy(ref, ref, sem).wait()
+
+
 def meet(plane, planes):
     barrier = pltpu.get_barrier_semaphore()
     y, r, x, z = place()
@@ -131,38 +135,17 @@
     y, r, x, z = place()
     return (
         remote(
-            source.at[:, LEFT], tok_z.at[d], send_sem.at[d], recv_sem.at[d], moved(0, d, r)[0]
+            source.at[:, LEFT], tok_z.at[d], send_sem.at[0], recv_sem.at[0], moved(0, d, r)[0]
         ),
         remote(
-            source.at[:, RIGHT],
-            tok_x.at[d],
-            send_sem.at[4 + d],
-            recv_sem.at[4 + d],
-            moved(d, 0, r)[0],
+            source.at[:, RIGHT], tok_x.at[d], send_sem.at[1], recv_sem.at[1], moved(d, 0, r)[0]
         ),
     )
 
 
-def slot_copies(out, into, core, there, dz, dx, send_sem, recv_sem, sign):
-    y, r, x, z = place()
-    at = there * CHIPS + dz * 4 + dx
-    to = core * CHIPS + dz * 4 + dx
-    return (
-        lambda: remote(
-            out.at[there, dz, dx, :, LEFT],
-            into.at[core, dz, dx, :, LEFT],
-            send_sem.at[at],
-            recv_sem.at[to],
-            moved(sign * dx, 0, there)[0],
-        ),
-        lambda: remote(
-            out.at[there, dz, dx, :, RIGHT],
-            into.at[core, dz, dx, :, RIGHT],
-            send_sem.at[GROUP + at],
-            recv_sem.at[GROUP + to],
-            moved(0, sign * dz, there)[0],
-        ),
-    )
+def spread_done(tok_z, tok_x, sem):
+    done(tok_z.at[pl.ds(1, 3)], sem.at[0])
+    done(tok_x.at[pl.ds(1, 3)], sem.at[1])
 
 
 def is_local(core, offset):
@@ -170,60 +153,29 @@
     return (core == r) & (offset == 0)
 
 
-def send_slots(out, into, there, dz, dx, send_sem, recv_sem, sign, local_sem=None):
+def send_slots(out, into, there, dz, dx, send_sem, recv_left, recv_right, sign, local_sem=None):
     y, r, x, z = place()
 
-    def keep(cols):
+    def one(cols, offset, device, recv_sem):
         source, target = out.at[there, dz, dx, :, cols], into.at[r, dz, dx, :, cols]
-        if local_sem is None:
-            target[...] = source[...]
-        else:
-            copy = pltpu.make_async_copy(source, target, local_sem)
-            copy.start()
-            copy.wait()
-
-    left, right = slot_copies(out, into, r, there, dz, dx, send_sem, recv_sem, sign)
-
-    @pl.when(jnp.logical_not(is_local(there, dx)))
-    def _():
-        left().start()
-
-    @pl.when(is_local(there, dx))
-    def _():
-        keep(LEFT)
-
-    @pl.when(jnp.logical_not(is_local(there, dz)))
-    def _():
-        right().start()
-
-    @pl.when(is_local(there, dz))
-    def _():
-        keep(RIGHT)
-
-
-def slots_arrived(out, into, core, dz, dx, send_sem, recv_sem, left=True, right=True):
-    copies = slot_copies(out, into, core, core, dz, dx, send_sem, recv_sem, 1)
-    for copy, offset, wanted in zip(copies, (dx, dz), (left, right)):
-        if wanted:
-
-            @pl.when(jnp.logical_not(is_local(core, offset)))
-            def _():
-                copy().wait_recv()
-
-
-def block_sent(out, into, there, dz, dx, send_sem, recv_sem):
-    copies = slot_copies(out, into, there, there, dz, dx, send_sem, recv_sem, 1)
-    for copy, offset in zip(copies, (dx, dz)):
 
         @pl.when(jnp.logical_not(is_local(there, offset)))
         def _():
-            copy().wait_send()
-
-
-def slots_sent(out, into, send_sem, recv_sem):
-    @pl.loop(0, GROUP)
-    def _(k):
-        block_sent(out, into, k // CHIPS, lax.rem(k // 4, 4), lax.rem(k, 4), send_sem, recv_sem)
+            remote(source, target, send_sem, recv_sem, device).start()
+
+        @pl.when(is_local(there, offset))
+        def _():
+            if local_sem is None:
+                target[...] = source[...]
+            else:
+                pltpu.make_async_copy(source, target, local_sem).start()
+
+    one(LEFT, dx, moved(sign * dx, 0, there)[0], recv_left)
+    one(RIGHT, dz, moved(0, sign * dz, there)[0], recv_right)
+
+
+def all_slots(ref):
+    return ref.at[:, :, :, :, pl.ds(0, 896)]
 
 
 def line_rows(line, d, axis):
@@ -252,29 +204,19 @@
     y, r, x, z = place()
     return (
         lambda: remote(
-            out.at[d, :, LEFT],
-            into.at[d, :, LEFT],
-            send_sem.at[d],
-            recv_sem.at[d],
-            moved(0, -d, r)[0],
+            out.at[d, :, LEFT], into.at[d, :, LEFT], send_sem, recv_sem, moved(0, -d, r)[0]
         ),
         lambda: remote(
-            out.at[d, :, RIGHT],
-            into.at[d, :, RIGHT],
-            send_sem.at[4 + d],
-            recv_sem.at[4 + d],
-            moved(-d, 0, r)[0],
+            out.at[d, :, RIGHT], into.at[d, :, RIGHT], send_sem, recv_sem, moved(-d, 0, r)[0]
         ),
     )
 
 
-def fold_parts(out, into, mid, slots, slot_send, slot_recv, posz_ref, posx_ref, send_sem, recv_sem):
+def fold_parts(out, into, mid, slot_recv, posz_ref, posx_ref, send_sem, recv_sem):
     @pl.loop(0, 4)
     def _(d):
-        if slots is not None:
-            for core in range(2):
-                for i in range(4):
-                    slots_arrived(slots, mid, core, d, i, slot_send, slot_recv, right=False)
+        if slot_recv is not None:
+            done(mid.at[0, 0, :, :, pl.ds(0, 896)], slot_recv.at[d])
         left = add_up(mid, posz_ref, d, 0)
 
         @pl.when(d == 0)
@@ -286,10 +228,8 @@
             out[d, :, 0:HALF] = left
             part_copies(d, out, into, send_sem, recv_sem)[0]().start()
 
-        if slots is not None:
-            for core in range(2):
-                for i in range(4):
-                    slots_arrived(slots, mid, core, i, d, slot_send, slot_recv, left=False)
+        if slot_recv is not None:
+            done(mid.at[0, 0, :, :, pl.ds(0, 896)], slot_recv.at[4 + d])
         right = add_up(mid, posx_ref, d, 1)
 
         @pl.when(d == 0)
@@ -301,19 +241,6 @@
             out[d, :, HALF:D] = right
             part_copies(d, out, into, send_sem, recv_sem)[1]().start()
 
-
-def parts_arrived(out, into, send_sem, recv_sem):
-    @pl.loop(1, 4)
-    def _(d):
-        for copy in part_copies(d, out, into, send_sem, recv_sem):
-            copy().wait_recv()
-
-
-def parts_sent(out, into, send_sem, recv_sem):
-    @pl.loop(1, 4)
-    def _(d):
-        for copy in part_copies(d, out, into, send_sem, recv_sem):
-            copy().wait_send()
 
 def front_kernel(
     length_ref,
@@ -383,43 +310,45 @@
     def line_step(d):
         mine_q, mine_o = w_ref.at[r, z, x, :, front], w_ref.at[r, z, x, :, rear]
         return (
-            remote(mine_q, mine_q, w_send.at[d], w_recv.at[d], moved(0, d, r)[0]),
-            remote(mine_o, mine_o, w_send.at[4 + d], w_recv.at[4 + d], moved(d, 0, r)[0]),
+            remote(mine_q, mine_q, w_send.at[0], w_recv.at[d], moved(0, d, r)[0]),
+            remote(mine_o, mine_o, w_send.at[0], w_recv.at[4 + d], moved(d, 0, r)[0]),
         )
 
     def cross_step(e, d):
-        at = 8 + 4 * e + d
         from_z = w_ref.at[r, lax.rem(z - e + 4, 4), x, :, front]
         from_x = w_ref.at[r, z, lax.rem(x - e + 4, 4), :, rear]
         return (
-            remote(from_z, from_z, w_send.at[at], w_recv.at[at], moved(d, 0, r)[0]),
-            remote(from_x, from_x, w_send.at[16 + at], w_recv.at[16 + at], moved(0, d, r)[0]),
+            remote(from_z, from_z, w_send.at[1], w_recv.at[8 + d], moved(d, 0, r)[0]),
+            remote(from_x, from_x, w_send.at[1], w_recv.at[8 + d], moved(0, d, r)[0]),
         )
 
     w_ref[r, z, x, :, quarter] = wo_ref[:, pl.ds(pl.multiple_of(256 * y, 256), 256)]
 
     def output_line(d):
         own = w_ref.at[r, z, x, :, quarter]
-        return remote(own, own, o_send.at[d], o_recv.at[d], moved(0, d, r)[0])
+        return remote(own, own, o_send.at[0], o_recv.at[0], moved(0, d, r)[0])
 
     def output_cross(d):
         own = w_ref.at[r, :, x, :, quarter]
-        return remote(own, own, o_send.at[4 + d], o_recv.at[4 + d], moved(d, 0, r)[0])
+        return remote(own, own, o_send.at[1], o_recv.at[1], moved(d, 0, r)[0])
 
     def output_plane(n):
         own = w_ref.at[r, :, :, :, quarter]
-        return remote(own, own, o_send.at[8 + n], o_recv.at[8 + n], plane_shift(n)[0])
+        return remote(own, own, o_send.at[2], o_recv.at[2], plane_shift(n)[0])
 
     def output_core():
         own = w_ref.at[r, :, :, :, output]
-        return remote(own, own, o_send.at[0], o_recv.at[0], sibling)
+        return remote(own, own, o_send.at[3], o_recv.at[3], sibling)
+
+    def some(rows, width):
+        return w_ref.at[0, pl.ds(0, rows), :, :, pl.ds(0, width)]
 
     def core_step(d):
         from_x = w_ref.at[r, :, lax.rem(x - d + 4, 4), :, front]
         from_z = w_ref.at[r, lax.rem(z - d + 4, 4), :, :, rear]
         return (
-            remote(from_x, from_x, core_send.at[d], core_recv.at[d], sibling),
-            remote(from_z, from_z, core_send.at[4 + d], core_recv.at[4 + d], sibling),
+            remote(from_x, from_x, core_send.at[0], core_recv.at[0], sibling),
+            remote(from_z, from_z, core_send.at[0], core_recv.at[0], sibling),
         )
 
     @pl.loop(1, 4)
@@ -484,15 +413,15 @@
             remote(
                 posz_out.at[to_z],
                 posz_ref.at[d],
-                pos_send.at[d],
-                pos_recv.at[d],
+                pos_send.at[0],
+                pos_recv.at[0],
                 moved(0, d, r)[0],
             ),
             remote(
                 posx_out.at[to_x],
                 posx_ref.at[d],
-                pos_send.at[4 + d],
-                pos_recv.at[4 + d],
+                pos_send.at[1],
+                pos_recv.at[1],
                 moved(d, 0, r)[0],
             ),
         )
@@ -502,9 +431,7 @@
         for copy in pos_step(d):
             copy.start()
 
-    @pl.loop(1, 4)
-    def _(d):
-        output_line(d).wait_recv()
+    done(w_ref.at[0, 0, pl.ds(0, 3), :, pl.ds(0, 256)], o_recv.at[0])
 
     @pl.loop(1, 4)
     def _(d):
@@ -532,12 +459,9 @@
     scale = lax.rsqrt(jnp.mean(inputs * inputs, axis=1, keepdims=True) + epsilon)
     normed_ref[...] = (inputs * scale * again_ref[...]).astype(bf16)
 
-    @pl.loop(1, 4)
-    def _(d):
-        for copy in spread(d, cot_ref, tok_z, tok_x, first_send, first_recv):
-            copy.wait_recv()
-        for copy in pos_step(d):
-            copy.wait_recv()
+    spread_done(tok_z, tok_x, first_recv)
+    done(posz_ref.at[pl.ds(1, 3)], pos_recv.at[0])
+    done(posx_ref.at[pl.ds(1, 3)], pos_recv.at[1])
 
     @pl.loop(0, 4)
     def _(d):
@@ -549,20 +473,14 @@
                 outgoing[core, d, i, :, 0:HALF] = left[part]
                 outgoing[core, i, d, :, HALF:D] = right[part]
 
+    done(some(3, 256), o_recv.at[1])
+
+    for n in range(1, PLANES):
+        output_plane(n).start()
+
     @pl.loop(1, 4)
     def _(d):
-        output_cross(d).wait_recv()
-
-    for n in range(1, PLANES):
-        output_plane(n).start()
-
-    @pl.loop(1, 4)
-    def _(d):
-        @pl.loop(0, 4)
-        def _(e):
-            for copy in cross_step(e, d):
-                copy.wait_recv()
-
+        done(some(1, 2 * D), w_recv.at[8 + d])
         for copy in core_step(d):
             copy.start()
 
@@ -572,13 +490,19 @@
         dz = lax.rem(dx + k // 4, 4)
         for core in range(2):
             send_slots(
-                outgoing, grads_ref, core, dz, dx, slot_send, slot_recv, 1, store_sem.at[1]
+                outgoing,
+                grads_ref,
+                core,
+                dz,
+                dx,
+                slot_send.at[0],
+                slot_recv.at[0],
+                slot_recv.at[0],
+                1,
+                store_sem.at[1],
             )
 
-    @pl.loop(0, 4)
-    def _(d):
-        for copy in core_step(d):
-            copy.wait_recv()
+    done(some(4, 2 * D), core_recv.at[0])
 
     cosine, sine = cos_ref[...], sin_ref[...]
     here = pl.ds(pl.multiple_of(r * tokens, tokens), tokens)
@@ -612,8 +536,7 @@
     key_copy.wait_recv()
     value_copy.wait_recv()
 
-    for n in range(1, PLANES):
-        output_plane(n).wait_recv()
+    done(some(4, 768), o_recv.at[2])
     output_core().start()
 
     key_live = lax.broadcasted_iota(jnp.int32, (2 * tokens, 1), 0) < length_ref[0]
@@ -648,46 +571,20 @@
     picked = jnp.exp(logits - jnp.max(logits, axis=0, keepdims=True))
     gates_ref[...] = picked / jnp.sum(picked, axis=0, keepdims=True)
 
-    @pl.loop(0, GROUP)
-    def _(k):
-        slots_arrived(
-            outgoing,
-            grads_ref,
-            k // CHIPS,
-            lax.rem(k // 4, 4),
-            lax.rem(k, 4),
-            slot_send,
-            slot_recv,
-        )
-
-    slots_sent(outgoing, grads_ref, slot_send, slot_recv)
-
-    @pl.loop(1, 4)
-    def _(d):
-        for copies in (
-            line_step(d),
-            core_step(d),
-            pos_step(d),
-            spread(d, cot_ref, tok_z, tok_x, first_send, first_recv),
-        ):
-            for copy in copies:
-                copy.wait_send()
-
-        @pl.loop(0, 4)
-        def _(e):
-            for copy in cross_step(e, d):
-                copy.wait_send()
-
-    @pl.loop(1, 4)
-    def _(d):
-        output_line(d).wait_send()
-        output_cross(d).wait_send()
-        output_plane(d).wait_send()
-
+    done(all_slots(grads_ref), slot_recv.at[0])
+    done(grads_ref.at[0, 0], store_sem.at[1])
+    done(all_slots(outgoing), slot_send.at[0])
+    done(w_ref.at[0, 0, pl.ds(0, 3), :, pl.ds(0, 2 * D)], w_send.at[0])
+    done(some(3, 2 * D), w_send.at[1])
+    done(some(4, 2 * D), core_send.at[0])
+    done(w_ref.at[0, 0, pl.ds(0, 3), :, pl.ds(0, 256)], o_send.at[0])
+    done(some(3, 256), o_send.at[1])
+    done(some(4, 768), o_send.at[2])
     output_core().wait_send()
+    spread_done(tok_z, tok_x, first_send)
+    done(posz_ref.at[pl.ds(1, 3)], pos_send.at[0])
+    done(posx_ref.at[pl.ds(1, 3)], pos_send.at[1])
     weights_out.wait()
-    for copy in core_step(0):
-        copy.wait_send()
     key_copy.wait_send()
     value_copy.wait_send()
 
@@ -723,7 +620,7 @@
         pltpu.VMEM((2, 4, 4, CAP, D), bf16),
     ]
     scratch += [pltpu.SemaphoreType.DMA((2,))]
-    for count in (40, 12, 8, 2, 8, 2 * GROUP, 8):
+    for count in (12, 4, 1, 2, 2, 1, 2):
         scratch += [pltpu.SemaphoreType.DMA((count,))] * 2
     return pl.pallas_call(
         front_kernel,
@@ -790,7 +687,6 @@
     gate_in,
     dot_out,
     dot_in,
-    rg_ref,
     gdot_ref,
     expert_ref,
     relay_in,
@@ -899,14 +795,14 @@
         tok_z[0] = routed_ref[:, 0:HALF]
         tok_x[0] = routed_ref[:, HALF:D]
 
-        def small(k, out, into, sign, base, arriving=False):
+        def small(k, out, into, sign, base):
             there, dz, dx = k // CHIPS, lax.rem(k // 4, 4), lax.rem(k, 4)
-            slot = k if arriving else r * CHIPS + lax.rem(k, CHIPS)
+            slot = r * CHIPS + lax.rem(k, CHIPS)
             return remote(
                 out.at[k],
                 into.at[slot],
-                small_send.at[base + k],
-                small_recv.at[base + slot],
+                small_send.at[base],
+                small_recv.at[base],
                 moved(sign * dx, sign * dz, there)[0],
             )
 
@@ -931,10 +827,7 @@
             def _():
                 small(k, gate_out, gate_in, 1, 0).start()
 
-        @pl.loop(1, 4)
-        def _(d):
-            for copy in spread(d, routed_ref, tok_z, tok_x, first_send, first_recv):
-                copy.wait_recv()
+        spread_done(tok_z, tok_x, first_recv)
 
         @pl.loop(0, 4)
         def _(g):
@@ -952,30 +845,41 @@
                     part = slice(core * CAP, core * CAP + CAP)
                     outgoing[core, dz, dx, :, 0:HALF] = left[part].astype(bf16)
                     outgoing[core, dz, dx, :, HALF:D] = right[part].astype(bf16)
-                    send_slots(outgoing, arrived, core, dz, dx, slot_send, slot_recv, 1)
+                    came = slot_recv.at[2 * g + r]
+                    send_slots(outgoing, arrived, core, dz, dx, slot_send.at[g], came, came, 1)
 
         def keep_produced(k):
             core, dz, dx = k // CHIPS, lax.rem(k // 4, 4), lax.rem(k, 4)
             return pltpu.make_async_copy(
-                grads_ref.at[core, dz, dx], prod_hbm.at[core, dz, dx], store_sem.at[k]
+                grads_ref.at[core, dz, dx],
+                prod_hbm.at[core, dz, dx],
+                store_sem.at[lax.rem(dz - dx + 4, 4)],
             )
 
         for load in loads:
             load.wait()
+        done(gate_in.at[pl.ds(0, GROUP - 1)], small_recv.at[0])
 
         @pl.loop(0, 8)
         def _(c):
             g, core = c // 2, lax.rem(c, 2)
+
+            @pl.when(core == r)
+            def _():
+                done(arrived.at[0, 0, pl.ds(0, 3)], slot_recv.at[c])
+
+            @pl.when(core != r)
+            def _():
+                done(arrived.at[0, 0], slot_recv.at[c])
+
+            @pl.when(core == 0)
+            def _():
+                done(outgoing.at[0, pl.ds(0, 2), :, :, pl.ds(0, 896)], slot_send.at[g])
+
             rows, gate_cols, grads = [], [], []
             for dx in range(4):
                 dz = lax.rem(dx + g, 4)
                 k = core * CHIPS + dz * 4 + dx
-                slots_arrived(outgoing, arrived, core, dz, dx, slot_send, slot_recv)
-
-                @pl.when(jnp.logical_not(own_slot(k)))
-                def _():
-                    small(k, gate_out, gate_in, 1, 0, True).wait_recv()
-
                 rows.append(arrived[core, dz, dx])
                 gate_cols.append(as_column(gate_in[k, 0:1, 0:CAP]))
                 grads.append(grads_ref[core, dz, dx])
@@ -1002,9 +906,18 @@
                 dz = lax.rem(dx + g, 4)
                 k = core * CHIPS + dz * 4 + dx
                 part = slice(dx * CAP, dx * CAP + CAP)
-                block_sent(outgoing, arrived, core, dz, dx, slot_send, slot_recv)
                 outgoing[core, dz, dx] = row_grads[part]
-                send_slots(outgoing, mid, core, dz, dx, back_send, back_recv, -1)
+                send_slots(
+                    outgoing,
+                    mid,
+                    core,
+                    dz,
+                    dx,
+                    back_send.at[0],
+                    back_recv.at[dz],
+                    back_recv.at[4 + dx],
+                    -1,
+                )
                 dot_out[k, 0:1, 0:CAP] = as_row(dots[part])
 
                 @pl.when(own_slot(k))
@@ -1013,7 +926,7 @@
 
                 @pl.when(jnp.logical_not(own_slot(k)))
                 def _():
-                    small(k, dot_out, dot_in, -1, GROUP).start()
+                    small(k, dot_out, dot_in, -1, 1).start()
 
                 grads_ref[core, dz, dx] = produced[part]
                 keep_produced(k).start()
@@ -1023,11 +936,22 @@
                 pre_grads[core, dz, dx, :, HALF:D] = up_grad[part]
 
         def send_results(g):
+            done(prod_hbm.at[0, pl.ds(0, 2)], store_sem.at[g])
             for dx in range(4):
-                dz = (dx + g) % 4
+                dz = lax.rem(dx + g, 4)
                 for core in range(2):
-                    keep_produced(core * CHIPS + dz * 4 + dx).wait()
-                    send_slots(prod_hbm, mid_hbm, core, dz, dx, c_send, c_recv, -1, load_sem.at[4])
+                    send_slots(
+                        prod_hbm,
+                        mid_hbm,
+                        core,
+                        dz,
+                        dx,
+                        c_send.at[0],
+                        c_recv.at[0],
+                        c_recv.at[0],
+                        -1,
+                        load_sem.at[8],
+                    )
 
         send_results(0)
 
@@ -1056,16 +980,13 @@
             parts_out,
             parts_in,
             mid,
-            outgoing,
-            back_send,
             back_recv,
             posz_ref,
             posx_ref,
-            part_send,
-            part_recv,
+            part_send.at[0],
+            part_recv.at[0],
         )
-        for g in range(1, 4):
-            send_results(g)
+        pl.loop(1, 4)(send_results)
 
         @pl.loop(1, 4)
         def _(slot):
@@ -1074,12 +995,10 @@
         for n in range(2):
             direct(n).start()
 
+        done(dot_in.at[pl.ds(0, GROUP - 1)], small_recv.at[1])
+
         @pl.loop(0, GROUP)
         def _(k):
-            @pl.when(jnp.logical_not(own_slot(k)))
-            def _():
-                small(k, dot_out, dot_in, -1, GROUP, True).wait_recv()
-
             there, dz, dx = k // CHIPS, lax.rem(k // 4, 4), lax.rem(k, 4)
             _, expert = moved(dx, dz, there)
             at = pl.ds(expert, 1)
@@ -1088,24 +1007,15 @@
                 jnp.where(picks(pos_ref[at, :]), dots, 0.0), axis=0, keepdims=True
             )
 
-        parts_arrived(parts_out, parts_in, part_send, part_recv)
-        rg_ref[...] = (parts_in[0].astype(f32) + parts_in[1].astype(f32)) + (
+        done(parts_in.at[pl.ds(1, 3)], part_recv.at[0])
+        hgrad_ref[...] = (parts_in[0].astype(f32) + parts_in[1].astype(f32)) + (
             parts_in[2].astype(f32) + parts_in[3].astype(f32)
         )
-        slots_sent(outgoing, mid, back_send, back_recv)
-        parts_sent(parts_out, parts_in, part_send, part_recv)
-
-        @pl.loop(1, 4)
-        def _(d):
-            for copy in spread(d, routed_ref, tok_z, tok_x, first_send, first_recv):
-                copy.wait_send()
-
-        @pl.loop(0, GROUP)
-        def _(k):
-            @pl.when(jnp.logical_not(own_slot(k)))
-            def _():
-                small(k, gate_out, gate_in, 1, 0).wait_send()
-                small(k, dot_out, dot_in, -1, GROUP).wait_send()
+        done(all_slots(outgoing), back_send.at[0])
+        done(parts_out.at[pl.ds(1, 3)], part_send.at[0])
+        spread_done(tok_z, tok_x, first_send)
+        done(gate_in.at[pl.ds(0, GROUP - 1)], small_send.at[0])
+        done(dot_in.at[pl.ds(0, GROUP - 1)], small_send.at[1])
 
     pl.run_scoped(
         expert_phase,
@@ -1176,7 +1086,7 @@
         router_part = router_part + dot(rest, routed_ref[...], ((1,), (0,)))
         routed_grad = dot(high, router_ref[...], ((0,), (0,)))
         routed_grad = routed_grad + dot(rest, router_ref[...], ((0,), (0,)))
-        routed_grad = routed_grad + rg_ref[...]
+        routed_grad = routed_grad + hgrad_ref[...]
         live = (
             r * tokens + lax.broadcasted_iota(jnp.int32, (tokens, 1), 0) < length_ref[0]
         ).astype(f32)
@@ -1197,7 +1107,7 @@
 
         def tiny(k):
             device, other = step_of(k, 1)
-            return remote(small_out.at[other], small_in.at[me], sm_send.at[k], sm_recv.at[k], device)
+            return remote(small_out.at[other], small_in.at[me], sm_send.at[0], sm_recv.at[0], device)
 
         @pl.loop(1, GROUP)
         def _(k):
@@ -1216,52 +1126,49 @@
 
         def first_step(p, d):
             left, right = columns(p)
-            at = 8 * p + d
             return (
                 remote(
                     weight_part.at[lax.rem(z + d, 4), :, :, left],
                     rs_in.at[d, :, :, left],
-                    rs_send.at[at],
-                    rs_recv.at[at],
+                    rs_send.at[p],
+                    rs_recv.at[p],
                     moved(0, d, r)[0],
                 ),
                 remote(
                     weight_part.at[:, lax.rem(x + d, 4), :, right],
                     rs_in.at[d, :, :, right],
-                    rs_send.at[4 + at],
-                    rs_recv.at[4 + at],
+                    rs_send.at[p],
+                    rs_recv.at[p],
                     moved(d, 0, r)[0],
                 ),
             )
 
         def second_step(p, d):
             left, right = columns(p)
-            at = 8 * p + d
             return (
                 remote(
                     rs_out.at[lax.rem(x + d, 4), :, left],
                     rs_in2.at[d, :, left],
-                    rs_send2.at[at],
-                    rs_recv2.at[at],
+                    rs_send2.at[p],
+                    rs_recv2.at[p],
                     moved(d, 0, r)[0],
                 ),
                 remote(
                     rs_out.at[lax.rem(z + d, 4), :, right],
                     rs_in2.at[d, :, right],
-                    rs_send2.at[4 + at],
-                    rs_recv2.at[4 + at],
+                    rs_send2.at[p],
+                    rs_recv2.at[p],
                     moved(0, d, r)[0],
                 ),
             )
 
         def across(p, n):
             cols = pl.ds(p * D, D)
-            at = 3 * p + n - 1
             return remote(
                 y_out.at[:, cols],
                 y_parts.at[y, :, cols],
-                ys_send.at[at],
-                ys_recv.at[at],
+                ys_send.at[p],
+                ys_recv.at[p],
                 plane_shift(n)[0],
             )
 
@@ -1276,10 +1183,7 @@
         def sum_second(p):
             left, right = columns(p)
 
-            @pl.loop(1, 4)
-            def _(d):
-                for copy in first_step(p, d):
-                    copy.wait_recv()
+            done(rs_in.at[pl.ds(1, 3), :, :, pl.ds(p * D, D)], rs_recv.at[p])
 
             total = weight_part[z, :, :, left].astype(f32)
             other = weight_part[:, x, :, right].astype(f32)
@@ -1297,10 +1201,7 @@
         def sum_third(p):
             left, right = columns(p)
 
-            @pl.loop(1, 4)
-            def _(d):
-                for copy in second_step(p, d):
-                    copy.wait_recv()
+            done(rs_in2.at[pl.ds(1, 3), :, pl.ds(p * D, D)], rs_recv2.at[p])
 
             total = rs_out[x, :, left].astype(f32)
             other = rs_out[z, :, right].astype(f32)
@@ -1402,8 +1303,7 @@
 
         def gain(k):
             device, _ = step_of(k, 1)
-            at = 3 * GROUP + k
-            return remote(gain_out, gain_in.at[me], sm_send.at[at], sm_recv.at[at], device)
+            return remote(gain_out, gain_in.at[me], sm_send.at[3], sm_recv.at[3], device)
 
         @pl.loop(1, GROUP)
         def _(k):
@@ -1427,14 +1327,12 @@
 
         sum_second(2)
 
-        @pl.loop(1, GROUP)
-        def _(k):
-            tiny(k).wait_recv()
+        done(small_in.at[pl.ds(0, GROUP - 1)], sm_recv.at[0])
 
         def small_across(n):
             device, _ = plane_shift(n)
             return remote(
-                small_y, small_y_in.at[y], sm_send.at[GROUP + n], sm_recv.at[GROUP + n], device
+                small_y, small_y_in.at[y], sm_send.at[1], sm_recv.at[1], device
             )
 
         small_y[...] = jnp.sum(small_in[...], axis=0)
@@ -1442,12 +1340,8 @@
         for n in range(1, PLANES):
             small_across(n).start()
 
-        @pl.loop(0, GROUP)
-        def _(k):
-            slots_arrived(
-                prod_hbm, mid_hbm, k // CHIPS, lax.rem(k // 4, 4), lax.rem(k, 4), c_send, c_recv
-            )
-
+        done(all_slots(mid_hbm), c_recv.at[0])
+        done(mid_hbm.at[0, 0], load_sem.at[8])
         results_in = pltpu.make_async_copy(mid_hbm, mid, load_sem.at[10])
         results_in.start()
         results_in.wait()
@@ -1456,44 +1350,37 @@
             parts_in2,
             mid,
             None,
-            c_send,
-            c_recv,
             posz_ref,
             posx_ref,
-            part_send2,
-            part_recv2,
+            part_send2.at[0],
+            part_recv2.at[0],
         )
         sum_third(2)
         sum_second(0)
 
-        for n in range(1, PLANES):
-            small_across(n).wait_recv()
+        done(small_y_in.at[pl.ds(0, 3)], sm_recv.at[1])
         totals = small_y_in[0] + small_y_in[1] + small_y_in[2] + small_y_in[3]
         mgain_out[...] = totals[8:16]
         router_all[me] = totals[0:8]
 
         def router_row(k):
             device, _ = step_of(k, 1)
-            at = 2 * GROUP + k
             return remote(
-                router_all.at[me], router_all.at[me], sm_send.at[at], sm_recv.at[at], device
+                router_all.at[me], router_all.at[me], sm_send.at[2], sm_recv.at[2], device
             )
 
         @pl.loop(1, GROUP)
         def _(k):
             router_row(k).start()
 
-        @pl.loop(1, GROUP)
-        def _(k):
-            gain(k).wait_recv()
+        done(gain_in.at[pl.ds(0, GROUP - 1)], sm_recv.at[3])
 
         gain_y[...] = jnp.sum(gain_in[...], axis=0)
         gain_y_in[y] = gain_y[...]
 
         def gain_across(n):
             device, _ = plane_shift(n)
-            at = 4 * GROUP + n
-            return remote(gain_y, gain_y_in.at[y], sm_send.at[at], sm_recv.at[at], device)
+            return remote(gain_y, gain_y_in.at[y], sm_send.at[4], sm_recv.at[4], device)
 
         for n in range(1, PLANES):
             gain_across(n).start()
@@ -1507,37 +1394,31 @@
 
         sum_third(1)
 
-        parts_arrived(parts_out2, parts_in2, part_send2, part_recv2)
+        done(parts_in2.at[pl.ds(1, 3)], part_recv2.at[0])
         mixture = (parts_in2[0].astype(f32) + parts_in2[1].astype(f32)) + (
             parts_in2[2].astype(f32) + parts_in2[3].astype(f32)
         )
         hout_ref[...] = ((middle_ref[...] + mixture) * live).astype(bf16)
 
-        for n in range(1, PLANES):
-            gain_across(n).wait_recv()
+        done(gain_y_in.at[pl.ds(0, 3)], sm_recv.at[4])
         again_out[...] = (gain_y_in[0] + gain_y_in[1]) + (gain_y_in[2] + gain_y_in[3])
 
-        @pl.loop(1, GROUP)
-        def _(k):
-            router_row(k).wait_recv()
+        done(router_all.at[pl.ds(0, GROUP - 1)], sm_recv.at[2])
 
         router_out[...] = router_all[...]
 
-        slots_sent(prod_hbm, mid_hbm, c_send, c_recv)
-        parts_sent(parts_out2, parts_in2, part_send2, part_recv2)
-
-        @pl.loop(1, GROUP)
-        def _(k):
-            tiny(k).wait_send()
-            router_row(k).wait_send()
-            gain(k).wait_send()
-
-        @pl.loop(1, 4)
-        def _(d):
-            for p in range(3):
-                for copy in first_step(p, d) + second_step(p, d):
-                    copy.wait_send()
-
+        done(all_slots(mid_hbm), c_send.at[0])
+        done(parts_out2.at[pl.ds(1, 3)], part_send2.at[0])
+        done(small_in.at[pl.ds(0, GROUP - 1)], sm_send.at[0])
+        done(small_y_in.at[pl.ds(0, 3)], sm_send.at[1])
+        done(router_all.at[pl.ds(0, GROUP - 1)], sm_send.at[2])
+        done(gain_in.at[pl.ds(0, GROUP - 1)], sm_send.at[3])
+        done(gain_y_in.at[pl.ds(0, 3)], sm_send.at[4])
+        for p in range(3):
+            done(rs_in.at[pl.ds(1, 3), :, :, pl.ds(p * D, D)], rs_send.at[p])
+            done(rs_in2.at[pl.ds(1, 3), :, pl.ds(p * D, D)], rs_send2.at[p])
+            done(y_parts.at[pl.ds(0, 3), :, pl.ds(p * D, D)], ys_recv.at[p])
+            done(y_parts.at[pl.ds(0, 3), :, pl.ds(p * D, D)], ys_send.at[p])
         for n in range(2):
             for copy in (relayed(n), direct(n), merged(n), handed(n), passed_on(n)):
                 copy.wait_send()
@@ -1547,11 +1428,6 @@
             sib_keyval(p).wait_send()
             for part in range(2):
                 sib_grads(p, part).wait_send()
-        for n in range(1, PLANES):
-            small_across(n).wait_send()
-            gain_across(n).wait_send()
-            for p in range(3):
-                across(p, n).wait()
         for n in range(2):
             passed_on(n).wait_recv()
         quarter_out.wait()
@@ -1604,7 +1480,6 @@
         pltpu.VMEM((GROUP, 8, 128), f32),
         pltpu.VMEM((GROUP, 8, 128), f32),
         pltpu.VMEM((GROUP, 8, 128), f32),
-        pltpu.VMEM((tokens, D), f32),
         pltpu.VMEM((EXPERTS, tokens), f32),
         pltpu.VMEM((4, 2, 384, HALF), bf16),
         pltpu.VMEM((2, 384, HALF), bf16),
@@ -1623,7 +1498,7 @@
         pltpu.VMEM((PLANES, 8, 128), f32),
         pltpu.VMEM((GROUP, 8, 128), f32),
     ]
-    for count in (11, GROUP, 8, 8, 2 * GROUP, 2 * GROUP, 2 * GROUP, 2 * GROUP, 8, 8, 2 * GROUP, 2 * GROUP, 2 * GROUP, 2 * GROUP, 8, 8, 10, 10, 9, 9, 24, 24, 24, 24, 9, 9, 5 * GROUP, 5 * GROUP):
+    for count in (11, 4, 2, 2, 4, 8, 1, 8, 1, 1, 2, 2, 1, 1, 1, 1, 10, 10, 9, 9, 3, 3, 3, 3, 3, 3, 5, 5):
         scratch += [sems((count,))]
     in_specs = [pl.BlockSpec(memory_space=pltpu.SMEM)] + [vmem] * len(arrays)
     for n in (6, 7, 8, 9, 13, 16, 17, 18, 19, 20, 21):

time: 260 us -> 237 us (0.912)
  Pallas kernels: 257 us -> 234 us
    pallas_call x1, Pallas kernels: 176 us -> 158 us  [rest(): pl.pallas_call(rest_kernel, out_shape=(shape((tokens, D), bf16), shape((t...]
    pallas_call x1, Pallas kernels: 74.7 us -> 70 us  [front(): pl.pallas_call(front_kernel, out_shape=out_shape, in_specs=[pl.BlockSpec(...]
where the time goes in v7:
time: 237 us
  Pallas kernels  234 us (99%)
    pallas_call x1, Pallas kernels, rest(): pl.pallas_call(rest_kernel, out_shape=(shape((tokens, D), bf16), shape((t...  158 us
    pallas_call x1, Pallas kernels, front(): pl.pallas_call(front_kernel, out_shape=out_shape, in_specs=[pl.BlockSpec(...  70 us
    pallas_call x1, Pallas kernels, spread_out(): pl.pallas_call(spread_kernel, grid=(4,), out_shape=(shape((TOKENS, D), bf...  6.1 us

profile of v7, /device:TPU:1, one launch (start us, length us, event | category | flops | bytes accessed | tf_op | source)
XLA Modules:
  0.0 236.6 jit_solution(13549726841438607845)
XLA Ops:
  1.3 0.8 multiply_sine_fusion
  2.1 70.0 %front.1 = (bf16[2,4,4,32,3072]{4,3,2,1,0:T(8,128)(2,1)}, bf16[256,1024]{1,0:T(8,128)(2,1)}, bf16[1024,256]{1,0:T(8,128)(2,1)}, bf16[512,512]{1,0:T(8,128)(2,1)}...) custom-call(s32[1]{0:T(128)S(6)} %copy.27.length_ref, ...), custom_call_target="tpu_custom_call" | custom-call | tf_op jit(solution)/shard_map/front/pallas_call | solution.py:625
  72.2 158.2 %rest.1 = (bf16[256,1024]{1,0:T(8,128)(2,1)}, f32[256,1024]{1,0:T(8,128)}, f32[8,128]{1,0:T(8,128)}, f32[8,128]{1,0:T(8,128)}, f32[32,8,128]{2,1,0:T(8,128)}, /*...) custom-call(s32[1]{0:T(128)S(6)} %copy.27.length_ref, ...), custom_call_target="tpu_custom_call" | custom-call | tf_op jit(solution)/shard_map/rest/pallas_call | solution.py:1506
  230.4 6.1 %spread_out.1 = (bf16[256,1024]{1,0:T(8,128)(2,1)}, f32[256,1024]{1,0:T(8,128)}, f32[32,1024]{1,0:T(8,128)}, f32[32,512]{1,0:T(8,128)}, f32[32,512]{1,0:T(8,128)...) custom-call(bf16[256,1024]{1,0:T(8,128)(2,1)} %get-tuple-element.59., ...), custom_call_target="tpu_custom_call" | custom-call | tf_op jit(solution)/shard_map/spread_out/pallas_call | solution.py:1582
  (2 shorter events, 0.0 us)

commit v8 on v7

--- a/solution.py
+++ b/solution.py
@@ -153,7 +153,19 @@
     return (core == r) & (offset == 0)
 
 
-def send_slots(out, into, there, dz, dx, send_sem, recv_left, recv_right, sign, local_sem=None):
+def send_slots(
+    out,
+    into,
+    there,
+    dz,
+    dx,
+    send_sem,
+    recv_left,
+    recv_right,
+    sign,
+    local_sem=None,
+    halves=(True, True),
+):
     y, r, x, z = place()
 
     def one(cols, offset, device, recv_sem):
@@ -170,8 +182,10 @@
             else:
                 pltpu.make_async_copy(source, target, local_sem).start()
 
-    one(LEFT, dx, moved(sign * dx, 0, there)[0], recv_left)
-    one(RIGHT, dz, moved(0, sign * dz, there)[0], recv_right)
+    if halves[0]:
+        one(LEFT, dx, moved(sign * dx, 0, there)[0], recv_left)
+    if halves[1]:
+        one(RIGHT, dz, moved(0, sign * dz, there)[0], recv_right)
 
 
 def all_slots(ref):
@@ -212,7 +226,7 @@
     )
 
 
-def fold_parts(out, into, mid, slot_recv, posz_ref, posx_ref, send_sem, recv_sem):
+def fold_left(out, into, mid, slot_recv, posz_ref, send_sem, recv_sem):
     @pl.loop(0, 4)
     def _(d):
         if slot_recv is not None:
@@ -228,6 +242,10 @@
             out[d, :, 0:HALF] = left
             part_copies(d, out, into, send_sem, recv_sem)[0]().start()
 
+
+def fold_right(out, into, mid, slot_recv, posx_ref, send_sem, recv_sem):
+    @pl.loop(0, 4)
+    def _(d):
         if slot_recv is not None:
             done(mid.at[0, 0, :, :, pl.ds(0, 896)], slot_recv.at[4 + d])
         right = add_up(mid, posx_ref, d, 1)
@@ -455,23 +473,23 @@
     for copy in core_step(0):
         copy.start()
 
-    inputs = hidden_ref[...].astype(f32)
-    scale = lax.rsqrt(jnp.mean(inputs * inputs, axis=1, keepdims=True) + epsilon)
-    normed_ref[...] = (inputs * scale * again_ref[...]).astype(bf16)
-
-    spread_done(tok_z, tok_x, first_recv)
-    done(posz_ref.at[pl.ds(1, 3)], pos_recv.at[0])
-    done(posx_ref.at[pl.ds(1, 3)], pos_recv.at[1])
-
-    @pl.loop(0, 4)
-    def _(d):
+    def cut_slots(d):
         left = dot(line_hot(posz_ref, d, 0), tok_z[d], ((1,), (0,))).astype(bf16)
         right = dot(line_hot(posx_ref, d, 1), tok_x[d], ((1,), (0,))).astype(bf16)
+        sems = slot_send.at[0], slot_recv.at[0], slot_recv.at[0], 1, store_sem.at[1]
         for core in range(2):
             for i in range(4):
                 part = slice((core * 4 + i) * CAP, (core * 4 + i + 1) * CAP)
                 outgoing[core, d, i, :, 0:HALF] = left[part]
+                send_slots(outgoing, grads_ref, core, d, i, *sems, (True, False))
                 outgoing[core, i, d, :, HALF:D] = right[part]
+                send_slots(outgoing, grads_ref, core, i, d, *sems, (False, True))
+
+    cut_slots(0)
+
+    inputs = hidden_ref[...].astype(f32)
+    scale = lax.rsqrt(jnp.mean(inputs * inputs, axis=1, keepdims=True) + epsilon)
+    normed_ref[...] = (inputs * scale * again_ref[...]).astype(bf16)
 
     done(some(3, 256), o_recv.at[1])
 
@@ -483,24 +501,6 @@
         done(some(1, 2 * D), w_recv.at[8 + d])
         for copy in core_step(d):
             copy.start()
-
-    @pl.loop(0, CHIPS)
-    def _(k):
-        dx = lax.rem(k, 4)
-        dz = lax.rem(dx + k // 4, 4)
-        for core in range(2):
-            send_slots(
-                outgoing,
-                grads_ref,
-                core,
-                dz,
-                dx,
-                slot_send.at[0],
-                slot_recv.at[0],
-                slot_recv.at[0],
-                1,
-                store_sem.at[1],
-            )
 
     done(some(4, 2 * D), core_recv.at[0])
 
@@ -532,6 +532,11 @@
     value_copy.start()
     for p in range(2):
         q_ref[HALF * p : HALF * p + HALF, :] = turned(projected(D * p))
+
+    spread_done(tok_z, tok_x, first_recv)
+    done(posz_ref.at[pl.ds(1, 3)], pos_recv.at[0])
+    done(posx_ref.at[pl.ds(1, 3)], pos_recv.at[1])
+    pl.loop(1, 4)(cut_slots)
 
     key_copy.wait_recv()
     value_copy.wait_recv()
@@ -795,6 +800,21 @@
         tok_z[0] = routed_ref[:, 0:HALF]
         tok_x[0] = routed_ref[:, HALF:D]
 
+        def send_rows(core, dz, dx, g, halves):
+            came = slot_recv.at[2 * g + r]
+            sems = slot_send.at[g], came, came, 1, None
+            send_slots(outgoing, arrived, core, dz, dx, *sems, halves)
+
+        left = dot(line_hot(posz_ref, 0, 0), tok_z[0], ((1,), (0,))).astype(bf16)
+        right = dot(line_hot(posx_ref, 0, 1), tok_x[0], ((1,), (0,))).astype(bf16)
+        for core in range(2):
+            for i in range(4):
+                part = slice((core * 4 + i) * CAP, (core * 4 + i + 1) * CAP)
+                outgoing[core, 0, i, :, 0:HALF] = left[part]
+                send_rows(core, 0, i, (4 - i) % 4, (True, False))
+                outgoing[core, i, 0, :, HALF:D] = right[part]
+                send_rows(core, i, 0, i, (False, True))
+
         def small(k, out, into, sign, base):
             there, dz, dx = k // CHIPS, lax.rem(k // 4, 4), lax.rem(k, 4)
             slot = r * CHIPS + lax.rem(k, CHIPS)
@@ -833,20 +853,30 @@
         def _(g):
             for dx in range(4):
                 dz = lax.rem(dx + g, 4)
-                left_rows, right_rows = [], []
-                for core in range(2):
-                    at_x = core * 4 + lax.rem(x + dx, 4)
-                    at_z = core * 4 + lax.rem(z + dz, 4)
-                    left_rows.append(picks(posz_ref[dz, pl.ds(at_x, 1), :]))
-                    right_rows.append(picks(posx_ref[dx, pl.ds(at_z, 1), :]))
-                left = dot(as_hot(jnp.concatenate(left_rows, axis=0)), tok_z[dz], ((1,), (0,)))
-                right = dot(as_hot(jnp.concatenate(right_rows, axis=0)), tok_x[dx], ((1,), (0,)))
+
+                @pl.when(dz != 0)
+                def _():
+                    rows = [
+                        picks(posz_ref[dz, pl.ds(core * 4 + lax.rem(x + dx, 4), 1), :])
+                        for core in range(2)
+                    ]
+                    rows = dot(as_hot(jnp.concatenate(rows, axis=0)), tok_z[dz], ((1,), (0,)))
+                    for core in range(2):
+                        part = slice(core * CAP, core * CAP + CAP)
+                        outgoing[core, dz, dx, :, 0:HALF] = rows[part].astype(bf16)
+                        send_rows(core, dz, dx, g, (True, False))
+
+                if dx == 0:
+                    continue
+                rows = [
+                    picks(posx_ref[dx, pl.ds(core * 4 + lax.rem(z + dz, 4), 1), :])
+                    for core in range(2)
+                ]
+                rows = dot(as_hot(jnp.concatenate(rows, axis=0)), tok_x[dx], ((1,), (0,)))
                 for core in range(2):
                     part = slice(core * CAP, core * CAP + CAP)
-                    outgoing[core, dz, dx, :, 0:HALF] = left[part].astype(bf16)
-                    outgoing[core, dz, dx, :, HALF:D] = right[part].astype(bf16)
-                    came = slot_recv.at[2 * g + r]
-                    send_slots(outgoing, arrived, core, dz, dx, slot_send.at[g], came, came, 1)
+                    outgoing[core, dz, dx, :, HALF:D] = rows[part].astype(bf16)
+                    send_rows(core, dz, dx, g, (False, True))
 
         def keep_produced(k):
             core, dz, dx = k // CHIPS, lax.rem(k // 4, 4), lax.rem(k, 4)
@@ -976,16 +1006,9 @@
         for n in range(2):
             relayed(n).start()
 
-        fold_parts(
-            parts_out,
-            parts_in,
-            mid,
-            back_recv,
-            posz_ref,
-            posx_ref,
-            part_send.at[0],
-            part_recv.at[0],
-        )
+        sends = part_send.at[0], part_recv.at[0]
+        fold_left(parts_out, parts_in, mid, back_recv, posz_ref, *sends)
+        fold_right(parts_out, parts_in, mid, back_recv, posx_ref, *sends)
         pl.loop(1, 4)(send_results)
 
         @pl.loop(1, 4)
@@ -1036,11 +1059,11 @@
             for n, (source, target) in enumerate(
                 (
                     (w_hbm, w_ref),
+                    (mixed_hbm, mixed_ref),
                     (q_hbm, q_ref),
                     (k_hbm, k_ref),
                     (v_hbm, v_ref),
                     (normed_hbm, normed_ref),
-                    (mixed_hbm, mixed_ref),
                     (hidden_hbm, hidden_ref),
                 )
             )
@@ -1115,8 +1138,7 @@
 
         small_in[me] = small_out[me]
 
-        for load in loads:
-            load.wait()
+        loads[0].wait()
         mg_t[...] = dot(weight(2 * D, D), branch_own[...], ((1,), (1,))).astype(bf16)
 
         mine = pl.ds(pl.multiple_of(r * HALF, HALF), HALF)
@@ -1217,6 +1239,7 @@
 
         sib_mixed.wait_recv()
         sib_branch.wait_recv()
+        loads[1].wait()
         total = dot(mixed_ref[:, mine], branch_own[...], ((0,), (0,)))
         sum_first(2, total + dot(mixed_sib[...], branch_sib[...], ((0,), (0,))))
 
@@ -1279,6 +1302,8 @@
         def inputs_part(p):
             return dot(grad_t[p * D : p * D + D, :], weight(p * D, D), ((0,), (1,)))
 
+        for load in loads[2:5]:
+            load.wait()
         heads(0, 0, 4)
         sib_keyval(0).start()
         sib_grads(0, 0).start()
@@ -1286,34 +1311,6 @@
         heads(1, 0, 4)
         sib_keyval(1).start()
         sib_grads(1, 0).start()
-        whole_keyval(0)
-        sib_normed.wait_recv()
-        projections(0)
-        whole_keyval(1)
-        normed_grad = inputs_part(0)
-        projections(1)
-        normed_grad = normed_grad + inputs_part(1)
-
-        inputs = hidden_ref[...].astype(f32)
-        scale = lax.rsqrt(jnp.mean(inputs * inputs, axis=1, keepdims=True) + epsilon)
-        rows = inputs * scale
-        attn_part = jnp.sum(normed_grad * rows, axis=0, keepdims=True)
-        for j in range(8):
-            gain_out[j : j + 1, :] = attn_part[:, 128 * j : 128 * j + 128]
-
-        def gain(k):
-            device, _ = step_of(k, 1)
-            return remote(gain_out, gain_in.at[me], sm_send.at[3], sm_recv.at[3], device)
-
-        @pl.loop(1, GROUP)
-        def _(k):
-            gain(k).start()
-
-        gain_in[me] = gain_out[...]
-        scaled = normed_grad * again_ref[...]
-        inner = jnp.mean(scaled * rows, axis=1, keepdims=True)
-        hgrad_ref[...] += scale * (scaled - rows * inner)
-
         for n in range(2):
             direct(n).wait_recv()
             merged(n).wait_recv()
@@ -1325,8 +1322,41 @@
         for n in range(2):
             handed(n).start()
 
+        whole_keyval(0)
+        for load in loads[5:]:
+            load.wait()
+        sib_normed.wait_recv()
+        projections(0)
+        done(all_slots(mid_hbm), c_recv.at[0])
+        done(mid_hbm.at[0, 0], load_sem.at[8])
+        results_in = pltpu.make_async_copy(mid_hbm, mid, load_sem.at[10])
+        results_in.start()
+        whole_keyval(1)
+        normed_grad = inputs_part(0)
+        projections(1)
+        normed_grad = normed_grad + inputs_part(1)
+
+        inputs = hidden_ref[...].astype(f32)
+        scale = lax.rsqrt(jnp.mean(inputs * inputs, axis=1, keepdims=True) + epsilon)
+        rows = inputs * scale
+        attn_part = jnp.sum(normed_grad * rows, axis=0, keepdims=True)
+        for j in range(8):
+            gain_out[j : j + 1, :] = attn_part[:, 128 * j : 128 * j + 128]
+
+        def gain(k):
+            device, _ = step_of(k, 1)
+            return remote(gain_out, gain_in.at[me], sm_send.at[3], sm_recv.at[3], device)
+
+        @pl.loop(1, GROUP)
+        def _(k):
+            gain(k).start()
+
+        gain_in[me] = gain_out[...]
+        scaled = normed_grad * again_ref[...]
+        inner = jnp.mean(scaled * rows, axis=1, keepdims=True)
+        hgrad_ref[...] += scale * (scaled - rows * inner)
+
         sum_second(2)
-
         done(small_in.at[pl.ds(0, GROUP - 1)], sm_recv.at[0])
 
         def small_across(n):
@@ -1340,23 +1370,13 @@
         for n in range(1, PLANES):
             small_across(n).start()
 
-        done(all_slots(mid_hbm), c_recv.at[0])
-        done(mid_hbm.at[0, 0], load_sem.at[8])
-        results_in = pltpu.make_async_copy(mid_hbm, mid, load_sem.at[10])
-        results_in.start()
+        sum_second(0)
         results_in.wait()
-        fold_parts(
-            parts_out2,
-            parts_in2,
-            mid,
-            None,
-            posz_ref,
-            posx_ref,
-            part_send2.at[0],
-            part_recv2.at[0],
-        )
-        sum_third(2)
-        sum_second(0)
+        sends = part_send2.at[0], part_recv2.at[0]
+        fold_left(parts_out2, parts_in2, mid, None, posz_ref, *sends)
+        for n in range(2):
+            handed(n).wait_recv()
+            passed_on(n).start()
 
         done(small_y_in.at[pl.ds(0, 3)], sm_recv.at[1])
         totals = small_y_in[0] + small_y_in[1] + small_y_in[2] + small_y_in[3]
@@ -1373,6 +1393,11 @@
         def _(k):
             router_row(k).start()
 
+        sum_second(1)
+        fold_right(parts_out2, parts_in2, mid, None, posx_ref, *sends)
+        sum_third(2)
+        sum_third(0)
+
         done(gain_in.at[pl.ds(0, GROUP - 1)], sm_recv.at[3])
 
         gain_y[...] = jnp.sum(gain_in[...], axis=0)
@@ -1384,13 +1409,6 @@
 
         for n in range(1, PLANES):
             gain_across(n).start()
-
-        sum_second(1)
-        sum_third(0)
-
-        for n in range(2):
-            handed(n).wait_recv()
-            passed_on(n).start()
 
         sum_third(1)
 

time: 237 us -> 222 us (0.937)
  Pallas kernels: 234 us -> 220 us
    pallas_call x1, Pallas kernels: 158 us -> 147 us  [rest(): pl.pallas_call(rest_kernel, out_shape=(shape((tokens, D), bf16), shape((t...]
    pallas_call x1, Pallas kernels: 70 us -> 66.1 us  [front(): pl.pallas_call(front_kernel, out_shape=out_shape, in_specs=[pl.BlockSpec(...]
where the time goes in v8:
time: 222 us
  Pallas kernels  220 us (99%)
    pallas_call x1, Pallas kernels, rest(): pl.pallas_call(rest_kernel, out_shape=(shape((tokens, D), bf16), shape((t...  147 us
    pallas_call x1, Pallas kernels, front(): pl.pallas_call(front_kernel, out_shape=out_shape, in_specs=[pl.BlockSpec(...  66.1 us
    pallas_call x1, Pallas kernels, spread_out(): pl.pallas_call(spread_kernel, grid=(4,), out_shape=(shape((TOKENS, D), bf...  6.1 us

profile of v8, /device:TPU:1, one launch (start us, length us, event | category | flops | bytes accessed | tf_op | source)
XLA Modules:
  0.0 222.0 jit_solution(1398636536660753268)
XLA Ops:
  1.3 0.8 multiply_sine_fusion
  2.1 66.1 %front.1 = (bf16[2,4,4,32,3072]{4,3,2,1,0:T(8,128)(2,1)}, bf16[256,1024]{1,0:T(8,128)(2,1)}, bf16[1024,256]{1,0:T(8,128)(2,1)}, bf16[512,512]{1,0:T(8,128)(2,1)}...) custom-call(s32[1]{0:T(128)S(6)} %copy.27.length_ref, ...), custom_call_target="tpu_custom_call" | custom-call | tf_op jit(solution)/shard_map/front/pallas_call | solution.py:630
  68.3 147.4 %rest.1 = (bf16[256,1024]{1,0:T(8,128)(2,1)}, f32[256,1024]{1,0:T(8,128)}, f32[8,128]{1,0:T(8,128)}, f32[8,128]{1,0:T(8,128)}, f32[32,8,128]{2,1,0:T(8,128)}, /*...) custom-call(s32[1]{0:T(128)S(6)} %copy.27.length_ref, ...), custom_call_target="tpu_custom_call" | custom-call | tf_op jit(solution)/shard_map/rest/pallas_call | solution.py:1524
  215.7 6.1 %spread_out.1 = (bf16[256,1024]{1,0:T(8,128)(2,1)}, f32[256,1024]{1,0:T(8,128)}, f32[32,1024]{1,0:T(8,128)}, f32[32,512]{1,0:T(8,128)}, f32[32,512]{1,0:T(8,128)...) custom-call(bf16[256,1024]{1,0:T(8,128)(2,1)} %get-tuple-element.59., ...), custom_call_target="tpu_custom_call" | custom-call | tf_op jit(solution)/shard_map/spread_out/pallas_call | solution.py:1600
  (2 shorter events, 0.0 us)

commit v9 on v8

--- a/solution.py
+++ b/solution.py
@@ -1,5 +1,6 @@
 import jax
 import jax.numpy as jnp
+import numpy as np
 from jax import lax
 from jax.experimental import pallas as pl
 from jax.experimental.pallas import tpu as pltpu
@@ -143,9 +144,31 @@
     )
 
 
-def spread_done(tok_z, tok_x, sem):
-    done(tok_z.at[pl.ds(1, 3)], sem.at[0])
-    done(tok_x.at[pl.ds(1, 3)], sem.at[1])
+def pass_on(tok_z, tok_x, send_sem, recv_sem):
+    y, r, x, z = place()
+    copies = []
+    for n, (d, sign) in enumerate(((1, 1), (3, -1))):
+        rows = pl.ds(n * 128, 128)
+        for tok, at, device in (
+            (tok_z, 2, moved(0, sign, r)[0]),
+            (tok_x, 3, moved(sign, 0, r)[0]),
+        ):
+            copies.append(
+                remote(
+                    tok.at[d, rows], tok.at[2, rows], send_sem.at[at], recv_sem.at[at], device
+                )
+            )
+    return copies
+
+
+def near_done(tok_z, tok_x, sem):
+    done(tok_z.at[pl.ds(0, 2)], sem.at[0])
+    done(tok_x.at[pl.ds(0, 2)], sem.at[1])
+
+
+def far_done(tok_z, tok_x, sem):
+    done(tok_z.at[2], sem.at[2])
+    done(tok_x.at[2], sem.at[3])
 
 
 def is_local(core, offset):
@@ -214,50 +237,53 @@
     )
 
 
-def part_copies(d, out, into, send_sem, recv_sem):
+def part_copy(d, rows, axis, sign, out, into, send_sem, recv_sem):
     y, r, x, z = place()
-    return (
-        lambda: remote(
-            out.at[d, :, LEFT], into.at[d, :, LEFT], send_sem, recv_sem, moved(0, -d, r)[0]
-        ),
-        lambda: remote(
-            out.at[d, :, RIGHT], into.at[d, :, RIGHT], send_sem, recv_sem, moved(-d, 0, r)[0]
-        ),
-    )
-
-
-def fold_left(out, into, mid, slot_recv, posz_ref, send_sem, recv_sem):
-    @pl.loop(0, 4)
-    def _(d):
-        if slot_recv is not None:
-            done(mid.at[0, 0, :, :, pl.ds(0, 896)], slot_recv.at[d])
-        left = add_up(mid, posz_ref, d, 0)
-
-        @pl.when(d == 0)
-        def _():
-            into[0, :, 0:HALF] = left
-
-        @pl.when(d != 0)
-        def _():
-            out[d, :, 0:HALF] = left
-            part_copies(d, out, into, send_sem, recv_sem)[0]().start()
-
-
-def fold_right(out, into, mid, slot_recv, posx_ref, send_sem, recv_sem):
-    @pl.loop(0, 4)
-    def _(d):
-        if slot_recv is not None:
-            done(mid.at[0, 0, :, :, pl.ds(0, 896)], slot_recv.at[4 + d])
-        right = add_up(mid, posx_ref, d, 1)
-
-        @pl.when(d == 0)
-        def _():
-            into[0, :, HALF:D] = right
-
-        @pl.when(d != 0)
-        def _():
-            out[d, :, HALF:D] = right
-            part_copies(d, out, into, send_sem, recv_sem)[1]().start()
+    cols = (LEFT, RIGHT)[axis]
+    device = moved(sign * axis, sign * (1 - axis), r)[0]
+    part = pl.ds(rows, 128)
+    return remote(out.at[d, part, cols], into.at[d, part, cols], send_sem, recv_sem, device)
+
+
+def fold_start(out, into, mid, slot_recv, posz_ref, posx_ref, sems):
+    send_sem, recv_sem = sems
+    for d in (2, 0, 1, 3):
+        for axis, pos in enumerate((posz_ref, posx_ref)):
+            if slot_recv is not None:
+                done(mid.at[0, 0, :, :, pl.ds(0, 896)], slot_recv.at[4 * axis + d])
+            total = add_up(mid, pos, d, axis)
+            cols = slice(axis * HALF, axis * HALF + HALF)
+            if d == 0:
+                into[0, :, cols] = total
+                continue
+            out[d, :, cols] = total
+            if d == 2:
+                for rows, sign in ((0, -1), (128, 1)):
+                    args = rows, axis, sign, out, into, send_sem.at[0], recv_sem.at[axis]
+                    part_copy(2, *args).start()
+            else:
+                rows, sign = (128, -1) if d == 1 else (0, 1)
+                args = rows, axis, sign, out, into, send_sem.at[0], recv_sem.at[2]
+                part_copy(d, *args).start()
+
+
+def fold_end(out, into, sems):
+    send_sem, recv_sem = sems
+    for axis in range(2):
+        cols = slice(axis * HALF, axis * HALF + HALF)
+        done(into.at[2, :, (LEFT, RIGHT)[axis]], recv_sem.at[axis])
+        for d, rows, sign in ((1, 0, -1), (3, 128, 1)):
+            part = slice(rows, rows + 128)
+            total = out[d, part, cols].astype(jnp.float32) + into[2, part, cols].astype(jnp.float32)
+            out[d, part, cols] = total.astype(jnp.bfloat16)
+            args = rows, axis, sign, out, into, send_sem.at[0], recv_sem.at[2]
+            part_copy(d, *args).start()
+
+
+def folded(into, sems):
+    done(into.at[pl.ds(0, 2)], sems[1].at[2])
+    f32 = jnp.float32
+    return into[0].astype(f32) + (into[1].astype(f32) + into[3].astype(f32))
 
 
 def front_kernel(
@@ -465,8 +491,7 @@
             for copy in cross_step(e, d):
                 copy.start()
 
-    @pl.loop(1, 4)
-    def _(d):
+    for d in (1, 3):
         for copy in spread(d, cot_ref, tok_z, tok_x, first_send, first_recv):
             copy.start()
 
@@ -502,10 +527,20 @@
         for copy in core_step(d):
             copy.start()
 
+    near_done(tok_z, tok_x, first_recv)
+    for copy in pass_on(tok_z, tok_x, first_send, first_recv):
+        copy.start()
+    done(posz_ref.at[pl.ds(1, 3)], pos_recv.at[0])
+    done(posx_ref.at[pl.ds(1, 3)], pos_recv.at[1])
+
+    @pl.loop(0, 2)
+    def _(n):
+        cut_slots(1 + 2 * n)
+
     done(some(4, 2 * D), core_recv.at[0])
 
-    cosine, sine = cos_ref[...], sin_ref[...]
     here = pl.ds(pl.multiple_of(r * tokens, tokens), tokens)
+    cosine, sine = cos_ref[:, here], sin_ref[:, here]
 
     def projected(first):
         weight = w_ref[:, :, :, :, first : first + HALF].reshape(D, HALF)
@@ -533,10 +568,8 @@
     for p in range(2):
         q_ref[HALF * p : HALF * p + HALF, :] = turned(projected(D * p))
 
-    spread_done(tok_z, tok_x, first_recv)
-    done(posz_ref.at[pl.ds(1, 3)], pos_recv.at[0])
-    done(posx_ref.at[pl.ds(1, 3)], pos_recv.at[1])
-    pl.loop(1, 4)(cut_slots)
+    far_done(tok_z, tok_x, first_recv)
+    cut_slots(2)
 
     key_copy.wait_recv()
     value_copy.wait_recv()
@@ -586,7 +619,8 @@
     done(some(3, 256), o_send.at[1])
     done(some(4, 768), o_send.at[2])
     output_core().wait_send()
-    spread_done(tok_z, tok_x, first_send)
+    near_done(tok_z, tok_x, first_send)
+    far_done(tok_z, tok_x, first_send)
     done(posz_ref.at[pl.ds(1, 3)], pos_send.at[0])
     done(posx_ref.at[pl.ds(1, 3)], pos_send.at[1])
     weights_out.wait()
@@ -625,7 +659,7 @@
         pltpu.VMEM((2, 4, 4, CAP, D), bf16),
     ]
     scratch += [pltpu.SemaphoreType.DMA((2,))]
-    for count in (12, 4, 1, 2, 2, 1, 2):
+    for count in (12, 4, 1, 2, 4, 1, 2):
         scratch += [pltpu.SemaphoreType.DMA((count,))] * 2
     return pl.pallas_call(
         front_kernel,
@@ -792,8 +826,8 @@
         ]
         for load in loads:
             load.start()
-        @pl.loop(1, 4)
-        def _(d):
+
+        for d in (1, 3):
             for copy in spread(d, routed_ref, tok_z, tok_x, first_send, first_recv):
                 copy.start()
 
@@ -829,6 +863,10 @@
         def own_slot(k):
             return k == r * CHIPS
 
+        near_done(tok_z, tok_x, first_recv)
+        for copy in pass_on(tok_z, tok_x, first_send, first_recv):
+            copy.start()
+
         @pl.loop(0, GROUP)
         def _(k):
             there, dz, dx = k // CHIPS, lax.rem(k // 4, 4), lax.rem(k, 4)
@@ -847,7 +885,7 @@
             def _():
                 small(k, gate_out, gate_in, 1, 0).start()
 
-        spread_done(tok_z, tok_x, first_recv)
+        far_done(tok_z, tok_x, first_recv)
 
         @pl.loop(0, 4)
         def _(g):
@@ -1006,14 +1044,17 @@
         for n in range(2):
             relayed(n).start()
 
-        sends = part_send.at[0], part_recv.at[0]
-        fold_left(parts_out, parts_in, mid, back_recv, posz_ref, *sends)
-        fold_right(parts_out, parts_in, mid, back_recv, posx_ref, *sends)
-        pl.loop(1, 4)(send_results)
+        part_sems = part_send, part_recv
+        fold_start(parts_out, parts_in, mid, back_recv, posz_ref, posx_ref, part_sems)
 
         @pl.loop(1, 4)
         def _(slot):
             quarter_grads(slot, lax.rem(y + jnp.where(slot == 1, 1, jnp.where(slot == 2, 3, 0)), 4))
+
+            @pl.when(slot == 1)
+            def _():
+                fold_end(parts_out, parts_in, part_sems)
+                pl.loop(1, 4)(send_results)
 
         for n in range(2):
             direct(n).start()
@@ -1030,13 +1071,11 @@
                 jnp.where(picks(pos_ref[at, :]), dots, 0.0), axis=0, keepdims=True
             )
 
-        done(parts_in.at[pl.ds(1, 3)], part_recv.at[0])
-        hgrad_ref[...] = (parts_in[0].astype(f32) + parts_in[1].astype(f32)) + (
-            parts_in[2].astype(f32) + parts_in[3].astype(f32)
-        )
+        hgrad_ref[...] = folded(parts_in, part_sems)
         done(all_slots(outgoing), back_send.at[0])
-        done(parts_out.at[pl.ds(1, 3)], part_send.at[0])
-        spread_done(tok_z, tok_x, first_send)
+        done(parts_out.at[pl.ds(0, 3)], part_send.at[0])
+        near_done(tok_z, tok_x, first_send)
+        far_done(tok_z, tok_x, first_send)
         done(gate_in.at[pl.ds(0, GROUP - 1)], small_send.at[0])
         done(dot_in.at[pl.ds(0, GROUP - 1)], small_send.at[1])
 
@@ -1245,7 +1284,8 @@
 
         key_live = lax.broadcasted_iota(jnp.int32, (2 * tokens, 1), 0) < length_ref[0]
         score_scale = HEAD ** (-0.5)
-        cosine, sine = cos_ref[...], sin_ref[...]
+        here = pl.ds(pl.multiple_of(r * tokens, tokens), tokens)
+        cosine, sine = cos_ref[:, here], sin_ref[:, here]
         first_core = r == 0
 
         def key_head(p, i):
@@ -1372,8 +1412,8 @@
 
         sum_second(0)
         results_in.wait()
-        sends = part_send2.at[0], part_recv2.at[0]
-        fold_left(parts_out2, parts_in2, mid, None, posz_ref, *sends)
+        part_sems = part_send2, part_recv2
+        fold_start(parts_out2, parts_in2, mid, None, posz_ref, posx_ref, part_sems)
         for n in range(2):
             handed(n).wait_recv()
             passed_on(n).start()
@@ -1394,7 +1434,7 @@
             router_row(k).start()
 
         sum_second(1)
-        fold_right(parts_out2, parts_in2, mid, None, posx_ref, *sends)
+        fold_end(parts_out2, parts_in2, part_sems)
         sum_third(2)
         sum_third(0)
 
@@ -1412,10 +1452,7 @@
 
         sum_third(1)
 
-        done(parts_in2.at[pl.ds(1, 3)], part_recv2.at[0])
-        mixture = (parts_in2[0].astype(f32) + parts_in2[1].astype(f32)) + (
-            parts_in2[2].astype(f32) + parts_in2[3].astype(f32)
-        )
+        mixture = folded(parts_in2, part_sems)
         hout_ref[...] = ((middle_ref[...] + mixture) * live).astype(bf16)
 
         done(gain_y_in.at[pl.ds(0, 3)], sm_recv.at[4])
@@ -1426,7 +1463,7 @@
         router_out[...] = router_all[...]
 
         done(all_slots(mid_hbm), c_send.at[0])
-        done(parts_out2.at[pl.ds(1, 3)], part_send2.at[0])
+        done(parts_out2.at[pl.ds(0, 3)], part_send2.at[0])
         done(small_in.at[pl.ds(0, GROUP - 1)], sm_send.at[0])
         done(small_y_in.at[pl.ds(0, 3)], sm_send.at[1])
         done(router_all.at[pl.ds(0, GROUP - 1)], sm_send.at[2])
@@ -1516,7 +1553,7 @@
         pltpu.VMEM((PLANES, 8, 128), f32),
         pltpu.VMEM((GROUP, 8, 128), f32),
     ]
-    for count in (11, 4, 2, 2, 4, 8, 1, 8, 1, 1, 2, 2, 1, 1, 1, 1, 10, 10, 9, 9, 3, 3, 3, 3, 3, 3, 5, 5):
+    for count in (11, 4, 4, 4, 4, 8, 1, 8, 1, 3, 2, 2, 1, 1, 1, 3, 10, 10, 9, 9, 3, 3, 3, 3, 3, 3, 5, 5):
         scratch += [sems((count,))]
     in_specs = [pl.BlockSpec(memory_space=pltpu.SMEM)] + [vmem] * len(arrays)
     for n in (6, 7, 8, 9, 13, 16, 17, 18, 19, 20, 21):
@@ -1659,11 +1696,11 @@
     down_weight,
 ):
     tok_count = hidden_in.shape[0]
-    positions = lax.axis_index("row") * tok_count + jnp.arange(tok_count, dtype=jnp.int32)
     half_dim = HEAD // 2
-    frequency = rotary_base ** (-jnp.arange(half_dim, dtype=jnp.float32) / half_dim)
-    angles = frequency[:, None] * positions.astype(jnp.float32)[None, :]
-    cosine, sine = jnp.cos(angles), jnp.sin(angles)
+    frequency = rotary_base ** (-np.arange(half_dim, dtype=np.float32) / half_dim)
+    positions = np.arange(2 * tok_count, dtype=np.float32)
+    angles = frequency.astype(np.float32)[:, None] * positions[None, :]
+    cosine, sine = jnp.asarray(np.cos(angles)), jnp.asarray(np.sin(angles))
     router_t = router.T
     (
         weights,

time: 222 us -> 210 us (0.946)
  Pallas kernels: 220 us -> 208 us
    pallas_call x1, Pallas kernels: 147 us -> 139 us  [rest(): pl.pallas_call(rest_kernel, out_shape=(shape((tokens, D), bf16), shape((t...]
    pallas_call x1, Pallas kernels: 66.1 us -> 63.5 us  [front(): pl.pallas_call(front_kernel, out_shape=out_shape, in_specs=[pl.BlockSpec(...]
where the time goes in v9:
time: 210 us
  Pallas kernels  208 us (99%)
    pallas_call x1, Pallas kernels, rest(): pl.pallas_call(rest_kernel, out_shape=(shape((tokens, D), bf16), shape((t...  139 us
    pallas_call x1, Pallas kernels, front(): pl.pallas_call(front_kernel, out_shape=out_shape, in_specs=[pl.BlockSpec(...  63.5 us
    pallas_call x1, Pallas kernels, spread_out(): pl.pallas_call(spread_kernel, grid=(4,), out_shape=(shape((TOKENS, D), bf...  6.1 us

profile of v9, /device:TPU:1, one launch (start us, length us, event | category | flops | bytes accessed | tf_op | source)
XLA Modules:
  0.0 209.7 jit_solution(13285220058377900949)
XLA Ops:
  1.3 63.5 %front.1 = (bf16[2,4,4,32,3072]{4,3,2,1,0:T(8,128)(2,1)}, bf16[256,1024]{1,0:T(8,128)(2,1)}, bf16[1024,256]{1,0:T(8,128)(2,1)}, bf16[512,512]{1,0:T(8,128)(2,1)}...) custom-call(s32[1]{0:T(128)S(6)} %copy.29.length_ref, ...), custom_call_target="tpu_custom_call" | custom-call | tf_op jit(solution)/shard_map/front/pallas_call | solution.py:664
  64.8 138.7 %rest.1 = (bf16[256,1024]{1,0:T(8,128)(2,1)}, f32[256,1024]{1,0:T(8,128)}, f32[8,128]{1,0:T(8,128)}, f32[8,128]{1,0:T(8,128)}, f32[32,8,128]{2,1,0:T(8,128)}, /*...) custom-call(s32[1]{0:T(128)S(6)} %copy.29.length_ref, ...), custom_call_target="tpu_custom_call" | custom-call | tf_op jit(solution)/shard_map/rest/pallas_call | solution.py:1561
  203.4 6.1 %spread_out.1 = (bf16[256,1024]{1,0:T(8,128)(2,1)}, f32[256,1024]{1,0:T(8,128)}, f32[32,1024]{1,0:T(8,128)}, f32[32,512]{1,0:T(8,128)}, f32[32,512]{1,0:T(8,128)...) custom-call(bf16[256,1024]{1,0:T(8,128)(2,1)} %get-tuple-element.59., ...), custom_call_target="tpu_custom_call" | custom-call | tf_op jit(solution)/shard_map/spread_out/pallas_call | solution.py:1637

commit v10 on v9

--- a/solution.py
+++ b/solution.py
@@ -343,13 +343,30 @@
     sibling = moved(0, 0, 1 - r)[0]
     meet(False, True)
 
-    for p in range(2):
-        part = slice(256 * p, 256 * p + 256)
-        w_ref[r, z, x, :, D * p : D * p + HALF] = wq_ref[:, HALF * p : HALF * p + HALF]
-        w_ref[r, z, x, :, D * p + HALF : D * p + 768] = wk_ref[:, part]
-        w_ref[r, z, x, :, D * p + 768 : D * p + D] = wv_ref[:, part]
-    front, rear, output = pl.ds(0, D), pl.ds(D, D), pl.ds(2 * D, D)
-    quarter = pl.ds(pl.multiple_of(2 * D + 256 * y, 256), 256)
+    w_ref[r, z, x, :, 0:HALF] = wq_ref[:, 0:HALF]
+    w_ref[r, z, x, :, HALF:768] = wk_ref[:, 0:256]
+    w_ref[r, z, x, :, 768:D] = wv_ref[:, 0:256]
+
+    @pl.when(y == 0)
+    def _():
+        w_ref[r, z, x, :, D : D + HALF] = wq_ref[:, HALF:D]
+
+    @pl.when(y == 1)
+    def _():
+        w_ref[r, z, x, :, D + HALF : D + 768] = wk_ref[:, 256:HALF]
+        w_ref[r, z, x, :, D + 768 : 2 * D] = wv_ref[:, 256:HALF]
+
+    @pl.when(y > 1)
+    def _():
+        own = pl.ds(pl.multiple_of(HALF * (y - 2), HALF), HALF)
+        w_ref[r, z, x, :, pl.ds(pl.multiple_of(D + HALF * y, HALF), HALF)] = wo_ref[:, own]
+
+    front, rear = pl.ds(0, HALF), pl.ds(HALF, HALF)
+
+    def quarter(plane, part=None):
+        if part is None:
+            return pl.ds(pl.multiple_of(D + HALF * plane, HALF), HALF)
+        return pl.ds(pl.multiple_of(D + HALF * plane + 256 * part, 256), 256)
 
     def line_step(d):
         mine_q, mine_o = w_ref.at[r, z, x, :, front], w_ref.at[r, z, x, :, rear]
@@ -366,23 +383,32 @@
             remote(from_x, from_x, w_send.at[1], w_recv.at[8 + d], moved(0, d, r)[0]),
         )
 
-    w_ref[r, z, x, :, quarter] = wo_ref[:, pl.ds(pl.multiple_of(256 * y, 256), 256)]
-
-    def output_line(d):
-        own = w_ref.at[r, z, x, :, quarter]
-        return remote(own, own, o_send.at[0], o_recv.at[0], moved(0, d, r)[0])
-
-    def output_cross(d):
-        own = w_ref.at[r, :, x, :, quarter]
-        return remote(own, own, o_send.at[1], o_recv.at[1], moved(d, 0, r)[0])
-
-    def output_plane(n):
-        own = w_ref.at[r, :, :, :, quarter]
+    def later_line(d):
+        left, right = w_ref.at[r, z, x, :, quarter(y, 0)], w_ref.at[r, z, x, :, quarter(y, 1)]
+        return (
+            remote(left, left, o_send.at[0], o_recv.at[0], moved(0, d, r)[0]),
+            remote(right, right, o_send.at[0], o_recv.at[0], moved(d, 0, r)[0]),
+        )
+
+    def later_cross(d):
+        left, right = w_ref.at[r, :, x, :, quarter(y, 0)], w_ref.at[r, z, :, :, quarter(y, 1)]
+        return (
+            remote(left, left, o_send.at[1], o_recv.at[1], moved(d, 0, r)[0]),
+            remote(right, right, o_send.at[1], o_recv.at[1], moved(0, d, r)[0]),
+        )
+
+    def later_plane(n):
+        own = w_ref.at[r, :, :, :, quarter(y)]
         return remote(own, own, o_send.at[2], o_recv.at[2], plane_shift(n)[0])
 
-    def output_core():
-        own = w_ref.at[r, :, :, :, output]
-        return remote(own, own, o_send.at[3], o_recv.at[3], sibling)
+    def later_relay(n):
+        device, came_from = plane_shift(1 + 2 * n)[0], plane_shift(3 - 2 * n)[1]
+        part = w_ref.at[r, :, :, :, quarter(came_from, n)]
+        return remote(part, part, o_send.at[4], o_recv.at[4], device)
+
+    def later_core(n):
+        part = w_ref.at[r, :, :, :, quarter(plane_shift(n)[1])]
+        return remote(part, part, o_send.at[3], o_recv.at[3], sibling)
 
     def some(rows, width):
         return w_ref.at[0, pl.ds(0, rows), :, :, pl.ds(0, width)]
@@ -404,7 +430,8 @@
     def _(d):
         for copy in cross_step(0, d):
             copy.start()
-        output_line(d).start()
+        for copy in later_line(d):
+            copy.start()
 
     tokens = hidden_ref.shape[0]
     experts_iota = lax.broadcasted_iota(jnp.int32, (EXPERTS, tokens), 0).astype(f32)
@@ -475,11 +502,12 @@
         for copy in pos_step(d):
             copy.start()
 
-    done(w_ref.at[0, 0, pl.ds(0, 3), :, pl.ds(0, 256)], o_recv.at[0])
+    done(w_ref.at[0, 0, pl.ds(0, 3), :, pl.ds(0, HALF)], o_recv.at[0])
 
     @pl.loop(1, 4)
     def _(d):
-        output_cross(d).start()
+        for copy in later_cross(d):
+            copy.start()
 
     @pl.loop(1, 4)
     def _(e):
@@ -516,14 +544,15 @@
     scale = lax.rsqrt(jnp.mean(inputs * inputs, axis=1, keepdims=True) + epsilon)
     normed_ref[...] = (inputs * scale * again_ref[...]).astype(bf16)
 
-    done(some(3, 256), o_recv.at[1])
-
-    for n in range(1, PLANES):
-        output_plane(n).start()
+    done(some(3, HALF), o_recv.at[1])
+
+    for n in (1, 3):
+        later_plane(n).start()
+    later_core(0).start()
 
     @pl.loop(1, 4)
     def _(d):
-        done(some(1, 2 * D), w_recv.at[8 + d])
+        done(some(1, D), w_recv.at[8 + d])
         for copy in core_step(d):
             copy.start()
 
@@ -537,7 +566,7 @@
     def _(n):
         cut_slots(1 + 2 * n)
 
-    done(some(4, 2 * D), core_recv.at[0])
+    done(some(4, D), core_recv.at[0])
 
     here = pl.ds(pl.multiple_of(r * tokens, tokens), tokens)
     cosine, sine = cos_ref[:, here], sin_ref[:, here]
@@ -553,35 +582,42 @@
             parts += [first * cosine - second * sine, second * cosine + first * sine]
         return jnp.concatenate(parts, axis=0).astype(bf16)
 
-    key_copy = remote(
-        k_ref.at[:, here], k_ref.at[:, here], kv_send.at[0], kv_recv.at[0], sibling
-    )
-    value_copy = remote(
-        v_ref.at[:, here], v_ref.at[:, here], kv_send.at[1], kv_recv.at[1], sibling
-    )
-    for p in range(2):
+    def keys_values(p):
+        rows = pl.ds(256 * p, 256)
+        return [
+            remote(
+                ref.at[rows, here],
+                ref.at[rows, here],
+                kv_send.at[2 * p + n],
+                kv_recv.at[2 * p + n],
+                sibling,
+            )
+            for n, ref in enumerate((k_ref, v_ref))
+        ]
+
+    def project(p):
         both = projected(D * p + HALF)
         k_ref[256 * p : 256 * p + 256, here] = turned(both[0:256])
         v_ref[256 * p : 256 * p + 256, here] = both[256:512].astype(bf16)
-    key_copy.start()
-    value_copy.start()
-    for p in range(2):
+        for copy in keys_values(p):
+            copy.start()
         q_ref[HALF * p : HALF * p + HALF, :] = turned(projected(D * p))
 
+    project(0)
     far_done(tok_z, tok_x, first_recv)
     cut_slots(2)
-
-    key_copy.wait_recv()
-    value_copy.wait_recv()
-
-    done(some(4, 768), o_recv.at[2])
-    output_core().start()
+    done(some(4, D), o_recv.at[2])
+    for n in range(2):
+        later_relay(n).start()
+    for n in (1, 3):
+        later_core(n).start()
+    for copy in keys_values(0):
+        copy.wait_recv()
 
     key_live = lax.broadcasted_iota(jnp.int32, (2 * tokens, 1), 0) < length_ref[0]
     score_scale = HEAD ** (-0.5)
 
-    @pl.loop(0, KV_HEADS)
-    def _(g):
+    def attend(g):
         head = pl.ds(pl.multiple_of(g * HEAD, HEAD), HEAD)
         keys, values = k_ref[head, :], v_ref[head, :]
         for j in range(2):
@@ -595,8 +631,15 @@
             probs = (weights * (1.0 / total)).astype(bf16)
             mixed_t[at, :] = dot(values, probs, ((1,), (0,))).astype(bf16)
 
+    pl.loop(0, 4)(attend)
+    done(some(4, HALF), o_recv.at[4])
+    later_core(2).start()
+    done(some(4, 2 * D), o_recv.at[3])
+    project(1)
+    for copy in keys_values(1):
+        copy.wait_recv()
+    pl.loop(4, 8)(attend)
     mixed_ref[...] = mixed_t[...].T
-    output_core().wait_recv()
     weights_out = pltpu.make_async_copy(w_ref, w_hbm, store_sem.at[0])
     weights_out.start()
     w_out = w_ref[:, :, :, :, 2 * D : 3 * D].reshape(D, D)
@@ -612,20 +655,22 @@
     done(all_slots(grads_ref), slot_recv.at[0])
     done(grads_ref.at[0, 0], store_sem.at[1])
     done(all_slots(outgoing), slot_send.at[0])
-    done(w_ref.at[0, 0, pl.ds(0, 3), :, pl.ds(0, 2 * D)], w_send.at[0])
-    done(some(3, 2 * D), w_send.at[1])
-    done(some(4, 2 * D), core_send.at[0])
-    done(w_ref.at[0, 0, pl.ds(0, 3), :, pl.ds(0, 256)], o_send.at[0])
-    done(some(3, 256), o_send.at[1])
-    done(some(4, 768), o_send.at[2])
-    output_core().wait_send()
+    done(w_ref.at[0, 0, pl.ds(0, 3), :, pl.ds(0, D)], w_send.at[0])
+    done(some(3, D), w_send.at[1])
+    done(some(4, D), core_send.at[0])
+    done(w_ref.at[0, 0, pl.ds(0, 3), :, pl.ds(0, HALF)], o_send.at[0])
+    done(some(3, HALF), o_send.at[1])
+    done(some(4, D), o_send.at[2])
+    done(some(4, 2 * D), o_send.at[3])
+    done(some(4, HALF), o_send.at[4])
     near_done(tok_z, tok_x, first_send)
     far_done(tok_z, tok_x, first_send)
     done(posz_ref.at[pl.ds(1, 3)], pos_send.at[0])
     done(posx_ref.at[pl.ds(1, 3)], pos_send.at[1])
     weights_out.wait()
-    key_copy.wait_send()
-    value_copy.wait_send()
+    for p in range(2):
+        for copy in keys_values(p):
+            copy.wait_send()
 
 
 def front(length, *arrays):
@@ -659,7 +704,7 @@
         pltpu.VMEM((2, 4, 4, CAP, D), bf16),
     ]
     scratch += [pltpu.SemaphoreType.DMA((2,))]
-    for count in (12, 4, 1, 2, 4, 1, 2):
+    for count in (12, 5, 1, 4, 4, 1, 2):
         scratch += [pltpu.SemaphoreType.DMA((count,))] * 2
     return pl.pallas_call(
         front_kernel,
@@ -1605,20 +1650,22 @@
     f32 = jnp.float32
     hout_out[...] = hout_ref[...]
     hgrad_out[...] = hgrad_ref[...]
-    for p in range(2):
-        q_out[:, p * HALF : p * HALF + HALF] = own_ref[:, p * D : p * D + HALF]
-        k_out[:, p * 256 : p * 256 + 256] = own_ref[:, p * D + HALF : p * D + 768]
-        v_out[:, p * 256 : p * 256 + 256] = own_ref[:, p * D + 768 : p * D + D]
-    o_out[...] = own_ref[:, 2 * D : 3 * D]
-    for h in range(2):
-        gate_out[0, 128 * h : 128 * h + 128, :] = esum_ref[0, h, 0:128, :].astype(f32)
-        up_out[0, 128 * h : 128 * h + 128, :] = esum_ref[0, h, 128:256, :].astype(f32)
-        down_out[0, 64 * h : 64 * h + 64, 0:HALF] = esum_ref[0, h, 256:320, :].astype(f32)
-        down_out[0, 64 * h : 64 * h + 64, HALF:D] = esum_ref[0, h, 320:384, :].astype(f32)
-    for j in range(8):
-        router_out[:, 128 * j : 128 * j + 128] = router_ref[:, j, :]
-    again_out[...] = again_ref[...]
-    mgain_out[...] = mgain_ref[...]
+    gate_out[0] = esum_ref[0, 0, 0:128, :].astype(f32)
+    up_out[0] = esum_ref[0, 0, 128:256, :].astype(f32)
+    down_out[0, :, 0:HALF] = esum_ref[0, 0, 256:320, :].astype(f32)
+    down_out[0, :, HALF:D] = esum_ref[0, 0, 320:384, :].astype(f32)
+
+    @pl.when(pl.program_id(0) == 0)
+    def _():
+        for p in range(2):
+            q_out[:, p * HALF : p * HALF + HALF] = own_ref[:, p * D : p * D + HALF]
+            k_out[:, p * 256 : p * 256 + 256] = own_ref[:, p * D + HALF : p * D + 768]
+            v_out[:, p * 256 : p * 256 + 256] = own_ref[:, p * D + 768 : p * D + D]
+        o_out[...] = own_ref[:, 2 * D : 3 * D]
+        for j in range(8):
+            router_out[:, 128 * j : 128 * j + 128] = router_ref[:, j, :]
+        again_out[...] = again_ref[...]
+        mgain_out[...] = mgain_ref[...]
 
 
 def spread_out(*arrays):
@@ -1636,7 +1683,7 @@
 
     return pl.pallas_call(
         spread_kernel,
-        grid=(4,),
+        grid=(8,),
         out_shape=(
             shape((TOKENS, D), bf16),
             shape((TOKENS, D), f32),
@@ -1652,24 +1699,24 @@
             shape((8, 128), f32),
         ),
         in_specs=[
-            rows(64, D),
-            rows(64, D),
+            rows(32, D),
+            rows(32, D),
             whole(32, 3 * D),
-            pl.BlockSpec((1, 2, 384, HALF), lambda i: (i, 0, 0, 0)),
+            pl.BlockSpec((1, 1, 384, HALF), lambda i: (i // 2, i % 2, 0, 0)),
             whole(GROUP, 8, 128),
             whole(8, 128),
             whole(8, 128),
         ],
         out_specs=[
-            rows(64, D),
-            rows(64, D),
+            rows(32, D),
+            rows(32, D),
             whole(32, D),
             whole(32, HALF),
             whole(32, HALF),
             whole(32, D),
-            expert_rows(256, HALF),
-            expert_rows(256, HALF),
-            expert_rows(128, D),
+            expert_rows(128, HALF),
+            expert_rows(128, HALF),
+            expert_rows(64, D),
             whole(EXPERTS, D),
             whole(8, 128),
             whole(8, 128),

time: 210 us -> 207 us (0.986)
  Pallas kernels: 208 us -> 205 us
    pallas_call x1, Pallas kernels: 63.5 us -> 58.1 us  [front(): pl.pallas_call(front_kernel, out_shape=out_shape, in_specs=[pl.BlockSpec(...]
where the time goes in v10:
time: 207 us; the launch traced here: 206 us
  Pallas kernels  205 us (99%)
    pallas_call x1, Pallas kernels, rest(): pl.pallas_call(rest_kernel, out_shape=(shape((tokens, D), bf16), shape((t...  139 us
    pallas_call x1, Pallas kernels, front(): pl.pallas_call(front_kernel, out_shape=out_shape, in_specs=[pl.BlockSpec(...  58.1 us
    pallas_call x1, Pallas kernels, spread_out(): pl.pallas_call(spread_kernel, grid=(8,), out_shape=(shape((TOKENS, D), bf...  8.13 us

profile of v10, /device:TPU:1, one launch (start us, length us, event | category | flops | bytes accessed | tf_op | source)
XLA Modules:
  0.0 206.4 jit_solution(3157177262271090024)
XLA Ops:
  1.3 58.1 %front.1 = (bf16[2,4,4,32,3072]{4,3,2,1,0:T(8,128)(2,1)}, bf16[256,1024]{1,0:T(8,128)(2,1)}, bf16[1024,256]{1,0:T(8,128)(2,1)}, bf16[512,512]{1,0:T(8,128)(2,1)}...) custom-call(s32[1]{0:T(128)S(6)} %copy.29.length_ref, ...), custom_call_target="tpu_custom_call" | custom-call | tf_op jit(solution)/shard_map/front/pallas_call | solution.py:709
  59.4 138.7 %rest.1 = (bf16[256,1024]{1,0:T(8,128)(2,1)}, f32[256,1024]{1,0:T(8,128)}, f32[8,128]{1,0:T(8,128)}, f32[8,128]{1,0:T(8,128)}, f32[32,8,128]{2,1,0:T(8,128)}, /*...) custom-call(s32[1]{0:T(128)S(6)} %copy.29.length_ref, ...), custom_call_target="tpu_custom_call" | custom-call | tf_op jit(solution)/shard_map/rest/pallas_call | solution.py:1606
  198.1 8.1 %spread_out.1 = (bf16[256,1024]{1,0:T(8,128)(2,1)}, f32[256,1024]{1,0:T(8,128)}, f32[32,1024]{1,0:T(8,128)}, f32[32,512]{1,0:T(8,128)}, f32[32,512]{1,0:T(8,128)...) custom-call(bf16[256,1024]{1,0:T(8,128)(2,1)} %get-tuple-element.59., ...), custom_call_target="tpu_custom_call" | custom-call | tf_op jit(solution)/shard_map/spread_out/pallas_call | solution.py:1684

commit v11 on v10

--- a/solution.py
+++ b/solution.py
@@ -810,6 +810,7 @@
     sib_recv,
     rs_send,
     rs_recv,
+    rr_recv,
     rs_send2,
     rs_recv2,
     ys_send,
@@ -1286,14 +1287,53 @@
                 for copy in first_step(p, d):
                     copy.start()
 
+        def near_step(p, n, axis, kind):
+            cols = columns(p)[axis]
+            to, far = ((z, x)[axis] + 1 + 2 * n) % 4, ((z, x)[axis] + 2) % 4
+            sign = 1 - 2 * n
+            device = moved(sign * axis, sign * (1 - axis), r)[0]
+            target, slot = (far, 2) if kind == 0 else (to, 1 + 2 * n)
+            half = n if kind != 1 else 1 - n
+            blocks = pl.ds(2 * half, 2)
+            if axis == 0:
+                source = weight_part.at[target, blocks, :, cols]
+            else:
+                source = weight_part.at[blocks, target, :, cols]
+            recv = rr_recv.at[p] if kind == 0 else rs_recv.at[p]
+            return remote(source, rs_in.at[slot, blocks, :, cols], rs_send.at[p], recv, device)
+
+        def sum_start(p, total):
+            weight_part[:, :, :, p * D : p * D + D] = total.astype(bf16).reshape(4, 4, 32, D)
+            for kind in range(2):
+                for axis in range(2):
+                    for n in range(2):
+                        near_step(p, n, axis, kind).start()
+
+        def sum_relay(p):
+            done(rs_in.at[2, :, :, pl.ds(p * D, D)], rr_recv.at[p])
+            for axis in range(2):
+                cols = columns(p)[axis]
+                for n in range(2):
+                    to = lax.rem((z, x)[axis] + 1 + 2 * n, 4)
+                    blocks = pl.ds(2 * n, 2)
+                    more = rs_in[2, blocks, :, cols].astype(f32)
+                    if axis == 0:
+                        mine_too = weight_part[to, blocks, :, cols].astype(f32)
+                        weight_part[to, blocks, :, cols] = (more + mine_too).astype(bf16)
+                    else:
+                        mine_too = weight_part[blocks, to, :, cols].astype(f32)
+                        weight_part[blocks, to, :, cols] = (more + mine_too).astype(bf16)
+                    near_step(p, n, axis, 2).start()
+
         def sum_second(p):
             left, right = columns(p)
 
-            done(rs_in.at[pl.ds(1, 3), :, :, pl.ds(p * D, D)], rs_recv.at[p])
+            count, slots = (3, (1, 2, 3)) if p == 1 else (2, (1, 3))
+            done(rs_in.at[pl.ds(0, count), :, :, pl.ds(p * D, D)], rs_recv.at[p])
 
             total = weight_part[z, :, :, left].astype(f32)
             other = weight_part[:, x, :, right].astype(f32)
-            for d in range(1, 4):
+            for d in slots:
                 total = total + rs_in[d, :, :, left].astype(f32)
                 other = other + rs_in[d, :, :, right].astype(f32)
             rs_out[:, :, left] = total.astype(bf16)
@@ -1325,7 +1365,7 @@
         sib_branch.wait_recv()
         loads[1].wait()
         total = dot(mixed_ref[:, mine], branch_own[...], ((0,), (0,)))
-        sum_first(2, total + dot(mixed_sib[...], branch_sib[...], ((0,), (0,))))
+        sum_start(2, total + dot(mixed_sib[...], branch_sib[...], ((0,), (0,))))
 
         key_live = lax.broadcasted_iota(jnp.int32, (2 * tokens, 1), 0) < length_ref[0]
         score_scale = HEAD ** (-0.5)
@@ -1382,7 +1422,8 @@
             for part in range(2):
                 sib_grads(p, part).wait_recv()
             total = dot(normed_ref[:, mine], grad_t[rows, :], ((0,), (1,)))
-            sum_first(p, total + dot(normed_sib[...], grad_sib[rows, :], ((0,), (1,))))
+            summing = sum_first if p == 1 else sum_start
+            summing(p, total + dot(normed_sib[...], grad_sib[rows, :], ((0,), (1,))))
 
         def inputs_part(p):
             return dot(grad_t[p * D : p * D + D, :], weight(p * D, D), ((0,), (1,)))
@@ -1393,6 +1434,7 @@
         sib_keyval(0).start()
         sib_grads(0, 0).start()
 
+        sum_relay(2)
         heads(1, 0, 4)
         sib_keyval(1).start()
         sib_grads(1, 0).start()
@@ -1419,6 +1461,7 @@
         whole_keyval(1)
         normed_grad = inputs_part(0)
         projections(1)
+        sum_relay(0)
         normed_grad = normed_grad + inputs_part(1)
 
         inputs = hidden_ref[...].astype(f32)
@@ -1598,7 +1641,7 @@
         pltpu.VMEM((PLANES, 8, 128), f32),
         pltpu.VMEM((GROUP, 8, 128), f32),
     ]
-    for count in (11, 4, 4, 4, 4, 8, 1, 8, 1, 3, 2, 2, 1, 1, 1, 3, 10, 10, 9, 9, 3, 3, 3, 3, 3, 3, 5, 5):
+    for count in (11, 4, 4, 4, 4, 8, 1, 8, 1, 3, 2, 2, 1, 1, 1, 3, 10, 10, 9, 9, 3, 3, 3, 3, 3, 3, 3, 5, 5):
         scratch += [sems((count,))]
     in_specs = [pl.BlockSpec(memory_space=pltpu.SMEM)] + [vmem] * len(arrays)
     for n in (6, 7, 8, 9, 13, 16, 17, 18, 19, 20, 21):
@@ -1646,44 +1689,78 @@
     router_out,
     again_out,
     mgain_out,
+    esum,
+    gate,
+    up,
+    down,
+    hout,
+    hgrad,
+    in_sem,
+    out_sem,
 ):
     f32 = jnp.float32
-    hout_out[...] = hout_ref[...]
-    hgrad_out[...] = hgrad_ref[...]
-    gate_out[0] = esum_ref[0, 0, 0:128, :].astype(f32)
-    up_out[0] = esum_ref[0, 0, 128:256, :].astype(f32)
-    down_out[0, :, 0:HALF] = esum_ref[0, 0, 256:320, :].astype(f32)
-    down_out[0, :, HALF:D] = esum_ref[0, 0, 320:384, :].astype(f32)
-
-    @pl.when(pl.program_id(0) == 0)
-    def _():
-        for p in range(2):
-            q_out[:, p * HALF : p * HALF + HALF] = own_ref[:, p * D : p * D + HALF]
-            k_out[:, p * 256 : p * 256 + 256] = own_ref[:, p * D + HALF : p * D + 768]
-            v_out[:, p * 256 : p * 256 + 256] = own_ref[:, p * D + 768 : p * D + D]
-        o_out[...] = own_ref[:, 2 * D : 3 * D]
-        for j in range(8):
-            router_out[:, 128 * j : 128 * j + 128] = router_ref[:, j, :]
-        again_out[...] = again_ref[...]
-        mgain_out[...] = mgain_ref[...]
+
+    def quarter_in(n):
+        return pltpu.make_async_copy(esum_ref.at[n], esum.at[n], in_sem.at[n])
+
+    def quarter_out(n):
+        wide, narrow = pl.ds(256 * n, 256), pl.ds(128 * n, 128)
+        return [
+            pltpu.make_async_copy(source.at[rows], target.at[0, rows], out_sem.at[3 * n + m])
+            for m, (source, target, rows) in enumerate(
+                ((gate, gate_out, wide), (up, up_out, wide), (down, down_out, narrow))
+            )
+        ]
+
+    for n in range(4):
+        quarter_in(n).start()
+    rows_in = [
+        pltpu.make_async_copy(hout_ref, hout, in_sem.at[4]),
+        pltpu.make_async_copy(hgrad_ref, hgrad, in_sem.at[5]),
+    ]
+    rows_out = [
+        pltpu.make_async_copy(hout, hout_out, out_sem.at[12]),
+        pltpu.make_async_copy(hgrad, hgrad_out, out_sem.at[13]),
+    ]
+    for copy in rows_in:
+        copy.start()
+    for n in range(4):
+        quarter_in(n).wait()
+        for h in range(2):
+            rows = pl.ds(256 * n + 128 * h, 128)
+            gate[rows, :] = esum[n, h, 0:128, :].astype(f32)
+            up[rows, :] = esum[n, h, 128:256, :].astype(f32)
+            rows = pl.ds(128 * n + 64 * h, 64)
+            down[rows, 0:HALF] = esum[n, h, 256:320, :].astype(f32)
+            down[rows, HALF:D] = esum[n, h, 320:384, :].astype(f32)
+        for copy in quarter_out(n):
+            copy.start()
+        if n < 2:
+            rows_in[n].wait()
+            rows_out[n].start()
+    for p in range(2):
+        q_out[:, p * HALF : p * HALF + HALF] = own_ref[:, p * D : p * D + HALF]
+        k_out[:, p * 256 : p * 256 + 256] = own_ref[:, p * D + HALF : p * D + 768]
+        v_out[:, p * 256 : p * 256 + 256] = own_ref[:, p * D + 768 : p * D + D]
+    o_out[...] = own_ref[:, 2 * D : 3 * D]
+    for j in range(8):
+        router_out[:, 128 * j : 128 * j + 128] = router_ref[:, j, :]
+    again_out[...] = again_ref[...]
+    mgain_out[...] = mgain_ref[...]
+    for copy in rows_out:
+        copy.wait()
+    for n in range(4):
+        for copy in quarter_out(n):
+            copy.wait()
 
 
 def spread_out(*arrays):
     f32, bf16 = jnp.float32, jnp.bfloat16
     shape = jax.ShapeDtypeStruct
-
-    def whole(*dims):
-        return pl.BlockSpec(dims, lambda i: (0,) * len(dims))
-
-    def rows(count, width):
-        return pl.BlockSpec((count, width), lambda i: (i, 0))
-
-    def expert_rows(count, width):
-        return pl.BlockSpec((1, count, width), lambda i: (0, i, 0))
-
+    vmem = pl.BlockSpec(memory_space=pltpu.VMEM)
+    hbm = pl.BlockSpec(memory_space=pl.ANY)
     return pl.pallas_call(
         spread_kernel,
-        grid=(8,),
         out_shape=(
             shape((TOKENS, D), bf16),
             shape((TOKENS, D), f32),
@@ -1698,29 +1775,19 @@
             shape((8, 128), f32),
             shape((8, 128), f32),
         ),
-        in_specs=[
-            rows(32, D),
-            rows(32, D),
-            whole(32, 3 * D),
-            pl.BlockSpec((1, 1, 384, HALF), lambda i: (i // 2, i % 2, 0, 0)),
-            whole(GROUP, 8, 128),
-            whole(8, 128),
-            whole(8, 128),
+        in_specs=[hbm, hbm, vmem, hbm, vmem, vmem, vmem],
+        out_specs=[hbm, hbm] + [vmem] * 4 + [hbm] * 3 + [vmem] * 3,
+        scratch_shapes=[
+            pltpu.VMEM((4, 2, 384, HALF), bf16),
+            pltpu.VMEM((D, HALF), f32),
+            pltpu.VMEM((D, HALF), f32),
+            pltpu.VMEM((HALF, D), f32),
+            pltpu.VMEM((TOKENS, D), bf16),
+            pltpu.VMEM((TOKENS, D), f32),
+            pltpu.SemaphoreType.DMA((6,)),
+            pltpu.SemaphoreType.DMA((14,)),
         ],
-        out_specs=[
-            rows(32, D),
-            rows(32, D),
-            whole(32, D),
-            whole(32, HALF),
-            whole(32, HALF),
-            whole(32, D),
-            expert_rows(128, HALF),
-            expert_rows(128, HALF),
-            expert_rows(64, D),
-            whole(EXPERTS, D),
-            whole(8, 128),
-            whole(8, 128),
-        ],
+        compiler_params=pltpu.CompilerParams(vmem_limit_bytes=32 << 20),
         name="spread_out",
     )(*arrays)
 

time: 207 us -> 219 us (1.058)
  local copies, waits for them, and re-layouts: 0 us -> 7.39 us
  Pallas kernels: 205 us -> 209 us
    unnamed x0 -> x14, local copies, waits for them, and re-layouts: none -> 7.39 us
    pallas_call x1, Pallas kernels: 139 us -> 146 us  [rest(): pl.pallas_call(rest_kernel, out_shape=(shape((tokens, D), bf16), shape((t...]
    pallas_call x1, Pallas kernels: 8.13 us -> 4.45 us  [spread_out(): pl.pallas_call(spread_kernel, out_shape=(shape((TOKENS, D), bf16), shape(...]
where the time goes in v11:
time: 219 us; the launch traced here: 218 us
  Pallas kernels  209 us (95%)
  local copies, waits for them, and re-layouts  7.39 us (3%)
    pallas_call x1, Pallas kernels, rest(): pl.pallas_call(rest_kernel, out_shape=(shape((tokens, D), bf16), shape((t...  146 us
    pallas_call x1, Pallas kernels, front(): pl.pallas_call(front_kernel, out_shape=out_shape, in_specs=[pl.BlockSpec(...  58.2 us
    unnamed x14, local copies, waits for them, and re-layouts  7.39 us
    pallas_call x1, Pallas kernels, spread_out(): pl.pallas_call(spread_kernel, out_shape=(shape((TOKENS, D), bf16), shape(...  4.45 us

profile of v11, /device:TPU:1, one launch (start us, length us, event | category | flops | bytes accessed | tf_op | source)
XLA Modules:
  0.0 217.5 jit_solution(4264138378177548372)
XLA Ops:
  1.3 58.2 %front.1 = (bf16[2,4,4,32,3072]{4,3,2,1,0:T(8,128)(2,1)}, bf16[256,1024]{1,0:T(8,128)(2,1)}, bf16[1024,256]{1,0:T(8,128)(2,1)}, bf16[512,512]{1,0:T(8,128)(2,1)}...) custom-call(s32[1]{0:T(128)S(6)} %copy.29.length_ref, ...), custom_call_target="tpu_custom_call" | custom-call | tf_op jit(solution)/shard_map/front/pallas_call | solution.py:709
  59.5 145.9 %rest.1 = (bf16[256,1024]{1,0:T(8,128)(2,1)}, f32[256,1024]{1,0:T(8,128)}, f32[8,128]{1,0:T(8,128)}, f32[8,128]{1,0:T(8,128)}, f32[32,8,128]{2,1,0:T(8,128)}, /*...) custom-call(s32[1]{0:T(128)S(6)} %copy.29.length_ref, ...), custom_call_target="tpu_custom_call" | custom-call | tf_op jit(solution)/shard_map/rest/pallas_call | solution.py:1649
  205.5 0.0 copy-start
  205.5 1.9 copy-done
  207.4 0.0 copy-start.1
  207.4 1.2 copy-done.1
  208.6 0.0 copy-start.2
  208.6 1.0 copy-done.2
  209.6 0.0 copy-start.3
  209.6 1.0 copy-done.3
  210.6 0.0 copy-start.4
  210.6 0.9 copy-done.4
  211.5 0.0 copy-start.5
  211.5 0.7 copy-done.5
  212.2 0.0 copy-start.6
  212.2 0.7 copy-done.6
  212.9 4.4 %spread_out.1 = (bf16[256,1024]{1,0:T(8,128)(2,1)}, f32[256,1024]{1,0:T(8,128)}, f32[32,1024]{1,0:T(8,128)}, f32[32,512]{1,0:T(8,128)}, f32[32,512]{1,0:T(8,128)...) custom-call(bf16[256,1024]{1,0:T(8,128)(2,1)S(1)} %copy-done.2, ...), custom_call_target="tpu_custom_call" | custom-call | tf_op jit(solution)/shard_map/spread_out/pallas_call | solution.py:1762
Async XLA Ops:
  205.5 1.9 copy-start
  207.4 1.2 copy-start.1
  208.6 1.0 copy-start.2
  209.6 1.0 copy-start.3
  210.6 0.9 copy-start.4
  211.5 0.7 copy-start.5
  212.2 0.7 copy-start.6

commit v12 on v11

--- a/solution.py
+++ b/solution.py
@@ -810,7 +810,6 @@
     sib_recv,
     rs_send,
     rs_recv,
-    rr_recv,
     rs_send2,
     rs_recv2,
     ys_send,
@@ -1287,53 +1286,14 @@
                 for copy in first_step(p, d):
                     copy.start()
 
-        def near_step(p, n, axis, kind):
-            cols = columns(p)[axis]
-            to, far = ((z, x)[axis] + 1 + 2 * n) % 4, ((z, x)[axis] + 2) % 4
-            sign = 1 - 2 * n
-            device = moved(sign * axis, sign * (1 - axis), r)[0]
-            target, slot = (far, 2) if kind == 0 else (to, 1 + 2 * n)
-            half = n if kind != 1 else 1 - n
-            blocks = pl.ds(2 * half, 2)
-            if axis == 0:
-                source = weight_part.at[target, blocks, :, cols]
-            else:
-                source = weight_part.at[blocks, target, :, cols]
-            recv = rr_recv.at[p] if kind == 0 else rs_recv.at[p]
-            return remote(source, rs_in.at[slot, blocks, :, cols], rs_send.at[p], recv, device)
-
-        def sum_start(p, total):
-            weight_part[:, :, :, p * D : p * D + D] = total.astype(bf16).reshape(4, 4, 32, D)
-            for kind in range(2):
-                for axis in range(2):
-                    for n in range(2):
-                        near_step(p, n, axis, kind).start()
-
-        def sum_relay(p):
-            done(rs_in.at[2, :, :, pl.ds(p * D, D)], rr_recv.at[p])
-            for axis in range(2):
-                cols = columns(p)[axis]
-                for n in range(2):
-                    to = lax.rem((z, x)[axis] + 1 + 2 * n, 4)
-                    blocks = pl.ds(2 * n, 2)
-                    more = rs_in[2, blocks, :, cols].astype(f32)
-                    if axis == 0:
-                        mine_too = weight_part[to, blocks, :, cols].astype(f32)
-                        weight_part[to, blocks, :, cols] = (more + mine_too).astype(bf16)
-                    else:
-                        mine_too = weight_part[blocks, to, :, cols].astype(f32)
-                        weight_part[blocks, to, :, cols] = (more + mine_too).astype(bf16)
-                    near_step(p, n, axis, 2).start()
-
         def sum_second(p):
             left, right = columns(p)
 
-            count, slots = (3, (1, 2, 3)) if p == 1 else (2, (1, 3))
-            done(rs_in.at[pl.ds(0, count), :, :, pl.ds(p * D, D)], rs_recv.at[p])
+            done(rs_in.at[pl.ds(1, 3), :, :, pl.ds(p * D, D)], rs_recv.at[p])
 
             total = weight_part[z, :, :, left].astype(f32)
             other = weight_part[:, x, :, right].astype(f32)
-            for d in slots:
+            for d in range(1, 4):
                 total = total + rs_in[d, :, :, left].astype(f32)
                 other = other + rs_in[d, :, :, right].astype(f32)
             rs_out[:, :, left] = total.astype(bf16)
@@ -1365,7 +1325,7 @@
         sib_branch.wait_recv()
         loads[1].wait()
         total = dot(mixed_ref[:, mine], branch_own[...], ((0,), (0,)))
-        sum_start(2, total + dot(mixed_sib[...], branch_sib[...], ((0,), (0,))))
+        sum_first(2, total + dot(mixed_sib[...], branch_sib[...], ((0,), (0,))))
 
         key_live = lax.broadcasted_iota(jnp.int32, (2 * tokens, 1), 0) < length_ref[0]
         score_scale = HEAD ** (-0.5)
@@ -1422,8 +1382,7 @@
             for part in range(2):
                 sib_grads(p, part).wait_recv()
             total = dot(normed_ref[:, mine], grad_t[rows, :], ((0,), (1,)))
-            summing = sum_first if p == 1 else sum_start
-            summing(p, total + dot(normed_sib[...], grad_sib[rows, :], ((0,), (1,))))
+            sum_first(p, total + dot(normed_sib[...], grad_sib[rows, :], ((0,), (1,))))
 
         def inputs_part(p):
             return dot(grad_t[p * D : p * D + D, :], weight(p * D, D), ((0,), (1,)))
@@ -1434,7 +1393,6 @@
         sib_keyval(0).start()
         sib_grads(0, 0).start()
 
-        sum_relay(2)
         heads(1, 0, 4)
         sib_keyval(1).start()
         sib_grads(1, 0).start()
@@ -1461,7 +1419,6 @@
         whole_keyval(1)
         normed_grad = inputs_part(0)
         projections(1)
-        sum_relay(0)
         normed_grad = normed_grad + inputs_part(1)
 
         inputs = hidden_ref[...].astype(f32)
@@ -1641,7 +1598,7 @@
         pltpu.VMEM((PLANES, 8, 128), f32),
         pltpu.VMEM((GROUP, 8, 128), f32),
     ]
-    for count in (11, 4, 4, 4, 4, 8, 1, 8, 1, 3, 2, 2, 1, 1, 1, 3, 10, 10, 9, 9, 3, 3, 3, 3, 3, 3, 3, 5, 5):
+    for count in (11, 4, 4, 4, 4, 8, 1, 8, 1, 3, 2, 2, 1, 1, 1, 3, 10, 10, 9, 9, 3, 3, 3, 3, 3, 3, 5, 5):
         scratch += [sems((count,))]
     in_specs = [pl.BlockSpec(memory_space=pltpu.SMEM)] + [vmem] * len(arrays)
     for n in (6, 7, 8, 9, 13, 16, 17, 18, 19, 20, 21):
@@ -1787,7 +1744,7 @@
             pltpu.SemaphoreType.DMA((6,)),
             pltpu.SemaphoreType.DMA((14,)),
         ],
-        compiler_params=pltpu.CompilerParams(vmem_limit_bytes=32 << 20),
+        compiler_params=pltpu.CompilerParams(vmem_limit_bytes=60 << 20),
         name="spread_out",
     )(*arrays)
 

time: 219 us -> 205 us (0.936)
  local copies, waits for them, and re-layouts: 7.39 us -> 0 us
  Pallas kernels: 209 us -> 204 us
    unnamed x14 -> x0, local copies, waits for them, and re-layouts: 7.39 us -> none
    pallas_call x1, Pallas kernels: 146 us -> 139 us  [rest(): pl.pallas_call(rest_kernel, out_shape=(shape((tokens, D), bf16), shape((t...]
    pallas_call x1, Pallas kernels: 4.45 us -> 6.88 us  [spread_out(): pl.pallas_call(spread_kernel, out_shape=(shape((TOKENS, D), bf16), shape(...]
where the time goes in v12:
time: 205 us
  Pallas kernels  204 us (100%)
    pallas_call x1, Pallas kernels, rest(): pl.pallas_call(rest_kernel, out_shape=(shape((tokens, D), bf16), shape((t...  139 us
    pallas_call x1, Pallas kernels, front(): pl.pallas_call(front_kernel, out_shape=out_shape, in_specs=[pl.BlockSpec(...  58.1 us
    pallas_call x1, Pallas kernels, spread_out(): pl.pallas_call(spread_kernel, out_shape=(shape((TOKENS, D), bf16), shape(...  6.88 us

profile of v12, /device:TPU:1, one launch (start us, length us, event | category | flops | bytes accessed | tf_op | source)
XLA Modules:
  0.0 205.2 jit_solution(15936476418091151983)
XLA Ops:
  1.3 58.1 %front.1 = (bf16[2,4,4,32,3072]{4,3,2,1,0:T(8,128)(2,1)}, bf16[256,1024]{1,0:T(8,128)(2,1)}, bf16[1024,256]{1,0:T(8,128)(2,1)}, bf16[512,512]{1,0:T(8,128)(2,1)}...) custom-call(s32[1]{0:T(128)S(6)} %copy.29.length_ref, ...), custom_call_target="tpu_custom_call" | custom-call | tf_op jit(solution)/shard_map/front/pallas_call | solution.py:709
  59.4 138.7 %rest.1 = (bf16[256,1024]{1,0:T(8,128)(2,1)}, f32[256,1024]{1,0:T(8,128)}, f32[8,128]{1,0:T(8,128)}, f32[8,128]{1,0:T(8,128)}, f32[32,8,128]{2,1,0:T(8,128)}, /*...) custom-call(s32[1]{0:T(128)S(6)} %copy.29.length_ref, ...), custom_call_target="tpu_custom_call" | custom-call | tf_op jit(solution)/shard_map/rest/pallas_call | solution.py:1606
  198.1 6.9 %spread_out.1 = (bf16[256,1024]{1,0:T(8,128)(2,1)}, f32[256,1024]{1,0:T(8,128)}, f32[32,1024]{1,0:T(8,128)}, f32[32,512]{1,0:T(8,128)}, f32[32,512]{1,0:T(8,128)...) custom-call(bf16[256,1024]{1,0:T(8,128)(2,1)} %get-tuple-element.59., ...), custom_call_target="tpu_custom_call" | custom-call | tf_op jit(solution)/shard_map/spread_out/pallas_call | solution.py:1719

commit v13 on v10

--- a/solution.py
+++ b/solution.py
@@ -1650,10 +1650,14 @@
     f32 = jnp.float32
     hout_out[...] = hout_ref[...]
     hgrad_out[...] = hgrad_ref[...]
-    gate_out[0] = esum_ref[0, 0, 0:128, :].astype(f32)
-    up_out[0] = esum_ref[0, 0, 128:256, :].astype(f32)
-    down_out[0, :, 0:HALF] = esum_ref[0, 0, 256:320, :].astype(f32)
-    down_out[0, :, HALF:D] = esum_ref[0, 0, 320:384, :].astype(f32)
+    for n in range(2):
+        for h in range(2):
+            rows = slice(256 * n + 128 * h, 256 * n + 128 * h + 128)
+            gate_out[0, rows, :] = esum_ref[n, h, 0:128, :].astype(f32)
+            up_out[0, rows, :] = esum_ref[n, h, 128:256, :].astype(f32)
+            rows = slice(128 * n + 64 * h, 128 * n + 64 * h + 64)
+            down_out[0, rows, 0:HALF] = esum_ref[n, h, 256:320, :].astype(f32)
+            down_out[0, rows, HALF:D] = esum_ref[n, h, 320:384, :].astype(f32)
 
     @pl.when(pl.program_id(0) == 0)
     def _():
@@ -1683,7 +1687,7 @@
 
     return pl.pallas_call(
         spread_kernel,
-        grid=(8,),
+        grid=(2,),
         out_shape=(
             shape((TOKENS, D), bf16),
             shape((TOKENS, D), f32),
@@ -1699,28 +1703,29 @@
             shape((8, 128), f32),
         ),
         in_specs=[
-            rows(32, D),
-            rows(32, D),
+            rows(128, D),
+            rows(128, D),
             whole(32, 3 * D),
-            pl.BlockSpec((1, 1, 384, HALF), lambda i: (i // 2, i % 2, 0, 0)),
+            pl.BlockSpec((2, 2, 384, HALF), lambda i: (i, 0, 0, 0)),
             whole(GROUP, 8, 128),
             whole(8, 128),
             whole(8, 128),
         ],
         out_specs=[
-            rows(32, D),
-            rows(32, D),
+            rows(128, D),
+            rows(128, D),
             whole(32, D),
             whole(32, HALF),
             whole(32, HALF),
             whole(32, D),
-            expert_rows(128, HALF),
-            expert_rows(128, HALF),
-            expert_rows(64, D),
+            expert_rows(512, HALF),
+            expert_rows(512, HALF),
+            expert_rows(256, D),
             whole(EXPERTS, D),
             whole(8, 128),
             whole(8, 128),
         ],
+        compiler_params=pltpu.CompilerParams(vmem_limit_bytes=60 << 20),
         name="spread_out",
     )(*arrays)
 

time: 207 us -> 204 us (0.986)
  Pallas kernels: 205 us -> 202 us
    pallas_call x1, Pallas kernels: 8.13 us -> 5.58 us  [spread_out(): pl.pallas_call(spread_kernel, grid=(2,), out_shape=(shape((TOKENS, D), bf...]
where the time goes in v13:
time: 204 us
  Pallas kernels  202 us (99%)
    pallas_call x1, Pallas kernels, rest(): pl.pallas_call(rest_kernel, out_shape=(shape((tokens, D), bf16), shape((t...  139 us
    pallas_call x1, Pallas kernels, front(): pl.pallas_call(front_kernel, out_shape=out_shape, in_specs=[pl.BlockSpec(...  58.1 us
    pallas_call x1, Pallas kernels, spread_out(): pl.pallas_call(spread_kernel, grid=(2,), out_shape=(shape((TOKENS, D), bf...  5.58 us

profile of v13, /device:TPU:1, one launch (start us, length us, event | category | flops | bytes accessed | tf_op | source)
XLA Modules:
  0.0 203.9 jit_solution(168899370587863660)
XLA Ops:
  1.3 58.1 %front.1 = (bf16[2,4,4,32,3072]{4,3,2,1,0:T(8,128)(2,1)}, bf16[256,1024]{1,0:T(8,128)(2,1)}, bf16[1024,256]{1,0:T(8,128)(2,1)}, bf16[512,512]{1,0:T(8,128)(2,1)}...) custom-call(s32[1]{0:T(128)S(6)} %copy.29.length_ref, ...), custom_call_target="tpu_custom_call" | custom-call | tf_op jit(solution)/shard_map/front/pallas_call | solution.py:709
  59.4 138.7 %rest.1 = (bf16[256,1024]{1,0:T(8,128)(2,1)}, f32[256,1024]{1,0:T(8,128)}, f32[8,128]{1,0:T(8,128)}, f32[8,128]{1,0:T(8,128)}, f32[32,8,128]{2,1,0:T(8,128)}, /*...) custom-call(s32[1]{0:T(128)S(6)} %copy.29.length_ref, ...), custom_call_target="tpu_custom_call" | custom-call | tf_op jit(solution)/shard_map/rest/pallas_call | solution.py:1606
  198.1 5.6 %spread_out.1 = (bf16[256,1024]{1,0:T(8,128)(2,1)}, f32[256,1024]{1,0:T(8,128)}, f32[32,1024]{1,0:T(8,128)}, f32[32,512]{1,0:T(8,128)}, f32[32,512]{1,0:T(8,128)...) custom-call(bf16[256,1024]{1,0:T(8,128)(2,1)} %get-tuple-element.59., ...), custom_call_target="tpu_custom_call" | custom-call | tf_op jit(solution)/shard_map/spread_out/pallas_call | solution.py:1688

commit v14 on v13

--- a/solution.py
+++ b/solution.py
@@ -1138,17 +1138,19 @@
     )
 
     def finish_phase(w_ref, q_ref, k_ref, v_ref, normed_ref, mixed_ref, hidden_ref, parts_out2, quarter_sum, relay_out, branch_own, mg_t, grad_t, kv_own, kv_out, weight_part, rs_out, y_out, small_out, small_y, gain_out, gain_y):
+        early, late = pl.ds(0, 2 * D), pl.ds(2 * D, D)
         loads = [
             pltpu.make_async_copy(source, target, load_sem.at[n])
             for n, (source, target) in enumerate(
                 (
-                    (w_hbm, w_ref),
+                    (w_hbm.at[:, :, :, :, late], w_ref.at[:, :, :, :, late]),
                     (mixed_hbm, mixed_ref),
                     (q_hbm, q_ref),
                     (k_hbm, k_ref),
                     (v_hbm, v_ref),
                     (normed_hbm, normed_ref),
                     (hidden_hbm, hidden_ref),
+                    (w_hbm.at[:, :, :, :, early], w_ref.at[:, :, :, :, early]),
                 )
             )
         ]

time: 204 us -> 204 us (level)
  no operation moved by 1% of the time
where the time goes in v14:
time: 204 us
  Pallas kernels  202 us (99%)
    pallas_call x1, Pallas kernels, rest(): pl.pallas_call(rest_kernel, out_shape=(shape((tokens, D), bf16), shape((t...  138 us
    pallas_call x1, Pallas kernels, front(): pl.pallas_call(front_kernel, out_shape=out_shape, in_specs=[pl.BlockSpec(...  58.1 us
    pallas_call x1, Pallas kernels, spread_out(): pl.pallas_call(spread_kernel, grid=(2,), out_shape=(shape((TOKENS, D), bf...  5.58 us

profile of v14, /device:TPU:1, one launch (start us, length us, event | category | flops | bytes accessed | tf_op | source)
XLA Modules:
  0.0 203.6 jit_solution(16474133818744523555)
XLA Ops:
  1.3 58.1 %front.1 = (bf16[2,4,4,32,3072]{4,3,2,1,0:T(8,128)(2,1)}, bf16[256,1024]{1,0:T(8,128)(2,1)}, bf16[1024,256]{1,0:T(8,128)(2,1)}, bf16[512,512]{1,0:T(8,128)(2,1)}...) custom-call(s32[1]{0:T(128)S(6)} %copy.29.length_ref, ...), custom_call_target="tpu_custom_call" | custom-call | tf_op jit(solution)/shard_map/front/pallas_call | solution.py:709
  59.4 138.4 %rest.1 = (bf16[256,1024]{1,0:T(8,128)(2,1)}, f32[256,1024]{1,0:T(8,128)}, f32[8,128]{1,0:T(8,128)}, f32[8,128]{1,0:T(8,128)}, f32[32,8,128]{2,1,0:T(8,128)}, /*...) custom-call(s32[1]{0:T(128)S(6)} %copy.29.length_ref, ...), custom_call_target="tpu_custom_call" | custom-call | tf_op jit(solution)/shard_map/rest/pallas_call | solution.py:1608
  197.9 5.6 %spread_out.1 = (bf16[256,1024]{1,0:T(8,128)(2,1)}, f32[256,1024]{1,0:T(8,128)}, f32[32,1024]{1,0:T(8,128)}, f32[32,512]{1,0:T(8,128)}, f32[32,512]{1,0:T(8,128)...) custom-call(bf16[256,1024]{1,0:T(8,128)(2,1)} %get-tuple-element.59., ...), custom_call_target="tpu_custom_call" | custom-call | tf_op jit(solution)/shard_map/spread_out/pallas_call | solution.py:1690
